TPU v7x, 32 devices: a whole 2x2x4 slice. The times are simulated.
32 devices in a mesh: dp: 4 (over y, x), ctx: 8 (over z, core).
Axes of the slice: x: 2, y: 2, z: 4, core: 2. Of those that a mesh axis runs over, the one named last changes fastest.
Arguments:
- tokens: bfloat16 [4, 1024, 768], P('dp', 'ctx'), may hold values from -6 to 6
- pair_of_rank: int32 [8], replicated, may hold values from 0 to 7, each once
- first_gain: bfloat16 [768], P('dp'), may hold values from 0.25 to 1.75
- first_shift: bfloat16 [768], P('dp'), may hold values from -1.75 to 1.75
- w_input: bfloat16 [768, 2304], P('dp'), may hold values from -0.3125 to 0.3125
- query_bias: bfloat16 [768], P('dp'), may hold values from -1.75 to 1.75
- value_bias: bfloat16 [768], P('dp'), may hold values from -1.75 to 1.75
- w_output: bfloat16 [768, 768], P('dp'), may hold values from -1.25 to 1.25
- output_bias: bfloat16 [768], P('dp'), may hold values from -1.75 to 1.75
- second_gain: bfloat16 [768], P('dp'), may hold values from 0.25 to 1.75
- second_shift: bfloat16 [768], P('dp'), may hold values from -1.75 to 1.75
- w_expand: bfloat16 [768, 3072], P('dp'), may hold values from -0.21875 to 0.21875
- expand_bias: bfloat16 [3072], P('dp'), may hold values from -1.75 to 1.75
- w_contract: bfloat16 [3072, 768], P('dp'), may hold values from -0.109375 to 0.109375
- contract_bias: bfloat16 [768], P('dp'), may hold values from -3.5 to 3.5
- cotangent: bfloat16 [4, 1024, 768], P('dp', 'ctx'), may hold values from -6 to 6
Outputs:
- out: bfloat16 [4, 1024, 768], P('dp', 'ctx')
- grad_tokens: float32 [4, 1024, 768], P('dp', 'ctx')
- grad_first_gain: float32 [768], P('dp')
- grad_first_shift: float32 [768], P('dp')
- grad_input: float32 [768, 2304], P('dp')
- grad_query_bias: float32 [768], P('dp')
- grad_value_bias: float32 [768], P('dp')
- grad_output: float32 [768, 768], P('dp')
- grad_output_bias: float32 [768], P('dp')
- grad_second_gain: float32 [768], P('dp')
- grad_second_shift: float32 [768], P('dp')
- grad_expand: float32 [768, 3072], P('dp')
- grad_expand_bias: float32 [3072], P('dp')
- grad_contract: float32 [3072, 768], P('dp')
- grad_contract_bias: float32 [768], P('dp')
Inputs may be any that keep to these rules, and one draw needn't show every extreme that they name: Context rank r holds the blocks pair_of_rank[r] and 15 - pair_of_rank[r] of every sequence, each of 64 positions; every value occurs once.
All inputs are finite; a program needn't handle non-finite values.
Results may differ from a plain program's by a relative error of at most 0.024.
Values may be sent and summed in bfloat16 or wider, within the bound.
No kernel may reach another device: no remote copies, remote signals or barrier semaphores. Data moves between devices by JAX's collectives and lax.ppermute only.
A program may use at most 256 MiB of HBM per device.

v0:
```python
import math

import jax
import jax.numpy as jnp
from jax import lax
from jax.sharding import PartitionSpec as P

HEADS = 12
HEAD_DIM = 64


NEG_BIG = -1e30
NORM_EPS = 1e-05
GELU_SCALE = 0.7978845608028654
GELU_CUBIC = 0.044715


def gelu_tanh(values):
    return (
        0.5
        * values
        * (1.0 + jnp.tanh(GELU_SCALE * (values + GELU_CUBIC * values * values * values)))
    )


def layer_norm(values, gain_row, shift_row):
    centre = values - jnp.mean(values, axis=-1, keepdims=True)
    spread = jnp.mean(centre * centre, axis=-1, keepdims=True)
    return centre * lax.rsqrt(spread + NORM_EPS) * gain_row + shift_row


def lookup_pair(pair_table, positions):
    ranks_all = jnp.arange(pair_table.shape[0], dtype=jnp.int32)
    return jnp.sum(jnp.where(positions[..., None] == ranks_all, pair_table, 0), axis=-1)


def group_count(blocks, sub_rows):
    chosen_count = 1
    for candidate in range(1, blocks + 1):
        if blocks % candidate == 0 and candidate * sub_rows <= max(512, sub_rows):
            chosen_count = candidate
    return chosen_count


def slot_mask(slot_ids, wanted, rank_count):
    return (slot_ids == wanted).reshape((-1,) + (1,) * (rank_count - 1))


def slot_add(values, slot_ids):
    early_sum = jnp.sum(jnp.where(slot_mask(slot_ids, 0, values.ndim), values, 0.0), axis=0)
    late_sum = jnp.sum(jnp.where(slot_mask(slot_ids, 1, values.ndim), values, 0.0), axis=0)
    return jnp.stack([early_sum, late_sum])


def slot_max(values, slot_ids):
    early_max = jnp.max(jnp.where(slot_mask(slot_ids, 0, values.ndim), values, NEG_BIG), axis=0)
    late_max = jnp.max(jnp.where(slot_mask(slot_ids, 1, values.ndim), values, NEG_BIG), axis=0)
    return jnp.stack([early_max, late_max])


def slot_pick(per_slot, slot_ids):
    return jnp.where(slot_mask(slot_ids, 0, per_slot.ndim), per_slot[0][None], per_slot[1][None])


def query_tiles(blocks, chosen):
    target = chosen.shape + blocks.shape[2:]
    chosen_view = chosen.reshape((-1,) + (1,) * (blocks.ndim - 2))
    late_part = jnp.broadcast_to(blocks[1], target)
    picked = jnp.where(chosen_view, blocks[0], blocks[1])
    return jnp.concatenate([late_part, picked], axis=0)


def key_tiles(blocks, chosen):
    target = chosen.shape + blocks.shape[2:]
    chosen_view = chosen.reshape((-1,) + (1,) * (blocks.ndim - 2))
    early_part = jnp.broadcast_to(blocks[0], target)
    picked = jnp.where(chosen_view, blocks[0], blocks[1])
    return jnp.concatenate([early_part, picked], axis=0)


def tile_slots(chosen):
    late_slot = jnp.where(chosen, 0, 1).astype(jnp.int32)
    query_slot = jnp.concatenate([jnp.ones_like(late_slot), late_slot])
    key_slot = jnp.concatenate([jnp.zeros_like(late_slot), late_slot])
    return (query_slot, key_slot)


def tile_mask(is_own, query_places, key_places):
    visible = key_places[:, None, :] <= query_places[:, :, None]
    visible = jnp.logical_or(visible, jnp.logical_not(is_own)[:, None, None])
    return jnp.concatenate([jnp.ones_like(visible), visible], axis=0)


def tile_scores(tile_query, tile_key, score_scale):
    return (
        jnp.einsum("tqhd,tkhd->thqk", tile_query, tile_key, preferred_element_type=jnp.float32)
        * score_scale
    )


def tile_probs(tile_query, tile_key, tile_visible, row_lse, score_scale):
    scores = tile_scores(tile_query, tile_key, score_scale)
    return jnp.where(tile_visible[:, None], jnp.exp(scores - row_lse[..., None]), 0.0)


def tile_dscore(probs, tile_dout, tile_value, row_delta):
    grad_probs = jnp.einsum(
        "tqhd,tkhd->thqk", tile_dout, tile_value, preferred_element_type=jnp.float32
    )
    return (probs * (grad_probs - row_delta[..., None])).astype(jnp.bfloat16)


def stats_update(running, tile_query, tile_key, query_slot, tile_visible, score_scale):
    run_peak, run_total = running
    visible = tile_visible[:, None]
    masked = jnp.where(visible, tile_scores(tile_query, tile_key, score_scale), NEG_BIG)
    new_peak = jnp.maximum(run_peak, slot_max(jnp.max(masked, axis=-1), query_slot))
    weights = jnp.where(visible, jnp.exp(masked - slot_pick(new_peak, query_slot)[..., None]), 0.0)
    run_total = run_total * jnp.exp(run_peak - new_peak) + slot_add(
        jnp.sum(weights, axis=-1), query_slot
    )
    return (new_peak, run_total)


def values_update(
    running, tile_query, tile_key, tile_value, query_slot, tile_visible, row_lse, score_scale
):
    probs = tile_probs(tile_query, tile_key, tile_visible, row_lse, score_scale)
    part_out = jnp.einsum(
        "thqk,tkhd->tqhd",
        probs.astype(jnp.bfloat16),
        tile_value,
        preferred_element_type=jnp.float32,
    )
    return running + slot_add(part_out, query_slot)


def sweep_piece(carried, pieces, block_rows, my_rank, pair_table, update):
    piece_rows = pieces[0].shape[1]
    sub_rows = math.gcd(piece_rows, block_rows)
    unit_count = piece_rows // sub_rows
    group_size = group_count(unit_count, sub_rows)

    def group_step(loop_index, running):
        offset = loop_index * (group_size * sub_rows)
        slices = tuple(
            (
                lax.dynamic_slice_in_dim(member, offset, group_size * sub_rows, 1).reshape(
                    (2, group_size, sub_rows) + member.shape[2:]
                )
                for member in pieces
            )
        )
        places = offset + jnp.arange(group_size * sub_rows, dtype=jnp.int32).reshape(
            group_size, sub_rows
        )
        far_ranks = places[:, 0] // block_rows
        far_pair = lookup_pair(pair_table, far_ranks)
        return update(running, slices, far_pair, far_ranks == my_rank, places % block_rows, offset)

    return lax.fori_loop(0, unit_count // group_size, group_step, carried)


def per_device(
    tokens,
    pair_of_rank,
    first_gain,
    first_shift,
    w_input,
    query_bias,
    value_bias,
    w_output,
    output_bias,
    second_gain,
    second_shift,
    w_expand,
    expand_bias,
    w_contract,
    contract_bias,
    cotangent,
):
    gathered = (
        lax.all_gather(first_gain, "dp", axis=0, tiled=True),
        lax.all_gather(first_shift, "dp", axis=0, tiled=True),
        lax.all_gather(w_input, "dp", axis=0, tiled=True),
        lax.all_gather(query_bias, "dp", axis=0, tiled=True),
        lax.all_gather(value_bias, "dp", axis=0, tiled=True),
        lax.all_gather(w_output, "dp", axis=0, tiled=True),
        lax.all_gather(output_bias, "dp", axis=0, tiled=True),
        lax.all_gather(second_gain, "dp", axis=0, tiled=True),
        lax.all_gather(second_shift, "dp", axis=0, tiled=True),
        lax.all_gather(w_expand, "dp", axis=0, tiled=True),
        lax.all_gather(expand_bias, "dp", axis=0, tiled=True),
        lax.all_gather(w_contract, "dp", axis=0, tiled=True),
        lax.all_gather(contract_bias, "dp", axis=0, tiled=True),
    )
    (
        full_first_gain,
        full_first_shift,
        full_input,
        full_query_bias,
        full_value_bias,
        full_output,
        full_output_bias,
        full_second_gain,
        full_second_shift,
        full_expand,
        full_expand_bias,
        full_contract,
        full_contract_bias,
    ) = gathered
    model_width = tokens.shape[2]
    block_rows = tokens.shape[1] // 2
    score_scale = HEAD_DIM ** (-0.5)
    slot_view = (2, block_rows, model_width)
    head_view = (2, block_rows, HEADS, HEAD_DIM)
    my_rank = lax.axis_index("ctx")
    my_pair = lookup_pair(pair_of_rank, my_rank)
    own_places = jnp.arange(block_rows, dtype=jnp.int32)[None, :]
    diag_mask = (own_places <= own_places.reshape(-1, 1))[None]
    zero_slot = jnp.zeros((1,), jnp.int32)

    def split_heads(member):
        return member.reshape(member.shape[:3] + (HEADS, HEAD_DIM))

    token_rows = tokens[0].astype(jnp.float32)
    normed_full, first_pullback = jax.vjp(
        layer_norm,
        token_rows,
        full_first_gain.astype(jnp.float32),
        full_first_shift.astype(jnp.float32),
    )
    normed = normed_full.astype(jnp.bfloat16)
    mixed_rows = jnp.dot(normed, full_input, preferred_element_type=jnp.float32)
    query_rows = (mixed_rows[:, :model_width] + full_query_bias.astype(jnp.float32)).astype(
        jnp.bfloat16
    )
    key_rows = mixed_rows[:, model_width : 2 * model_width].astype(jnp.bfloat16)
    value_rows = (mixed_rows[:, 2 * model_width :] + full_value_bias.astype(jnp.float32)).astype(
        jnp.bfloat16
    )
    own_query = query_rows.reshape(head_view)
    own_key = key_rows.reshape(head_view)
    own_value = value_rows.reshape(head_view)
    diag_query = own_query[0][None]
    diag_key = own_key[0][None]
    diag_value = own_value[0][None]
    key_slots = key_rows.reshape(slot_view)
    value_slots = value_rows.reshape(slot_view)
    query_slots = query_rows.reshape(slot_view)

    def stats_group(running, slices, far_pair, is_own, far_places, first_row):
        chosen = far_pair < my_pair
        query_slot, key_slot = tile_slots(chosen)
        return stats_update(
            running,
            query_tiles(own_query[:, None], chosen),
            key_tiles(split_heads(slices[0]), chosen),
            query_slot,
            tile_mask(is_own, own_places, far_places),
            score_scale,
        )

    stats_start = (
        jnp.full((2, HEADS, block_rows), NEG_BIG, jnp.float32),
        jnp.zeros((2, HEADS, block_rows), jnp.float32),
    )
    stats_start = stats_update(stats_start, diag_query, diag_key, zero_slot, diag_mask, score_scale)
    run_peak, run_total = sweep_piece(
        stats_start,
        (lax.all_gather(key_slots, "ctx", axis=1, tiled=True),),
        block_rows,
        my_rank,
        pair_of_rank,
        stats_group,
    )
    row_lse = run_peak + jnp.log(run_total)

    def values_group(running, slices, far_pair, is_own, far_places, first_row):
        chosen = far_pair < my_pair
        query_slot, key_slot = tile_slots(chosen)
        return values_update(
            running,
            query_tiles(own_query[:, None], chosen),
            key_tiles(split_heads(slices[0]), chosen),
            key_tiles(split_heads(slices[1]), chosen),
            query_slot,
            tile_mask(is_own, own_places, far_places),
            slot_pick(row_lse, query_slot),
            score_scale,
        )

    values_start = values_update(
        jnp.zeros(head_view, jnp.float32),
        diag_query,
        diag_key,
        diag_value,
        zero_slot,
        diag_mask,
        row_lse[0][None],
        score_scale,
    )
    attended = sweep_piece(
        values_start,
        (
            lax.all_gather(key_slots, "ctx", axis=1, tiled=True),
            lax.all_gather(value_slots, "ctx", axis=1, tiled=True),
        ),
        block_rows,
        my_rank,
        pair_of_rank,
        values_group,
    )
    attended_low = attended.reshape(2 * block_rows, model_width).astype(jnp.bfloat16)
    middle = (
        token_rows
        + jnp.dot(attended_low, full_output, preferred_element_type=jnp.float32)
        + full_output_bias.astype(jnp.float32)
    )
    normed_full_two, second_pullback = jax.vjp(
        layer_norm,
        middle,
        full_second_gain.astype(jnp.float32),
        full_second_shift.astype(jnp.float32),
    )
    normed_two = normed_full_two.astype(jnp.bfloat16)
    hidden = jnp.dot(
        normed_two, full_expand, preferred_element_type=jnp.float32
    ) + full_expand_bias.astype(jnp.float32)
    active_full, gelu_pullback = jax.vjp(gelu_tanh, hidden)
    active_low = active_full.astype(jnp.bfloat16)
    result = (
        middle
        + jnp.dot(active_low, full_contract, preferred_element_type=jnp.float32)
        + full_contract_bias.astype(jnp.float32)
    )
    block_out = result.astype(jnp.bfloat16)[None]
    back_input, back_output, back_expand, back_contract = (
        lax.all_gather(w_input, "dp", axis=0, tiled=True),
        lax.all_gather(w_output, "dp", axis=0, tiled=True),
        lax.all_gather(w_expand, "dp", axis=0, tiled=True),
        lax.all_gather(w_contract, "dp", axis=0, tiled=True),
    )
    grad_out_low = cotangent[0]
    grad_out = grad_out_low.astype(jnp.float32)
    grad_contract = jnp.einsum(
        "rf,rd->fd", active_low, grad_out_low, preferred_element_type=jnp.float32
    )
    grad_contract_bias = jnp.sum(grad_out, axis=0)
    grad_active = jnp.einsum(
        "rd,fd->rf", grad_out_low, back_contract, preferred_element_type=jnp.float32
    )
    grad_hidden = gelu_pullback(grad_active)[0].astype(jnp.bfloat16)
    grad_expand = jnp.einsum(
        "rd,rf->df", normed_two, grad_hidden, preferred_element_type=jnp.float32
    )
    grad_expand_bias = jnp.sum(grad_hidden.astype(jnp.float32), axis=0)
    grad_normed_two = jnp.einsum(
        "rf,df->rd", grad_hidden, back_expand, preferred_element_type=jnp.float32
    )
    grad_middle_part, grad_second_gain, grad_second_shift = second_pullback(grad_normed_two)
    grad_middle = grad_out + grad_middle_part
    grad_branch = grad_middle.astype(jnp.bfloat16)
    grad_output = jnp.einsum(
        "rd,re->de", attended_low, grad_branch, preferred_element_type=jnp.float32
    )
    grad_output_bias = jnp.sum(grad_branch.astype(jnp.float32), axis=0)
    grad_attended = jnp.einsum(
        "re,de->rd", grad_branch, back_output, preferred_element_type=jnp.float32
    ).astype(jnp.bfloat16)
    own_dout = grad_attended.reshape(head_view)
    dout_slots = grad_attended.reshape(slot_view)
    delta_rows = jnp.sum(own_dout.astype(jnp.float32) * attended, axis=-1)
    row_delta = jnp.transpose(delta_rows, (0, 2, 1))
    lse_rows = jnp.transpose(row_lse, (0, 2, 1))
    far_lse, far_delta = (
        lax.all_gather(lse_rows, "ctx", axis=1, tiled=True),
        lax.all_gather(delta_rows, "ctx", axis=1, tiled=True),
    )
    diag_probs = tile_probs(diag_query, diag_key, diag_mask, row_lse[0][None], score_scale)
    diag_dscore = tile_dscore(diag_probs, own_dout[0][None], diag_value, row_delta[0][None])
    query_start = slot_add(
        jnp.einsum("thqk,tkhd->tqhd", diag_dscore, diag_key, preferred_element_type=jnp.float32)
        * score_scale,
        zero_slot,
    )
    key_start = slot_add(
        jnp.einsum("thqk,tqhd->tkhd", diag_dscore, diag_query, preferred_element_type=jnp.float32)
        * score_scale,
        zero_slot,
    )
    value_start = slot_add(
        jnp.einsum(
            "thqk,tqhd->tkhd",
            diag_probs.astype(jnp.bfloat16),
            own_dout[0][None],
            preferred_element_type=jnp.float32,
        ),
        zero_slot,
    )

    def query_grad_group(running, slices, far_pair, is_own, far_places, first_row):
        chosen = far_pair < my_pair
        query_slot, key_slot = tile_slots(chosen)
        tile_key = key_tiles(split_heads(slices[0]), chosen)
        tile_value = key_tiles(split_heads(slices[1]), chosen)
        probs = tile_probs(
            query_tiles(own_query[:, None], chosen),
            tile_key,
            tile_mask(is_own, own_places, far_places),
            slot_pick(row_lse, query_slot),
            score_scale,
        )
        dscore = tile_dscore(
            probs,
            query_tiles(own_dout[:, None], chosen),
            tile_value,
            slot_pick(row_delta, query_slot),
        )
        part_grad = (
            jnp.einsum("thqk,tkhd->tqhd", dscore, tile_key, preferred_element_type=jnp.float32)
            * score_scale
        )
        return running + slot_add(part_grad, query_slot)

    def key_grad_group(running, slices, far_pair, is_own, far_places, first_row):
        chosen = my_pair < far_pair
        query_slot, key_slot = tile_slots(chosen)
        group_size = far_places.shape[0]
        sub_rows = far_places.shape[1]
        tile_query = query_tiles(split_heads(slices[0]), chosen)
        tile_dout = query_tiles(split_heads(slices[1]), chosen)
        lse_part = lax.dynamic_slice_in_dim(far_lse, first_row, group_size * sub_rows, 1).reshape(
            2, group_size, sub_rows, HEADS
        )
        delta_part = lax.dynamic_slice_in_dim(
            far_delta, first_row, group_size * sub_rows, 1
        ).reshape(2, group_size, sub_rows, HEADS)
        tile_lse = jnp.transpose(query_tiles(lse_part, chosen), (0, 2, 1))
        tile_delta = jnp.transpose(query_tiles(delta_part, chosen), (0, 2, 1))
        tile_key = key_tiles(own_key[:, None], chosen)
        tile_value = key_tiles(own_value[:, None], chosen)
        probs = tile_probs(
            tile_query, tile_key, tile_mask(is_own, far_places, own_places), tile_lse, score_scale
        )
        dscore = tile_dscore(probs, tile_dout, tile_value, tile_delta)
        key_part = (
            jnp.einsum("thqk,tqhd->tkhd", dscore, tile_query, preferred_element_type=jnp.float32)
            * score_scale
        )
        value_part = jnp.einsum(
            "thqk,tqhd->tkhd",
            probs.astype(jnp.bfloat16),
            tile_dout,
            preferred_element_type=jnp.float32,
        )
        return (
            running[0] + slot_add(key_part, key_slot),
            running[1] + slot_add(value_part, key_slot),
        )

    grad_query_sum = sweep_piece(
        query_start,
        (
            lax.all_gather(key_slots, "ctx", axis=1, tiled=True),
            lax.all_gather(value_slots, "ctx", axis=1, tiled=True),
        ),
        block_rows,
        my_rank,
        pair_of_rank,
        query_grad_group,
    )
    grad_key_sum, grad_value_sum = sweep_piece(
        (key_start, value_start),
        (
            lax.all_gather(query_slots, "ctx", axis=1, tiled=True),
            lax.all_gather(dout_slots, "ctx", axis=1, tiled=True),
        ),
        block_rows,
        my_rank,
        pair_of_rank,
        key_grad_group,
    )
    flat_rows = 2 * block_rows
    grad_query_low = grad_query_sum.reshape(flat_rows, model_width).astype(jnp.bfloat16)
    grad_key_low = grad_key_sum.reshape(flat_rows, model_width).astype(jnp.bfloat16)
    grad_value_low = grad_value_sum.reshape(flat_rows, model_width).astype(jnp.bfloat16)
    grad_mixed = jnp.concatenate([grad_query_low, grad_key_low, grad_value_low], axis=1)
    grad_input = jnp.einsum("rd,re->de", normed, grad_mixed, preferred_element_type=jnp.float32)
    grad_query_bias = jnp.sum(grad_query_low.astype(jnp.float32), axis=0)
    grad_value_bias = jnp.sum(grad_value_low.astype(jnp.float32), axis=0)
    grad_normed = jnp.einsum(
        "re,de->rd", grad_mixed, back_input, preferred_element_type=jnp.float32
    )
    grad_token_part, grad_first_gain, grad_first_shift = first_pullback(grad_normed)
    grad_tokens = (grad_middle + grad_token_part)[None]
    grad_local = (
        grad_first_gain,
        grad_first_shift,
        grad_input,
        grad_query_bias,
        grad_value_bias,
        grad_output,
        grad_output_bias,
        grad_second_gain,
        grad_second_shift,
        grad_expand,
        grad_expand_bias,
        grad_contract,
        grad_contract_bias,
    )
    grad_owned = (
        lax.psum_scatter(
            grad_local[0].astype(jnp.bfloat16), "dp", scatter_dimension=0, tiled=True
        ).astype(jnp.float32),
        lax.psum_scatter(
            grad_local[1].astype(jnp.bfloat16), "dp", scatter_dimension=0, tiled=True
        ).astype(jnp.float32),
        lax.psum_scatter(
            grad_local[2].astype(jnp.bfloat16), "dp", scatter_dimension=0, tiled=True
        ).astype(jnp.float32),
        lax.psum_scatter(
            grad_local[3].astype(jnp.bfloat16), "dp", scatter_dimension=0, tiled=True
        ).astype(jnp.float32),
        lax.psum_scatter(
            grad_local[4].astype(jnp.bfloat16), "dp", scatter_dimension=0, tiled=True
        ).astype(jnp.float32),
        lax.psum_scatter(
            grad_local[5].astype(jnp.bfloat16), "dp", scatter_dimension=0, tiled=True
        ).astype(jnp.float32),
        lax.psum_scatter(
            grad_local[6].astype(jnp.bfloat16), "dp", scatter_dimension=0, tiled=True
        ).astype(jnp.float32),
        lax.psum_scatter(
            grad_local[7].astype(jnp.bfloat16), "dp", scatter_dimension=0, tiled=True
        ).astype(jnp.float32),
        lax.psum_scatter(
            grad_local[8].astype(jnp.bfloat16), "dp", scatter_dimension=0, tiled=True
        ).astype(jnp.float32),
        lax.psum_scatter(
            grad_local[9].astype(jnp.bfloat16), "dp", scatter_dimension=0, tiled=True
        ).astype(jnp.float32),
        lax.psum_scatter(
            grad_local[10].astype(jnp.bfloat16), "dp", scatter_dimension=0, tiled=True
        ).astype(jnp.float32),
        lax.psum_scatter(
            grad_local[11].astype(jnp.bfloat16), "dp", scatter_dimension=0, tiled=True
        ).astype(jnp.float32),
        lax.psum_scatter(
            grad_local[12].astype(jnp.bfloat16), "dp", scatter_dimension=0, tiled=True
        ).astype(jnp.float32),
    )
    grad_final = tuple(
        lax.psum(
            (
                grad_owned[0],
                grad_owned[1],
                grad_owned[2],
                grad_owned[3],
                grad_owned[4],
                grad_owned[5],
                grad_owned[6],
                grad_owned[7],
                grad_owned[8],
                grad_owned[9],
                grad_owned[10],
                grad_owned[11],
                grad_owned[12],
            ),
            "ctx",
        )
    )
    return (block_out, grad_tokens) + tuple(grad_final)


def solution(mesh):
    return jax.shard_map(
        per_device,
        mesh=mesh,
        in_specs=(
            P("dp", "ctx", None),
            P(),
            P("dp"),
            P("dp"),
            P("dp", None),
            P("dp"),
            P("dp"),
            P("dp", None),
            P("dp"),
            P("dp"),
            P("dp"),
            P("dp", None),
            P("dp"),
            P("dp", None),
            P("dp"),
            P("dp", "ctx", None),
        ),
        out_specs=(
            P("dp", "ctx", None),
            P("dp", "ctx", None),
            P("dp"),
            P("dp"),
            P("dp", None),
            P("dp"),
            P("dp"),
            P("dp", None),
            P("dp"),
            P("dp"),
            P("dp"),
            P("dp", None),
            P("dp"),
            P("dp", None),
            P("dp"),
        ),
        check_vma=False,
    )
```

profile of v0, /device:TPU:0, one launch (start us, length us, event | category | flops | bytes accessed | tf_op | source)
XLA Modules:
  0.0 670.0 jit_solution(10373780281282297727)
XLA Ops:
  15.8 17.8 %all-reduce.29 = (bf16[768]{0:T(1024)(128)(2,1)S(1)}, bf16[768]{0:T(1024)(128)(2,1)S(1)}, bf16[768]{0:T(1024)(128)(2,1)S(1)}, bf16[768]{0:T(1024)(128)(2,1)S(1)}...) all-reduce(bf16[768]{0:T(1024)(128)(2,1)S(1)} %dynamic-update-slice, ...), channel_id=1, replica_groups=mesh['dp'=4,'ctx'=8] {'dp'}, use_global_device_ids=true, to_apply=%add.11 | all-reduce | flops 5376 | bytes 21504
  35.9 24.1 %all-gather.10.cloned.1.call-done = bf16[768,2304]{1,0:T(8,128)(2,1)} async-done(((bf16[192,2304]{1,0:T(8,128)(2,1)}), bf16[768,2304]{1,0:T(8,128)(2,1)}) %all-gather.10.cloned.1.call-update) | async-done | bytes 3538960 | tf_op jit(solution)/shard_map/all_gather | solution.py:185
  60.0 2.8 fusion.137
  67.3 8.1 %all-gather = bf16[4,1,768]{2,1,0:T(2,128)(2,1)S(1)} all-gather(bf16[1,1,768]{2,1,0:T(2,128)(2,1)S(1)} %reshape.532), channel_id=1, replica_groups=mesh['dp'=4,'ctx'=8] {'dp'}, dimensions={0}, use_global_device_ids=true | all-gather | bytes 7680 | tf_op jit(solution)/shard_map/all_gather | solution.py:193
  83.9 5.2 all-gather.12.cloned.1.call-done
  89.1 9.3 %slice_reduce_fusion.6 = (bf16[512,768]{1,0:T(8,128)(2,1)}, bf16[512,768]{1,0:T(8,128)(2,1)}) fusion(bf16[2,512,768]{2,0,1:T(2,128)(2,1)} %all-gather.12.cloned.1.call-done), kind=kLoop, calls=%fused_computation.78 | loop fusion | bytes 3145728 | tf_op jit(solution)/shard_map/while/body/eval_jaxpr/slice | solution.py:77
  98.4 2.8 reshape.551
  101.1 14.8 %all-gather.14.cloned.1.call-done = bf16[2,512,768]{2,0,1:T(2,128)(2,1)} async-done(((bf16[2,64,768]{2,0,1:T(2,128)(2,1)}), bf16[2,512,768]{2,0,1:T(2,128)(2,1)}) %all-gather.14.cloned.1.call-update) | async-done | bytes 1572880 | tf_op jit(solution)/shard_map/all_gather | solution.py:307
  115.9 9.4 %slice_reduce_fusion.4 = (bf16[512,768]{1,0:T(8,128)(2,1)}, bf16[512,768]{1,0:T(8,128)(2,1)}) fusion(bf16[2,512,768]{2,0,1:T(2,128)(2,1)} %all-gather.14.cloned.1.call-done), kind=kLoop, calls=%fused_computation.76 | loop fusion | bytes 3145728 | tf_op jit(solution)/shard_map/while/body/eval_jaxpr/slice | solution.py:77
  125.2 3.8 reshape.552
  129.0 3.8 reshape.565
  132.8 3.8 reshape.566
  136.5 4.1 copy_select_fusion.2
  141.7 2.3 select_reduce_fusion.9
  144.3 2.4 select_reduce_fusion.8
  147.5 5.0 select_reduce_fusion.7
  154.0 1.8 fusion.138
  156.1 47.6 %all-gather.18.cloned.1.call-done = bf16[768,3072]{1,0:T(8,128)(2,1)} async-done(((bf16[192,3072]{1,0:T(8,128)(2,1)}), bf16[768,3072]{1,0:T(8,128)(2,1)}) %all-gather.18.cloned.1.call-update) | async-done | bytes 4718608 | tf_op jit(solution)/shard_map/all_gather | solution.py:192
  203.7 3.2 convolution_add_fusion
  206.9 55.6 %all-gather.20.cloned.1.call-done = bf16[3072,768]{1,0:T(8,128)(2,1)} async-done(((bf16[768,768]{1,0:T(8,128)(2,1)}), bf16[3072,768]{1,0:T(8,128)(2,1)}) %all-gather.20.cloned.1.call-update) | async-done | bytes 4718608 | tf_op jit(solution)/shard_map/all_gather | solution.py:194
  262.5 5.4 fusion.143
  267.9 2.3 multiply_reduce_fusion.1
  274.3 2.5 convolution_convert_fusion.3
  276.9 4.8 convolution_convert_fusion.1
  283.9 1.8 broadcast_in_dim.698
  285.7 1.7 copy.361
  287.4 1.8 broadcast_in_dim.702
  289.2 1.7 copy.374
  290.8 2.2 reshape.553
  293.0 4.7 convolution_convert_fusion
  297.8 9.6 %slice_reduce_fusion.2 = (bf16[512,768]{1,0:T(8,128)(2,1)}, bf16[512,768]{1,0:T(8,128)(2,1)}) fusion(bf16[2,512,768]{2,0,1:T(2,128)(2,1)} %all-gather.22.cloned.1.call-done), kind=kLoop, calls=%fused_computation.74 | loop fusion | bytes 3145728 | tf_op jit(solution)/shard_map/while/body/eval_jaxpr/slice | solution.py:69
  307.4 3.8 reshape.554
  311.2 3.8 reshape.567
  317.8 15.0 %all_gather.80 = f32[2,512,12]{2,0,1:T(2,128)S(1)} all-gather(f32[2,64,12]{2,0,1:T(2,128)} %copy.363), channel_id=1, replica_groups=mesh['dp'=4,'ctx'=8] {'ctx'}, dimensions={1}, use_global_device_ids=true | all-gather | bytes 55296 | tf_op jit(solution)/shard_map/all_gather | solution.py:377
  334.0 1.7 copy.418
  335.7 1.7 copy.419
  337.4 1.6 fusion.134
  339.0 1.8 broadcast_in_dim.688
  340.8 1.7 copy.343
  342.5 1.8 reshape.504
  344.3 1.7 copy.336
  346.0 2.4 copy.339
  348.4 2.3 multiply_reduce_fusion
  352.1 14.9 %all_gather.82 = f32[2,512,12]{2,0,1:T(2,128)S(1)} all-gather(f32[2,64,12]{2,0,1:T(2,128)} %copy.375), channel_id=1, replica_groups=mesh['dp'=4,'ctx'=8] {'ctx'}, dimensions={1}, use_global_device_ids=true | all-gather | bytes 55296 | tf_op jit(solution)/shard_map/all_gather | solution.py:378
  368.3 1.7 copy.422
  370.0 1.7 copy.423
  382.1 1.5 broadcast_in_dim.689
  383.6 10.0 %select_reduce_fusion.5 = (f32[12,64,64]{1,2,0:T(8,128)}, f32[12,64,64]{1,2,0:T(8,128)}) fusion(pred[16]{0:T(512)(128)(4,1)S(1)} %copy-done.60, pred[16]{0:T(512)(128)(4,1)S(1)} %copy-done.72, f32[16,12,64,64]{2,3,1,0:T(8,128)} %copy-done.3, f32[16,12,64]{2,1,0:T(8,128)S(1)} %broadcast_select_fusion.4, f32[16,12,64]{2,1,0:T(8,128)S(1)} %copy-done.44, ...), kind=kOutput, calls=%fused_computation.7 | convolution fusion | flops 212238336 | bytes 8421408 | tf_op jit(solution)/shard_map/while/body/eval_jaxpr/thqk,tkhd->tqhd/dot_general | solution.py:421
  393.7 9.3 %slice_reduce_fusion = (bf16[512,768]{1,0:T(8,128)(2,1)}, bf16[512,768]{1,0:T(8,128)(2,1)}) fusion(bf16[2,512,768]{2,0,1:T(2,128)(2,1)} %all-gather.24.cloned.1.call-done), kind=kLoop, calls=%fused_computation.72 | loop fusion | bytes 3145728 | tf_op jit(solution)/shard_map/while/body/eval_jaxpr/slice | solution.py:69
  402.9 3.8 reshape.555
  406.7 3.8 reshape.568
  410.5 5.6 copy_select_fusion
  416.6 1.9 fusion.16
  418.9 4.2 fusion.2
  424.7 13.7 %select_reduce_fusion.3 = (f32[12,64,64]{1,2,0:T(8,128)}, f32[12,64,64]{1,2,0:T(8,128)}, f32[12,64,64]{1,2,0:T(8,128)}, f32[12,64,64]{1,2,0:T(8,128)}) fusion(pred[16]{0:T(512)(128)(4,1)S(1)} %copy-done.82, pred[16]{0:T(512)(128)(4,1)S(1)} %copy-done.81, f32[16,12,64,64]{2,3,1,0:T(8,128)} %fusion.2, bf16[8,64,12,64]{3,1,2,0:T(8,128)(2,1)} %copy-done.4, ...), kind=kOutput, calls=%fused_computation.3 | convolution fusion | flops 217645056 | bytes 11960352 | tf_op jit(solution)/shard_map/while/body/eval_jaxpr/thqk,tqhd->tkhd/dot_general | solution.py:448
  438.4 2.2 fusion.65
  440.6 1.9 copy.383
  443.8 3.1 fusion.125
  452.4 3.6 convolution_convert_fusion.2
  457.9 3.6 fusion.122
  461.9 15.3 %all-reduce.28 = (bf16[768]{0:T(1024)(128)(2,1)S(1)}, bf16[768]{0:T(1024)(128)(2,1)S(1)}, bf16[768]{0:T(1024)(128)(2,1)S(1)}, bf16[768]{0:T(1024)(128)(2,1)S(1)}...) all-reduce(bf16[768]{0:T(1024)(128)(2,1)S(1)} %dynamic-update-slice, ...), channel_id=1, replica_groups=mesh['dp'=4,'ctx'=8] {'dp'}, use_global_device_ids=true, to_apply=%add.17 | all-reduce | flops 9984 | bytes 39936
  478.9 4.1 fusion.63
  483.0 34.4 %reduce-scatter.5.cloned.1.call-done = bf16[192,2304]{1,0:T(8,128)(2,1)} async-done(((bf16[768,2304]{1,0:T(8,128)(2,1)}), bf16[192,2304]{1,0:T(8,128)(2,1)}) %reduce-scatter.5.cloned.1.call-update) | async-done | bytes 884752 | tf_op jit(solution)/shard_map/reduce_scatter | solution.py:519
  517.4 145.4 %all-reduce.31 = (f32[192]{0:T(256)}, f32[192]{0:T(256)}, f32[192,2304]{1,0:T(8,128)}, f32[192]{0:T(256)}, f32[192]{0:T(256)}, /*index=5*/f32[192,768]{1,0:T(8,1...) all-reduce(f32[192]{0:T(256)S(1)} %dynamic-slice_convert_fusion.8, ...), channel_id=1, replica_groups=mesh['dp'=4,'ctx'=8] {'ctx'}, use_global_device_ids=true, to_apply=%region_29.30 | all-reduce | flops 1771776 | bytes 10635264 | tf_op jit(solution)/shard_map/psum | solution.py:554
  (327 shorter events, 61.0 us)
Async XLA Ops:
  7.2 52.9 %all-gather.10.cloned.1.call-start = ((), (), s32[]{:S(2)}) async-start(), calls=%async_computation.4 | async-start | bytes 4423680 | tf_op jit(solution)/shard_map/all_gather | solution.py:185
  7.9 81.2 %all-gather.12.cloned.1.call-start = ((), (), s32[]{:S(2)}) async-start(), calls=%async_computation.5 | async-start | bytes 1769472 | tf_op jit(solution)/shard_map/all_gather | solution.py:271
  33.7 29.2 %copy-start.51 = (f32[768]{0:T(1024)}, f32[768]{0:T(1024)S(1)}, u32[]{:S(2)}) copy-start(f32[768]{0:T(1024)S(1)} %convert_element_type.196) | copy-start | bytes 9220
  33.7 29.2 %copy-start.38 = (f32[768]{0:T(1024)}, f32[768]{0:T(1024)S(1)}, u32[]{:S(2)}) copy-start(f32[768]{0:T(1024)S(1)} %convert_element_type.195) | copy-start | bytes 9220
  34.7 28.1 %copy-start.53 = (f32[128]{0:T(128)}, f32[128]{0:T(128)S(1)}, u32[]{:S(2)}) copy-start(f32[128]{0:T(128)S(1)} %broadcast_multiply_fusion.1) | copy-start | bytes 1540
  35.9 27.0 %copy-start.76 = (f32[128]{0:T(128)}, f32[128]{0:T(128)S(1)}, u32[]{:S(2)}) copy-start(f32[128]{0:T(128)S(1)} %fusion.77) | copy-start | bytes 1540
  35.9 27.0 %copy-start.62 = (f32[128]{0:T(128)}, f32[128]{0:T(128)S(1)}, u32[]{:S(2)}) copy-start(f32[128]{0:T(128)S(1)} %fusion.98) | copy-start | bytes 1540
  63.8 52.0 %all-gather.14.cloned.1.call-start = ((), (), s32[]{:S(2)}) async-start(), calls=%async_computation.6 | async-start | bytes 1769472 | tf_op jit(solution)/shard_map/all_gather | solution.py:307
  64.9 12.7 %copy-start.79 = (s32[8]{0:T(128)S(1)}, s32[8]{0:T(128)}, u32[]{:S(2)}) copy-start(s32[8]{0:T(128)} %param.17) | copy-start | bytes 100
  64.9 88.8 %all-gather.16.cloned.1.call-start = ((), (), s32[]{:S(2)}) async-start(), calls=%async_computation.7 | async-start | bytes 1474560 | tf_op jit(solution)/shard_map/all_gather | solution.py:188
  65.5 138.2 %all-gather.18.cloned.1.call-start = ((), (), s32[]{:S(2)}) async-start(), calls=%async_computation.8 | async-start | bytes 5898240 | tf_op jit(solution)/shard_map/all_gather | solution.py:192
  66.1 196.4 %all-gather.20.cloned.1.call-start = ((), (), s32[]{:S(2)}) async-start(), calls=%async_computation.9 | async-start | bytes 5898240 | tf_op jit(solution)/shard_map/all_gather | solution.py:194
  66.6 231.2 %all-gather.22.cloned.1.call-start = ((), (), s32[]{:S(2)}) async-start(), calls=%async_computation.10 | async-start | bytes 1769472 | tf_op jit(solution)/shard_map/all_gather | solution.py:476
  83.3 310.3 %all-gather.24.cloned.1.call-start = ((), (), s32[]{:S(2)}) async-start(), calls=%async_computation.11 | async-start | bytes 1769472 | tf_op jit(solution)/shard_map/all_gather | solution.py:477
  83.8 63.2 %copy-start.40 = (f32[12,64]{1,0:T(8,128)}, f32[12,64]{1,0:T(8,128)S(1)}, u32[]{:S(2)}) copy-start(f32[12,64]{1,0:T(8,128)S(1)} %get-tuple-element.281) | copy-start | bytes 9220
  132.8 3.8 copy-start.68
  140.6 3.4 copy-start.24
  140.6 3.4 copy-start.25
  140.6 6.9 %copy-start.22 = (bf16[8,64,12,64]{3,1,2,0:T(8,128)(2,1)}, bf16[8,64,12,64]{3,1,2,0:T(8,128)(2,1)S(1)}, u32[]{:S(2)}) copy-start(bf16[8,64,12,64]{3,1,2,0:T(8,128)(2,1)S(1)} %get-tuple-element.232) | copy-start | bytes 2359300
  140.6 6.9 %copy-start.23 = (bf16[8,64,12,64]{3,1,2,0:T(8,128)(2,1)}, bf16[8,64,12,64]{3,1,2,0:T(8,128)(2,1)S(1)}, u32[]{:S(2)}) copy-start(bf16[8,64,12,64]{3,1,2,0:T(8,128)(2,1)S(1)} %get-tuple-element.233) | copy-start | bytes 2359300
  144.0 3.5 copy-start.3
  146.9 5.6 copy-start.47
  146.9 5.6 copy-start.48
  147.0 5.5 copy-start.49
  147.1 5.4 copy-start.36
  147.2 5.3 copy-start.43
  147.5 5.5 copy-start.11
  152.9 3.0 copy-start.10
  153.5 50.2 %copy-start.50 = (f32[4,1,768]{2,1,0:T(1,128)S(1)}, f32[4,1,768]{2,1,0:T(1,128)}, u32[]{:S(2)}) copy-start(f32[4,1,768]{2,1,0:T(1,128)} %convert_element_type.252) | copy-start | bytes 36868
  153.7 50.0 %copy-start.20 = (bf16[128,768]{0,1:T(8,128)(2,1)}, bf16[128,768]{0,1:T(8,128)(2,1)S(1)}, u32[]{:S(2)}) copy-start(bf16[128,768]{0,1:T(8,128)(2,1)S(1)} %convert_element_type.205) | copy-start | bytes 589828
  155.9 112.0 %copy-start.55 = (f32[128]{0:T(128)}, f32[128]{0:T(128)S(1)}, u32[]{:S(2)}) copy-start(f32[128]{0:T(128)S(1)} %broadcast_multiply_fusion) | copy-start | bytes 1540
  156.1 111.8 %copy-start.61 = (f32[128]{0:T(128)}, f32[128]{0:T(128)S(1)}, u32[]{:S(2)}) copy-start(f32[128]{0:T(128)S(1)} %fusion.99) | copy-start | bytes 1540
  203.7 58.8 %copy-start.16 = (bf16[1,128,768]{2,1,0:T(8,128)(2,1)S(1)}, bf16[1,128,768]{2,1,0:T(8,128)(2,1)}, u32[]{:S(2)}) copy-start(bf16[1,128,768]{2,1,0:T(8,128)(2,1)} %param.31) | copy-start | bytes 589828
  262.5 5.4 copy-start.1
  267.9 3.4 copy-start.17
  274.3 183.5 %reduce-scatter.7.cloned.1.call-start = ((), (), s32[]{:S(2)}) async-start(), calls=%async_computation.13 | async-start | bytes 1474560 | tf_op jit(solution)/shard_map/reduce_scatter | solution.py:528
  276.8 206.1 %reduce-scatter.9.cloned.1.call-start = ((), (), s32[]{:S(2)}) async-start(), calls=%async_computation.14 | async-start | bytes 5898240 | tf_op jit(solution)/shard_map/reduce_scatter | solution.py:540
  281.7 201.2 %reduce-scatter.11.cloned.1.call-start = ((), (), s32[]{:S(2)}) async-start(), calls=%async_computation.15 | async-start | bytes 5898240 | tf_op jit(solution)/shard_map/reduce_scatter | solution.py:546
  297.8 219.6 %reduce-scatter.5.cloned.1.call-start = ((), (), s32[]{:S(2)}) async-start(), calls=%async_computation.12 | async-start | bytes 4423680 | tf_op jit(solution)/shard_map/reduce_scatter | solution.py:519
  311.1 3.8 copy-start.41
  367.1 9.3 %copy-start.37 = (f32[12,64]{1,0:T(8,128)S(1)}, f32[12,64]{1,0:T(8,128)}, u32[]{:S(2)}) copy-start(f32[12,64]{1,0:T(8,128)} %copy-done.36) | copy-start | bytes 9220
  374.1 5.5 copy-start.15
  376.4 4.2 copy-start.59
  377.6 3.1 copy-start.19
  377.6 3.1 copy-start.69
  380.7 2.9 copy-start.34
  406.7 3.8 copy-start.29
  406.7 3.8 copy-start.30
  406.7 3.8 copy-start.70
  418.5 4.6 copy-start
  438.4 5.4 copy-start.26
  438.4 5.4 copy-start.27
  448.2 4.2 copy-start.39
  448.2 4.2 copy-start.52
  448.2 4.2 copy-start.54
  452.4 3.6 copy-start.12
  457.9 3.6 copy-start.77
  457.9 3.7 copy-start.63
  457.9 3.9 copy-start.64
  457.9 4.0 copy-start.65
  457.9 4.0 copy-start.66
  457.9 4.0 copy-start.67
  457.9 20.0 %copy-start.75 = (f32[128]{0:T(128)S(1)}, f32[128]{0:T(128)}, u32[]{:S(2)}) copy-start(f32[128]{0:T(128)} %copy-done.74) | copy-start | bytes 1540
  478.8 38.5 %copy-start.35 = (bf16[192,768]{1,0:T(8,128)(2,1)S(1)}, bf16[192,768]{1,0:T(8,128)(2,1)}, u32[]{:S(2)}) copy-start(bf16[192,768]{1,0:T(8,128)(2,1)} %reduce-scatter.7.cloned.1.call-done) | copy-start | bytes 884740
  (31 other events, 59.6 us)
Sparse Core Ops, SparseCore 0:
  9.9 50.1 all-gather.9
  64.0 25.0 all-gather.11
  91.3 24.5 all-gather.13
  117.6 27.2 all-gather.15
  146.6 57.0 all-gather.17
  205.3 57.0 all-gather.19
  264.1 25.0 all-gather.21
  291.4 24.5 all-gather.23
  318.9 28.0 reduce-scatter.6
  349.9 57.0 reduce-scatter.8
  410.0 57.0 reduce-scatter.10
  470.1 47.2 reduce-scatter.4
where the time goes:
time: 676 us; the launch traced here: 670 us
  blocking collectives  217 us (32%)
  waiting for transfers between devices  184 us (27%)
  local copies, waits for them, and re-layouts  132 us (20%)
  matrix products  81.3 us (12%)
  other arithmetic  37.1 us (5%)
  between operations  17.9 us (3%)
    psum x1, blocking collectives, per_device(): lax.psum((grad_owned[0], grad_owned[1], grad_owned[2], grad_owned[3], gra...  145 us
    all_gather x1, waiting for transfers between devices, per_device(): lax.all_gather(w_contract, 'dp', axis=0, tiled=True)  55.6 us
    all_gather x1, waiting for transfers between devices, per_device(): lax.all_gather(w_expand, 'dp', axis=0, tiled=True)  47.6 us
    reduce_scatter x1, waiting for transfers between devices, per_device(): lax.psum_scatter(grad_local[2].astype(jnp.bfloat16), 'dp', scatter_dimens...  34.4 us
    unnamed x2, blocking collectives  33.2 us
    all_gather x1, waiting for transfers between devices, per_device(): lax.all_gather(w_input, 'dp', axis=0, tiled=True)  24.1 us
    slice x4, local copies, waits for them, and re-layouts, key_tiles(): picked = jnp.where(chosen_view, blocks[0], blocks[1])  19.9 us
    slice x2, local copies, waits for them, and re-layouts, query_tiles(): picked = jnp.where(chosen_view, blocks[0], blocks[1])  18.8 us
  transfers between devices with their start and end apart: 12, of which 6 were waited for; matrix products, arithmetic and copies ran while one was open for 37% of the time, Pallas kernels for 0%

commit v1 on v0

--- a/solution.py
+++ b/solution.py
@@ -3,6 +3,8 @@
 import jax
 import jax.numpy as jnp
 from jax import lax
+from jax.experimental import pallas as pl
+from jax.experimental.pallas import tpu as pltpu
 from jax.sharding import PartitionSpec as P
 
 HEADS = 12
@@ -573,9 +575,773 @@
     return (block_out, grad_tokens) + tuple(grad_final)
 
 
+VMEM_BYTES = 40 * 1024 * 1024
+
+
+def mm(left, right):
+    return lax.dot_general(
+        left, right, (((1,), (0,)), ((), ())), preferred_element_type=jnp.float32
+    )
+
+
+def mm_nt(left, right):
+    return lax.dot_general(
+        left, right, (((1,), (1,)), ((), ())), preferred_element_type=jnp.float32
+    )
+
+
+def mm_tn(left, right):
+    return lax.dot_general(
+        left, right, (((0,), (0,)), ((), ())), preferred_element_type=jnp.float32
+    )
+
+
+def aligned(index, size):
+    return pl.ds(pl.multiple_of(index * size, size), size)
+
+
+def norm_stats(values):
+    centre = values - jnp.mean(values, axis=-1, keepdims=True)
+    spread = jnp.mean(centre * centre, axis=-1, keepdims=True)
+    scale = lax.rsqrt(spread + NORM_EPS)
+    return centre * scale, scale
+
+
+def norm_back(grad_normed, gain_row, xhat, scale):
+    weighted = grad_normed * gain_row
+    return scale * (
+        weighted
+        - jnp.mean(weighted, axis=-1, keepdims=True)
+        - xhat * jnp.mean(weighted * xhat, axis=-1, keepdims=True)
+    )
+
+
+def column_sums(values):
+    return jnp.sum(values, axis=0, keepdims=True)
+
+
+def shape_of(dims, dtype):
+    return jax.ShapeDtypeStruct(dims, dtype)
+
+
+def local_call(kernel, name, outs, args, scalars=0, scratch=(), flops=0):
+    moved = sum(math.prod(a.shape) * a.dtype.itemsize for a in tuple(args) + tuple(outs))
+    return pl.pallas_call(
+        kernel,
+        out_shape=tuple(outs),
+        in_specs=[pl.BlockSpec(memory_space=pltpu.SMEM)] * scalars
+        + [pl.BlockSpec(memory_space=pltpu.VMEM)] * (len(args) - scalars),
+        out_specs=tuple(pl.BlockSpec(memory_space=pltpu.VMEM) for _ in outs),
+        scratch_shapes=list(scratch),
+        compiler_params=pltpu.CompilerParams(vmem_limit_bytes=VMEM_BYTES),
+        cost_estimate=pl.CostEstimate(flops=flops, bytes_accessed=moved, transcendentals=0),
+        name=name,
+    )(*args)
+
+
+def place_of_block(pair_ref, info_ref, ranks, step, half, other_core):
+    core = jnp.bitwise_xor(info_ref[2], other_core)
+    rank = 2 * jnp.bitwise_xor(info_ref[1], step) + core
+    pair = pair_ref[rank]
+    return pair if half == 0 else 2 * ranks - 1 - pair
+
+
+def fill_mask(bias_ref, pair_ref, info_ref, ranks, parts, block):
+    rows = 2 * parts * block
+    lanes = lax.broadcasted_iota(jnp.int32, (1, rows), 1)
+    query_place = lanes % block
+    for step in range(parts):
+        for half in range(2):
+            place = place_of_block(pair_ref, info_ref, ranks, step, half, 0)
+            query_place = query_place + jnp.where(
+                lanes // block == 2 * step + half, place * block, 0
+            )
+    ahead = lax.broadcasted_iota(jnp.int32, (block, rows), 0) - query_place
+    for other in range(2):
+        for step in range(parts):
+            for half in range(2):
+                place = place_of_block(pair_ref, info_ref, ranks, step, half, other)
+                start = other * rows + (2 * step + half) * block
+                bias_ref[start : start + block, :] = jnp.where(
+                    ahead <= -place * block, 0.0, NEG_BIG
+                )
+
+
+def head_parallel(ranks, chips, seq_parts):
+    parts = chips
+    hw = HEADS // chips * HEAD_DIM
+
+    def core_swap(member):
+        return lax.ppermute(member, "ctx", [(i, i ^ 1) for i in range(ranks)])
+
+    def chip_swap(member, step):
+        return lax.ppermute(
+            member, "ctx", [(i, 2 * ((i // 2) ^ step) + i % 2) for i in range(ranks)]
+        )
+
+    def seq_swap(member, step):
+        return lax.ppermute(member, "dp", [(i, i ^ step) for i in range(seq_parts)])
+
+    def per_device_heads(
+        tokens,
+        pair_of_rank,
+        first_gain,
+        first_shift,
+        w_input,
+        query_bias,
+        value_bias,
+        w_output,
+        output_bias,
+        second_gain,
+        second_shift,
+        w_expand,
+        expand_bias,
+        w_contract,
+        contract_bias,
+        cotangent,
+    ):
+        bf, f32 = jnp.bfloat16, jnp.float32
+        rows, width = tokens.shape[1:]
+        block = rows // 2
+        own_width = width // seq_parts
+        ff = expand_bias.shape[0]
+        total = parts * rows
+        half_width = width // 2
+        half_ff = ff // 2
+        sub = own_width // parts
+        half_own = own_width // 2
+        small_rows = 16
+        others = range(1, parts)
+        seq_id = lax.axis_index("dp")
+        rank = lax.axis_index("ctx")
+        chip = rank // 2
+        core = rank % 2
+        info = jnp.stack([seq_id, chip, core]).astype(jnp.int32)
+
+        own_tokens = tokens[0]
+        token_parts = [own_tokens] + [chip_swap(own_tokens, k) for k in others]
+        small_own = jnp.stack(
+            [
+                first_gain,
+                first_shift,
+                query_bias,
+                value_bias,
+                output_bias,
+                second_gain,
+                second_shift,
+                contract_bias,
+            ]
+        )
+        small_own = jnp.pad(small_own, ((0, small_rows - 8), (0, 3 * hw - own_width)))
+        w_heads = jnp.concatenate(
+            [
+                lax.dynamic_slice(w_input, (0, base * width + chip * hw), (own_width, hw))
+                for base in range(3)
+            ],
+            axis=1,
+        )
+        packed = jnp.concatenate([w_heads, small_own], axis=0)
+        packed_parts = [packed] + [seq_swap(packed, j) for j in others]
+        out_parts = [w_output] + [seq_swap(w_output, j) for j in others]
+        expand_own = [
+            lax.dynamic_slice(w_expand, (0, jnp.bitwise_xor(seq_id, j) * ff), (own_width, ff))
+            for j in range(seq_parts)
+        ]
+        expand_parts = [expand_own[0]] + [seq_swap(expand_own[j], j) for j in others]
+        own_cot = cotangent[0]
+        cot_parts = [own_cot] + [seq_swap(own_cot, j) for j in others]
+
+        def qkv_kernel(info_ref, *refs):
+            toks, packs = refs[:parts], refs[parts : 2 * parts]
+            q_ref, kv_ref, normed_ref, w_ref, vec_ref, vec_scr = refs[2 * parts :]
+            for j in range(parts):
+                place = jnp.bitwise_xor(info_ref[0], j)
+                w_ref[aligned(place, own_width), :] = packs[j][0:own_width, :]
+                vec_scr[place] = packs[j][own_width : own_width + small_rows, 0:own_width].astype(
+                    f32
+                )
+            vectors = jnp.concatenate([vec_scr[j] for j in range(parts)], axis=1)
+            vec_ref[...] = vectors
+            chosen = vec_scr[info_ref[1]]
+            for k in range(parts):
+                xhat, _ = norm_stats(toks[k][...].astype(f32))
+                normed_ref[k * rows : (k + 1) * rows, :] = (
+                    xhat * vectors[0:1] + vectors[1:2]
+                ).astype(bf)
+            mixed = mm(normed_ref[...], w_ref[...])
+            q_ref[...] = (mixed[:, 0:hw] + chosen[2:3]).astype(bf)
+            kv_ref[:, 0:hw] = mixed[:, hw : 2 * hw].astype(bf)
+            kv_ref[:, hw : 2 * hw] = (mixed[:, 2 * hw :] + chosen[3:4]).astype(bf)
+
+        query, own_kv, normed, w_heads_full, vectors = local_call(
+            qkv_kernel,
+            "project",
+            [
+                shape_of((total, hw), bf),
+                shape_of((total, 2 * hw), bf),
+                shape_of((total, width), bf),
+                shape_of((width, 3 * hw), bf),
+                shape_of((small_rows, width), f32),
+            ],
+            [info] + token_parts + packed_parts,
+            scalars=1,
+            scratch=[pltpu.VMEM((parts, small_rows, own_width), f32)],
+            flops=2 * total * width * 3 * hw,
+        )
+        far_kv = core_swap(own_kv)
+
+        head_count = hw // HEAD_DIM
+        scale = HEAD_DIM ** (-0.5)
+
+        def head_columns(ref, base, head):
+            start = base + head * HEAD_DIM
+            return ref[:, start : start + HEAD_DIM]
+
+        def attend_kernel(info_ref, pair_ref, q_ref, kv_ref, far_ref, *refs):
+            outs = refs[:parts]
+            flat_ref, lse_ref, bias_ref = refs[parts:]
+            fill_mask(bias_ref, pair_ref, info_ref, ranks, parts, block)
+            columns = []
+            for head in range(head_count):
+                keys = jnp.concatenate(
+                    [head_columns(kv_ref, 0, head), head_columns(far_ref, 0, head)], axis=0
+                )
+                values = jnp.concatenate(
+                    [head_columns(kv_ref, hw, head), head_columns(far_ref, hw, head)], axis=0
+                )
+                scores = mm_nt(keys, head_columns(q_ref, 0, head)) * scale + bias_ref[...]
+                peak = jnp.max(scores, axis=0, keepdims=True)
+                weights = jnp.exp(scores - peak)
+                mass = jnp.sum(weights, axis=0, keepdims=True)
+                lse_ref[head : head + 1, :] = peak + jnp.log(mass)
+                mixed = mm_tn(values, weights.astype(bf)) / mass
+                flat_ref[head * HEAD_DIM : (head + 1) * HEAD_DIM, :] = mixed
+            attended = flat_ref[...].T.astype(bf)
+            for k in range(parts):
+                outs[k][...] = attended[k * rows : (k + 1) * rows]
+
+        attend_out = local_call(
+            attend_kernel,
+            "attend",
+            [shape_of((rows, hw), bf)] * parts
+            + [shape_of((hw, total), f32), shape_of((8, total), f32)],
+            [info, pair_of_rank, query, own_kv, far_kv],
+            scalars=2,
+            scratch=[pltpu.VMEM((2 * total, total), f32)],
+            flops=2 * 2 * head_count * 2 * total * total * HEAD_DIM,
+        )
+        flat_attended, row_lse = attend_out[parts:]
+        att_parts = [attend_out[0]] + [chip_swap(attend_out[k], k) for k in others]
+
+        def middle_kernel(info_ref, tok_ref, vec_ref, *refs):
+            atts, outs = refs[:parts], refs[parts : 2 * parts]
+            mid_ref, normed_ref, w_scr = refs[2 * parts :]
+            for j in range(parts):
+                w_scr[jnp.bitwise_xor(info_ref[0], j)] = outs[j][...]
+            middle = tok_ref[...].astype(f32) + vec_ref[4:5]
+            for k in range(parts):
+                middle = middle + mm(atts[k][...], w_scr[jnp.bitwise_xor(info_ref[1], k)])
+            mid_ref[...] = middle
+            xhat, _ = norm_stats(middle)
+            normed_ref[...] = (xhat * vec_ref[5:6] + vec_ref[6:7]).astype(bf)
+
+        middle, own_normed_two = local_call(
+            middle_kernel,
+            "middle",
+            [shape_of((rows, width), f32), shape_of((rows, width), bf)],
+            [info, own_tokens, vectors] + att_parts + out_parts,
+            scalars=1,
+            scratch=[pltpu.VMEM((parts, own_width, width), bf)],
+            flops=2 * rows * width * width,
+        )
+        n2_parts = [own_normed_two] + [seq_swap(own_normed_two, j) for j in others]
+
+        def ffn_kernel(info_ref, bias_ref, wc_ref, *refs):
+            n2s = refs[:parts]
+            wes = refs[parts : 2 * parts]
+            cots = refs[2 * parts : 3 * parts]
+            gns = refs[3 * parts : 4 * parts]
+            active_ref, gh_ref, n2_ref, cot_ref, w_scr = refs[4 * parts :]
+            for j in range(parts):
+                w_scr[aligned(jnp.bitwise_xor(info_ref[0], j), own_width), :] = wes[j][...]
+                n2_ref[j * rows : (j + 1) * rows, :] = n2s[j][...]
+                cot_ref[j * rows : (j + 1) * rows, :] = cots[j][...]
+            hidden = mm(n2_ref[...], w_scr[...]) + bias_ref[...].astype(f32)
+            square = hidden * hidden
+            curve = jnp.tanh(GELU_SCALE * hidden * (1.0 + GELU_CUBIC * square))
+            active_ref[...] = (0.5 * hidden * (1.0 + curve)).astype(bf)
+            slope = 0.5 * (1.0 + curve) + 0.5 * hidden * (1.0 - curve * curve) * GELU_SCALE * (
+                1.0 + 3.0 * GELU_CUBIC * square
+            )
+            gh_ref[...] = (mm_nt(cot_ref[...], wc_ref[...]) * slope).astype(bf)
+            grad = mm_nt(gh_ref[...], w_scr[...]).astype(bf)
+            for j in range(parts):
+                gns[j][...] = grad[j * rows : (j + 1) * rows]
+
+        ffn_out = local_call(
+            ffn_kernel,
+            "feed",
+            [shape_of((rows, width), bf)] * parts
+            + [
+                shape_of((total, ff), bf),
+                shape_of((total, ff), bf),
+                shape_of((total, width), bf),
+                shape_of((total, width), bf),
+            ],
+            [info, expand_bias.reshape(1, ff), w_contract] + n2_parts + expand_parts + cot_parts,
+            scalars=1,
+            scratch=[pltpu.VMEM((width, ff), bf)],
+            flops=3 * 2 * total * width * ff,
+        )
+        active, grad_hidden, n2_all, cot_all = ffn_out[parts:]
+        gn_parts = [ffn_out[0]] + [seq_swap(ffn_out[j], j) for j in others]
+
+        def ffn_weights_kernel(info_ref, active_ref, gh_ref, n2_ref, cot_ref, wc_ref, *refs):
+            results = refs[:parts]
+            keep_ref, send_ref, bias_ref, scr = refs[parts:]
+            result = mm(active_ref[...], wc_ref[...]).astype(bf)
+            for j in range(parts):
+                results[j][...] = result[j * rows : (j + 1) * rows]
+            bias_ref[...] = column_sums(gh_ref[...].astype(f32))
+            core_id = info_ref[2]
+            for flip, out_ref in ((0, keep_ref), (1, send_ref)):
+                half = jnp.bitwise_xor(core_id, flip)
+                scr[...] = mm_tn(active_ref[...], cot_ref[:, aligned(half, half_width)]).astype(bf)
+                for part in range(parts):
+                    span = ff // parts
+                    out_ref[part, 0:span, :] = scr[part * span : (part + 1) * span, :]
+            for flip, out_ref in ((0, keep_ref), (1, send_ref)):
+                half = jnp.bitwise_xor(core_id, flip)
+                scr[...] = mm_tn(n2_ref[...], gh_ref[:, aligned(half, half_ff)]).astype(bf)
+                for part in range(parts):
+                    for j in range(seq_parts):
+                        at = ff // parts + j * sub
+                        row = j * own_width + part * sub
+                        out_ref[part, at : at + sub, :] = scr[row : row + sub, :]
+
+        span = ff // parts + own_width
+        fw_out = local_call(
+            ffn_weights_kernel,
+            "feed_weights",
+            [shape_of((rows, width), bf)] * parts
+            + [
+                shape_of((parts, span, half_width), bf),
+                shape_of((parts, span, half_width), bf),
+                shape_of((1, ff), f32),
+            ],
+            [info, active, grad_hidden, n2_all, cot_all, w_contract],
+            scalars=1,
+            scratch=[pltpu.VMEM((width, half_width), bf)],
+            flops=3 * 2 * total * width * ff,
+        )
+        ffn_keep, ffn_send, grad_expand_row = fw_out[parts:]
+        res_parts = [fw_out[0]] + [seq_swap(fw_out[j], j) for j in others]
+        ffn_far = core_swap(ffn_send)
+
+        def pick_kernel(info_ref, keep_ref, far_ref, *outs):
+            for k in range(parts):
+                at = jnp.bitwise_xor(info_ref[1], k)
+                outs[k][...] = (keep_ref[at].astype(f32) + far_ref[at].astype(f32)).astype(bf)
+
+        ffn_chunks = local_call(
+            pick_kernel,
+            "feed_chunks",
+            [shape_of((span, half_width), bf)] * parts,
+            [info, ffn_keep, ffn_far],
+            scalars=1,
+        )
+        ffn_parts = [ffn_chunks[0]] + [chip_swap(ffn_chunks[k], k) for k in others]
+
+        def back_kernel(info_ref, mid_ref, vec_ref, cot_ref, *refs):
+            gns, outs = refs[:parts], refs[parts : 2 * parts]
+            douts = refs[2 * parts : 3 * parts]
+            gmid_ref, branch_ref, sums_ref, w_scr = refs[3 * parts :]
+            for j in range(parts):
+                w_scr[jnp.bitwise_xor(info_ref[0], j)] = outs[j][...]
+            grad = gns[0][...].astype(f32)
+            for j in others:
+                grad = grad + gns[j][...].astype(f32)
+            xhat, spread = norm_stats(mid_ref[...])
+            cot = cot_ref[...].astype(f32)
+            grad_middle = cot + norm_back(grad, vec_ref[5:6], xhat, spread)
+            gmid_ref[...] = grad_middle
+            branch = grad_middle.astype(bf)
+            branch_ref[...] = branch
+            for k in range(parts):
+                douts[k][...] = mm_nt(branch, w_scr[jnp.bitwise_xor(info_ref[1], k)]).astype(bf)
+            sums_ref[0:1, :] = column_sums(branch.astype(f32))
+            sums_ref[1:2, :] = column_sums(grad * xhat)
+            sums_ref[2:3, :] = column_sums(grad)
+            sums_ref[3:4, :] = column_sums(cot)
+
+        back_out = local_call(
+            back_kernel,
+            "middle_back",
+            [shape_of((rows, hw), bf)] * parts
+            + [
+                shape_of((rows, width), f32),
+                shape_of((rows, width), bf),
+                shape_of((8, width), f32),
+            ],
+            [info, middle, vectors, own_cot] + gn_parts + out_parts,
+            scalars=1,
+            scratch=[pltpu.VMEM((parts, own_width, width), bf)],
+            flops=2 * rows * width * width,
+        )
+        grad_middle, grad_branch, late_sums = back_out[parts:]
+        dout_parts = [back_out[0]] + [chip_swap(back_out[k], k) for k in others]
+
+        def out_weights_kernel(info_ref, branch_ref, *refs):
+            atts = refs[:parts]
+            keep_ref, send_ref = refs[parts:]
+            for flip, out_ref in ((0, keep_ref), (1, send_ref)):
+                half = jnp.bitwise_xor(info_ref[2], flip)
+                piece = branch_ref[:, aligned(half, half_width)]
+                for k in range(parts):
+                    out_ref[jnp.bitwise_xor(info_ref[1], k)] = mm_tn(atts[k][...], piece).astype(bf)
+
+        out_keep, out_send = local_call(
+            out_weights_kernel,
+            "output_weights",
+            [shape_of((parts, hw, half_width), bf)] * 2,
+            [info, grad_branch] + att_parts,
+            scalars=1,
+            flops=2 * rows * width * width,
+        )
+        out_far = core_swap(out_send)
+
+        def attend_back_kernel(info_ref, pair_ref, q_ref, kv_ref, far_ref, flat_ref, lse_ref, *refs):
+            douts = refs[:parts]
+            dq_ref, own_ref, send_ref, bias_ref, dout_ref = refs[parts:]
+            fill_mask(bias_ref, pair_ref, info_ref, ranks, parts, block)
+            for k in range(parts):
+                dout_ref[k * rows : (k + 1) * rows, :] = douts[k][...].astype(f32)
+            flat_dout = dout_ref[...].T
+            for head in range(head_count):
+                at = slice(head * HEAD_DIM, (head + 1) * HEAD_DIM)
+                keys = jnp.concatenate(
+                    [head_columns(kv_ref, 0, head), head_columns(far_ref, 0, head)], axis=0
+                )
+                values = jnp.concatenate(
+                    [head_columns(kv_ref, hw, head), head_columns(far_ref, hw, head)], axis=0
+                )
+                queries = head_columns(q_ref, 0, head)
+                dout = dout_ref[:, at].astype(bf)
+                dout_turned = flat_dout[at, :]
+                delta = column_sums(dout_turned * flat_ref[at, :])
+                scores = mm_nt(keys, queries) * scale + bias_ref[...]
+                probs = jnp.exp(scores - lse_ref[head : head + 1, :])
+                grad_value = mm(probs.astype(bf), dout)
+                grad_weights = mm(values, dout_turned.astype(bf))
+                grad_scores = (probs * (grad_weights - delta)).astype(bf)
+                grad_key = mm(grad_scores, queries) * scale
+                dq_ref[at, :] = mm_tn(keys, grad_scores) * scale
+                vat = slice(hw + head * HEAD_DIM, hw + (head + 1) * HEAD_DIM)
+                own_ref[:, at] = grad_key[0:total]
+                own_ref[:, vat] = grad_value[0:total]
+                send_ref[:, at] = grad_key[total:].astype(bf)
+                send_ref[:, vat] = grad_value[total:].astype(bf)
+
+        flat_dq, dkv_own, dkv_send = local_call(
+            attend_back_kernel,
+            "attend_back",
+            [
+                shape_of((hw, total), f32),
+                shape_of((total, 2 * hw), f32),
+                shape_of((total, 2 * hw), bf),
+            ],
+            [info, pair_of_rank, query, own_kv, far_kv, flat_attended, row_lse] + dout_parts,
+            scalars=2,
+            scratch=[pltpu.VMEM((2 * total, total), f32), pltpu.VMEM((total, hw), f32)],
+            flops=5 * 2 * head_count * 2 * total * total * HEAD_DIM,
+        )
+        dkv_far = core_swap(dkv_send)
+
+        def normed_back_kernel(dq_ref, own_ref, far_ref, w_ref, *refs):
+            toks = refs[:parts]
+            chunks = refs[parts : 2 * parts]
+            mixed_ref, sums_ref, bias_ref = refs[2 * parts :]
+            mixed_ref[:, 0:hw] = dq_ref[...].T.astype(bf)
+            mixed_ref[:, hw:] = (own_ref[...] + far_ref[...].astype(f32)).astype(bf)
+            shift_sum = jnp.zeros((1, width), f32)
+            gain_sum = jnp.zeros((1, width), f32)
+            for k in range(parts):
+                grad = mm_nt(mixed_ref[k * rows : (k + 1) * rows, :], w_ref[...])
+                chunks[k][...] = grad.astype(bf)
+                xhat, _ = norm_stats(toks[k][...].astype(f32))
+                shift_sum = shift_sum + column_sums(grad)
+                gain_sum = gain_sum + column_sums(grad * xhat)
+            sums_ref[0:1, :] = gain_sum
+            sums_ref[1:2, :] = shift_sum
+            bias_ref[0:1, :] = column_sums(mixed_ref[...].astype(f32))
+
+        nb_out = local_call(
+            normed_back_kernel,
+            "normed_back",
+            [shape_of((rows, width), bf)] * parts
+            + [
+                shape_of((total, 3 * hw), bf),
+                shape_of((8, width), f32),
+                shape_of((8, 3 * hw), f32),
+            ],
+            [flat_dq, dkv_own, dkv_far, w_heads_full] + token_parts,
+            flops=2 * total * width * 3 * hw,
+        )
+        grad_mixed, first_sums, mixed_sums = nb_out[parts:]
+        gt_parts = [nb_out[0]] + [chip_swap(nb_out[k], k) for k in others]
+
+        tall = half_own + small_rows
+
+        def input_weights_kernel(
+            info_ref, normed_ref, mixed_ref, first_ref, bias_ref, late_ref, row_ref, *refs
+        ):
+            keep_ref, send_ref, grad_scr, small_scr = refs
+            grad_scr[...] = mm_tn(normed_ref[...], mixed_ref[...])
+            core_id, chip_id, seq = info_ref[2], info_ref[1], info_ref[0]
+            small_scr[...] = jnp.zeros_like(small_scr)
+            for j in range(seq_parts):
+                at = slice(j * own_width, (j + 1) * own_width)
+                small_scr[j, 0:2, 0:own_width] = first_ref[0:2, at]
+                small_scr[j, 4:8, 0:own_width] = late_ref[0:4, at]
+            small_scr[chip_id, 2:3, 0:hw] = bias_ref[0:1, 0:hw]
+            small_scr[chip_id, 3:4, 0:hw] = bias_ref[0:1, 2 * hw : 3 * hw]
+            for j in range(ff // own_width):
+                small_scr[seq, 8 + j : 9 + j, 0:own_width] = row_ref[
+                    :, j * own_width : (j + 1) * own_width
+                ]
+            for flip, out_ref in ((0, keep_ref), (1, send_ref)):
+                half = jnp.bitwise_xor(core_id, flip)
+                for j in range(seq_parts):
+                    start = pl.multiple_of(j * own_width + half * half_own, 16)
+                    out_ref[j, 0:half_own, :] = grad_scr[pl.ds(start, half_own), :].astype(bf)
+                    out_ref[j, half_own:tall, :] = small_scr[j].astype(bf)
+
+        in_keep, in_send = local_call(
+            input_weights_kernel,
+            "input_weights",
+            [shape_of((seq_parts, tall, 3 * hw), bf)] * 2,
+            [info, normed, grad_mixed, first_sums, mixed_sums, late_sums, grad_expand_row],
+            scalars=1,
+            scratch=[
+                pltpu.VMEM((width, 3 * hw), f32),
+                pltpu.VMEM((seq_parts, small_rows, 3 * hw), f32),
+            ],
+            flops=2 * total * width * 3 * hw,
+        )
+        in_far = core_swap(in_send)
+
+        def owner_kernel(info_ref, keep_ref, far_ref, *refs):
+            ffns = refs[:parts]
+            con_ref = refs[parts]
+            outs = refs[parts + 1 :]
+            whole = ffns[0][...].astype(f32)
+            for k in others:
+                whole = whole + ffns[k][...].astype(f32)
+            con_ref[...] = whole.astype(bf)
+            for j in range(seq_parts):
+                to = jnp.bitwise_xor(info_ref[0], j)
+                start = pl.multiple_of(ff // parts + to * sub, 16)
+                outs[j][0:sub, :] = con_ref[pl.ds(start, sub), :]
+                outs[j][sub:, :] = (
+                    keep_ref[to].astype(f32) + far_ref[to].astype(f32)
+                ).astype(bf)
+
+        ow_out = local_call(
+            owner_kernel,
+            "owners",
+            [shape_of((span, half_width), bf)]
+            + [shape_of((sub + own_width, half_width), bf)] * seq_parts,
+            [info, out_keep, out_far] + ffn_parts,
+            scalars=1,
+        )
+        ffn_whole = ow_out[0]
+        ow_parts = [ow_out[1]] + [seq_swap(ow_out[1 + j], j) for j in others]
+
+        gather_rows = span + sub
+
+        def share_kernel(info_ref, whole_ref, *refs):
+            owned = refs[:seq_parts]
+            outs = refs[seq_parts : seq_parts + parts]
+            (scr,) = refs[seq_parts + parts :]
+            rows_out = owned[0][sub:, :].astype(f32)
+            for j in others:
+                rows_out = rows_out + owned[j][sub:, :].astype(f32)
+            scr[...] = rows_out.astype(bf)
+            for k in range(parts):
+                out_ref = outs[k]
+                out_ref[0 : ff // parts, :] = whole_ref[0 : ff // parts, :]
+                for j in range(seq_parts):
+                    start = pl.multiple_of(
+                        ff // parts + jnp.bitwise_xor(info_ref[0], j) * sub, 16
+                    )
+                    out_ref[pl.ds(start, sub), :] = owned[j][0:sub, :]
+                to = pl.multiple_of(jnp.bitwise_xor(info_ref[1], k) * sub, 16)
+                out_ref[span:, :] = scr[pl.ds(to, sub), :]
+
+        sh_out = local_call(
+            share_kernel,
+            "shares",
+            [shape_of((gather_rows, half_width), bf)] * parts,
+            [info, ffn_whole] + ow_parts,
+            scalars=1,
+            scratch=[pltpu.VMEM((own_width, half_width), bf)],
+        )
+        sh_parts = [sh_out[0]] + [chip_swap(sh_out[k], k) for k in others]
+        sh_far = [core_swap(member) for member in sh_parts]
+
+        def ffn_final_kernel(info_ref, *refs):
+            own, far = refs[:parts], refs[parts : 2 * parts]
+            con_ref, exp_ref = refs[2 * parts :]
+            for flip, members in ((0, own), (1, far)):
+                half = jnp.bitwise_xor(info_ref[2], flip)
+                lanes = aligned(half, half_width)
+                for k in range(parts):
+                    at = jnp.bitwise_xor(info_ref[1], k)
+                    con_ref[aligned(at, ff // parts), lanes] = members[k][
+                        0 : ff // parts, :
+                    ].astype(f32)
+                    for j in range(seq_parts):
+                        start = ff // parts + j * sub
+                        cols = pl.ds(pl.multiple_of(j * ff + half * half_ff, 128), half_ff)
+                        exp_ref[aligned(at, sub), cols] = members[k][
+                            start : start + sub, :
+                        ].astype(f32)
+
+        grad_contract, grad_expand = local_call(
+            ffn_final_kernel,
+            "feed_final",
+            [shape_of((ff, width), f32), shape_of((own_width, seq_parts * ff), f32)],
+            [info] + sh_parts + sh_far,
+            scalars=1,
+        )
+
+        def in_pick_kernel(info_ref, keep_ref, far_ref, *outs):
+            for j in range(seq_parts):
+                at = jnp.bitwise_xor(info_ref[0], j)
+                outs[j][...] = (keep_ref[at].astype(f32) + far_ref[at].astype(f32)).astype(bf)
+
+        in_chunks = local_call(
+            in_pick_kernel,
+            "input_chunks",
+            [shape_of((tall, 3 * hw), bf)] * seq_parts,
+            [info, in_keep, in_far],
+            scalars=1,
+        )
+        in_parts = [in_chunks[0]] + [seq_swap(in_chunks[j], j) for j in others]
+
+        def in_sum_kernel(*refs):
+            owned, shared = refs[:seq_parts], refs[seq_parts : seq_parts + parts]
+            (out_ref,) = refs[seq_parts + parts :]
+            whole = owned[0][...].astype(f32)
+            for j in others:
+                whole = whole + owned[j][...].astype(f32)
+            out_ref[0:tall, :] = whole.astype(bf)
+            rows_out = shared[0][span:, :].astype(f32)
+            for k in others:
+                rows_out = rows_out + shared[k][span:, :].astype(f32)
+            out_ref[tall:, 0:half_width] = rows_out.astype(bf)
+            out_ref[tall:, half_width:] = jnp.zeros((sub, 3 * hw - half_width), bf)
+
+        (in_whole,) = local_call(
+            in_sum_kernel,
+            "input_sum",
+            [shape_of((tall + sub, 3 * hw), bf)],
+            in_parts + sh_parts,
+        )
+        last_parts = [in_whole] + [chip_swap(in_whole, k) for k in others]
+        last_far = [core_swap(member) for member in last_parts]
+
+        def last_kernel(info_ref, *refs):
+            own, far = refs[:parts], refs[parts : 2 * parts]
+            gin_ref, gout_ref, small_ref, scr = refs[2 * parts :]
+            for flip, members in ((0, own), (1, far)):
+                half = jnp.bitwise_xor(info_ref[2], flip)
+                for k in range(parts):
+                    at = jnp.bitwise_xor(info_ref[1], k)
+                    scr[at, aligned(half, half_own), :] = members[k][0:half_own, :].astype(f32)
+                    gout_ref[aligned(at, sub), aligned(half, half_width)] = members[k][
+                        tall:, 0:half_width
+                    ].astype(f32)
+            for at in range(parts):
+                for base in range(3):
+                    start = base * width + at * hw
+                    gin_ref[:, start : start + hw] = scr[at, :, base * hw : (base + 1) * hw]
+            small = own[0][half_own:tall, 0:own_width].astype(f32)
+            for k in others:
+                small = small + own[k][half_own:tall, 0:own_width].astype(f32)
+            small_ref[...] = small
+
+        grad_input, grad_output, small_sums = local_call(
+            last_kernel,
+            "weights_final",
+            [
+                shape_of((own_width, 3 * width), f32),
+                shape_of((own_width, width), f32),
+                shape_of((small_rows, own_width), f32),
+            ],
+            [info] + last_parts + last_far,
+            scalars=1,
+            scratch=[pltpu.VMEM((parts, own_width, 3 * hw), f32)],
+        )
+
+        def out_kernel(mid_ref, vec_ref, *refs):
+            result = mid_ref[...] + vec_ref[7:8]
+            for j in range(seq_parts):
+                result = result + refs[j][...].astype(f32)
+            refs[seq_parts][0] = result.astype(bf)
+
+        (block_out,) = local_call(
+            out_kernel,
+            "result",
+            [shape_of((1, rows, width), bf)],
+            [middle, vectors] + res_parts,
+        )
+
+        def tokens_kernel(tok_ref, vec_ref, gmid_ref, *refs):
+            grad = refs[0][...].astype(f32)
+            for k in others:
+                grad = grad + refs[k][...].astype(f32)
+            xhat, spread = norm_stats(tok_ref[...].astype(f32))
+            refs[parts][0] = gmid_ref[...] + norm_back(grad, vec_ref[0:1], xhat, spread)
+
+        (grad_tokens,) = local_call(
+            tokens_kernel,
+            "tokens_back",
+            [shape_of((1, rows, width), f32)],
+            [own_tokens, vectors, grad_middle] + gt_parts,
+        )
+        small_of = [small_sums[i] for i in range(8)]
+        grad_expand_bias = small_sums[8 : 8 + ff // own_width].reshape(ff)
+        return (
+            block_out,
+            grad_tokens,
+            small_of[0],
+            small_of[1],
+            grad_input,
+            small_of[2],
+            small_of[3],
+            grad_output,
+            small_of[4],
+            small_of[5],
+            small_of[6],
+            grad_expand,
+            grad_expand_bias,
+            grad_contract,
+            small_of[7],
+        )
+
+    return per_device_heads
+
+
 def solution(mesh):
+    ranks = mesh.shape["ctx"]
+    chips = ranks // 2
+    if chips == mesh.shape["dp"] and HEADS % chips == 0 and chips & (chips - 1) == 0:
+        body = head_parallel(ranks, chips, mesh.shape["dp"])
+    else:
+        body = per_device
     return jax.shard_map(
-        per_device,
+        body,
         mesh=mesh,
         in_specs=(
             P("dp", "ctx", None),

time: 676 us -> 236 us (0.35)
  blocking collectives: 217 us -> 0 us
  local copies, waits for them, and re-layouts: 132 us -> 11.7 us
  matrix products: 81.3 us -> 0 us
  starting transfers between devices: 0.69 us -> 73.5 us
  waiting for transfers between devices: 184 us -> 113 us
  other arithmetic: 37.1 us -> 0.19 us
  Pallas kernels: 0 us -> 36.7 us
  between operations: 17.9 us -> 0.99 us
    all_gather x8 -> x0, waiting for transfers between devices: 147 us -> none  [the longest x1 55.6 us: per_device(): lax.all_gather(w_contract, 'dp', axis=0, tiled=True)]
    psum x1 -> x0, blocking collectives: 145 us -> none  [per_device(): lax.psum((grad_owned[0], grad_owned[1], grad_owned[2], grad_owned[3], gra...]
    ppermute x0 -> x61, waiting for transfers between devices: none -> 113 us  [the longest x21 69.4 us: chip_swap(): lax.ppermute(member, 'ctx', [(i, 2 * (i // 2 ^ step) + i % 2) for i in ra...]
    dot_general x24 -> x0, matrix products: 81.3 us -> none  [the longest x1 13.7 us: key_grad_group(): jnp.einsum('thqk,tqhd->tkhd', dscore, tile_query, preferred_element_type=...]
    ppermute x0 -> x61, starting transfers between devices: none -> 73.5 us  [the longest x21 41.5 us: chip_swap(): lax.ppermute(member, 'ctx', [(i, 2 * (i // 2 ^ step) + i % 2) for i in ra...]
    slice x11 -> x2, local copies, waits for them, and re-layouts: 42.9 us -> 0.6 us  [the longest x1 0.6 us: per_device_heads(): small_of = [small_sums[i] for i in range(8)]]
    all_gather x3 -> x0, blocking collectives: 38 us -> none  [the longest x1 15 us: per_device(): lax.all_gather(lse_rows, 'ctx', axis=1, tiled=True)]
    pallas_call x0 -> x19, Pallas kernels: none -> 36.7 us  [local_call(): pl.pallas_call(kernel, out_shape=tuple(outs), in_specs=[pl.BlockSpec(memo...]
  transfers between devices with their start and end apart: 12 -> 61, of which waited for: 6 -> 26; matrix products, arithmetic and copies ran while one was open for 37% -> 3% of each run, Pallas kernels for 0% -> 11%
where the time goes in v1:
time: 236 us
  waiting for transfers between devices  113 us (48%)
  starting transfers between devices  73.5 us (31%)
  Pallas kernels  36.7 us (16%)
  local copies, waits for them, and re-layouts  11.7 us (5%)
    ppermute x21, waiting for transfers between devices, chip_swap(): lax.ppermute(member, 'ctx', [(i, 2 * (i // 2 ^ step) + i % 2) for i in ra...  69.4 us
    ppermute x27, waiting for transfers between devices, seq_swap(): return lax.ppermute(member, 'dp', [(i, i ^ step) for i in range(seq_parts)])  43.2 us
    ppermute x21, starting transfers between devices, chip_swap(): lax.ppermute(member, 'ctx', [(i, 2 * (i // 2 ^ step) + i % 2) for i in ra...  41.5 us
    pallas_call x19, Pallas kernels, local_call(): pl.pallas_call(kernel, out_shape=tuple(outs), in_specs=[pl.BlockSpec(memo...  36.7 us
    ppermute x27, starting transfers between devices, seq_swap(): return lax.ppermute(member, 'dp', [(i, i ^ step) for i in range(seq_parts)])  30.6 us
    another operation x9, local copies, waits for them, and re-layouts, per_device_heads(): jnp.stack([first_gain, first_shift, query_bias, value_bias, output_bias,...  5.3 us
  transfers between devices with their start and end apart: 61, of which 26 were waited for; matrix products, arithmetic and copies ran while one was open for 3% of the time, Pallas kernels for 11%

profile of v1, /device:TPU:0, one launch (start us, length us, event | category | flops | bytes accessed | tf_op | source)
XLA Modules:
  0.0 235.8 jit_solution(4505449501522267284)
XLA Ops:
  0.7 5.1 %collective-permute-start.2 = (bf16[128,768]{1,0:T(8,128)(2,1)}, bf16[128,768]{1,0:T(8,128)(2,1)S(1)}, u32[]{:S(2)}, u32[]{:S(2)}) collective-permute-start(bf16[128,768]{1,0:T(8,128)(2,1)} %bitcast.13), channel_id=1, source_target_pairs={{0,6},{1,7},{2,4},{3,5},{4,2},{5,3},{6,0},{7,1},{8,14},{9,15},{10,... | collective-permute-start | bytes 589832 | tf_op jit(solution)/shard_map/ppermute | solution.py:678
  5.8 1.2 constant_dynamic-slice_fusion.6
  12.4 2.5 %collective-permute-start.5 = (bf16[208,576]{1,0:T(8,128)(2,1)S(1)}, bf16[208,576]{1,0:T(8,128)(2,1)S(1)}, u32[]{:S(2)}, u32[]{:S(2)}) collective-permute-start(bf16[208,576]{1,0:T(8,128)(2,1)S(1)} %fusion.1.refs_4_), channel_id=1, source_target_pairs={{0,24},{8,16},{16,8},{24,0},{1,25},{9,17},{17,9},{25,1},{2,26},{10... | collective-permute-start | bytes 718856 | tf_op jit(solution)/shard_map/ppermute | solution.py:683
  16.7 9.0 %collective-permute-done.1.refs_2_ = bf16[128,768]{1,0:T(8,128)(2,1)S(1)} collective-permute-done((bf16[128,768]{1,0:T(8,128)(2,1)S(1)}, bf16[128,768]{1,0:T(8,128)(2,1)S(1)}, u32[]{:S(2)}, u32[]{:S(2)}) %collective-permute-start.1) | collective-permute-done | bytes 196640 | tf_op jit(solution)/shard_map/ppermute | solution.py:678
  25.8 1.2 collective-permute-done.4.refs_6_
  27.0 2.7 %project.1 = (bf16[512,192]{1,0:T(8,128)(2,1)S(1)}, bf16[512,384]{1,0:T(8,128)(2,1)}, bf16[512,768]{1,0:T(8,128)(2,1)S(1)}, bf16[768,576]{1,0:T(8,128)(2,1)S(1)}, f32[16,768]{1,0:T(8,128)S(1)}) custom-call(s32[3]{0:T(128)S(1)} %pad_add_fusion.info_ref, bf16[128,768]{1,0:T(8,128)(2,1)S(1)} %bitcast.16, bf16[128,768]{1,0:T(8,128)(2,1)S(1)} %collective-permute-done.refs_1_, ...), custom_call_target="tpu_custom_call" | custom-call | flops 452984832 | bytes 4055052 | tf_op jit(solution)/shard_map/project/pallas_call | solution.py:629
  31.3 1.6 collective-permute-start.12
  32.9 1.3 collective-permute-start.11
  34.8 1.6 collective-permute-start.21
  36.4 1.4 constant_dynamic-slice_fusion
  37.8 1.3 collective-permute-start.18
  39.1 4.3 %attend.1 = (bf16[128,192]{1,0:T(8,128)(2,1)S(1)}, bf16[128,192]{1,0:T(8,128)(2,1)S(1)}, bf16[128,192]{1,0:T(8,128)(2,1)S(1)}, bf16[128,192]{1,0:T(8,128)(2,1)S(...) custom-call(s32[3]{0:T(128)S(1)} %pad_add_fusion.info_ref, s32[8]{0:T(128)S(1)} %copy-done.10, ...), custom_call_target="tpu_custom_call" | custom-call | flops 402653184 | bytes 1589292 | tf_op jit(solution)/shard_map/attend/pallas_call | solution.py:629
  43.5 9.1 %collective-permute-done.21.refs_11_ = bf16[128,768]{1,0:T(8,128)(2,1)S(1)} collective-permute-done((bf16[128,768]{1,0:T(8,128)(2,1)S(1)}, bf16[128,768]{1,0:T(8,128)(2,1)S(1)}, u32[]{:S(2)}, u32[]{:S(2)}) %collective-permute-start.21) | collective-permute-done | bytes 196640 | tf_op jit(solution)/shard_map/ppermute | solution.py:683
  52.6 1.5 collective-permute-start.20
  54.9 1.4 collective-permute-start.8
  56.8 2.3 collective-permute-start.9
  59.2 2.2 collective-permute-done.8.refs_2_
  61.4 1.5 collective-permute-done.9.refs_3_
  62.9 1.4 collective-permute-start.17
  64.3 1.2 middle.1
  65.5 1.6 collective-permute-start.15
  67.9 1.2 collective-permute-start.13
  69.1 2.3 collective-permute-done.16.refs_5_
  71.4 4.4 %collective-permute-done.17.refs_6_ = bf16[192,768]{1,0:T(8,128)(2,1)S(1)} collective-permute-done((bf16[192,768]{1,0:T(8,128)(2,1)S(1)}, bf16[192,768]{1,0:T(8,128)(2,1)S(1)}, u32[]{:S(2)}, u32[]{:S(2)}) %collective-permute-start.17) | collective-permute-done | bytes 294944 | tf_op jit(solution)/shard_map/ppermute | solution.py:683
  75.8 2.1 collective-permute-done.14.refs_2_
  78.9 3.1 %feed.1 = (bf16[128,768]{1,0:T(8,128)(2,1)S(1)}, bf16[128,768]{1,0:T(8,128)(2,1)S(1)}, bf16[128,768]{1,0:T(8,128)(2,1)S(1)}, bf16[128,768]{1,0:T(8,128)(2,1)S(1)...) custom-call(s32[3]{0:T(128)S(1)} %pad_add_fusion.info_ref, ...), custom_call_target="tpu_custom_call" | custom-call | flops 1811939328 | bytes 7865868 | tf_op jit(solution)/shard_map/feed/pallas_call | solution.py:629
  82.0 3.4 %feed_weights.1 = (bf16[128,768]{1,0:T(8,128)(2,1)S(1)}, bf16[128,768]{1,0:T(8,128)(2,1)S(1)}, bf16[128,768]{1,0:T(8,128)(2,1)S(1)}, bf16[128,768]{1,0:T(8,128)(...) custom-call(s32[3]{0:T(128)S(1)} %pad_add_fusion.info_ref, ...), custom_call_target="tpu_custom_call" | custom-call | flops 1811939328 | bytes 7474188 | tf_op jit(solution)/shard_map/feed_weights/pallas_call | solution.py:629
  85.4 1.7 collective-permute-start.25
  87.7 1.3 collective-permute-start.27
  89.0 4.2 %collective-permute-done.25.refs_1_ = bf16[128,768]{1,0:T(8,128)(2,1)S(1)} collective-permute-done((bf16[128,768]{1,0:T(8,128)(2,1)S(1)}, bf16[128,768]{1,0:T(8,128)(2,1)S(1)}, u32[]{:S(2)}, u32[]{:S(2)}) %collective-permute-start.25) | collective-permute-done | bytes 196640 | tf_op jit(solution)/shard_map/ppermute | solution.py:683
  93.2 5.1 %collective-permute-done.26.refs_2_ = bf16[128,768]{1,0:T(8,128)(2,1)S(1)} collective-permute-done((bf16[128,768]{1,0:T(8,128)(2,1)S(1)}, bf16[128,768]{1,0:T(8,128)(2,1)S(1)}, u32[]{:S(2)}, u32[]{:S(2)}) %collective-permute-start.26) | collective-permute-done | bytes 196640 | tf_op jit(solution)/shard_map/ppermute | solution.py:683
  98.3 1.6 middle_back.1
  100.0 2.0 collective-permute-start.29
  102.0 2.4 %collective-permute-start.30 = (bf16[128,192]{1,0:T(8,128)(2,1)S(1)}, bf16[128,192]{1,0:T(8,128)(2,1)S(1)}, u32[]{:S(2)}, u32[]{:S(2)}) collective-permute-start(bf16[128,192]{1,0:T(8,128)(2,1)S(1)} %get-tuple-element.113), channel_id=1, source_target_pairs={{0,6},{1,7},{2,4},{3,5},{4,2},{5,3},{6,0},{7,1},{8,14},{9,15},{10,... | collective-permute-start | bytes 147464 | tf_op jit(solution)/shard_map/ppermute | solution.py:678
  104.4 2.8 %collective-permute-done.29.refs_2_ = bf16[128,192]{1,0:T(8,128)(2,1)S(1)} collective-permute-done((bf16[128,192]{1,0:T(8,128)(2,1)S(1)}, bf16[128,192]{1,0:T(8,128)(2,1)S(1)}, u32[]{:S(2)}, u32[]{:S(2)}) %collective-permute-start.29) | collective-permute-done | bytes 49184 | tf_op jit(solution)/shard_map/ppermute | solution.py:678
  108.1 5.4 %attend_back.1 = (f32[192,512]{1,0:T(8,128)S(1)}, f32[512,384]{1,0:T(8,128)S(1)}, bf16[512,384]{1,0:T(8,128)(2,1)S(1)}) custom-call(s32[3]{0:T(128)S(1)} %pad_add_fusion.info_ref, s32[8]{0:T(128)S(1)} %copy-done.10, bf16[512,192]{1,0:T(8,128)(2,1)S(1)} %copy-done.7, bf16[512,384]{1,0:T(8,128)(2,1)} %get-tuple-element.88.kv_ref, ...), custom_call_target="tpu_custom_call" | custom-call | flops 1006632960 | bytes 3162156 | tf_op jit(solution)/shard_map/attend_back/pallas_call | solution.py:629
  115.3 1.7 normed_back.1
  118.9 1.9 collective-permute-start.42
  120.9 1.5 collective-permute-start.43
  122.4 1.5 input_weights.1
  123.9 8.4 %collective-permute-done.41.refs_1_ = bf16[384,384]{1,0:T(8,128)(2,1)S(1)} collective-permute-done((bf16[384,384]{1,0:T(8,128)(2,1)S(1)}, bf16[384,384]{1,0:T(8,128)(2,1)S(1)}, u32[]{:S(2)}, u32[]{:S(2)}) %collective-permute-start.41) | collective-permute-done | bytes 294944 | tf_op jit(solution)/shard_map/ppermute | solution.py:678
  132.3 10.0 %collective-permute-done.42.refs_2_ = bf16[384,384]{1,0:T(8,128)(2,1)S(1)} collective-permute-done((bf16[384,384]{1,0:T(8,128)(2,1)S(1)}, bf16[384,384]{1,0:T(8,128)(2,1)S(1)}, u32[]{:S(2)}, u32[]{:S(2)}) %collective-permute-start.42) | collective-permute-done | bytes 294944 | tf_op jit(solution)/shard_map/ppermute | solution.py:678
  143.9 1.7 collective-permute-start.45
  145.5 1.4 collective-permute-start.46
  147.3 3.7 %collective-permute-done.44.refs_1_ = bf16[240,384]{1,0:T(8,128)(2,1)S(1)} collective-permute-done((bf16[240,384]{1,0:T(8,128)(2,1)S(1)}, bf16[240,384]{1,0:T(8,128)(2,1)S(1)}, u32[]{:S(2)}, u32[]{:S(2)}) %collective-permute-start.44) | collective-permute-done | bytes 184352 | tf_op jit(solution)/shard_map/ppermute | solution.py:683
  151.1 2.9 %collective-permute-done.46.refs_3_ = bf16[240,384]{1,0:T(8,128)(2,1)S(1)} collective-permute-done((bf16[240,384]{1,0:T(8,128)(2,1)S(1)}, bf16[240,384]{1,0:T(8,128)(2,1)S(1)}, u32[]{:S(2)}, u32[]{:S(2)}) %collective-permute-start.46) | collective-permute-done | bytes 184352 | tf_op jit(solution)/shard_map/ppermute | solution.py:683
  154.7 7.0 %collective-permute-start.47 = (bf16[432,384]{1,0:T(8,128)(2,1)S(1)}, bf16[432,384]{1,0:T(8,128)(2,1)S(1)}, u32[]{:S(2)}, u32[]{:S(2)}) collective-permute-start(bf16[432,384]{1,0:T(8,128)(2,1)S(1)} %get-tuple-element.149), channel_id=1, source_target_pairs={{0,2},{1,3},{2,0},{3,1},{4,6},{5,7},{6,4},{7,5},{8,10},{9,11},{10,... | collective-permute-start | bytes 995336 | tf_op jit(solution)/shard_map/ppermute | solution.py:678
  161.8 1.3 collective-permute-start.23
  164.7 2.3 collective-permute-start.49
  166.9 3.1 %collective-permute-done.23.refs_2_ = bf16[128,768]{1,0:T(8,128)(2,1)S(1)} collective-permute-done((bf16[128,768]{1,0:T(8,128)(2,1)S(1)}, bf16[128,768]{1,0:T(8,128)(2,1)S(1)}, u32[]{:S(2)}, u32[]{:S(2)}) %collective-permute-start.23) | collective-permute-done | bytes 196640 | tf_op jit(solution)/shard_map/ppermute | solution.py:683
  170.9 1.2 collective-permute-start.38
  172.1 5.1 %collective-permute-done.37.refs_2_ = bf16[112,576]{1,0:T(8,128)(2,1)S(1)} collective-permute-done((bf16[112,576]{1,0:T(8,128)(2,1)S(1)}, bf16[112,576]{1,0:T(8,128)(2,1)S(1)}, u32[]{:S(2)}, u32[]{:S(2)}) %collective-permute-start.37) | collective-permute-done | bytes 129056 | tf_op jit(solution)/shard_map/ppermute | solution.py:683
  177.1 1.8 collective-permute-start.24
  179.4 2.5 %collective-permute-start.33 = (bf16[128,768]{1,0:T(8,128)(2,1)S(1)}, bf16[128,768]{1,0:T(8,128)(2,1)S(1)}, u32[]{:S(2)}, u32[]{:S(2)}) collective-permute-start(bf16[128,768]{1,0:T(8,128)(2,1)S(1)} %get-tuple-element.120), channel_id=1, source_target_pairs={{0,4},{1,5},{2,6},{3,7},{4,0},{5,1},{6,2},{7,3},{8,12},{9,13},{10,... | collective-permute-start | bytes 589832 | tf_op jit(solution)/shard_map/ppermute | solution.py:678
  181.9 9.1 %collective-permute-done.48.refs_6_.refs_2_ = bf16[432,384]{1,0:T(8,128)(2,1)S(1)} collective-permute-done((bf16[432,384]{1,0:T(8,128)(2,1)S(1)}, bf16[432,384]{1,0:T(8,128)(2,1)S(1)}, u32[]{:S(2)}, u32[]{:S(2)}) %collective-permute-start.48) | collective-permute-done | bytes 331808 | tf_op jit(solution)/shard_map/ppermute | solution.py:678
  191.0 1.8 collective-permute-start.34
  192.9 2.1 collective-permute-start.52
  195.0 15.9 %collective-permute-done.33.refs_2_ = bf16[128,768]{1,0:T(8,128)(2,1)S(1)} collective-permute-done((bf16[128,768]{1,0:T(8,128)(2,1)S(1)}, bf16[128,768]{1,0:T(8,128)(2,1)S(1)}, u32[]{:S(2)}, u32[]{:S(2)}) %collective-permute-start.33) | collective-permute-done | bytes 196640 | tf_op jit(solution)/shard_map/ppermute | solution.py:678
  210.9 6.7 %collective-permute-start.51 = (bf16[160,576]{1,0:T(8,128)(2,1)S(1)}, bf16[160,576]{1,0:T(8,128)(2,1)S(1)}, u32[]{:S(2)}, u32[]{:S(2)}) collective-permute-start(bf16[160,576]{1,0:T(8,128)(2,1)S(1)} %input_sum.1.refs_0_), channel_id=1, source_target_pairs={{0,4},{1,5},{2,6},{3,7},{4,0},{5,1},{6,2},{7,3},{8,12},{9,13},{10,... | collective-permute-start | bytes 552968 | tf_op jit(solution)/shard_map/ppermute | solution.py:678
  217.7 7.1 %collective-permute-done.51.refs_2_ = bf16[160,576]{1,0:T(8,128)(2,1)S(1)} collective-permute-done((bf16[160,576]{1,0:T(8,128)(2,1)S(1)}, bf16[160,576]{1,0:T(8,128)(2,1)S(1)}, u32[]{:S(2)}, u32[]{:S(2)}) %collective-permute-start.51) | collective-permute-done | bytes 184352 | tf_op jit(solution)/shard_map/ppermute | solution.py:678
  224.8 1.7 collective-permute-done.50.refs_1_
  227.9 1.2 tokens_back.1
  229.1 3.0 %feed_final.1 = (f32[768,768]{1,0:T(8,128)}, f32[192,3072]{1,0:T(8,128)}) custom-call(s32[3]{0:T(128)S(1)} %pad_add_fusion.info_ref, bf16[432,384]{1,0:T(8,128)(2,1)S(1)} %get-tuple-element.148.refs_4_.refs_0_, bf16[432,384]{1,0:T(8,128)(2,1)S(1)} %collective-permute-done.47.refs_5_.refs_1_, bf16[432,384]{1,0:T(8,128)(2,1)S(1)} %collective-permute-done.48.refs_6_.refs_2_, ...), custom_call_target="tpu_custom_call" | custom-call | bytes 7372812 | tf_op jit(solution)/shard_map/feed_final/pallas_call | solution.py:629
  232.1 2.5 %weights_final.1 = (f32[192,2304]{1,0:T(8,128)}, f32[192,768]{1,0:T(8,128)}, f32[16,192]{1,0:T(8,128)S(1)}) custom-call(s32[3]{0:T(128)S(1)} %pad_add_fusion.info_ref, bf16[160,576]{1,0:T(8,128)(2,1)S(1)} %input_sum.1.refs_0_, bf16[160,576]{1,0:T(8,128)(2,1)S(1)} %collective-permute-done.50.refs_1_, bf16[160,576]{1,0:T(8,128)(2,1)S(1)} %collective-permute-done.51.refs_2_, ...), custom_call_target="tpu_custom_call" | custom-call | bytes 3846156 | tf_op jit(solution)/shard_map/weights_final/pallas_call | solution.py:629
  (118 shorter events, 26.4 us)
Async XLA Ops:
  0.7 15.3 %collective-permute-start.2 = (bf16[128,768]{1,0:T(8,128)(2,1)}, bf16[128,768]{1,0:T(8,128)(2,1)S(1)}, u32[]{:S(2)}, u32[]{:S(2)}) collective-permute-start(bf16[128,768]{1,0:T(8,128)(2,1)} %bitcast.13), channel_id=1, source_target_pairs={{0,6},{1,7},{2,4},{3,5},{4,2},{5,3},{6,0},{7,1},{8,14},{9,15},{10,... | collective-permute-start | bytes 589832 | tf_op jit(solution)/shard_map/ppermute | solution.py:678
  12.4 13.4 %collective-permute-start.5 = (bf16[208,576]{1,0:T(8,128)(2,1)S(1)}, bf16[208,576]{1,0:T(8,128)(2,1)S(1)}, u32[]{:S(2)}, u32[]{:S(2)}) collective-permute-start(bf16[208,576]{1,0:T(8,128)(2,1)S(1)} %fusion.1.refs_4_), channel_id=1, source_target_pairs={{0,24},{8,16},{16,8},{24,0},{1,25},{9,17},{17,9},{25,1},{2,26},{10... | collective-permute-start | bytes 718856 | tf_op jit(solution)/shard_map/ppermute | solution.py:683
  14.9 12.0 %collective-permute-start.4 = (bf16[208,576]{1,0:T(8,128)(2,1)S(1)}, bf16[208,576]{1,0:T(8,128)(2,1)S(1)}, u32[]{:S(2)}, u32[]{:S(2)}) collective-permute-start(bf16[208,576]{1,0:T(8,128)(2,1)S(1)} %fusion.1.refs_4_), channel_id=1, source_target_pairs={{0,16},{8,24},{16,0},{24,8},{1,17},{9,25},{17,1},{25,9},{2,18},{10... | collective-permute-start | bytes 718856 | tf_op jit(solution)/shard_map/ppermute | solution.py:683
  15.4 11.6 %collective-permute-start.3 = (bf16[208,576]{1,0:T(8,128)(2,1)S(1)}, bf16[208,576]{1,0:T(8,128)(2,1)S(1)}, u32[]{:S(2)}, u32[]{:S(2)}) collective-permute-start(bf16[208,576]{1,0:T(8,128)(2,1)S(1)} %fusion.1.refs_4_), channel_id=1, source_target_pairs={{0,8},{8,0},{16,24},{24,16},{1,9},{9,1},{17,25},{25,17},{2,10},{10... | collective-permute-start | bytes 718856 | tf_op jit(solution)/shard_map/ppermute | solution.py:683
  16.0 9.7 %collective-permute-start.1 = (bf16[128,768]{1,0:T(8,128)(2,1)S(1)}, bf16[128,768]{1,0:T(8,128)(2,1)S(1)}, u32[]{:S(2)}, u32[]{:S(2)}) collective-permute-start(bf16[128,768]{1,0:T(8,128)(2,1)S(1)} %bitcast.14), channel_id=1, source_target_pairs={{0,4},{1,5},{2,6},{3,7},{4,0},{5,1},{6,2},{7,3},{8,12},{9,13},{10,... | collective-permute-start | bytes 589832 | tf_op jit(solution)/shard_map/ppermute | solution.py:678
  16.0 9.8 %collective-permute-start = (bf16[128,768]{1,0:T(8,128)(2,1)S(1)}, bf16[128,768]{1,0:T(8,128)(2,1)S(1)}, u32[]{:S(2)}, u32[]{:S(2)}) collective-permute-start(bf16[128,768]{1,0:T(8,128)(2,1)S(1)} %bitcast.15), channel_id=1, source_target_pairs={{0,2},{1,3},{2,0},{3,1},{4,6},{5,7},{6,4},{7,5},{8,10},{9,11},{10,... | collective-permute-start | bytes 589832 | tf_op jit(solution)/shard_map/ppermute | solution.py:678
  31.3 6.5 %collective-permute-start.6 = (bf16[512,384]{1,0:T(8,128)(2,1)}, bf16[512,384]{1,0:T(8,128)(2,1)}, u32[]{:S(2)}, u32[]{:S(2)}) collective-permute-start(bf16[512,384]{1,0:T(8,128)(2,1)} %get-tuple-element.88.kv_ref), channel_id=1, source_target_pairs={{0,1},{1,0},{2,3},{3,2},{4,5},{5,4},{6,7},{7,6},{8,9},{9,8},{10,11... | collective-permute-start | bytes 1179656 | tf_op jit(solution)/shard_map/ppermute | solution.py:675
  31.3 21.3 %collective-permute-start.12 = (bf16[192,768]{1,0:T(8,128)(2,1)S(1)}, bf16[192,768]{1,0:T(8,128)(2,1)S(1)}, u32[]{:S(2)}, u32[]{:S(2)}) collective-permute-start(bf16[192,768]{1,0:T(8,128)(2,1)S(1)} %copy-done.1), channel_id=1, source_target_pairs={{0,24},{8,16},{16,8},{24,0},{1,25},{9,17},{17,9},{25,1},{2,26},{10... | collective-permute-start | bytes 884744 | tf_op jit(solution)/shard_map/ppermute | solution.py:683
  32.9 21.1 %collective-permute-start.11 = (bf16[192,768]{1,0:T(8,128)(2,1)S(1)}, bf16[192,768]{1,0:T(8,128)(2,1)S(1)}, u32[]{:S(2)}, u32[]{:S(2)}) collective-permute-start(bf16[192,768]{1,0:T(8,128)(2,1)S(1)} %copy-done.1), channel_id=1, source_target_pairs={{0,16},{8,24},{16,0},{24,8},{1,17},{9,25},{17,1},{25,9},{2,18},{10... | collective-permute-start | bytes 884744 | tf_op jit(solution)/shard_map/ppermute | solution.py:683
  34.2 20.6 %collective-permute-start.10 = (bf16[192,768]{1,0:T(8,128)(2,1)S(1)}, bf16[192,768]{1,0:T(8,128)(2,1)S(1)}, u32[]{:S(2)}, u32[]{:S(2)}) collective-permute-start(bf16[192,768]{1,0:T(8,128)(2,1)S(1)} %copy-done.1), channel_id=1, source_target_pairs={{0,8},{8,0},{16,24},{24,16},{1,9},{9,1},{17,25},{25,17},{2,10},{10... | collective-permute-start | bytes 884744 | tf_op jit(solution)/shard_map/ppermute | solution.py:683
  34.8 17.8 %collective-permute-start.21 = (bf16[128,768]{1,0:T(8,128)(2,1)S(1)}, bf16[128,768]{1,0:T(8,128)(2,1)S(1)}, u32[]{:S(2)}, u32[]{:S(2)}) collective-permute-start(bf16[128,768]{1,0:T(8,128)(2,1)S(1)} %bitcast.20), channel_id=1, source_target_pairs={{0,24},{8,16},{16,8},{24,0},{1,25},{9,17},{17,9},{25,1},{2,26},{10... | collective-permute-start | bytes 589832 | tf_op jit(solution)/shard_map/ppermute | solution.py:683
  37.8 30.1 %collective-permute-start.18 = (bf16[192,768]{1,0:T(8,128)(2,1)S(1)}, bf16[192,768]{1,0:T(8,128)(2,1)S(1)}, u32[]{:S(2)}, u32[]{:S(2)}) collective-permute-start(bf16[192,768]{1,0:T(8,128)(2,1)S(1)} %get-tuple-element.157), channel_id=1, source_target_pairs={{0,24},{8,16},{16,8},{24,0},{1,25},{9,17},{17,9},{25,1},{2,26},{10... | collective-permute-start | bytes 884744 | tf_op jit(solution)/shard_map/ppermute | solution.py:683
  43.5 25.6 %copy-start.11 = (bf16[768]{0:T(1024)(128)(2,1)S(1)}, bf16[768]{0:T(1024)(128)(2,1)}, u32[]{:S(2)}) copy-start(bf16[768]{0:T(1024)(128)(2,1)} %param.28) | copy-start | bytes 4612
  43.5 34.5 %copy-start.3 = (bf16[768,768]{1,0:T(8,128)(2,1)S(1)}, bf16[768,768]{1,0:T(8,128)(2,1)}, u32[]{:S(2)}) copy-start(bf16[768,768]{1,0:T(8,128)(2,1)} %wc_ref.3) | copy-start | bytes 3538948
  52.6 25.4 %copy-start.8 = (bf16[128,768]{1,0:T(8,128)(2,1)}, bf16[128,768]{1,0:T(8,128)(2,1)S(1)}, u32[]{:S(2)}) copy-start(bf16[128,768]{1,0:T(8,128)(2,1)S(1)} %collective-permute-done.21.refs_11_) | copy-start | bytes 589828
  52.6 4.3 %collective-permute-start.7 = (bf16[128,192]{1,0:T(8,128)(2,1)S(1)}, bf16[128,192]{1,0:T(8,128)(2,1)S(1)}, u32[]{:S(2)}, u32[]{:S(2)}) collective-permute-start(bf16[128,192]{1,0:T(8,128)(2,1)S(1)} %get-tuple-element.90), channel_id=1, source_target_pairs={{0,2},{1,3},{2,0},{3,1},{4,6},{5,7},{6,4},{7,5},{8,10},{9,11},{10,... | collective-permute-start | bytes 147464 | tf_op jit(solution)/shard_map/ppermute | solution.py:678
  52.6 12.9 %collective-permute-start.20 = (bf16[128,768]{1,0:T(8,128)(2,1)S(1)}, bf16[128,768]{1,0:T(8,128)(2,1)S(1)}, u32[]{:S(2)}, u32[]{:S(2)}) collective-permute-start(bf16[128,768]{1,0:T(8,128)(2,1)S(1)} %bitcast.21), channel_id=1, source_target_pairs={{0,16},{8,24},{16,0},{24,8},{1,17},{9,25},{17,1},{25,9},{2,18},{10... | collective-permute-start | bytes 589832 | tf_op jit(solution)/shard_map/ppermute | solution.py:683
  54.1 13.0 %collective-permute-start.19 = (bf16[128,768]{1,0:T(8,128)(2,1)S(1)}, bf16[128,768]{1,0:T(8,128)(2,1)S(1)}, u32[]{:S(2)}, u32[]{:S(2)}) collective-permute-start(bf16[128,768]{1,0:T(8,128)(2,1)S(1)} %bitcast.22), channel_id=1, source_target_pairs={{0,8},{8,0},{16,24},{24,16},{1,9},{9,1},{17,25},{25,17},{2,10},{10... | collective-permute-start | bytes 589832 | tf_op jit(solution)/shard_map/ppermute | solution.py:683
  54.9 6.6 %collective-permute-start.8 = (bf16[128,192]{1,0:T(8,128)(2,1)S(1)}, bf16[128,192]{1,0:T(8,128)(2,1)S(1)}, u32[]{:S(2)}, u32[]{:S(2)}) collective-permute-start(bf16[128,192]{1,0:T(8,128)(2,1)S(1)} %get-tuple-element.91), channel_id=1, source_target_pairs={{0,4},{1,5},{2,6},{3,7},{4,0},{5,1},{6,2},{7,3},{8,12},{9,13},{10,... | collective-permute-start | bytes 147464 | tf_op jit(solution)/shard_map/ppermute | solution.py:678
  56.8 6.1 %collective-permute-start.9 = (bf16[128,192]{1,0:T(8,128)(2,1)S(1)}, bf16[128,192]{1,0:T(8,128)(2,1)S(1)}, u32[]{:S(2)}, u32[]{:S(2)}) collective-permute-start(bf16[128,192]{1,0:T(8,128)(2,1)S(1)} %get-tuple-element.92), channel_id=1, source_target_pairs={{0,6},{1,7},{2,4},{3,5},{4,2},{5,3},{6,0},{7,1},{8,14},{9,15},{10,... | collective-permute-start | bytes 147464 | tf_op jit(solution)/shard_map/ppermute | solution.py:678
  61.4 9.9 %collective-permute-start.16 = (bf16[192,768]{1,0:T(8,128)(2,1)S(1)}, bf16[192,768]{1,0:T(8,128)(2,1)S(1)}, u32[]{:S(2)}, u32[]{:S(2)}) collective-permute-start(bf16[192,768]{1,0:T(8,128)(2,1)S(1)} %get-tuple-element.158), channel_id=1, source_target_pairs={{0,8},{8,0},{16,24},{24,16},{1,9},{9,1},{17,25},{25,17},{2,10},{10... | collective-permute-start | bytes 884744 | tf_op jit(solution)/shard_map/ppermute | solution.py:683
  62.9 12.9 %collective-permute-start.17 = (bf16[192,768]{1,0:T(8,128)(2,1)S(1)}, bf16[192,768]{1,0:T(8,128)(2,1)S(1)}, u32[]{:S(2)}, u32[]{:S(2)}) collective-permute-start(bf16[192,768]{1,0:T(8,128)(2,1)S(1)} %get-tuple-element.160), channel_id=1, source_target_pairs={{0,16},{8,24},{16,0},{24,8},{1,17},{9,25},{17,1},{25,9},{2,18},{10... | collective-permute-start | bytes 884744 | tf_op jit(solution)/shard_map/ppermute | solution.py:683
  65.5 10.3 %collective-permute-start.15 = (bf16[128,768]{1,0:T(8,128)(2,1)S(1)}, bf16[128,768]{1,0:T(8,128)(2,1)S(1)}, u32[]{:S(2)}, u32[]{:S(2)}) collective-permute-start(bf16[128,768]{1,0:T(8,128)(2,1)S(1)} %get-tuple-element.94.refs_0_), channel_id=1, source_target_pairs={{0,24},{8,16},{16,8},{24,0},{1,25},{9,17},{17,9},{25,1},{2,26},{10... | collective-permute-start | bytes 589832 | tf_op jit(solution)/shard_map/ppermute | solution.py:683
  67.1 10.8 %collective-permute-start.14 = (bf16[128,768]{1,0:T(8,128)(2,1)S(1)}, bf16[128,768]{1,0:T(8,128)(2,1)S(1)}, u32[]{:S(2)}, u32[]{:S(2)}) collective-permute-start(bf16[128,768]{1,0:T(8,128)(2,1)S(1)} %get-tuple-element.94.refs_0_), channel_id=1, source_target_pairs={{0,16},{8,24},{16,0},{24,8},{1,17},{9,25},{17,1},{25,9},{2,18},{10... | collective-permute-start | bytes 589832 | tf_op jit(solution)/shard_map/ppermute | solution.py:683
  67.9 10.1 %collective-permute-start.13 = (bf16[128,768]{1,0:T(8,128)(2,1)S(1)}, bf16[128,768]{1,0:T(8,128)(2,1)S(1)}, u32[]{:S(2)}, u32[]{:S(2)}) collective-permute-start(bf16[128,768]{1,0:T(8,128)(2,1)S(1)} %get-tuple-element.94.refs_0_), channel_id=1, source_target_pairs={{0,8},{8,0},{16,24},{24,16},{1,9},{9,1},{17,25},{25,17},{2,10},{10... | collective-permute-start | bytes 589832 | tf_op jit(solution)/shard_map/ppermute | solution.py:683
  85.4 31.7 %collective-permute-start.40 = (bf16[4,384,384]{2,1,0:T(8,128)(2,1)S(1)}, bf16[4,384,384]{2,1,0:T(8,128)(2,1)S(1)}, u32[]{:S(2)}, u32[]{:S(2)}) collective-permute-start(bf16[4,384,384]{2,1,0:T(8,128)(2,1)S(1)} %get-tuple-element.138), channel_id=1, source_target_pairs={{0,1},{1,0},{2,3},{3,2},{4,5},{5,4},{6,7},{7,6},{8,9},{9,8},{10,11... | collective-permute-start | bytes 3538952 | tf_op jit(solution)/shard_map/ppermute | solution.py:675
  85.4 7.8 %collective-permute-start.25 = (bf16[128,768]{1,0:T(8,128)(2,1)S(1)}, bf16[128,768]{1,0:T(8,128)(2,1)S(1)}, u32[]{:S(2)}, u32[]{:S(2)}) collective-permute-start(bf16[128,768]{1,0:T(8,128)(2,1)S(1)} %get-tuple-element.104), channel_id=1, source_target_pairs={{0,8},{8,0},{16,24},{24,16},{1,9},{9,1},{17,25},{25,17},{2,10},{10... | collective-permute-start | bytes 589832 | tf_op jit(solution)/shard_map/ppermute | solution.py:683
  87.1 11.2 %collective-permute-start.26 = (bf16[128,768]{1,0:T(8,128)(2,1)S(1)}, bf16[128,768]{1,0:T(8,128)(2,1)S(1)}, u32[]{:S(2)}, u32[]{:S(2)}) collective-permute-start(bf16[128,768]{1,0:T(8,128)(2,1)S(1)} %get-tuple-element.105), channel_id=1, source_target_pairs={{0,16},{8,24},{16,0},{24,8},{1,17},{9,25},{17,1},{25,9},{2,18},{10... | collective-permute-start | bytes 589832 | tf_op jit(solution)/shard_map/ppermute | solution.py:683
  87.7 10.6 %collective-permute-start.27 = (bf16[128,768]{1,0:T(8,128)(2,1)S(1)}, bf16[128,768]{1,0:T(8,128)(2,1)S(1)}, u32[]{:S(2)}, u32[]{:S(2)}) collective-permute-start(bf16[128,768]{1,0:T(8,128)(2,1)S(1)} %get-tuple-element.106), channel_id=1, source_target_pairs={{0,24},{8,16},{16,8},{24,0},{1,25},{9,17},{17,9},{25,1},{2,26},{10... | collective-permute-start | bytes 589832 | tf_op jit(solution)/shard_map/ppermute | solution.py:683
  99.9 4.5 %collective-permute-start.28 = (bf16[128,192]{1,0:T(8,128)(2,1)S(1)}, bf16[128,192]{1,0:T(8,128)(2,1)S(1)}, u32[]{:S(2)}, u32[]{:S(2)}) collective-permute-start(bf16[128,192]{1,0:T(8,128)(2,1)S(1)} %get-tuple-element.111), channel_id=1, source_target_pairs={{0,2},{1,3},{2,0},{3,1},{4,6},{5,7},{6,4},{7,5},{8,10},{9,11},{10,... | collective-permute-start | bytes 147464 | tf_op jit(solution)/shard_map/ppermute | solution.py:678
  100.0 7.2 %collective-permute-start.29 = (bf16[128,192]{1,0:T(8,128)(2,1)S(1)}, bf16[128,192]{1,0:T(8,128)(2,1)S(1)}, u32[]{:S(2)}, u32[]{:S(2)}) collective-permute-start(bf16[128,192]{1,0:T(8,128)(2,1)S(1)} %get-tuple-element.112), channel_id=1, source_target_pairs={{0,4},{1,5},{2,6},{3,7},{4,0},{5,1},{6,2},{7,3},{8,12},{9,13},{10,... | collective-permute-start | bytes 147464 | tf_op jit(solution)/shard_map/ppermute | solution.py:678
  102.0 6.2 %collective-permute-start.30 = (bf16[128,192]{1,0:T(8,128)(2,1)S(1)}, bf16[128,192]{1,0:T(8,128)(2,1)S(1)}, u32[]{:S(2)}, u32[]{:S(2)}) collective-permute-start(bf16[128,192]{1,0:T(8,128)(2,1)S(1)} %get-tuple-element.113), channel_id=1, source_target_pairs={{0,6},{1,7},{2,4},{3,5},{4,2},{5,3},{6,0},{7,1},{8,14},{9,15},{10,... | collective-permute-start | bytes 147464 | tf_op jit(solution)/shard_map/ppermute | solution.py:678
  113.5 1.8 collective-permute-start.31
  114.7 9.3 %collective-permute-start.39 = (bf16[4,192,384]{2,1,0:T(8,128)(2,1)S(1)}, bf16[4,192,384]{2,1,0:T(8,128)(2,1)S(1)}, u32[]{:S(2)}, u32[]{:S(2)}) collective-permute-start(bf16[4,192,384]{2,1,0:T(8,128)(2,1)S(1)} %get-tuple-element.136), channel_id=1, source_target_pairs={{0,1},{1,0},{2,3},{3,2},{4,5},{5,4},{6,7},{7,6},{8,9},{9,8},{10,11... | collective-permute-start | bytes 1769480 | tf_op jit(solution)/shard_map/ppermute | solution.py:675
  117.9 14.4 %collective-permute-start.41 = (bf16[384,384]{1,0:T(8,128)(2,1)S(1)}, bf16[384,384]{1,0:T(8,128)(2,1)S(1)}, u32[]{:S(2)}, u32[]{:S(2)}) collective-permute-start(bf16[384,384]{1,0:T(8,128)(2,1)S(1)} %get-tuple-element.140), channel_id=1, source_target_pairs={{0,2},{1,3},{2,0},{3,1},{4,6},{5,7},{6,4},{7,5},{8,10},{9,11},{10,... | collective-permute-start | bytes 884744 | tf_op jit(solution)/shard_map/ppermute | solution.py:678
  118.9 23.4 %collective-permute-start.42 = (bf16[384,384]{1,0:T(8,128)(2,1)S(1)}, bf16[384,384]{1,0:T(8,128)(2,1)S(1)}, u32[]{:S(2)}, u32[]{:S(2)}) collective-permute-start(bf16[384,384]{1,0:T(8,128)(2,1)S(1)} %get-tuple-element.141), channel_id=1, source_target_pairs={{0,4},{1,5},{2,6},{3,7},{4,0},{5,1},{6,2},{7,3},{8,12},{9,13},{10,... | collective-permute-start | bytes 884744 | tf_op jit(solution)/shard_map/ppermute | solution.py:678
  120.9 21.5 %collective-permute-start.43 = (bf16[384,384]{1,0:T(8,128)(2,1)S(1)}, bf16[384,384]{1,0:T(8,128)(2,1)S(1)}, u32[]{:S(2)}, u32[]{:S(2)}) collective-permute-start(bf16[384,384]{1,0:T(8,128)(2,1)S(1)} %get-tuple-element.142), channel_id=1, source_target_pairs={{0,6},{1,7},{2,4},{3,5},{4,2},{5,3},{6,0},{7,1},{8,14},{9,15},{10,... | collective-permute-start | bytes 884744 | tf_op jit(solution)/shard_map/ppermute | solution.py:678
  123.8 39.6 %collective-permute-start.35 = (bf16[4,112,576]{2,1,0:T(8,128)(2,1)S(1)}, bf16[4,112,576]{2,1,0:T(8,128)(2,1)S(1)}, u32[]{:S(2)}, u32[]{:S(2)}) collective-permute-start(bf16[4,112,576]{2,1,0:T(8,128)(2,1)S(1)} %get-tuple-element.129), channel_id=1, source_target_pairs={{0,1},{1,0},{2,3},{3,2},{4,5},{5,4},{6,7},{7,6},{8,9},{9,8},{10,11... | collective-permute-start | bytes 1548296 | tf_op jit(solution)/shard_map/ppermute | solution.py:675
  143.4 7.6 %collective-permute-start.44 = (bf16[240,384]{1,0:T(8,128)(2,1)S(1)}, bf16[240,384]{1,0:T(8,128)(2,1)S(1)}, u32[]{:S(2)}, u32[]{:S(2)}) collective-permute-start(bf16[240,384]{1,0:T(8,128)(2,1)S(1)} %get-tuple-element.145), channel_id=1, source_target_pairs={{0,8},{8,0},{16,24},{24,16},{1,9},{9,1},{17,25},{25,17},{2,10},{10... | collective-permute-start | bytes 552968 | tf_op jit(solution)/shard_map/ppermute | solution.py:683
  143.9 7.2 %collective-permute-start.45 = (bf16[240,384]{1,0:T(8,128)(2,1)S(1)}, bf16[240,384]{1,0:T(8,128)(2,1)S(1)}, u32[]{:S(2)}, u32[]{:S(2)}) collective-permute-start(bf16[240,384]{1,0:T(8,128)(2,1)S(1)} %get-tuple-element.146), channel_id=1, source_target_pairs={{0,16},{8,24},{16,0},{24,8},{1,17},{9,25},{17,1},{25,9},{2,18},{10... | collective-permute-start | bytes 552968 | tf_op jit(solution)/shard_map/ppermute | solution.py:683
  145.5 8.5 %collective-permute-start.46 = (bf16[240,384]{1,0:T(8,128)(2,1)S(1)}, bf16[240,384]{1,0:T(8,128)(2,1)S(1)}, u32[]{:S(2)}, u32[]{:S(2)}) collective-permute-start(bf16[240,384]{1,0:T(8,128)(2,1)S(1)} %get-tuple-element.147), channel_id=1, source_target_pairs={{0,24},{8,16},{16,8},{24,0},{1,25},{9,17},{17,9},{25,1},{2,26},{10... | collective-permute-start | bytes 552968 | tf_op jit(solution)/shard_map/ppermute | solution.py:683
  147.0 17.7 %collective-permute-start.22 = (bf16[128,768]{1,0:T(8,128)(2,1)S(1)}, bf16[128,768]{1,0:T(8,128)(2,1)S(1)}, u32[]{:S(2)}, u32[]{:S(2)}) collective-permute-start(bf16[128,768]{1,0:T(8,128)(2,1)S(1)} %get-tuple-element.100), channel_id=1, source_target_pairs={{0,8},{8,0},{16,24},{24,16},{1,9},{9,1},{17,25},{25,17},{2,10},{10... | collective-permute-start | bytes 589832 | tf_op jit(solution)/shard_map/ppermute | solution.py:683
  154.7 24.6 %collective-permute-start.47 = (bf16[432,384]{1,0:T(8,128)(2,1)S(1)}, bf16[432,384]{1,0:T(8,128)(2,1)S(1)}, u32[]{:S(2)}, u32[]{:S(2)}) collective-permute-start(bf16[432,384]{1,0:T(8,128)(2,1)S(1)} %get-tuple-element.149), channel_id=1, source_target_pairs={{0,2},{1,3},{2,0},{3,1},{4,6},{5,7},{6,4},{7,5},{8,10},{9,11},{10,... | collective-permute-start | bytes 995336 | tf_op jit(solution)/shard_map/ppermute | solution.py:678
  161.8 8.2 %collective-permute-start.23 = (bf16[128,768]{1,0:T(8,128)(2,1)S(1)}, bf16[128,768]{1,0:T(8,128)(2,1)S(1)}, u32[]{:S(2)}, u32[]{:S(2)}) collective-permute-start(bf16[128,768]{1,0:T(8,128)(2,1)S(1)} %get-tuple-element.101), channel_id=1, source_target_pairs={{0,16},{8,24},{16,0},{24,8},{1,17},{9,25},{17,1},{25,9},{2,18},{10... | collective-permute-start | bytes 589832 | tf_op jit(solution)/shard_map/ppermute | solution.py:683
  163.1 27.9 %collective-permute-start.48 = (bf16[432,384]{1,0:T(8,128)(2,1)S(1)}, bf16[432,384]{1,0:T(8,128)(2,1)S(1)}, u32[]{:S(2)}, u32[]{:S(2)}) collective-permute-start(bf16[432,384]{1,0:T(8,128)(2,1)S(1)} %get-tuple-element.150), channel_id=1, source_target_pairs={{0,4},{1,5},{2,6},{3,7},{4,0},{5,1},{6,2},{7,3},{8,12},{9,13},{10,... | collective-permute-start | bytes 995336 | tf_op jit(solution)/shard_map/ppermute | solution.py:678
  164.1 6.8 %collective-permute-start.36 = (bf16[112,576]{1,0:T(8,128)(2,1)S(1)}, bf16[112,576]{1,0:T(8,128)(2,1)S(1)}, u32[]{:S(2)}, u32[]{:S(2)}) collective-permute-start(bf16[112,576]{1,0:T(8,128)(2,1)S(1)} %get-tuple-element.131), channel_id=1, source_target_pairs={{0,8},{8,0},{16,24},{24,16},{1,9},{9,1},{17,25},{25,17},{2,10},{10... | collective-permute-start | bytes 387080 | tf_op jit(solution)/shard_map/ppermute | solution.py:683
  164.7 26.3 %collective-permute-start.49 = (bf16[432,384]{1,0:T(8,128)(2,1)S(1)}, bf16[432,384]{1,0:T(8,128)(2,1)S(1)}, u32[]{:S(2)}, u32[]{:S(2)}) collective-permute-start(bf16[432,384]{1,0:T(8,128)(2,1)S(1)} %get-tuple-element.151), channel_id=1, source_target_pairs={{0,6},{1,7},{2,4},{3,5},{4,2},{5,3},{6,0},{7,1},{8,14},{9,15},{10,... | collective-permute-start | bytes 995336 | tf_op jit(solution)/shard_map/ppermute | solution.py:678
  170.0 7.1 %collective-permute-start.37 = (bf16[112,576]{1,0:T(8,128)(2,1)S(1)}, bf16[112,576]{1,0:T(8,128)(2,1)S(1)}, u32[]{:S(2)}, u32[]{:S(2)}) collective-permute-start(bf16[112,576]{1,0:T(8,128)(2,1)S(1)} %get-tuple-element.132), channel_id=1, source_target_pairs={{0,16},{8,24},{16,0},{24,8},{1,17},{9,25},{17,1},{25,9},{2,18},{10... | collective-permute-start | bytes 387080 | tf_op jit(solution)/shard_map/ppermute | solution.py:683
  170.9 8.1 %collective-permute-start.38 = (bf16[112,576]{1,0:T(8,128)(2,1)S(1)}, bf16[112,576]{1,0:T(8,128)(2,1)S(1)}, u32[]{:S(2)}, u32[]{:S(2)}) collective-permute-start(bf16[112,576]{1,0:T(8,128)(2,1)S(1)} %get-tuple-element.133), channel_id=1, source_target_pairs={{0,24},{8,16},{16,8},{24,0},{1,25},{9,17},{17,9},{25,1},{2,26},{10... | collective-permute-start | bytes 387080 | tf_op jit(solution)/shard_map/ppermute | solution.py:683
  177.1 15.8 %collective-permute-start.24 = (bf16[128,768]{1,0:T(8,128)(2,1)S(1)}, bf16[128,768]{1,0:T(8,128)(2,1)S(1)}, u32[]{:S(2)}, u32[]{:S(2)}) collective-permute-start(bf16[128,768]{1,0:T(8,128)(2,1)S(1)} %get-tuple-element.102), channel_id=1, source_target_pairs={{0,24},{8,16},{16,8},{24,0},{1,25},{9,17},{17,9},{25,1},{2,26},{10... | collective-permute-start | bytes 589832 | tf_op jit(solution)/shard_map/ppermute | solution.py:683
  179.0 16.1 %collective-permute-start.32 = (bf16[128,768]{1,0:T(8,128)(2,1)S(1)}, bf16[128,768]{1,0:T(8,128)(2,1)S(1)}, u32[]{:S(2)}, u32[]{:S(2)}) collective-permute-start(bf16[128,768]{1,0:T(8,128)(2,1)S(1)} %get-tuple-element.119), channel_id=1, source_target_pairs={{0,2},{1,3},{2,0},{3,1},{4,6},{5,7},{6,4},{7,5},{8,10},{9,11},{10,... | collective-permute-start | bytes 589832 | tf_op jit(solution)/shard_map/ppermute | solution.py:678
  179.4 31.6 %collective-permute-start.33 = (bf16[128,768]{1,0:T(8,128)(2,1)S(1)}, bf16[128,768]{1,0:T(8,128)(2,1)S(1)}, u32[]{:S(2)}, u32[]{:S(2)}) collective-permute-start(bf16[128,768]{1,0:T(8,128)(2,1)S(1)} %get-tuple-element.120), channel_id=1, source_target_pairs={{0,4},{1,5},{2,6},{3,7},{4,0},{5,1},{6,2},{7,3},{8,12},{9,13},{10,... | collective-permute-start | bytes 589832 | tf_op jit(solution)/shard_map/ppermute | solution.py:678
  191.0 26.6 %collective-permute-start.57 = (bf16[432,384]{1,0:T(8,128)(2,1)S(1)}, bf16[432,384]{1,0:T(8,128)(2,1)S(1)}, u32[]{:S(2)}, u32[]{:S(2)}) collective-permute-start(bf16[432,384]{1,0:T(8,128)(2,1)S(1)} %get-tuple-element.148.refs_4_.refs_0_), channel_id=1, source_target_pairs={{0,1},{1,0},{2,3},{3,2},{4,5},{5,4},{6,7},{7,6},{8,9},{9,8},{10,11... | collective-permute-start | bytes 995336 | tf_op jit(solution)/shard_map/ppermute | solution.py:675
  191.0 19.9 %collective-permute-start.34 = (bf16[128,768]{1,0:T(8,128)(2,1)S(1)}, bf16[128,768]{1,0:T(8,128)(2,1)S(1)}, u32[]{:S(2)}, u32[]{:S(2)}) collective-permute-start(bf16[128,768]{1,0:T(8,128)(2,1)S(1)} %get-tuple-element.121), channel_id=1, source_target_pairs={{0,6},{1,7},{2,4},{3,5},{4,2},{5,3},{6,0},{7,1},{8,14},{9,15},{10,... | collective-permute-start | bytes 589832 | tf_op jit(solution)/shard_map/ppermute | solution.py:678
  192.9 24.7 %collective-permute-start.52 = (bf16[160,576]{1,0:T(8,128)(2,1)S(1)}, bf16[160,576]{1,0:T(8,128)(2,1)S(1)}, u32[]{:S(2)}, u32[]{:S(2)}) collective-permute-start(bf16[160,576]{1,0:T(8,128)(2,1)S(1)} %input_sum.1.refs_0_), channel_id=1, source_target_pairs={{0,6},{1,7},{2,4},{3,5},{4,2},{5,3},{6,0},{7,1},{8,14},{9,15},{10,... | collective-permute-start | bytes 552968 | tf_op jit(solution)/shard_map/ppermute | solution.py:678
  195.0 31.5 %collective-permute-start.58 = (bf16[432,384]{1,0:T(8,128)(2,1)S(1)}, bf16[432,384]{1,0:T(8,128)(2,1)S(1)}, u32[]{:S(2)}, u32[]{:S(2)}) collective-permute-start(bf16[432,384]{1,0:T(8,128)(2,1)S(1)} %collective-permute-done.47.refs_5_.refs_1_), channel_id=1, source_target_pairs={{0,1},{1,0},{2,3},{3,2},{4,5},{5,4},{6,7},{7,6},{8,9},{9,8},{10,11... | collective-permute-start | bytes 995336 | tf_op jit(solution)/shard_map/ppermute | solution.py:675
  210.9 16.1 %collective-permute-start.59 = (bf16[432,384]{1,0:T(8,128)(2,1)S(1)}, bf16[432,384]{1,0:T(8,128)(2,1)S(1)}, u32[]{:S(2)}, u32[]{:S(2)}) collective-permute-start(bf16[432,384]{1,0:T(8,128)(2,1)S(1)} %collective-permute-done.48.refs_6_.refs_2_), channel_id=1, source_target_pairs={{0,1},{1,0},{2,3},{3,2},{4,5},{5,4},{6,7},{7,6},{8,9},{9,8},{10,11... | collective-permute-start | bytes 995336 | tf_op jit(solution)/shard_map/ppermute | solution.py:675
  210.9 13.9 %collective-permute-start.51 = (bf16[160,576]{1,0:T(8,128)(2,1)S(1)}, bf16[160,576]{1,0:T(8,128)(2,1)S(1)}, u32[]{:S(2)}, u32[]{:S(2)}) collective-permute-start(bf16[160,576]{1,0:T(8,128)(2,1)S(1)} %input_sum.1.refs_0_), channel_id=1, source_target_pairs={{0,4},{1,5},{2,6},{3,7},{4,0},{5,1},{6,2},{7,3},{8,12},{9,13},{10,... | collective-permute-start | bytes 552968 | tf_op jit(solution)/shard_map/ppermute | solution.py:678
  217.6 8.9 %collective-permute-start.50 = (bf16[160,576]{1,0:T(8,128)(2,1)S(1)}, bf16[160,576]{1,0:T(8,128)(2,1)S(1)}, u32[]{:S(2)}, u32[]{:S(2)}) collective-permute-start(bf16[160,576]{1,0:T(8,128)(2,1)S(1)} %input_sum.1.refs_0_), channel_id=1, source_target_pairs={{0,2},{1,3},{2,0},{3,1},{4,6},{5,7},{6,4},{7,5},{8,10},{9,11},{10,... | collective-permute-start | bytes 552968 | tf_op jit(solution)/shard_map/ppermute | solution.py:678
  217.6 11.4 %collective-permute-start.60 = (bf16[432,384]{1,0:T(8,128)(2,1)S(1)}, bf16[432,384]{1,0:T(8,128)(2,1)S(1)}, u32[]{:S(2)}, u32[]{:S(2)}) collective-permute-start(bf16[432,384]{1,0:T(8,128)(2,1)S(1)} %collective-permute-done.49.refs_7_.refs_3_), channel_id=1, source_target_pairs={{0,1},{1,0},{2,3},{3,2},{4,5},{5,4},{6,7},{7,6},{8,9},{9,8},{10,11... | collective-permute-start | bytes 995336 | tf_op jit(solution)/shard_map/ppermute | solution.py:675
  224.8 7.3 %collective-permute-start.53 = (bf16[160,576]{1,0:T(8,128)(2,1)S(1)}, bf16[160,576]{1,0:T(8,128)(2,1)S(1)}, u32[]{:S(2)}, u32[]{:S(2)}) collective-permute-start(bf16[160,576]{1,0:T(8,128)(2,1)S(1)} %input_sum.1.refs_0_), channel_id=1, source_target_pairs={{0,1},{1,0},{2,3},{3,2},{4,5},{5,4},{6,7},{7,6},{8,9},{9,8},{10,11... | collective-permute-start | bytes 552968 | tf_op jit(solution)/shard_map/ppermute | solution.py:675
  226.5 5.6 %collective-permute-start.56 = (bf16[160,576]{1,0:T(8,128)(2,1)S(1)}, bf16[160,576]{1,0:T(8,128)(2,1)S(1)}, u32[]{:S(2)}, u32[]{:S(2)}) collective-permute-start(bf16[160,576]{1,0:T(8,128)(2,1)S(1)} %collective-permute-done.52.refs_3_), channel_id=1, source_target_pairs={{0,1},{1,0},{2,3},{3,2},{4,5},{5,4},{6,7},{7,6},{8,9},{9,8},{10,11... | collective-permute-start | bytes 552968 | tf_op jit(solution)/shard_map/ppermute | solution.py:675
  226.5 5.6 %collective-permute-start.55 = (bf16[160,576]{1,0:T(8,128)(2,1)S(1)}, bf16[160,576]{1,0:T(8,128)(2,1)S(1)}, u32[]{:S(2)}, u32[]{:S(2)}) collective-permute-start(bf16[160,576]{1,0:T(8,128)(2,1)S(1)} %collective-permute-done.51.refs_2_), channel_id=1, source_target_pairs={{0,1},{1,0},{2,3},{3,2},{4,5},{5,4},{6,7},{7,6},{8,9},{9,8},{10,11... | collective-permute-start | bytes 552968 | tf_op jit(solution)/shard_map/ppermute | solution.py:675
  227.0 5.1 %collective-permute-start.54 = (bf16[160,576]{1,0:T(8,128)(2,1)S(1)}, bf16[160,576]{1,0:T(8,128)(2,1)S(1)}, u32[]{:S(2)}, u32[]{:S(2)}) collective-permute-start(bf16[160,576]{1,0:T(8,128)(2,1)S(1)} %collective-permute-done.50.refs_1_), channel_id=1, source_target_pairs={{0,1},{1,0},{2,3},{3,2},{4,5},{5,4},{6,7},{7,6},{8,9},{9,8},{10,11... | collective-permute-start | bytes 552968 | tf_op jit(solution)/shard_map/ppermute | solution.py:675
  (9 other events, 70.1 us)

commit v2 on v1

--- a/solution.py
+++ b/solution.py
@@ -575,7 +575,7 @@
     return (block_out, grad_tokens) + tuple(grad_final)
 
 
-VMEM_BYTES = 40 * 1024 * 1024
+VMEM_BYTES = 28 * 1024 * 1024
 
 
 def mm(left, right):
@@ -624,19 +624,26 @@
     return jax.ShapeDtypeStruct(dims, dtype)
 
 
-def local_call(kernel, name, outs, args, scalars=0, scratch=(), flops=0):
+def local_call(
+    kernel, name, outs, args, scalars=0, scratch=(), flops=0, after=(), space=pltpu.VMEM, grant=VMEM_BYTES
+):
     moved = sum(math.prod(a.shape) * a.dtype.itemsize for a in tuple(args) + tuple(outs))
+
+    def ordered(*refs):
+        kernel(*refs[: len(args)], *refs[len(args) + len(after) :])
+
     return pl.pallas_call(
-        kernel,
+        ordered,
         out_shape=tuple(outs),
         in_specs=[pl.BlockSpec(memory_space=pltpu.SMEM)] * scalars
-        + [pl.BlockSpec(memory_space=pltpu.VMEM)] * (len(args) - scalars),
+        + [pl.BlockSpec(memory_space=space)] * (len(args) - scalars)
+        + [pl.BlockSpec(memory_space=pl.ANY)] * len(after),
         out_specs=tuple(pl.BlockSpec(memory_space=pltpu.VMEM) for _ in outs),
         scratch_shapes=list(scratch),
-        compiler_params=pltpu.CompilerParams(vmem_limit_bytes=VMEM_BYTES),
+        compiler_params=pltpu.CompilerParams(vmem_limit_bytes=grant),
         cost_estimate=pl.CostEstimate(flops=flops, bytes_accessed=moved, transcendentals=0),
         name=name,
-    )(*args)
+    )(*args, *after)
 
 
 def place_of_block(pair_ref, info_ref, ranks, step, half, other_core):
@@ -720,36 +727,80 @@
 
         own_tokens = tokens[0]
         token_parts = [own_tokens] + [chip_swap(own_tokens, k) for k in others]
-        small_own = jnp.stack(
-            [
-                first_gain,
-                first_shift,
-                query_bias,
-                value_bias,
-                output_bias,
-                second_gain,
-                second_shift,
-                contract_bias,
+        def pack_kernel(info_ref, w_ref, *refs):
+            vecs, (packed_ref, w_scr), scrs, (sems,) = (
+                refs[:8],
+                refs[8:10],
+                refs[10:18],
+                refs[18:],
+            )
+            copies = [
+                pltpu.make_async_copy(src, dst, sems.at[i])
+                for i, (src, dst) in enumerate(zip((w_ref, *vecs), (w_scr, *scrs)))
             ]
-        )
-        small_own = jnp.pad(small_own, ((0, small_rows - 8), (0, 3 * hw - own_width)))
-        w_heads = jnp.concatenate(
-            [
-                lax.dynamic_slice(w_input, (0, base * width + chip * hw), (own_width, hw))
-                for base in range(3)
-            ],
-            axis=1,
-        )
-        packed = jnp.concatenate([w_heads, small_own], axis=0)
+            for copy in copies:
+                copy.start()
+            for copy in copies:
+                copy.wait()
+            for at in range(chips):
+
+                @pl.when(info_ref[1] == at)
+                def _():
+                    for base in range(3):
+                        start = base * width + at * hw
+                        packed_ref[0:own_width, base * hw : (base + 1) * hw] = w_scr[
+                            :, start : start + hw
+                        ]
+
+            small = jnp.concatenate(
+                [v[...].astype(f32).reshape(1, own_width) for v in scrs], axis=0
+            )
+            small = jnp.concatenate([small, jnp.zeros_like(small)], axis=0)
+            packed_ref[own_width:, 0:own_width] = small.astype(bf)
+            packed_ref[own_width:, own_width:] = jnp.zeros((small_rows, 3 * hw - own_width), bf)
+
+        small_args = (
+            first_gain,
+            first_shift,
+            query_bias,
+            value_bias,
+            output_bias,
+            second_gain,
+            second_shift,
+            contract_bias,
+        )
+        (packed,) = local_call(
+            pack_kernel,
+            "pack",
+            [shape_of((own_width + small_rows, 3 * hw), bf)],
+            [info, w_input] + list(small_args),
+            scalars=1,
+            scratch=[pltpu.VMEM((own_width, 3 * width), bf)]
+            + [pltpu.VMEM((own_width,), bf)] * 8
+            + [pltpu.SemaphoreType.DMA((9,))],
+            space=pltpu.HBM,
+            grant=60 * 1024 * 1024,
+        )
         packed_parts = [packed] + [seq_swap(packed, j) for j in others]
+        own_cot = cotangent[0]
         out_parts = [w_output] + [seq_swap(w_output, j) for j in others]
-        expand_own = [
-            lax.dynamic_slice(w_expand, (0, jnp.bitwise_xor(seq_id, j) * ff), (own_width, ff))
-            for j in range(seq_parts)
-        ]
-        expand_parts = [expand_own[0]] + [seq_swap(expand_own[j], j) for j in others]
-        own_cot = cotangent[0]
-        cot_parts = [own_cot] + [seq_swap(own_cot, j) for j in others]
+
+        def pack_more_kernel(info_ref, we_ref, cot_ref, *refs):
+            for j in others:
+                refs[j - 1][0:own_width, :] = we_ref[
+                    :, aligned(jnp.bitwise_xor(info_ref[0], j), ff)
+                ]
+                refs[j - 1][own_width:, :] = cot_ref[...]
+
+        more = local_call(
+            pack_more_kernel,
+            "pack_more",
+            [shape_of((own_width + rows, width), bf)] * (seq_parts - 1),
+            [info, w_expand, own_cot],
+            scalars=1,
+            after=[packed],
+        )
+        more_parts = [seq_swap(more[j - 1], j) for j in others]
 
         def qkv_kernel(info_ref, *refs):
             toks, packs = refs[:parts], refs[parts : 2 * parts]
@@ -785,6 +836,7 @@
             ],
             [info] + token_parts + packed_parts,
             scalars=1,
+            after=out_parts[1:],
             scratch=[pltpu.VMEM((parts, small_rows, own_width), f32)],
             flops=2 * total * width * 3 * hw,
         )
@@ -835,83 +887,69 @@
 
         def middle_kernel(info_ref, tok_ref, vec_ref, *refs):
             atts, outs = refs[:parts], refs[parts : 2 * parts]
-            mid_ref, normed_ref, w_scr = refs[2 * parts :]
+            mid_ref, normed_ref, w_ref = refs[2 * parts :]
             for j in range(parts):
-                w_scr[jnp.bitwise_xor(info_ref[0], j)] = outs[j][...]
+                w_ref[jnp.bitwise_xor(info_ref[0], j)] = outs[j][...]
             middle = tok_ref[...].astype(f32) + vec_ref[4:5]
             for k in range(parts):
-                middle = middle + mm(atts[k][...], w_scr[jnp.bitwise_xor(info_ref[1], k)])
+                middle = middle + mm(atts[k][...], w_ref[jnp.bitwise_xor(info_ref[1], k)])
             mid_ref[...] = middle
             xhat, _ = norm_stats(middle)
             normed_ref[...] = (xhat * vec_ref[5:6] + vec_ref[6:7]).astype(bf)
 
-        middle, own_normed_two = local_call(
+        middle, own_normed_two, out_full = local_call(
             middle_kernel,
             "middle",
-            [shape_of((rows, width), f32), shape_of((rows, width), bf)],
+            [
+                shape_of((rows, width), f32),
+                shape_of((rows, width), bf),
+                shape_of((parts, own_width, width), bf),
+            ],
             [info, own_tokens, vectors] + att_parts + out_parts,
             scalars=1,
-            scratch=[pltpu.VMEM((parts, own_width, width), bf)],
             flops=2 * rows * width * width,
         )
         n2_parts = [own_normed_two] + [seq_swap(own_normed_two, j) for j in others]
 
-        def ffn_kernel(info_ref, bias_ref, wc_ref, *refs):
+        span = ff // parts + own_width
+
+        def ffn_kernel(info_ref, bias_ref, wc_ref, we_ref, own_cot_ref, *refs):
             n2s = refs[:parts]
-            wes = refs[parts : 2 * parts]
-            cots = refs[2 * parts : 3 * parts]
-            gns = refs[3 * parts : 4 * parts]
-            active_ref, gh_ref, n2_ref, cot_ref, w_scr = refs[4 * parts :]
-            for j in range(parts):
-                w_scr[aligned(jnp.bitwise_xor(info_ref[0], j), own_width), :] = wes[j][...]
-                n2_ref[j * rows : (j + 1) * rows, :] = n2s[j][...]
-                cot_ref[j * rows : (j + 1) * rows, :] = cots[j][...]
-            hidden = mm(n2_ref[...], w_scr[...]) + bias_ref[...].astype(f32)
+            mores = refs[parts : 2 * parts - 1]
+            gns = refs[2 * parts - 1 : 3 * parts - 1]
+            result_ref, keep_ref, send_ref, sum_ref = refs[3 * parts - 1 : 3 * parts + 3]
+            active_ref, gh_ref, n2_ref, cot_ref, w_scr, scr = refs[3 * parts + 3 :]
+            w_scr[aligned(info_ref[0], own_width), :] = we_ref[:, aligned(info_ref[0], ff)]
+            for j in range(seq_parts):
+                at = slice(j * rows, (j + 1) * rows)
+                n2_ref[at, :] = n2s[j][...]
+                if j == 0:
+                    cot_ref[at, :] = own_cot_ref[...]
+                    continue
+                place = jnp.bitwise_xor(info_ref[0], j)
+                w_scr[aligned(place, own_width), :] = mores[j - 1][0:own_width, :]
+                cot_ref[at, :] = mores[j - 1][own_width:, :]
+            hidden = mm(n2_ref[...], w_scr[...]) + bias_ref[...].astype(f32).reshape(1, ff)
             square = hidden * hidden
             curve = jnp.tanh(GELU_SCALE * hidden * (1.0 + GELU_CUBIC * square))
             active_ref[...] = (0.5 * hidden * (1.0 + curve)).astype(bf)
             slope = 0.5 * (1.0 + curve) + 0.5 * hidden * (1.0 - curve * curve) * GELU_SCALE * (
                 1.0 + 3.0 * GELU_CUBIC * square
             )
-            gh_ref[...] = (mm_nt(cot_ref[...], wc_ref[...]) * slope).astype(bf)
+            grad_hidden = mm_nt(cot_ref[...], wc_ref[...]) * slope
+            gh_ref[...] = grad_hidden.astype(bf)
+            sum_ref[...] = column_sums(gh_ref[...].astype(f32))
             grad = mm_nt(gh_ref[...], w_scr[...]).astype(bf)
             for j in range(parts):
                 gns[j][...] = grad[j * rows : (j + 1) * rows]
-
-        ffn_out = local_call(
-            ffn_kernel,
-            "feed",
-            [shape_of((rows, width), bf)] * parts
-            + [
-                shape_of((total, ff), bf),
-                shape_of((total, ff), bf),
-                shape_of((total, width), bf),
-                shape_of((total, width), bf),
-            ],
-            [info, expand_bias.reshape(1, ff), w_contract] + n2_parts + expand_parts + cot_parts,
-            scalars=1,
-            scratch=[pltpu.VMEM((width, ff), bf)],
-            flops=3 * 2 * total * width * ff,
-        )
-        active, grad_hidden, n2_all, cot_all = ffn_out[parts:]
-        gn_parts = [ffn_out[0]] + [seq_swap(ffn_out[j], j) for j in others]
-
-        def ffn_weights_kernel(info_ref, active_ref, gh_ref, n2_ref, cot_ref, wc_ref, *refs):
-            results = refs[:parts]
-            keep_ref, send_ref, bias_ref, scr = refs[parts:]
-            result = mm(active_ref[...], wc_ref[...]).astype(bf)
-            for j in range(parts):
-                results[j][...] = result[j * rows : (j + 1) * rows]
-            bias_ref[...] = column_sums(gh_ref[...].astype(f32))
+            result_ref[...] = mm(active_ref[...], wc_ref[...]).astype(bf)
             core_id = info_ref[2]
             for flip, out_ref in ((0, keep_ref), (1, send_ref)):
                 half = jnp.bitwise_xor(core_id, flip)
                 scr[...] = mm_tn(active_ref[...], cot_ref[:, aligned(half, half_width)]).astype(bf)
                 for part in range(parts):
-                    span = ff // parts
-                    out_ref[part, 0:span, :] = scr[part * span : (part + 1) * span, :]
-            for flip, out_ref in ((0, keep_ref), (1, send_ref)):
-                half = jnp.bitwise_xor(core_id, flip)
+                    rows_to = ff // parts
+                    out_ref[part, 0:rows_to, :] = scr[part * rows_to : (part + 1) * rows_to, :]
                 scr[...] = mm_tn(n2_ref[...], gh_ref[:, aligned(half, half_ff)]).astype(bf)
                 for part in range(parts):
                     for j in range(seq_parts):
@@ -919,45 +957,58 @@
                         row = j * own_width + part * sub
                         out_ref[part, at : at + sub, :] = scr[row : row + sub, :]
 
-        span = ff // parts + own_width
-        fw_out = local_call(
-            ffn_weights_kernel,
-            "feed_weights",
+        ffn_out = local_call(
+            ffn_kernel,
+            "feed",
             [shape_of((rows, width), bf)] * parts
             + [
+                shape_of((total, width), bf),
                 shape_of((parts, span, half_width), bf),
                 shape_of((parts, span, half_width), bf),
                 shape_of((1, ff), f32),
             ],
-            [info, active, grad_hidden, n2_all, cot_all, w_contract],
+            [info, expand_bias, w_contract, w_expand, own_cot] + n2_parts + more_parts,
             scalars=1,
-            scratch=[pltpu.VMEM((width, half_width), bf)],
-            flops=3 * 2 * total * width * ff,
-        )
-        ffn_keep, ffn_send, grad_expand_row = fw_out[parts:]
-        res_parts = [fw_out[0]] + [seq_swap(fw_out[j], j) for j in others]
+            scratch=[
+                pltpu.VMEM((total, ff), bf),
+                pltpu.VMEM((total, ff), bf),
+                pltpu.VMEM((total, width), bf),
+                pltpu.VMEM((total, width), bf),
+                pltpu.VMEM((width, ff), bf),
+                pltpu.VMEM((width, half_ff), bf),
+            ],
+            flops=6 * 2 * total * width * ff,
+        )
+        result, ffn_keep, ffn_send, grad_expand_row = ffn_out[parts:]
+        gn_parts = [ffn_out[0]] + [seq_swap(ffn_out[j], j) for j in others]
         ffn_far = core_swap(ffn_send)
 
-        def pick_kernel(info_ref, keep_ref, far_ref, *outs):
+        def halve_kernel(info_ref, keep_ref, far_ref, own_ref, out_ref):
             for k in range(parts):
                 at = jnp.bitwise_xor(info_ref[1], k)
-                outs[k][...] = (keep_ref[at].astype(f32) + far_ref[at].astype(f32)).astype(bf)
-
-        ffn_chunks = local_call(
-            pick_kernel,
-            "feed_chunks",
-            [shape_of((span, half_width), bf)] * parts,
+                piece = keep_ref[at].astype(f32) + far_ref[at].astype(f32)
+                if k % 2:
+                    out_ref[k // 2] = piece.astype(bf)
+                else:
+                    own_ref[k // 2] = piece
+
+        rs_own, rs_send = local_call(
+            halve_kernel,
+            "feed_halves",
+            [
+                shape_of((parts // 2, span, half_width), f32),
+                shape_of((parts // 2, span, half_width), bf),
+            ],
             [info, ffn_keep, ffn_far],
             scalars=1,
-        )
-        ffn_parts = [ffn_chunks[0]] + [chip_swap(ffn_chunks[k], k) for k in others]
-
-        def back_kernel(info_ref, mid_ref, vec_ref, cot_ref, *refs):
-            gns, outs = refs[:parts], refs[parts : 2 * parts]
-            douts = refs[2 * parts : 3 * parts]
-            gmid_ref, branch_ref, sums_ref, w_scr = refs[3 * parts :]
-            for j in range(parts):
-                w_scr[jnp.bitwise_xor(info_ref[0], j)] = outs[j][...]
+            after=gn_parts[1:],
+        )
+        rs_far = chip_swap(rs_send, 1)
+
+        def back_kernel(info_ref, mid_ref, vec_ref, cot_ref, w_ref, *refs):
+            gns = refs[:parts]
+            douts = refs[parts : 2 * parts]
+            gmid_ref, branch_ref, sums_ref = refs[2 * parts :]
             grad = gns[0][...].astype(f32)
             for j in others:
                 grad = grad + gns[j][...].astype(f32)
@@ -968,7 +1019,7 @@
             branch = grad_middle.astype(bf)
             branch_ref[...] = branch
             for k in range(parts):
-                douts[k][...] = mm_nt(branch, w_scr[jnp.bitwise_xor(info_ref[1], k)]).astype(bf)
+                douts[k][...] = mm_nt(branch, w_ref[jnp.bitwise_xor(info_ref[1], k)]).astype(bf)
             sums_ref[0:1, :] = column_sums(branch.astype(f32))
             sums_ref[1:2, :] = column_sums(grad * xhat)
             sums_ref[2:3, :] = column_sums(grad)
@@ -983,9 +1034,9 @@
                 shape_of((rows, width), bf),
                 shape_of((8, width), f32),
             ],
-            [info, middle, vectors, own_cot] + gn_parts + out_parts,
+            [info, middle, vectors, own_cot, out_full] + gn_parts,
             scalars=1,
-            scratch=[pltpu.VMEM((parts, own_width, width), bf)],
+            after=[rs_send],
             flops=2 * rows * width * width,
         )
         grad_middle, grad_branch, late_sums = back_out[parts:]
@@ -1009,6 +1060,25 @@
             flops=2 * rows * width * width,
         )
         out_far = core_swap(out_send)
+
+        fold = own_width // 2
+
+        def out_chunks_kernel(info_ref, result_ref, keep_ref, far_ref, *outs):
+            for j in range(seq_parts):
+                to = jnp.bitwise_xor(info_ref[0], j)
+                outs[j][0:rows, :] = result_ref[j * rows : (j + 1) * rows, :]
+                whole = (keep_ref[to].astype(f32) + far_ref[to].astype(f32)).astype(bf)
+                outs[j][rows:, 0:half_width] = whole[0:fold]
+                outs[j][rows:, half_width:] = whole[fold:]
+
+        out_chunks = local_call(
+            out_chunks_kernel,
+            "output_chunks",
+            [shape_of((rows + fold, width), bf)] * seq_parts,
+            [info, result, out_keep, out_far],
+            scalars=1,
+        )
+        oc_parts = [out_chunks[0]] + [seq_swap(out_chunks[j], j) for j in others]
 
         def attend_back_kernel(info_ref, pair_ref, q_ref, kv_ref, far_ref, flat_ref, lse_ref, *refs):
             douts = refs[:parts]
@@ -1052,22 +1122,38 @@
             ],
             [info, pair_of_rank, query, own_kv, far_kv, flat_attended, row_lse] + dout_parts,
             scalars=2,
+            after=[out_chunks[0]],
             scratch=[pltpu.VMEM((2 * total, total), f32), pltpu.VMEM((total, hw), f32)],
             flops=5 * 2 * head_count * 2 * total * total * HEAD_DIM,
         )
         dkv_far = core_swap(dkv_send)
 
+        def quarter_kernel(own_ref, far_ref, keep_ref, send_ref):
+            keep_ref[...] = own_ref[0] + far_ref[0].astype(f32)
+            send_ref[...] = (own_ref[1] + far_ref[1].astype(f32)).astype(bf)
+
+        rs_own_two, rs_send_two = local_call(
+            quarter_kernel,
+            "feed_quarters",
+            [shape_of((span, half_width), f32), shape_of((span, half_width), bf)],
+            [rs_own, rs_far],
+            after=[dkv_send],
+        )
+        rs_far_two = chip_swap(rs_send_two, 2)
+
         def normed_back_kernel(dq_ref, own_ref, far_ref, w_ref, *refs):
             toks = refs[:parts]
-            chunks = refs[parts : 2 * parts]
-            mixed_ref, sums_ref, bias_ref = refs[2 * parts :]
+            keep_ref, send_ref, mixed_ref, sums_ref, bias_ref = refs[parts:]
             mixed_ref[:, 0:hw] = dq_ref[...].T.astype(bf)
             mixed_ref[:, hw:] = (own_ref[...] + far_ref[...].astype(f32)).astype(bf)
             shift_sum = jnp.zeros((1, width), f32)
             gain_sum = jnp.zeros((1, width), f32)
             for k in range(parts):
                 grad = mm_nt(mixed_ref[k * rows : (k + 1) * rows, :], w_ref[...])
-                chunks[k][...] = grad.astype(bf)
+                if k % 2:
+                    send_ref[k // 2] = grad.astype(bf)
+                else:
+                    keep_ref[k // 2] = grad
                 xhat, _ = norm_stats(toks[k][...].astype(f32))
                 shift_sum = shift_sum + column_sums(grad)
                 gain_sum = gain_sum + column_sums(grad * xhat)
@@ -1078,17 +1164,19 @@
         nb_out = local_call(
             normed_back_kernel,
             "normed_back",
-            [shape_of((rows, width), bf)] * parts
-            + [
+            [
+                shape_of((parts // 2, rows, width), f32),
+                shape_of((parts // 2, rows, width), bf),
                 shape_of((total, 3 * hw), bf),
                 shape_of((8, width), f32),
                 shape_of((8, 3 * hw), f32),
             ],
             [flat_dq, dkv_own, dkv_far, w_heads_full] + token_parts,
             flops=2 * total * width * 3 * hw,
-        )
-        grad_mixed, first_sums, mixed_sums = nb_out[parts:]
-        gt_parts = [nb_out[0]] + [chip_swap(nb_out[k], k) for k in others]
+            after=[rs_send_two],
+        )
+        gt_keep, gt_send, grad_mixed, first_sums, mixed_sums = nb_out
+        gt_far = chip_swap(gt_send, 1)
 
         tall = half_own + small_rows
 
@@ -1130,186 +1218,210 @@
         )
         in_far = core_swap(in_send)
 
-        def owner_kernel(info_ref, keep_ref, far_ref, *refs):
-            ffns = refs[:parts]
-            con_ref = refs[parts]
-            outs = refs[parts + 1 :]
-            whole = ffns[0][...].astype(f32)
-            for k in others:
-                whole = whole + ffns[k][...].astype(f32)
-            con_ref[...] = whole.astype(bf)
+        def out_sum_kernel(info_ref, mid_ref, vec_ref, *refs):
+            owned = refs[:seq_parts]
+            keep_ref, send_ref, block_ref, scr = refs[seq_parts:]
+            result = mid_ref[...] + vec_ref[7:8]
+            outs = jnp.zeros((fold, width), f32)
             for j in range(seq_parts):
-                to = jnp.bitwise_xor(info_ref[0], j)
-                start = pl.multiple_of(ff // parts + to * sub, 16)
-                outs[j][0:sub, :] = con_ref[pl.ds(start, sub), :]
-                outs[j][sub:, :] = (
-                    keep_ref[to].astype(f32) + far_ref[to].astype(f32)
-                ).astype(bf)
-
-        ow_out = local_call(
-            owner_kernel,
+                result = result + owned[j][0:rows, :].astype(f32)
+                outs = outs + owned[j][rows:, :].astype(f32)
+            block_ref[0] = result.astype(bf)
+            scr[0:fold, :] = outs[:, 0:half_width]
+            scr[fold:, :] = outs[:, half_width:]
+            for k in range(parts):
+                piece = scr[aligned(jnp.bitwise_xor(info_ref[1], k), sub), :]
+                if k % 2:
+                    send_ref[k // 2] = piece.astype(bf)
+                else:
+                    keep_ref[k // 2] = piece
+
+        os_keep, os_send, block_out = local_call(
+            out_sum_kernel,
+            "output_sum",
+            [
+                shape_of((parts // 2, sub, half_width), f32),
+                shape_of((parts // 2, sub, half_width), bf),
+                shape_of((1, rows, width), bf),
+            ],
+            [info, middle, vectors] + oc_parts,
+            scalars=1,
+            scratch=[pltpu.VMEM((own_width, half_width), f32)],
+            after=[in_send],
+        )
+        os_far = chip_swap(os_send, 1)
+
+        def dp_pack_kernel(info_ref, own_ref, far_two_ref, keep_ref, far_ref, *refs):
+            con_ref, scr = refs[seq_parts:]
+            whole = own_ref[...] + far_two_ref[...].astype(f32)
+            con_ref[...] = whole[0 : ff // parts].astype(bf)
+            scr[...] = whole[ff // parts :]
+            for j in range(seq_parts):
+                at = jnp.bitwise_xor(info_ref[0], j)
+                refs[j][0:tall, :] = (keep_ref[at].astype(f32) + far_ref[at].astype(f32)).astype(
+                    bf
+                )
+                refs[j][tall:, 0:half_ff] = scr[aligned(at, sub), :].astype(bf)
+                refs[j][tall:, half_ff:] = jnp.zeros((sub, 3 * hw - half_ff), bf)
+
+        dp_out = local_call(
+            dp_pack_kernel,
             "owners",
-            [shape_of((span, half_width), bf)]
-            + [shape_of((sub + own_width, half_width), bf)] * seq_parts,
-            [info, out_keep, out_far] + ffn_parts,
+            [shape_of((tall + sub, 3 * hw), bf)] * seq_parts
+            + [shape_of((ff // parts, half_width), bf)],
+            [info, rs_own_two, rs_far_two, in_keep, in_far],
             scalars=1,
-        )
-        ffn_whole = ow_out[0]
-        ow_parts = [ow_out[1]] + [seq_swap(ow_out[1 + j], j) for j in others]
-
-        gather_rows = span + sub
-
-        def share_kernel(info_ref, whole_ref, *refs):
+            scratch=[pltpu.VMEM((own_width, half_ff), f32)],
+            after=[block_out],
+        )
+        dp_parts = [dp_out[0]] + [seq_swap(dp_out[j], j) for j in others]
+        con_one = dp_out[seq_parts]
+        con_two = chip_swap(con_one, 2)
+
+        wide = tall + sub
+        tail = own_width * half_ff // (3 * hw)
+        over = own_width - tail
+
+        def dp_sum_kernel(info_ref, gk_ref, gf_ref, ok_ref, of_ref, *refs):
             owned = refs[:seq_parts]
-            outs = refs[seq_parts : seq_parts + parts]
-            (scr,) = refs[seq_parts + parts :]
-            rows_out = owned[0][sub:, :].astype(f32)
+            last_ref, gown_ref, gsend_ref, scr = refs[seq_parts:]
+            whole = owned[0][0:tall, :].astype(f32)
             for j in others:
-                rows_out = rows_out + owned[j][sub:, :].astype(f32)
-            scr[...] = rows_out.astype(bf)
-            for k in range(parts):
-                out_ref = outs[k]
-                out_ref[0 : ff // parts, :] = whole_ref[0 : ff // parts, :]
-                for j in range(seq_parts):
-                    start = pl.multiple_of(
-                        ff // parts + jnp.bitwise_xor(info_ref[0], j) * sub, 16
-                    )
-                    out_ref[pl.ds(start, sub), :] = owned[j][0:sub, :]
-                to = pl.multiple_of(jnp.bitwise_xor(info_ref[1], k) * sub, 16)
-                out_ref[span:, :] = scr[pl.ds(to, sub), :]
-
-        sh_out = local_call(
-            share_kernel,
+                whole = whole + owned[j][0:tall, :].astype(f32)
+            last_ref[0:tall, :] = whole.astype(bf)
+            for j in range(seq_parts):
+                place = jnp.bitwise_xor(info_ref[0], j)
+                scr[aligned(place, sub), :] = owned[j][tall:, 0:half_ff]
+            last_ref[tall : tall + tail, 0:half_ff] = scr[0:tail, :]
+            last_ref[tall : tall + over, half_ff:] = scr[tail:, 0 : half_ff // 2]
+            last_ref[tall + over : tall + tail, half_ff:] = scr[tail:, half_ff // 2 :]
+            for k in range(2):
+                at = slice(tall + tail + k * sub, tall + tail + (k + 1) * sub)
+                last_ref[at, 0:half_width] = (ok_ref[k] + of_ref[k].astype(f32)).astype(bf)
+                last_ref[at, half_width:] = jnp.zeros((sub, 3 * hw - half_width), bf)
+            gown_ref[...] = gk_ref[0] + gf_ref[0].astype(f32)
+            gsend_ref[...] = (gk_ref[1] + gf_ref[1].astype(f32)).astype(bf)
+
+        last_one, gt_own, gt_send_two = local_call(
+            dp_sum_kernel,
             "shares",
-            [shape_of((gather_rows, half_width), bf)] * parts,
-            [info, ffn_whole] + ow_parts,
+            [
+                shape_of((tall + tail + 2 * sub, 3 * hw), bf),
+                shape_of((rows, width), f32),
+                shape_of((rows, width), bf),
+            ],
+            [info, gt_keep, gt_far, os_keep, os_far] + dp_parts,
             scalars=1,
-            scratch=[pltpu.VMEM((own_width, half_width), bf)],
-        )
-        sh_parts = [sh_out[0]] + [chip_swap(sh_out[k], k) for k in others]
-        sh_far = [core_swap(member) for member in sh_parts]
-
-        def ffn_final_kernel(info_ref, *refs):
-            own, far = refs[:parts], refs[parts : 2 * parts]
-            con_ref, exp_ref = refs[2 * parts :]
-            for flip, members in ((0, own), (1, far)):
-                half = jnp.bitwise_xor(info_ref[2], flip)
-                lanes = aligned(half, half_width)
+            scratch=[pltpu.VMEM((own_width, half_ff), bf)],
+            after=[con_two],
+        )
+        last_one_far = chip_swap(last_one, 2)
+        gt_far_two = chip_swap(gt_send_two, 2)
+        con_one_far = chip_swap(con_one, 1)
+        con_two_far = chip_swap(con_two, 1)
+        con_parts = [con_one, con_one_far, con_two, con_two_far]
+        con_far = [core_swap(member) for member in con_parts]
+
+        def contract_kernel(info_ref, *refs):
+            con_ref = refs[2 * parts]
+            for flip in range(2):
+                lanes = aligned(jnp.bitwise_xor(info_ref[2], flip), half_width)
                 for k in range(parts):
                     at = jnp.bitwise_xor(info_ref[1], k)
-                    con_ref[aligned(at, ff // parts), lanes] = members[k][
-                        0 : ff // parts, :
-                    ].astype(f32)
-                    for j in range(seq_parts):
-                        start = ff // parts + j * sub
-                        cols = pl.ds(pl.multiple_of(j * ff + half * half_ff, 128), half_ff)
-                        exp_ref[aligned(at, sub), cols] = members[k][
-                            start : start + sub, :
-                        ].astype(f32)
-
-        grad_contract, grad_expand = local_call(
-            ffn_final_kernel,
-            "feed_final",
-            [shape_of((ff, width), f32), shape_of((own_width, seq_parts * ff), f32)],
-            [info] + sh_parts + sh_far,
+                    con_ref[aligned(at, ff // parts), lanes] = refs[flip * parts + k][...].astype(
+                        f32
+                    )
+
+        (grad_contract,) = local_call(
+            contract_kernel,
+            "contract_final",
+            [shape_of((ff, width), f32)],
+            [info] + con_parts + con_far,
             scalars=1,
         )
 
-        def in_pick_kernel(info_ref, keep_ref, far_ref, *outs):
-            for j in range(seq_parts):
-                at = jnp.bitwise_xor(info_ref[0], j)
-                outs[j][...] = (keep_ref[at].astype(f32) + far_ref[at].astype(f32)).astype(bf)
-
-        in_chunks = local_call(
-            in_pick_kernel,
-            "input_chunks",
-            [shape_of((tall, 3 * hw), bf)] * seq_parts,
-            [info, in_keep, in_far],
-            scalars=1,
-        )
-        in_parts = [in_chunks[0]] + [seq_swap(in_chunks[j], j) for j in others]
-
-        def in_sum_kernel(*refs):
-            owned, shared = refs[:seq_parts], refs[seq_parts : seq_parts + parts]
-            (out_ref,) = refs[seq_parts + parts :]
-            whole = owned[0][...].astype(f32)
-            for j in others:
-                whole = whole + owned[j][...].astype(f32)
-            out_ref[0:tall, :] = whole.astype(bf)
-            rows_out = shared[0][span:, :].astype(f32)
-            for k in others:
-                rows_out = rows_out + shared[k][span:, :].astype(f32)
-            out_ref[tall:, 0:half_width] = rows_out.astype(bf)
-            out_ref[tall:, half_width:] = jnp.zeros((sub, 3 * hw - half_width), bf)
-
-        (in_whole,) = local_call(
-            in_sum_kernel,
-            "input_sum",
-            [shape_of((tall + sub, 3 * hw), bf)],
-            in_parts + sh_parts,
-        )
-        last_parts = [in_whole] + [chip_swap(in_whole, k) for k in others]
-        last_far = [core_swap(member) for member in last_parts]
+        def last_pair_kernel(own_ref, far_ref, out_ref):
+            for slot, (first, second) in enumerate(((own_ref, far_ref), (far_ref, own_ref))):
+                out_ref[slot, 0 : tall + tail, :] = first[0 : tall + tail, :]
+                outs = first[tall + tail : wide + tail, :].astype(f32)
+                outs = outs + second[wide + tail :, :].astype(f32)
+                out_ref[slot, tall + tail :, :] = outs.astype(bf)
+
+        (last_two,) = local_call(
+            last_pair_kernel,
+            "input_pair",
+            [shape_of((2, wide + tail, 3 * hw), bf)],
+            [last_one, last_one_far],
+            after=[gt_far_two, con_one_far, con_two_far],
+        )
+        last_two_far = chip_swap(last_two, 1)
+        core_two = core_swap(last_two)
+        core_two_far = core_swap(last_two_far)
+
+        def tokens_kernel(tok_ref, vec_ref, gmid_ref, own_ref, far_ref, out_ref):
+            grad = own_ref[...] + far_ref[...].astype(f32)
+            xhat, spread = norm_stats(tok_ref[...].astype(f32))
+            out_ref[0] = gmid_ref[...] + norm_back(grad, vec_ref[0:1], xhat, spread)
+
+        (grad_tokens,) = local_call(
+            tokens_kernel,
+            "tokens_back",
+            [shape_of((1, rows, width), f32)],
+            [own_tokens, vectors, grad_middle, gt_own, gt_far_two],
+        )
 
         def last_kernel(info_ref, *refs):
-            own, far = refs[:parts], refs[parts : 2 * parts]
-            gin_ref, gout_ref, small_ref, scr = refs[2 * parts :]
-            for flip, members in ((0, own), (1, far)):
+            gin_ref, gout_ref, small_ref, exp_ref, scr = refs[4:]
+
+            def member(far_core, k):
+                return refs[2 * far_core + k % 2][k // 2]
+
+            for flip in range(2):
                 half = jnp.bitwise_xor(info_ref[2], flip)
                 for k in range(parts):
                     at = jnp.bitwise_xor(info_ref[1], k)
-                    scr[at, aligned(half, half_own), :] = members[k][0:half_own, :].astype(f32)
-                    gout_ref[aligned(at, sub), aligned(half, half_width)] = members[k][
-                        tall:, 0:half_width
-                    ].astype(f32)
+                    piece = member(flip, k).astype(f32)
+                    scr[at, aligned(half, half_own), :] = piece[0:half_own]
+                    gout_ref[aligned(at, sub), aligned(half, half_width)] = piece[
+                        tall + tail :, 0:half_width
+                    ]
+                    turned = jnp.concatenate(
+                        [
+                            piece[tall : tall + over, half_ff:],
+                            piece[tall + over : tall + tail, half_ff:],
+                        ],
+                        axis=1,
+                    )
+                    turned = jnp.concatenate(
+                        [piece[tall : tall + tail, 0:half_ff], turned], axis=0
+                    )
+                    for j in range(seq_parts):
+                        cols = pl.ds(pl.multiple_of(j * ff + half * half_ff, 128), half_ff)
+                        exp_ref[aligned(at, sub), cols] = turned[j * sub : (j + 1) * sub]
             for at in range(parts):
                 for base in range(3):
                     start = base * width + at * hw
                     gin_ref[:, start : start + hw] = scr[at, :, base * hw : (base + 1) * hw]
-            small = own[0][half_own:tall, 0:own_width].astype(f32)
+            small = member(0, 0)[half_own:tall, 0:own_width].astype(f32)
             for k in others:
-                small = small + own[k][half_own:tall, 0:own_width].astype(f32)
+                small = small + member(0, k)[half_own:tall, 0:own_width].astype(f32)
             small_ref[...] = small
 
-        grad_input, grad_output, small_sums = local_call(
+        grad_input, grad_output, small_sums, grad_expand = local_call(
             last_kernel,
             "weights_final",
             [
                 shape_of((own_width, 3 * width), f32),
                 shape_of((own_width, width), f32),
                 shape_of((small_rows, own_width), f32),
+                shape_of((own_width, seq_parts * ff), f32),
             ],
-            [info] + last_parts + last_far,
+            [info, last_two, last_two_far, core_two, core_two_far],
             scalars=1,
+            after=[grad_tokens, grad_contract],
             scratch=[pltpu.VMEM((parts, own_width, 3 * hw), f32)],
         )
 
-        def out_kernel(mid_ref, vec_ref, *refs):
-            result = mid_ref[...] + vec_ref[7:8]
-            for j in range(seq_parts):
-                result = result + refs[j][...].astype(f32)
-            refs[seq_parts][0] = result.astype(bf)
-
-        (block_out,) = local_call(
-            out_kernel,
-            "result",
-            [shape_of((1, rows, width), bf)],
-            [middle, vectors] + res_parts,
-        )
-
-        def tokens_kernel(tok_ref, vec_ref, gmid_ref, *refs):
-            grad = refs[0][...].astype(f32)
-            for k in others:
-                grad = grad + refs[k][...].astype(f32)
-            xhat, spread = norm_stats(tok_ref[...].astype(f32))
-            refs[parts][0] = gmid_ref[...] + norm_back(grad, vec_ref[0:1], xhat, spread)
-
-        (grad_tokens,) = local_call(
-            tokens_kernel,
-            "tokens_back",
-            [shape_of((1, rows, width), f32)],
-            [own_tokens, vectors, grad_middle] + gt_parts,
-        )
         small_of = [small_sums[i] for i in range(8)]
         grad_expand_bias = small_sums[8 : 8 + ff // own_width].reshape(ff)
         return (

time: 236 us -> 221 us (0.936)
  starting transfers between devices: 73.5 us -> 51 us
  waiting for transfers between devices: 113 us -> 125 us
  local copies, waits for them, and re-layouts: 11.7 us -> 5.49 us
    ppermute x21 -> x19, starting transfers between devices: 41.5 us -> 25 us  [chip_swap(): lax.ppermute(member, 'ctx', [(i, 2 * (i // 2 ^ step) + i % 2) for i in ra...]
    ppermute x21 -> x19, waiting for transfers between devices: 69.4 us -> 76.6 us  [chip_swap(): lax.ppermute(member, 'ctx', [(i, 2 * (i // 2 ^ step) + i % 2) for i in ra...]
    ppermute x27 -> x21, starting transfers between devices: 30.6 us -> 24.3 us  [seq_swap(): return lax.ppermute(member, 'dp', [(i, i ^ step) for i in range(seq_parts)])]
    another operation x9 -> x0, local copies, waits for them, and re-layouts: 5.3 us -> none  [per_device_heads(): jnp.stack([first_gain, first_shift, query_bias, value_bias, output_bias,...]
    ppermute x27 -> x21, waiting for transfers between devices: 43.2 us -> 46.4 us  [seq_swap(): return lax.ppermute(member, 'dp', [(i, i ^ step) for i in range(seq_parts)])]
    dynamic_slice x2 -> x0, local copies, waits for them, and re-layouts: 2.56 us -> none  [the longest x1 1.35 us: per_device_heads(): lax.dynamic_slice(w_expand, (0, jnp.bitwise_xor(seq_id, j) * ff), (own_wi...]
    pallas_call x19 -> x21, Pallas kernels: 36.7 us -> 37.7 us  [local_call(): pl.pallas_call(ordered, out_shape=tuple(outs), in_specs=[pl.BlockSpec(mem...]
  transfers between devices with their start and end apart: 61 -> 51, of which waited for: 26 -> 23; matrix products, arithmetic and copies ran while one was open for 3% -> 0% of each run, Pallas kernels for 11% -> 10%
where the time goes in v2:
time: 221 us
  waiting for transfers between devices  125 us (57%)
  starting transfers between devices  51 us (23%)
  Pallas kernels  37.7 us (17%)
  local copies, waits for them, and re-layouts  5.49 us (2%)
    ppermute x19, waiting for transfers between devices, chip_swap(): lax.ppermute(member, 'ctx', [(i, 2 * (i // 2 ^ step) + i % 2) for i in ra...  76.6 us
    ppermute x21, waiting for transfers between devices, seq_swap(): return lax.ppermute(member, 'dp', [(i, i ^ step) for i in range(seq_parts)])  46.4 us
    pallas_call x21, Pallas kernels, local_call(): pl.pallas_call(ordered, out_shape=tuple(outs), in_specs=[pl.BlockSpec(mem...  37.7 us
    ppermute x19, starting transfers between devices, chip_swap(): lax.ppermute(member, 'ctx', [(i, 2 * (i // 2 ^ step) + i % 2) for i in ra...  25 us
    ppermute x21, starting transfers between devices, seq_swap(): return lax.ppermute(member, 'dp', [(i, i ^ step) for i in range(seq_parts)])  24.3 us
  transfers between devices with their start and end apart: 51, of which 23 were waited for; matrix products, arithmetic and copies ran while one was open for 0% of the time, Pallas kernels for 10%

profile of v2, /device:TPU:0, one launch (start us, length us, event | category | flops | bytes accessed | tf_op | source)
XLA Modules:
  0.0 221.0 jit_solution(295638198102879867)
XLA Ops:
  0.7 5.1 %collective-permute-start.2 = (bf16[128,768]{1,0:T(8,128)(2,1)}, bf16[128,768]{1,0:T(8,128)(2,1)S(1)}, u32[]{:S(2)}, u32[]{:S(2)}) collective-permute-start(bf16[128,768]{1,0:T(8,128)(2,1)} %bitcast.13), channel_id=1, source_target_pairs={{0,6},{1,7},{2,4},{3,5},{4,2},{5,3},{6,0},{7,1},{8,14},{9,15},{10,... | collective-permute-start | bytes 589832 | tf_op jit(solution)/shard_map/ppermute | solution.py:685
  6.4 2.9 %pack.1.refs_5_.refs_3_ = bf16[208,576]{1,0:T(8,128)(2,1)} custom-call(s32[3]{0:T(128)} %pad_add_fusion.refs_0_, bf16[192,2304]{1,0:T(8,128)(2,1)} %refs_1_.5, bf16[192]{0:T(256)(128)(2,1)} %refs_2_.2, bf16[192]{0:T(256)(128)(2,1)} %refs_3_.2, bf16[192]{0:T(256)(128)(2,1)} %refs_4_.1, bf16[192]{0:T(256)(128)(2,1)} %refs_5_.1, bf16[192]{0:T(256)(128)(2,1)} %refs_6_.1, ...), custom_call_target="tpu_custom_call" | custom-call | bytes 1127436 | tf_op jit(solution)/shard_map/pack/pallas_call | solution.py:635
  9.3 2.5 %collective-permute-start.5 = (bf16[208,576]{1,0:T(8,128)(2,1)}, bf16[208,576]{1,0:T(8,128)(2,1)S(1)}, u32[]{:S(2)}, u32[]{:S(2)}) collective-permute-start(bf16[208,576]{1,0:T(8,128)(2,1)} %pack.1.refs_5_.refs_3_), channel_id=1, source_target_pairs={{0,24},{8,16},{16,8},{24,0},{1,25},{9,17},{17,9},{25,1},{2,26},{10... | collective-permute-start | bytes 718856 | tf_op jit(solution)/shard_map/ppermute | solution.py:690
  13.5 9.2 %collective-permute-done.1.refs_3_.refs_6_ = bf16[128,768]{1,0:T(8,128)(2,1)S(1)} collective-permute-done((bf16[128,768]{1,0:T(8,128)(2,1)}, bf16[128,768]{1,0:T(8,128)(2,1)S(1)}, u32[]{:S(2)}, u32[]{:S(2)}) %collective-permute-start.1) | collective-permute-done | bytes 196640 | tf_op jit(solution)/shard_map/ppermute | solution.py:685
  22.7 2.4 %collective-permute-start.8 = (bf16[192,768]{1,0:T(8,128)(2,1)S(1)}, bf16[192,768]{1,0:T(8,128)(2,1)S(1)}, u32[]{:S(2)}, u32[]{:S(2)}) collective-permute-start(bf16[192,768]{1,0:T(8,128)(2,1)S(1)} %copy-done.6), channel_id=1, source_target_pairs={{0,24},{8,16},{16,8},{24,0},{1,25},{9,17},{17,9},{25,1},{2,26},{10... | collective-permute-start | bytes 884744 | tf_op jit(solution)/shard_map/ppermute | solution.py:690
  26.2 11.2 %collective-permute-done.4.refs_7_ = bf16[208,576]{1,0:T(8,128)(2,1)S(1)} collective-permute-done((bf16[208,576]{1,0:T(8,128)(2,1)}, bf16[208,576]{1,0:T(8,128)(2,1)S(1)}, u32[]{:S(2)}, u32[]{:S(2)}) %collective-permute-start.4) | collective-permute-done | bytes 239648 | tf_op jit(solution)/shard_map/ppermute | solution.py:690
  37.5 0.9 copy-done.2
  39.1 1.9 project.1
  41.8 1.6 collective-permute-start.16
  43.3 0.9 collective-permute-start.17
  44.3 1.1 collective-permute-start.18
  45.3 3.7 %attend.1 = (bf16[128,192]{1,0:T(8,128)(2,1)S(1)}, bf16[128,192]{1,0:T(8,128)(2,1)S(1)}, bf16[128,192]{1,0:T(8,128)(2,1)S(1)}, bf16[128,192]{1,0:T(8,128)(2,1)S(...) custom-call(s32[3]{0:T(128)S(1)} %copy-done.8, s32[8]{0:T(128)S(1)} %copy-done.11, ...), custom_call_target="tpu_custom_call" | custom-call | flops 402653184 | bytes 1589292 | tf_op jit(solution)/shard_map/attend/pallas_call | solution.py:635
  49.1 1.8 collective-permute-start.10
  50.9 1.1 collective-permute-start.11
  52.0 1.4 collective-permute-done.10.refs_4_.refs_3_
  53.4 2.3 %collective-permute-start.12 = (bf16[128,192]{1,0:T(8,128)(2,1)S(1)}, bf16[128,192]{1,0:T(8,128)(2,1)S(1)}, u32[]{:S(2)}, u32[]{:S(2)}) collective-permute-start(bf16[128,192]{1,0:T(8,128)(2,1)S(1)} %get-tuple-element.88), channel_id=1, source_target_pairs={{0,6},{1,7},{2,4},{3,5},{4,2},{5,3},{6,0},{7,1},{8,14},{9,15},{10,... | collective-permute-start | bytes 147464 | tf_op jit(solution)/shard_map/ppermute | solution.py:685
  55.7 2.2 %collective-permute-done.11.refs_5_.refs_4_ = bf16[128,192]{1,0:T(8,128)(2,1)S(1)} collective-permute-done((bf16[128,192]{1,0:T(8,128)(2,1)S(1)}, bf16[128,192]{1,0:T(8,128)(2,1)S(1)}, u32[]{:S(2)}, u32[]{:S(2)}) %collective-permute-start.11) | collective-permute-done | bytes 49184 | tf_op jit(solution)/shard_map/ppermute | solution.py:685
  58.0 1.6 collective-permute-done.12.refs_6_.refs_5_
  59.6 1.2 middle.1
  60.8 2.2 collective-permute-start.15
  63.0 0.9 collective-permute-start.14
  64.4 7.2 %collective-permute-done.17.refs_10_ = bf16[320,768]{1,0:T(8,128)(2,1)S(1)} collective-permute-done((bf16[320,768]{1,0:T(8,128)(2,1)S(1)}, bf16[320,768]{1,0:T(8,128)(2,1)S(1)}, u32[]{:S(2)}, u32[]{:S(2)}) %collective-permute-start.17) | collective-permute-done | bytes 491552 | tf_op jit(solution)/shard_map/ppermute | solution.py:690
  71.6 4.0 %collective-permute-done.14.refs_7_ = bf16[128,768]{1,0:T(8,128)(2,1)S(1)} collective-permute-done((bf16[128,768]{1,0:T(8,128)(2,1)S(1)}, bf16[128,768]{1,0:T(8,128)(2,1)S(1)}, u32[]{:S(2)}, u32[]{:S(2)}) %collective-permute-start.14) | collective-permute-done | bytes 196640 | tf_op jit(solution)/shard_map/ppermute | solution.py:690
  75.6 5.4 %feed.1 = (bf16[128,768]{1,0:T(8,128)(2,1)S(1)}, bf16[128,768]{1,0:T(8,128)(2,1)S(1)}, bf16[128,768]{1,0:T(8,128)(2,1)S(1)}, bf16[128,768]{1,0:T(8,128)(2,1)S(1)...) custom-call(s32[3]{0:T(128)S(1)} %copy-done.8, ...), custom_call_target="tpu_custom_call" | custom-call | flops 3623878656 | bytes 8753676 | tf_op jit(solution)/shard_map/feed/pallas_call | solution.py:635
  81.9 1.3 collective-permute-start.20
  83.2 1.5 collective-permute-start.21
  84.7 4.2 %collective-permute-done.19.refs_3_.refs_6_ = bf16[128,768]{1,0:T(8,128)(2,1)S(1)} collective-permute-done((bf16[128,768]{1,0:T(8,128)(2,1)S(1)}, bf16[128,768]{1,0:T(8,128)(2,1)S(1)}, u32[]{:S(2)}, u32[]{:S(2)}) %collective-permute-start.19) | collective-permute-done | bytes 196640 | tf_op jit(solution)/shard_map/ppermute | solution.py:690
  89.3 3.8 %collective-permute-done.21.refs_5_.refs_8_ = bf16[128,768]{1,0:T(8,128)(2,1)S(1)} collective-permute-done((bf16[128,768]{1,0:T(8,128)(2,1)S(1)}, bf16[128,768]{1,0:T(8,128)(2,1)S(1)}, u32[]{:S(2)}, u32[]{:S(2)}) %collective-permute-start.21) | collective-permute-done | bytes 196640 | tf_op jit(solution)/shard_map/ppermute | solution.py:690
  93.1 0.8 feed_halves.1
  93.9 1.4 middle_back.1
  95.3 1.0 output_weights.1
  96.5 2.3 %collective-permute-start.31 = (bf16[2,384,384]{2,1,0:T(8,128)(2,1)S(1)}, bf16[2,384,384]{2,1,0:T(8,128)(2,1)S(1)}, u32[]{:S(2)}, u32[]{:S(2)}) collective-permute-start(bf16[2,384,384]{2,1,0:T(8,128)(2,1)S(1)} %get-tuple-element.102.refs_9_), channel_id=1, source_target_pairs={{0,2},{1,3},{2,0},{3,1},{4,6},{5,7},{6,4},{7,5},{8,10},{9,11},{10,... | collective-permute-start | bytes 1769480 | tf_op jit(solution)/shard_map/ppermute | solution.py:685
  98.9 2.8 %collective-permute-start.28 = (bf16[128,192]{1,0:T(8,128)(2,1)S(1)}, bf16[128,192]{1,0:T(8,128)(2,1)S(1)}, u32[]{:S(2)}, u32[]{:S(2)}) collective-permute-start(bf16[128,192]{1,0:T(8,128)(2,1)S(1)} %get-tuple-element.115), channel_id=1, source_target_pairs={{0,4},{1,5},{2,6},{3,7},{4,0},{5,1},{6,2},{7,3},{8,12},{9,13},{10,... | collective-permute-start | bytes 147464 | tf_op jit(solution)/shard_map/ppermute | solution.py:685
  101.6 1.5 collective-permute-start.29
  103.9 11.6 %collective-permute-done.27.refs_8_ = bf16[128,192]{1,0:T(8,128)(2,1)S(1)} collective-permute-done((bf16[128,192]{1,0:T(8,128)(2,1)S(1)}, bf16[128,192]{1,0:T(8,128)(2,1)S(1)}, u32[]{:S(2)}, u32[]{:S(2)}) %collective-permute-start.27) | collective-permute-done | bytes 49184 | tf_op jit(solution)/shard_map/ppermute | solution.py:685
  115.5 3.4 %collective-permute-done.29.refs_10_ = bf16[128,192]{1,0:T(8,128)(2,1)S(1)} collective-permute-done((bf16[128,192]{1,0:T(8,128)(2,1)S(1)}, bf16[128,192]{1,0:T(8,128)(2,1)S(1)}, u32[]{:S(2)}, u32[]{:S(2)}) %collective-permute-start.29) | collective-permute-done | bytes 49184 | tf_op jit(solution)/shard_map/ppermute | solution.py:685
  118.9 4.8 %attend_back.1 = (f32[192,512]{1,0:T(8,128)S(1)}, f32[512,384]{1,0:T(8,128)S(1)}, bf16[512,384]{1,0:T(8,128)(2,1)S(1)}) custom-call(s32[3]{0:T(128)S(1)} %copy-done.8, s32[8]{0:T(128)S(1)} %copy-done.11, bf16[512,192]{1,0:T(8,128)(2,1)S(1)} %get-tuple-element.83.refs_2_, bf16[512,384]{1,0:T(8,128)(2,1)S(1)} %get-tuple-element.84.refs_3_, ...), custom_call_target="tpu_custom_call" | custom-call | flops 1006632960 | bytes 3162156 | tf_op jit(solution)/shard_map/attend_back/pallas_call | solution.py:635
  123.8 0.9 collective-permute-start.24
  125.5 1.8 normed_back.1
  127.4 1.5 input_weights.1
  129.0 0.8 collective-permute-start.25
  129.9 1.4 collective-permute-start.26
  131.3 3.4 %collective-permute-done.24.refs_4_ = bf16[224,768]{1,0:T(8,128)(2,1)S(1)} collective-permute-done((bf16[224,768]{1,0:T(8,128)(2,1)S(1)}, bf16[224,768]{1,0:T(8,128)(2,1)S(1)}, u32[]{:S(2)}, u32[]{:S(2)}) %collective-permute-start.24) | collective-permute-done | bytes 344096 | tf_op jit(solution)/shard_map/ppermute | solution.py:690
  134.8 12.0 %collective-permute-done.25.refs_5_ = bf16[224,768]{1,0:T(8,128)(2,1)S(1)} collective-permute-done((bf16[224,768]{1,0:T(8,128)(2,1)S(1)}, bf16[224,768]{1,0:T(8,128)(2,1)S(1)}, u32[]{:S(2)}, u32[]{:S(2)}) %collective-permute-start.25) | collective-permute-done | bytes 344096 | tf_op jit(solution)/shard_map/ppermute | solution.py:690
  146.7 1.5 output_sum.1
  148.3 0.9 copy-done.7
  150.0 0.9 collective-permute-start.36
  150.9 1.5 collective-permute-start.37
  152.4 1.2 collective-permute-start.38
  153.6 2.1 collective-permute-start.39
  155.7 6.4 %collective-permute-done.39.refs_9_.refs_3_ = bf16[192,384]{1,0:T(8,128)(2,1)S(1)} collective-permute-done((bf16[192,384]{1,0:T(8,128)(2,1)S(1)}, bf16[192,384]{1,0:T(8,128)(2,1)S(1)}, u32[]{:S(2)}, u32[]{:S(2)}) %collective-permute-start.39) | collective-permute-done | bytes 147488 | tf_op jit(solution)/shard_map/ppermute | solution.py:685
  163.0 1.3 collective-permute-start.41
  164.3 1.7 collective-permute-start.40
  165.9 1.1 collective-permute-start.42
  167.1 0.9 collective-permute-start.43
  168.0 12.7 %collective-permute-done.42.refs_3_.refs_2_ = bf16[192,384]{1,0:T(8,128)(2,1)S(1)} collective-permute-done((bf16[192,384]{1,0:T(8,128)(2,1)S(1)}, bf16[192,384]{1,0:T(8,128)(2,1)S(1)}, u32[]{:S(2)}, u32[]{:S(2)}) %collective-permute-start.42) | collective-permute-done | bytes 147488 | tf_op jit(solution)/shard_map/ppermute | solution.py:685
  180.7 1.6 collective-permute-done.43.refs_4_
  182.2 9.0 %collective-permute-done.40.refs_4_.refs_2_ = bf16[128,768]{1,0:T(8,128)(2,1)S(1)} collective-permute-done((bf16[128,768]{1,0:T(8,128)(2,1)S(1)}, bf16[128,768]{1,0:T(8,128)(2,1)S(1)}, u32[]{:S(2)}, u32[]{:S(2)}) %collective-permute-start.40) | collective-permute-done | bytes 196640 | tf_op jit(solution)/shard_map/ppermute | solution.py:685
  191.4 17.4 %collective-permute-done.44.refs_2_ = bf16[2,288,576]{2,1,0:T(8,128)(2,1)S(1)} collective-permute-done((bf16[2,288,576]{2,1,0:T(8,128)(2,1)S(1)}, bf16[2,288,576]{2,1,0:T(8,128)(2,1)S(1)}, u32[]{:S(2)}, u32[]{:S(2)}) %collective-permute-start.44) | collective-permute-done | bytes 663584 | tf_op jit(solution)/shard_map/ppermute | solution.py:685
  209.9 1.4 collective-permute-done.47.refs_5_
  211.4 1.1 tokens_back.1.refs_5_
  212.6 2.1 contract_final.1.refs_6_
  214.8 1.7 copy-done
  216.4 3.3 %weights_final.1 = (f32[192,2304]{1,0:T(8,128)}, f32[192,768]{1,0:T(8,128)}, f32[16,192]{1,0:T(8,128)S(1)}, f32[192,3072]{1,0:T(8,128)}) custom-call(s32[3]{0:T(128)S(1)} %copy-done.8, bf16[2,288,576]{2,1,0:T(8,128)(2,1)S(1)} %input_pair.1.refs_1_, bf16[2,288,576]{2,1,0:T(8,128)(2,1)S(1)} %collective-permute-done.44.refs_2_, ...), custom_call_target="tpu_custom_call" | custom-call | bytes 7385100 | tf_op jit(solution)/shard_map/weights_final/pallas_call | solution.py:635
  (87 shorter events, 13.1 us)
Async XLA Ops:
  0.6 11.1 %copy-start.1 = (bf16[1,128,768]{2,1,0:T(8,128)(2,1)S(1)}, bf16[1,128,768]{2,1,0:T(8,128)(2,1)}, u32[]{:S(2)}) copy-start(bf16[1,128,768]{2,1,0:T(8,128)(2,1)} %param.16) | copy-start | bytes 589828
  0.7 11.9 %copy-start.6 = (bf16[192,768]{1,0:T(8,128)(2,1)S(1)}, bf16[192,768]{1,0:T(8,128)(2,1)}, u32[]{:S(2)}) copy-start(bf16[192,768]{1,0:T(8,128)(2,1)} %refs_7_.3) | copy-start | bytes 884740
  0.7 12.4 %collective-permute-start.2 = (bf16[128,768]{1,0:T(8,128)(2,1)}, bf16[128,768]{1,0:T(8,128)(2,1)S(1)}, u32[]{:S(2)}, u32[]{:S(2)}) collective-permute-start(bf16[128,768]{1,0:T(8,128)(2,1)} %bitcast.13), channel_id=1, source_target_pairs={{0,6},{1,7},{2,4},{3,5},{4,2},{5,3},{6,0},{7,1},{8,14},{9,15},{10,... | collective-permute-start | bytes 589832 | tf_op jit(solution)/shard_map/ppermute | solution.py:685
  5.8 16.9 %collective-permute-start.1 = (bf16[128,768]{1,0:T(8,128)(2,1)}, bf16[128,768]{1,0:T(8,128)(2,1)S(1)}, u32[]{:S(2)}, u32[]{:S(2)}) collective-permute-start(bf16[128,768]{1,0:T(8,128)(2,1)} %bitcast.14), channel_id=1, source_target_pairs={{0,4},{1,5},{2,6},{3,7},{4,0},{5,1},{6,2},{7,3},{8,12},{9,13},{10,... | collective-permute-start | bytes 589832 | tf_op jit(solution)/shard_map/ppermute | solution.py:685
  6.4 34.7 %copy-start.5 = (bf16[1,128,768]{2,1,0:T(8,128)(2,1)S(1)}, bf16[1,128,768]{2,1,0:T(8,128)(2,1)}, u32[]{:S(2)}) copy-start(bf16[1,128,768]{2,1,0:T(8,128)(2,1)} %param.31) | copy-start | bytes 589828
  9.3 16.4 %collective-permute-start.5 = (bf16[208,576]{1,0:T(8,128)(2,1)}, bf16[208,576]{1,0:T(8,128)(2,1)S(1)}, u32[]{:S(2)}, u32[]{:S(2)}) collective-permute-start(bf16[208,576]{1,0:T(8,128)(2,1)} %pack.1.refs_5_.refs_3_), channel_id=1, source_target_pairs={{0,24},{8,16},{16,8},{24,0},{1,25},{9,17},{17,9},{25,1},{2,26},{10... | collective-permute-start | bytes 718856 | tf_op jit(solution)/shard_map/ppermute | solution.py:690
  11.8 13.4 %collective-permute-start = (bf16[128,768]{1,0:T(8,128)(2,1)S(1)}, bf16[128,768]{1,0:T(8,128)(2,1)S(1)}, u32[]{:S(2)}, u32[]{:S(2)}) collective-permute-start(bf16[128,768]{1,0:T(8,128)(2,1)S(1)} %bitcast.15), channel_id=1, source_target_pairs={{0,2},{1,3},{2,0},{3,1},{4,6},{5,7},{6,4},{7,5},{8,10},{9,11},{10,... | collective-permute-start | bytes 589832 | tf_op jit(solution)/shard_map/ppermute | solution.py:685
  12.6 24.9 %collective-permute-start.7 = (bf16[192,768]{1,0:T(8,128)(2,1)S(1)}, bf16[192,768]{1,0:T(8,128)(2,1)S(1)}, u32[]{:S(2)}, u32[]{:S(2)}) collective-permute-start(bf16[192,768]{1,0:T(8,128)(2,1)S(1)} %copy-done.6), channel_id=1, source_target_pairs={{0,16},{8,24},{16,0},{24,8},{1,17},{9,25},{17,1},{25,9},{2,18},{10... | collective-permute-start | bytes 884744 | tf_op jit(solution)/shard_map/ppermute | solution.py:690
  13.1 24.4 %collective-permute-start.6 = (bf16[192,768]{1,0:T(8,128)(2,1)S(1)}, bf16[192,768]{1,0:T(8,128)(2,1)S(1)}, u32[]{:S(2)}, u32[]{:S(2)}) collective-permute-start(bf16[192,768]{1,0:T(8,128)(2,1)S(1)} %copy-done.6), channel_id=1, source_target_pairs={{0,8},{8,0},{16,24},{24,16},{1,9},{9,1},{17,25},{25,17},{2,10},{10... | collective-permute-start | bytes 884744 | tf_op jit(solution)/shard_map/ppermute | solution.py:690
  22.7 14.8 %collective-permute-start.8 = (bf16[192,768]{1,0:T(8,128)(2,1)S(1)}, bf16[192,768]{1,0:T(8,128)(2,1)S(1)}, u32[]{:S(2)}, u32[]{:S(2)}) collective-permute-start(bf16[192,768]{1,0:T(8,128)(2,1)S(1)} %copy-done.6), channel_id=1, source_target_pairs={{0,24},{8,16},{16,8},{24,0},{1,25},{9,17},{17,9},{25,1},{2,26},{10... | collective-permute-start | bytes 884744 | tf_op jit(solution)/shard_map/ppermute | solution.py:690
  25.1 12.2 %collective-permute-start.4 = (bf16[208,576]{1,0:T(8,128)(2,1)}, bf16[208,576]{1,0:T(8,128)(2,1)S(1)}, u32[]{:S(2)}, u32[]{:S(2)}) collective-permute-start(bf16[208,576]{1,0:T(8,128)(2,1)} %pack.1.refs_5_.refs_3_), channel_id=1, source_target_pairs={{0,16},{8,24},{16,0},{24,8},{1,17},{9,25},{17,1},{25,9},{2,18},{10... | collective-permute-start | bytes 718856 | tf_op jit(solution)/shard_map/ppermute | solution.py:690
  25.6 11.8 %collective-permute-start.3 = (bf16[208,576]{1,0:T(8,128)(2,1)}, bf16[208,576]{1,0:T(8,128)(2,1)S(1)}, u32[]{:S(2)}, u32[]{:S(2)}) collective-permute-start(bf16[208,576]{1,0:T(8,128)(2,1)} %pack.1.refs_5_.refs_3_), channel_id=1, source_target_pairs={{0,8},{8,0},{16,24},{24,16},{1,9},{9,1},{17,25},{25,17},{2,10},{10... | collective-permute-start | bytes 718856 | tf_op jit(solution)/shard_map/ppermute | solution.py:690
  37.5 1.0 copy-start.2
  38.4 0.7 copy-start.8
  39.1 2.0 copy-start.4
  41.0 4.3 %copy-start.11 = (s32[8]{0:T(128)S(1)}, s32[8]{0:T(128)}, u32[]{:S(2)}) copy-start(s32[8]{0:T(128)} %refs_1_.9) | copy-start | bytes 100
  41.0 4.3 %collective-permute-start.9 = (bf16[512,384]{1,0:T(8,128)(2,1)S(1)}, bf16[512,384]{1,0:T(8,128)(2,1)S(1)}, u32[]{:S(2)}, u32[]{:S(2)}) collective-permute-start(bf16[512,384]{1,0:T(8,128)(2,1)S(1)} %get-tuple-element.84.refs_3_), channel_id=1, source_target_pairs={{0,1},{1,0},{2,3},{3,2},{4,5},{5,4},{6,7},{7,6},{8,9},{9,8},{10,11... | collective-permute-start | bytes 1179656 | tf_op jit(solution)/shard_map/ppermute | solution.py:682
  41.8 22.0 %collective-permute-start.16 = (bf16[320,768]{1,0:T(8,128)(2,1)S(1)}, bf16[320,768]{1,0:T(8,128)(2,1)S(1)}, u32[]{:S(2)}, u32[]{:S(2)}) collective-permute-start(bf16[320,768]{1,0:T(8,128)(2,1)S(1)} %get-tuple-element.91), channel_id=1, source_target_pairs={{0,8},{8,0},{16,24},{24,16},{1,9},{9,1},{17,25},{25,17},{2,10},{10... | collective-permute-start | bytes 1474568 | tf_op jit(solution)/shard_map/ppermute | solution.py:690
  43.3 28.3 %collective-permute-start.17 = (bf16[320,768]{1,0:T(8,128)(2,1)S(1)}, bf16[320,768]{1,0:T(8,128)(2,1)S(1)}, u32[]{:S(2)}, u32[]{:S(2)}) collective-permute-start(bf16[320,768]{1,0:T(8,128)(2,1)S(1)} %get-tuple-element.92), channel_id=1, source_target_pairs={{0,16},{8,24},{16,0},{24,8},{1,17},{9,25},{17,1},{25,9},{2,18},{10... | collective-permute-start | bytes 1474568 | tf_op jit(solution)/shard_map/ppermute | solution.py:690
  44.3 27.3 %collective-permute-start.18 = (bf16[320,768]{1,0:T(8,128)(2,1)S(1)}, bf16[320,768]{1,0:T(8,128)(2,1)S(1)}, u32[]{:S(2)}, u32[]{:S(2)}) collective-permute-start(bf16[320,768]{1,0:T(8,128)(2,1)S(1)} %get-tuple-element.93), channel_id=1, source_target_pairs={{0,24},{8,16},{16,8},{24,0},{1,25},{9,17},{17,9},{25,1},{2,26},{10... | collective-permute-start | bytes 1474568 | tf_op jit(solution)/shard_map/ppermute | solution.py:690
  49.1 26.5 %copy-start.9 = (bf16[768,768]{1,0:T(8,128)(2,1)S(1)}, bf16[768,768]{1,0:T(8,128)(2,1)}, u32[]{:S(2)}) copy-start(bf16[768,768]{1,0:T(8,128)(2,1)} %refs_2_.3) | copy-start | bytes 3538948
  49.1 26.5 %copy-start.10 = (bf16[768]{0:T(1024)(128)(2,1)S(1)}, bf16[768]{0:T(1024)(128)(2,1)}, u32[]{:S(2)}) copy-start(bf16[768]{0:T(1024)(128)(2,1)} %refs_1_.8) | copy-start | bytes 4612
  49.1 4.3 %collective-permute-start.10 = (bf16[128,192]{1,0:T(8,128)(2,1)S(1)}, bf16[128,192]{1,0:T(8,128)(2,1)S(1)}, u32[]{:S(2)}, u32[]{:S(2)}) collective-permute-start(bf16[128,192]{1,0:T(8,128)(2,1)S(1)} %get-tuple-element.86), channel_id=1, source_target_pairs={{0,2},{1,3},{2,0},{3,1},{4,6},{5,7},{6,4},{7,5},{8,10},{9,11},{10,... | collective-permute-start | bytes 147464 | tf_op jit(solution)/shard_map/ppermute | solution.py:685
  50.9 7.1 %collective-permute-start.11 = (bf16[128,192]{1,0:T(8,128)(2,1)S(1)}, bf16[128,192]{1,0:T(8,128)(2,1)S(1)}, u32[]{:S(2)}, u32[]{:S(2)}) collective-permute-start(bf16[128,192]{1,0:T(8,128)(2,1)S(1)} %get-tuple-element.87), channel_id=1, source_target_pairs={{0,4},{1,5},{2,6},{3,7},{4,0},{5,1},{6,2},{7,3},{8,12},{9,13},{10,... | collective-permute-start | bytes 147464 | tf_op jit(solution)/shard_map/ppermute | solution.py:685
  53.4 6.2 %collective-permute-start.12 = (bf16[128,192]{1,0:T(8,128)(2,1)S(1)}, bf16[128,192]{1,0:T(8,128)(2,1)S(1)}, u32[]{:S(2)}, u32[]{:S(2)}) collective-permute-start(bf16[128,192]{1,0:T(8,128)(2,1)S(1)} %get-tuple-element.88), channel_id=1, source_target_pairs={{0,6},{1,7},{2,4},{3,5},{4,2},{5,3},{6,0},{7,1},{8,14},{9,15},{10,... | collective-permute-start | bytes 147464 | tf_op jit(solution)/shard_map/ppermute | solution.py:685
  60.8 10.8 %collective-permute-start.15 = (bf16[128,768]{1,0:T(8,128)(2,1)S(1)}, bf16[128,768]{1,0:T(8,128)(2,1)S(1)}, u32[]{:S(2)}, u32[]{:S(2)}) collective-permute-start(bf16[128,768]{1,0:T(8,128)(2,1)S(1)} %get-tuple-element.90.refs_5_), channel_id=1, source_target_pairs={{0,24},{8,16},{16,8},{24,0},{1,25},{9,17},{17,9},{25,1},{2,26},{10... | collective-permute-start | bytes 589832 | tf_op jit(solution)/shard_map/ppermute | solution.py:690
  63.0 12.7 %collective-permute-start.14 = (bf16[128,768]{1,0:T(8,128)(2,1)S(1)}, bf16[128,768]{1,0:T(8,128)(2,1)S(1)}, u32[]{:S(2)}, u32[]{:S(2)}) collective-permute-start(bf16[128,768]{1,0:T(8,128)(2,1)S(1)} %get-tuple-element.90.refs_5_), channel_id=1, source_target_pairs={{0,16},{8,24},{16,0},{24,8},{1,17},{9,25},{17,1},{25,9},{2,18},{10... | collective-permute-start | bytes 589832 | tf_op jit(solution)/shard_map/ppermute | solution.py:690
  63.8 11.8 %collective-permute-start.13 = (bf16[128,768]{1,0:T(8,128)(2,1)S(1)}, bf16[128,768]{1,0:T(8,128)(2,1)S(1)}, u32[]{:S(2)}, u32[]{:S(2)}) collective-permute-start(bf16[128,768]{1,0:T(8,128)(2,1)S(1)} %get-tuple-element.90.refs_5_), channel_id=1, source_target_pairs={{0,8},{8,0},{16,24},{24,16},{1,9},{9,1},{17,25},{25,17},{2,10},{10... | collective-permute-start | bytes 589832 | tf_op jit(solution)/shard_map/ppermute | solution.py:690
  81.1 12.0 %collective-permute-start.22 = (bf16[4,384,384]{2,1,0:T(8,128)(2,1)S(1)}, bf16[4,384,384]{2,1,0:T(8,128)(2,1)S(1)}, u32[]{:S(2)}, u32[]{:S(2)}) collective-permute-start(bf16[4,384,384]{2,1,0:T(8,128)(2,1)S(1)} %get-tuple-element.101), channel_id=1, source_target_pairs={{0,1},{1,0},{2,3},{3,2},{4,5},{5,4},{6,7},{7,6},{8,9},{9,8},{10,11... | collective-permute-start | bytes 3538952 | tf_op jit(solution)/shard_map/ppermute | solution.py:682
  81.1 7.8 %collective-permute-start.19 = (bf16[128,768]{1,0:T(8,128)(2,1)S(1)}, bf16[128,768]{1,0:T(8,128)(2,1)S(1)}, u32[]{:S(2)}, u32[]{:S(2)}) collective-permute-start(bf16[128,768]{1,0:T(8,128)(2,1)S(1)} %get-tuple-element.97), channel_id=1, source_target_pairs={{0,8},{8,0},{16,24},{24,16},{1,9},{9,1},{17,25},{25,17},{2,10},{10... | collective-permute-start | bytes 589832 | tf_op jit(solution)/shard_map/ppermute | solution.py:690
  81.9 7.4 %collective-permute-start.20 = (bf16[128,768]{1,0:T(8,128)(2,1)S(1)}, bf16[128,768]{1,0:T(8,128)(2,1)S(1)}, u32[]{:S(2)}, u32[]{:S(2)}) collective-permute-start(bf16[128,768]{1,0:T(8,128)(2,1)S(1)} %get-tuple-element.98), channel_id=1, source_target_pairs={{0,16},{8,24},{16,0},{24,8},{1,17},{9,25},{17,1},{25,9},{2,18},{10... | collective-permute-start | bytes 589832 | tf_op jit(solution)/shard_map/ppermute | solution.py:690
  83.2 9.9 %collective-permute-start.21 = (bf16[128,768]{1,0:T(8,128)(2,1)S(1)}, bf16[128,768]{1,0:T(8,128)(2,1)S(1)}, u32[]{:S(2)}, u32[]{:S(2)}) collective-permute-start(bf16[128,768]{1,0:T(8,128)(2,1)S(1)} %get-tuple-element.99), channel_id=1, source_target_pairs={{0,24},{8,16},{16,8},{24,0},{1,25},{9,17},{17,9},{25,1},{2,26},{10... | collective-permute-start | bytes 589832 | tf_op jit(solution)/shard_map/ppermute | solution.py:690
  96.4 6.8 %collective-permute-start.23 = (bf16[4,192,384]{2,1,0:T(8,128)(2,1)S(1)}, bf16[4,192,384]{2,1,0:T(8,128)(2,1)S(1)}, u32[]{:S(2)}, u32[]{:S(2)}) collective-permute-start(bf16[4,192,384]{2,1,0:T(8,128)(2,1)S(1)} %get-tuple-element.105), channel_id=1, source_target_pairs={{0,1},{1,0},{2,3},{3,2},{4,5},{5,4},{6,7},{7,6},{8,9},{9,8},{10,11... | collective-permute-start | bytes 1769480 | tf_op jit(solution)/shard_map/ppermute | solution.py:682
  96.5 28.2 %collective-permute-start.31 = (bf16[2,384,384]{2,1,0:T(8,128)(2,1)S(1)}, bf16[2,384,384]{2,1,0:T(8,128)(2,1)S(1)}, u32[]{:S(2)}, u32[]{:S(2)}) collective-permute-start(bf16[2,384,384]{2,1,0:T(8,128)(2,1)S(1)} %get-tuple-element.102.refs_9_), channel_id=1, source_target_pairs={{0,2},{1,3},{2,0},{3,1},{4,6},{5,7},{6,4},{7,5},{8,10},{9,11},{10,... | collective-permute-start | bytes 1769480 | tf_op jit(solution)/shard_map/ppermute | solution.py:685
  98.8 16.7 %collective-permute-start.27 = (bf16[128,192]{1,0:T(8,128)(2,1)S(1)}, bf16[128,192]{1,0:T(8,128)(2,1)S(1)}, u32[]{:S(2)}, u32[]{:S(2)}) collective-permute-start(bf16[128,192]{1,0:T(8,128)(2,1)S(1)} %get-tuple-element.114), channel_id=1, source_target_pairs={{0,2},{1,3},{2,0},{3,1},{4,6},{5,7},{6,4},{7,5},{8,10},{9,11},{10,... | collective-permute-start | bytes 147464 | tf_op jit(solution)/shard_map/ppermute | solution.py:685
  98.9 16.6 %collective-permute-start.28 = (bf16[128,192]{1,0:T(8,128)(2,1)S(1)}, bf16[128,192]{1,0:T(8,128)(2,1)S(1)}, u32[]{:S(2)}, u32[]{:S(2)}) collective-permute-start(bf16[128,192]{1,0:T(8,128)(2,1)S(1)} %get-tuple-element.115), channel_id=1, source_target_pairs={{0,4},{1,5},{2,6},{3,7},{4,0},{5,1},{6,2},{7,3},{8,12},{9,13},{10,... | collective-permute-start | bytes 147464 | tf_op jit(solution)/shard_map/ppermute | solution.py:685
  101.6 17.3 %collective-permute-start.29 = (bf16[128,192]{1,0:T(8,128)(2,1)S(1)}, bf16[128,192]{1,0:T(8,128)(2,1)S(1)}, u32[]{:S(2)}, u32[]{:S(2)}) collective-permute-start(bf16[128,192]{1,0:T(8,128)(2,1)S(1)} %get-tuple-element.116), channel_id=1, source_target_pairs={{0,6},{1,7},{2,4},{3,5},{4,2},{5,3},{6,0},{7,1},{8,14},{9,15},{10,... | collective-permute-start | bytes 147464 | tf_op jit(solution)/shard_map/ppermute | solution.py:685
  123.7 1.8 collective-permute-start.30
  123.8 10.9 %collective-permute-start.24 = (bf16[224,768]{1,0:T(8,128)(2,1)S(1)}, bf16[224,768]{1,0:T(8,128)(2,1)S(1)}, u32[]{:S(2)}, u32[]{:S(2)}) collective-permute-start(bf16[224,768]{1,0:T(8,128)(2,1)S(1)} %get-tuple-element.107), channel_id=1, source_target_pairs={{0,8},{8,0},{16,24},{24,16},{1,9},{9,1},{17,25},{25,17},{2,10},{10... | collective-permute-start | bytes 1032200 | tf_op jit(solution)/shard_map/ppermute | solution.py:690
  128.8 19.5 %collective-permute-start.35 = (bf16[4,112,576]{2,1,0:T(8,128)(2,1)S(1)}, bf16[4,112,576]{2,1,0:T(8,128)(2,1)S(1)}, u32[]{:S(2)}, u32[]{:S(2)}) collective-permute-start(bf16[4,112,576]{2,1,0:T(8,128)(2,1)S(1)} %get-tuple-element.128.refs_7_), channel_id=1, source_target_pairs={{0,1},{1,0},{2,3},{3,2},{4,5},{5,4},{6,7},{7,6},{8,9},{9,8},{10,11... | collective-permute-start | bytes 1548296 | tf_op jit(solution)/shard_map/ppermute | solution.py:682
  129.0 17.7 %collective-permute-start.25 = (bf16[224,768]{1,0:T(8,128)(2,1)S(1)}, bf16[224,768]{1,0:T(8,128)(2,1)S(1)}, u32[]{:S(2)}, u32[]{:S(2)}) collective-permute-start(bf16[224,768]{1,0:T(8,128)(2,1)S(1)} %get-tuple-element.108), channel_id=1, source_target_pairs={{0,16},{8,24},{16,0},{24,8},{1,17},{9,25},{17,1},{25,9},{2,18},{10... | collective-permute-start | bytes 1032200 | tf_op jit(solution)/shard_map/ppermute | solution.py:690
  129.9 16.9 %collective-permute-start.26 = (bf16[224,768]{1,0:T(8,128)(2,1)S(1)}, bf16[224,768]{1,0:T(8,128)(2,1)S(1)}, u32[]{:S(2)}, u32[]{:S(2)}) collective-permute-start(bf16[224,768]{1,0:T(8,128)(2,1)S(1)} %get-tuple-element.109), channel_id=1, source_target_pairs={{0,24},{8,16},{16,8},{24,0},{1,25},{9,17},{17,9},{25,1},{2,26},{10... | collective-permute-start | bytes 1032200 | tf_op jit(solution)/shard_map/ppermute | solution.py:690
  131.3 17.0 %collective-permute-start.34 = (bf16[384,384]{1,0:T(8,128)(2,1)S(1)}, bf16[384,384]{1,0:T(8,128)(2,1)S(1)}, u32[]{:S(2)}, u32[]{:S(2)}) collective-permute-start(bf16[384,384]{1,0:T(8,128)(2,1)S(1)} %get-tuple-element.122.refs_8_), channel_id=1, source_target_pairs={{0,4},{1,5},{2,6},{3,7},{4,0},{5,1},{6,2},{7,3},{8,12},{9,13},{10,... | collective-permute-start | bytes 884744 | tf_op jit(solution)/shard_map/ppermute | solution.py:685
  134.7 21.0 %collective-permute-start.32 = (bf16[2,128,768]{2,1,0:T(8,128)(2,1)S(1)}, bf16[2,128,768]{2,1,0:T(8,128)(2,1)S(1)}, u32[]{:S(2)}, u32[]{:S(2)}) collective-permute-start(bf16[2,128,768]{2,1,0:T(8,128)(2,1)S(1)} %get-tuple-element.132), channel_id=1, source_target_pairs={{0,2},{1,3},{2,0},{3,1},{4,6},{5,7},{6,4},{7,5},{8,10},{9,11},{10,... | collective-permute-start | bytes 1179656 | tf_op jit(solution)/shard_map/ppermute | solution.py:685
  148.3 5.3 %collective-permute-start.33 = (bf16[2,48,384]{2,1,0:T(8,128)(2,1)S(1)}, bf16[2,48,384]{2,1,0:T(8,128)(2,1)S(1)}, u32[]{:S(2)}, u32[]{:S(2)}) collective-permute-start(bf16[2,48,384]{2,1,0:T(8,128)(2,1)S(1)} %get-tuple-element.134), channel_id=1, source_target_pairs={{0,2},{1,3},{2,0},{3,1},{4,6},{5,7},{6,4},{7,5},{8,10},{9,11},{10,... | collective-permute-start | bytes 221192 | tf_op jit(solution)/shard_map/ppermute | solution.py:685
  148.3 0.9 copy-start.7
  150.0 12.1 %collective-permute-start.36 = (bf16[160,576]{1,0:T(8,128)(2,1)S(1)}, bf16[160,576]{1,0:T(8,128)(2,1)S(1)}, u32[]{:S(2)}, u32[]{:S(2)}) collective-permute-start(bf16[160,576]{1,0:T(8,128)(2,1)S(1)} %get-tuple-element.138), channel_id=1, source_target_pairs={{0,8},{8,0},{16,24},{24,16},{1,9},{9,1},{17,25},{25,17},{2,10},{10... | collective-permute-start | bytes 552968 | tf_op jit(solution)/shard_map/ppermute | solution.py:690
  150.9 11.2 %collective-permute-start.37 = (bf16[160,576]{1,0:T(8,128)(2,1)S(1)}, bf16[160,576]{1,0:T(8,128)(2,1)S(1)}, u32[]{:S(2)}, u32[]{:S(2)}) collective-permute-start(bf16[160,576]{1,0:T(8,128)(2,1)S(1)} %get-tuple-element.139), channel_id=1, source_target_pairs={{0,16},{8,24},{16,0},{24,8},{1,17},{9,25},{17,1},{25,9},{2,18},{10... | collective-permute-start | bytes 552968 | tf_op jit(solution)/shard_map/ppermute | solution.py:690
  152.4 9.7 %collective-permute-start.38 = (bf16[160,576]{1,0:T(8,128)(2,1)S(1)}, bf16[160,576]{1,0:T(8,128)(2,1)S(1)}, u32[]{:S(2)}, u32[]{:S(2)}) collective-permute-start(bf16[160,576]{1,0:T(8,128)(2,1)S(1)} %get-tuple-element.140), channel_id=1, source_target_pairs={{0,24},{8,16},{16,8},{24,0},{1,25},{9,17},{17,9},{25,1},{2,26},{10... | collective-permute-start | bytes 552968 | tf_op jit(solution)/shard_map/ppermute | solution.py:690
  153.6 8.5 %collective-permute-start.39 = (bf16[192,384]{1,0:T(8,128)(2,1)S(1)}, bf16[192,384]{1,0:T(8,128)(2,1)S(1)}, u32[]{:S(2)}, u32[]{:S(2)}) collective-permute-start(bf16[192,384]{1,0:T(8,128)(2,1)S(1)} %get-tuple-element.141.refs_1_), channel_id=1, source_target_pairs={{0,4},{1,5},{2,6},{3,7},{4,0},{5,1},{6,2},{7,3},{8,12},{9,13},{10,... | collective-permute-start | bytes 442376 | tf_op jit(solution)/shard_map/ppermute | solution.py:685
  163.0 28.2 %collective-permute-start.41 = (bf16[336,576]{1,0:T(8,128)(2,1)S(1)}, bf16[336,576]{1,0:T(8,128)(2,1)S(1)}, u32[]{:S(2)}, u32[]{:S(2)}) collective-permute-start(bf16[336,576]{1,0:T(8,128)(2,1)S(1)} %get-tuple-element.144.refs_0_), channel_id=1, source_target_pairs={{0,4},{1,5},{2,6},{3,7},{4,0},{5,1},{6,2},{7,3},{8,12},{9,13},{10,... | collective-permute-start | bytes 1161224 | tf_op jit(solution)/shard_map/ppermute | solution.py:685
  164.3 26.9 %collective-permute-start.40 = (bf16[128,768]{1,0:T(8,128)(2,1)S(1)}, bf16[128,768]{1,0:T(8,128)(2,1)S(1)}, u32[]{:S(2)}, u32[]{:S(2)}) collective-permute-start(bf16[128,768]{1,0:T(8,128)(2,1)S(1)} %get-tuple-element.143), channel_id=1, source_target_pairs={{0,4},{1,5},{2,6},{3,7},{4,0},{5,1},{6,2},{7,3},{8,12},{9,13},{10,... | collective-permute-start | bytes 589832 | tf_op jit(solution)/shard_map/ppermute | solution.py:685
  165.9 14.7 %collective-permute-start.42 = (bf16[192,384]{1,0:T(8,128)(2,1)S(1)}, bf16[192,384]{1,0:T(8,128)(2,1)S(1)}, u32[]{:S(2)}, u32[]{:S(2)}) collective-permute-start(bf16[192,384]{1,0:T(8,128)(2,1)S(1)} %get-tuple-element.141.refs_1_), channel_id=1, source_target_pairs={{0,2},{1,3},{2,0},{3,1},{4,6},{5,7},{6,4},{7,5},{8,10},{9,11},{10,... | collective-permute-start | bytes 442376 | tf_op jit(solution)/shard_map/ppermute | solution.py:685
  167.1 15.1 %collective-permute-start.43 = (bf16[192,384]{1,0:T(8,128)(2,1)S(1)}, bf16[192,384]{1,0:T(8,128)(2,1)S(1)}, u32[]{:S(2)}, u32[]{:S(2)}) collective-permute-start(bf16[192,384]{1,0:T(8,128)(2,1)S(1)} %collective-permute-done.39.refs_9_.refs_3_), channel_id=1, source_target_pairs={{0,2},{1,3},{2,0},{3,1},{4,6},{5,7},{6,4},{7,5},{8,10},{9,11},{10,... | collective-permute-start | bytes 442376 | tf_op jit(solution)/shard_map/ppermute | solution.py:685
  191.3 17.6 %collective-permute-start.44 = (bf16[2,288,576]{2,1,0:T(8,128)(2,1)S(1)}, bf16[2,288,576]{2,1,0:T(8,128)(2,1)S(1)}, u32[]{:S(2)}, u32[]{:S(2)}) collective-permute-start(bf16[2,288,576]{2,1,0:T(8,128)(2,1)S(1)} %input_pair.1.refs_1_), channel_id=1, source_target_pairs={{0,2},{1,3},{2,0},{3,1},{4,6},{5,7},{6,4},{7,5},{8,10},{9,11},{10,... | collective-permute-start | bytes 1990664 | tf_op jit(solution)/shard_map/ppermute | solution.py:685
  191.3 23.4 %collective-permute-start.45 = (bf16[2,288,576]{2,1,0:T(8,128)(2,1)S(1)}, bf16[2,288,576]{2,1,0:T(8,128)(2,1)S(1)}, u32[]{:S(2)}, u32[]{:S(2)}) collective-permute-start(bf16[2,288,576]{2,1,0:T(8,128)(2,1)S(1)} %input_pair.1.refs_1_), channel_id=1, source_target_pairs={{0,1},{1,0},{2,3},{3,2},{4,5},{5,4},{6,7},{7,6},{8,9},{9,8},{10,11... | collective-permute-start | bytes 1990664 | tf_op jit(solution)/shard_map/ppermute | solution.py:682
  208.8 5.9 %collective-permute-start.46 = (bf16[2,288,576]{2,1,0:T(8,128)(2,1)S(1)}, bf16[2,288,576]{2,1,0:T(8,128)(2,1)S(1)}, u32[]{:S(2)}, u32[]{:S(2)}) collective-permute-start(bf16[2,288,576]{2,1,0:T(8,128)(2,1)S(1)} %collective-permute-done.44.refs_2_), channel_id=1, source_target_pairs={{0,1},{1,0},{2,3},{3,2},{4,5},{5,4},{6,7},{7,6},{8,9},{9,8},{10,11... | collective-permute-start | bytes 1990664 | tf_op jit(solution)/shard_map/ppermute | solution.py:682
  208.8 2.4 %collective-permute-start.47 = (bf16[192,384]{1,0:T(8,128)(2,1)S(1)}, bf16[192,384]{1,0:T(8,128)(2,1)S(1)}, u32[]{:S(2)}, u32[]{:S(2)}) collective-permute-start(bf16[192,384]{1,0:T(8,128)(2,1)S(1)} %get-tuple-element.141.refs_1_), channel_id=1, source_target_pairs={{0,1},{1,0},{2,3},{3,2},{4,5},{5,4},{6,7},{7,6},{8,9},{9,8},{10,11... | collective-permute-start | bytes 442376 | tf_op jit(solution)/shard_map/ppermute | solution.py:682
  209.3 3.1 %collective-permute-start.48 = (bf16[192,384]{1,0:T(8,128)(2,1)S(1)}, bf16[192,384]{1,0:T(8,128)(2,1)S(1)}, u32[]{:S(2)}, u32[]{:S(2)}) collective-permute-start(bf16[192,384]{1,0:T(8,128)(2,1)S(1)} %collective-permute-done.42.refs_3_.refs_2_), channel_id=1, source_target_pairs={{0,1},{1,0},{2,3},{3,2},{4,5},{5,4},{6,7},{7,6},{8,9},{9,8},{10,11... | collective-permute-start | bytes 442376 | tf_op jit(solution)/shard_map/ppermute | solution.py:682
  209.3 3.1 %collective-permute-start.49 = (bf16[192,384]{1,0:T(8,128)(2,1)S(1)}, bf16[192,384]{1,0:T(8,128)(2,1)S(1)}, u32[]{:S(2)}, u32[]{:S(2)}) collective-permute-start(bf16[192,384]{1,0:T(8,128)(2,1)S(1)} %collective-permute-done.39.refs_9_.refs_3_), channel_id=1, source_target_pairs={{0,1},{1,0},{2,3},{3,2},{4,5},{5,4},{6,7},{7,6},{8,9},{9,8},{10,11... | collective-permute-start | bytes 442376 | tf_op jit(solution)/shard_map/ppermute | solution.py:682
  211.3 1.4 collective-permute-start.50
  212.5 2.3 %copy-start.3 = (f32[1,128,768]{2,1,0:T(8,128)S(1)}, f32[1,128,768]{2,1,0:T(8,128)}, u32[]{:S(2)}) copy-start(f32[1,128,768]{2,1,0:T(8,128)} %tokens_back.1.refs_5_) | copy-start | bytes 1179652
  214.8 1.7 copy-start

commit v3 on v2

--- a/solution.py
+++ b/solution.py
@@ -575,7 +575,8 @@
     return (block_out, grad_tokens) + tuple(grad_final)
 
 
-VMEM_BYTES = 28 * 1024 * 1024
+VMEM_BYTES = 16 * 1024 * 1024
+VMEM_LARGE = 28 * 1024 * 1024
 
 
 def mm(left, right):
@@ -725,39 +726,43 @@
         core = rank % 2
         info = jnp.stack([seq_id, chip, core]).astype(jnp.int32)
 
-        own_tokens = tokens[0]
-        token_parts = [own_tokens] + [chip_swap(own_tokens, k) for k in others]
-        def pack_kernel(info_ref, w_ref, *refs):
-            vecs, (packed_ref, w_scr), scrs, (sems,) = (
-                refs[:8],
-                refs[8:10],
-                refs[10:18],
-                refs[18:],
-            )
+        side = width - 3 * hw
+        pack_rows = 2 * half_own
+
+        def pack_kernel(info_ref, tok_ref, w_ref, wo_ref, *refs):
+            vecs = refs[:8]
+            packed_ref, tokens_ref, w_scr, wo_scr = refs[8:12]
+            scrs, sems = refs[12:20], refs[20]
+            mine = pl.ds(pl.multiple_of(info_ref[2] * half_own, half_own), half_own)
+            pairs = [(w_ref.at[mine], w_scr), (wo_ref.at[mine], wo_scr), (tok_ref, tokens_ref)]
+            pairs += list(zip(vecs, scrs))
             copies = [
-                pltpu.make_async_copy(src, dst, sems.at[i])
-                for i, (src, dst) in enumerate(zip((w_ref, *vecs), (w_scr, *scrs)))
+                pltpu.make_async_copy(src, dst, sems.at[i]) for i, (src, dst) in enumerate(pairs)
             ]
             for copy in copies:
                 copy.start()
             for copy in copies:
                 copy.wait()
+            at_w = slice(half_own, 2 * half_own)
             for at in range(chips):
 
                 @pl.when(info_ref[1] == at)
                 def _():
                     for base in range(3):
                         start = base * width + at * hw
-                        packed_ref[0:own_width, base * hw : (base + 1) * hw] = w_scr[
+                        packed_ref[at_w, base * hw : (base + 1) * hw] = w_scr[
                             :, start : start + hw
                         ]
 
+            packed_ref[0:half_own, :] = wo_scr[...]
             small = jnp.concatenate(
                 [v[...].astype(f32).reshape(1, own_width) for v in scrs], axis=0
             )
             small = jnp.concatenate([small, jnp.zeros_like(small)], axis=0)
-            packed_ref[own_width:, 0:own_width] = small.astype(bf)
-            packed_ref[own_width:, own_width:] = jnp.zeros((small_rows, 3 * hw - own_width), bf)
+            packed_ref[half_own : half_own + small_rows, 3 * hw :] = small.astype(bf)
+            packed_ref[half_own + small_rows :, 3 * hw :] = jnp.zeros(
+                (half_own - small_rows, side), bf
+            )
 
         small_args = (
             first_gain,
@@ -769,48 +774,85 @@
             second_shift,
             contract_bias,
         )
-        (packed,) = local_call(
+        packed, own_tokens = local_call(
             pack_kernel,
             "pack",
-            [shape_of((own_width + small_rows, 3 * hw), bf)],
-            [info, w_input] + list(small_args),
+            [shape_of((pack_rows, width), bf), shape_of((rows, width), bf)],
+            [info, tokens[0], w_input, w_output] + list(small_args),
             scalars=1,
-            scratch=[pltpu.VMEM((own_width, 3 * width), bf)]
+            scratch=[pltpu.VMEM((half_own, 3 * width), bf), pltpu.VMEM((half_own, width), bf)]
             + [pltpu.VMEM((own_width,), bf)] * 8
-            + [pltpu.SemaphoreType.DMA((9,))],
+            + [pltpu.SemaphoreType.DMA((11,))],
             space=pltpu.HBM,
             grant=60 * 1024 * 1024,
         )
-        packed_parts = [packed] + [seq_swap(packed, j) for j in others]
+        token_parts = [own_tokens] + [chip_swap(own_tokens, k) for k in others]
+        packed_near = [seq_swap(packed, j) for j in others]
+
+        def stack_kernel(*refs):
+            depth = refs[0].shape[0]
+            for i, ref in enumerate(refs[:-1]):
+                refs[-1][i * depth : (i + 1) * depth, :] = ref[...]
+
+        (packed_all,) = local_call(
+            stack_kernel,
+            "pack_stack",
+            [shape_of(((seq_parts - 1) * pack_rows, width), bf)],
+            packed_near,
+            after=token_parts[1:],
+        )
+        packed_far = core_swap(packed_all)
         own_cot = cotangent[0]
-        out_parts = [w_output] + [seq_swap(w_output, j) for j in others]
 
         def pack_more_kernel(info_ref, we_ref, cot_ref, *refs):
             for j in others:
-                refs[j - 1][0:own_width, :] = we_ref[
-                    :, aligned(jnp.bitwise_xor(info_ref[0], j), ff)
+                start = pl.multiple_of(info_ref[2] * half_own, half_own)
+                refs[j - 1][0:half_own, :] = we_ref[
+                    pl.ds(start, half_own), aligned(jnp.bitwise_xor(info_ref[0], j), ff)
                 ]
-                refs[j - 1][own_width:, :] = cot_ref[...]
+                refs[j - 1][half_own:, :] = cot_ref[...]
 
         more = local_call(
             pack_more_kernel,
             "pack_more",
-            [shape_of((own_width + rows, width), bf)] * (seq_parts - 1),
+            [shape_of((half_own + rows, width), bf)] * (seq_parts - 1),
             [info, w_expand, own_cot],
             scalars=1,
             after=[packed],
         )
         more_parts = [seq_swap(more[j - 1], j) for j in others]
 
-        def qkv_kernel(info_ref, *refs):
-            toks, packs = refs[:parts], refs[parts : 2 * parts]
-            q_ref, kv_ref, normed_ref, w_ref, vec_ref, vec_scr = refs[2 * parts :]
-            for j in range(parts):
+        def qkv_kernel(info_ref, w_own_ref, wo_own_ref, *refs):
+            toks, own_pack, packs = refs[:parts], refs[parts], refs[parts + 1 : parts + 3]
+            q_ref, kv_ref, normed_ref, w_ref, vec_ref, wo_ref, vec_scr = refs[parts + 3 :]
+            for at in range(chips):
+
+                @pl.when(info_ref[1] == at)
+                def _():
+                    for base in range(3):
+                        start = base * width + at * hw
+                        w_ref[aligned(info_ref[0], own_width), base * hw : (base + 1) * hw] = (
+                            w_own_ref[:, start : start + hw]
+                        )
+
+            wo_ref[info_ref[0]] = wo_own_ref[...]
+            at_small = slice(half_own, half_own + small_rows)
+            vec_scr[info_ref[0]] = own_pack[at_small, 3 * hw :].astype(f32)
+            for j in others:
                 place = jnp.bitwise_xor(info_ref[0], j)
-                w_ref[aligned(place, own_width), :] = packs[j][0:own_width, :]
-                vec_scr[place] = packs[j][own_width : own_width + small_rows, 0:own_width].astype(
-                    f32
-                )
+                base = (j - 1) * pack_rows
+                vec_scr[place] = packs[0][
+                    base + half_own : base + half_own + small_rows, 3 * hw :
+                ].astype(f32)
+                for flip in range(2):
+                    member = packs[flip]
+                    half = jnp.bitwise_xor(info_ref[2], flip)
+                    down = pl.multiple_of(half * half_own, half_own)
+                    wo_ref[place, pl.ds(down, half_own), :] = member[base : base + half_own, :]
+                    start = pl.multiple_of(place * own_width + half * half_own, half_own)
+                    w_ref[pl.ds(start, half_own), :] = member[
+                        base + half_own : base + pack_rows, 0 : 3 * hw
+                    ]
             vectors = jnp.concatenate([vec_scr[j] for j in range(parts)], axis=1)
             vec_ref[...] = vectors
             chosen = vec_scr[info_ref[1]]
@@ -824,7 +866,7 @@
             kv_ref[:, 0:hw] = mixed[:, hw : 2 * hw].astype(bf)
             kv_ref[:, hw : 2 * hw] = (mixed[:, 2 * hw :] + chosen[3:4]).astype(bf)
 
-        query, own_kv, normed, w_heads_full, vectors = local_call(
+        query, own_kv, normed, w_heads_full, vectors, out_full = local_call(
             qkv_kernel,
             "project",
             [
@@ -833,10 +875,10 @@
                 shape_of((total, width), bf),
                 shape_of((width, 3 * hw), bf),
                 shape_of((small_rows, width), f32),
+                shape_of((parts, own_width, width), bf),
             ],
-            [info] + token_parts + packed_parts,
+            [info, w_input, w_output] + token_parts + [packed, packed_all, packed_far],
             scalars=1,
-            after=out_parts[1:],
             scratch=[pltpu.VMEM((parts, small_rows, own_width), f32)],
             flops=2 * total * width * 3 * hw,
         )
@@ -881,15 +923,14 @@
             scalars=2,
             scratch=[pltpu.VMEM((2 * total, total), f32)],
             flops=2 * 2 * head_count * 2 * total * total * HEAD_DIM,
+            grant=VMEM_LARGE,
         )
         flat_attended, row_lse = attend_out[parts:]
         att_parts = [attend_out[0]] + [chip_swap(attend_out[k], k) for k in others]
 
-        def middle_kernel(info_ref, tok_ref, vec_ref, *refs):
-            atts, outs = refs[:parts], refs[parts : 2 * parts]
-            mid_ref, normed_ref, w_ref = refs[2 * parts :]
-            for j in range(parts):
-                w_ref[jnp.bitwise_xor(info_ref[0], j)] = outs[j][...]
+        def middle_kernel(info_ref, tok_ref, vec_ref, w_ref, *refs):
+            atts = refs[:parts]
+            mid_ref, normed_ref = refs[parts:]
             middle = tok_ref[...].astype(f32) + vec_ref[4:5]
             for k in range(parts):
                 middle = middle + mm(atts[k][...], w_ref[jnp.bitwise_xor(info_ref[1], k)])
@@ -897,28 +938,38 @@
             xhat, _ = norm_stats(middle)
             normed_ref[...] = (xhat * vec_ref[5:6] + vec_ref[6:7]).astype(bf)
 
-        middle, own_normed_two, out_full = local_call(
+        middle, own_normed_two = local_call(
             middle_kernel,
             "middle",
-            [
-                shape_of((rows, width), f32),
-                shape_of((rows, width), bf),
-                shape_of((parts, own_width, width), bf),
-            ],
-            [info, own_tokens, vectors] + att_parts + out_parts,
+            [shape_of((rows, width), f32), shape_of((rows, width), bf)],
+            [info, own_tokens, vectors, out_full] + att_parts,
             scalars=1,
             flops=2 * rows * width * width,
         )
+
+        def expand_stack_kernel(*refs):
+            for i, ref in enumerate(refs[:-1]):
+                refs[-1][i * half_own : (i + 1) * half_own, :] = ref[0:half_own, :]
+
+        (expand_all,) = local_call(
+            expand_stack_kernel,
+            "expand_stack",
+            [shape_of(((seq_parts - 1) * half_own, ff), bf)],
+            more_parts,
+            after=[own_normed_two],
+        )
+        expand_far = core_swap(expand_all)
         n2_parts = [own_normed_two] + [seq_swap(own_normed_two, j) for j in others]
 
         span = ff // parts + own_width
 
-        def ffn_kernel(info_ref, bias_ref, wc_ref, we_ref, own_cot_ref, *refs):
+        def ffn_kernel(info_ref, bias_ref, wc_ref, we_ref, own_cot_ref, far_we_ref, *refs):
             n2s = refs[:parts]
             mores = refs[parts : 2 * parts - 1]
             gns = refs[2 * parts - 1 : 3 * parts - 1]
-            result_ref, keep_ref, send_ref, sum_ref = refs[3 * parts - 1 : 3 * parts + 3]
-            active_ref, gh_ref, n2_ref, cot_ref, w_scr, scr = refs[3 * parts + 3 :]
+            results = refs[3 * parts - 1 : 4 * parts - 1]
+            keep_ref, send_ref, sum_ref = refs[4 * parts - 1 : 4 * parts + 2]
+            active_ref, gh_ref, n2_ref, cot_ref, w_scr, scr = refs[4 * parts + 2 :]
             w_scr[aligned(info_ref[0], own_width), :] = we_ref[:, aligned(info_ref[0], ff)]
             for j in range(seq_parts):
                 at = slice(j * rows, (j + 1) * rows)
@@ -927,8 +978,15 @@
                     cot_ref[at, :] = own_cot_ref[...]
                     continue
                 place = jnp.bitwise_xor(info_ref[0], j)
-                w_scr[aligned(place, own_width), :] = mores[j - 1][0:own_width, :]
-                cot_ref[at, :] = mores[j - 1][own_width:, :]
+                for flip in range(2):
+                    half = jnp.bitwise_xor(info_ref[2], flip)
+                    start = pl.multiple_of(place * own_width + half * half_own, half_own)
+                    w_scr[pl.ds(start, half_own), :] = (
+                        far_we_ref[(j - 1) * half_own : j * half_own, :]
+                        if flip
+                        else mores[j - 1][0:half_own, :]
+                    )
+                cot_ref[at, :] = mores[j - 1][half_own:, :]
             hidden = mm(n2_ref[...], w_scr[...]) + bias_ref[...].astype(f32).reshape(1, ff)
             square = hidden * hidden
             curve = jnp.tanh(GELU_SCALE * hidden * (1.0 + GELU_CUBIC * square))
@@ -942,7 +1000,9 @@
             grad = mm_nt(gh_ref[...], w_scr[...]).astype(bf)
             for j in range(parts):
                 gns[j][...] = grad[j * rows : (j + 1) * rows]
-            result_ref[...] = mm(active_ref[...], wc_ref[...]).astype(bf)
+            result = mm(active_ref[...], wc_ref[...]).astype(bf)
+            for j in range(seq_parts):
+                results[j][...] = result[j * rows : (j + 1) * rows]
             core_id = info_ref[2]
             for flip, out_ref in ((0, keep_ref), (1, send_ref)):
                 half = jnp.bitwise_xor(core_id, flip)
@@ -960,14 +1020,13 @@
         ffn_out = local_call(
             ffn_kernel,
             "feed",
-            [shape_of((rows, width), bf)] * parts
+            [shape_of((rows, width), bf)] * 2 * parts
             + [
-                shape_of((total, width), bf),
                 shape_of((parts, span, half_width), bf),
                 shape_of((parts, span, half_width), bf),
                 shape_of((1, ff), f32),
             ],
-            [info, expand_bias, w_contract, w_expand, own_cot] + n2_parts + more_parts,
+            [info, expand_bias, w_contract, w_expand, own_cot, expand_far] + n2_parts + more_parts,
             scalars=1,
             scratch=[
                 pltpu.VMEM((total, ff), bf),
@@ -978,8 +1037,10 @@
                 pltpu.VMEM((width, half_ff), bf),
             ],
             flops=6 * 2 * total * width * ff,
-        )
-        result, ffn_keep, ffn_send, grad_expand_row = ffn_out[parts:]
+            grant=VMEM_LARGE,
+        )
+        results = ffn_out[parts : 2 * parts]
+        ffn_keep, ffn_send, grad_expand_row = ffn_out[2 * parts :]
         gn_parts = [ffn_out[0]] + [seq_swap(ffn_out[j], j) for j in others]
         ffn_far = core_swap(ffn_send)
 
@@ -1001,7 +1062,6 @@
             ],
             [info, ffn_keep, ffn_far],
             scalars=1,
-            after=gn_parts[1:],
         )
         rs_far = chip_swap(rs_send, 1)
 
@@ -1061,24 +1121,18 @@
         )
         out_far = core_swap(out_send)
 
-        fold = own_width // 2
-
-        def out_chunks_kernel(info_ref, result_ref, keep_ref, far_ref, *outs):
-            for j in range(seq_parts):
-                to = jnp.bitwise_xor(info_ref[0], j)
-                outs[j][0:rows, :] = result_ref[j * rows : (j + 1) * rows, :]
-                whole = (keep_ref[to].astype(f32) + far_ref[to].astype(f32)).astype(bf)
-                outs[j][rows:, 0:half_width] = whole[0:fold]
-                outs[j][rows:, half_width:] = whole[fold:]
-
-        out_chunks = local_call(
-            out_chunks_kernel,
-            "output_chunks",
-            [shape_of((rows + fold, width), bf)] * seq_parts,
-            [info, result, out_keep, out_far],
-            scalars=1,
-        )
-        oc_parts = [out_chunks[0]] + [seq_swap(out_chunks[j], j) for j in others]
+        def quarter_kernel(own_ref, far_ref, keep_ref, send_ref):
+            keep_ref[...] = own_ref[0] + far_ref[0].astype(f32)
+            send_ref[...] = (own_ref[1] + far_ref[1].astype(f32)).astype(bf)
+
+        rs_own_two, rs_send_two = local_call(
+            quarter_kernel,
+            "feed_quarters",
+            [shape_of((span, half_width), f32), shape_of((span, half_width), bf)],
+            [rs_own, rs_far],
+            after=[dout_parts[parts - 1]],
+        )
+        rs_far_two = chip_swap(rs_send_two, 2)
 
         def attend_back_kernel(info_ref, pair_ref, q_ref, kv_ref, far_ref, flat_ref, lse_ref, *refs):
             douts = refs[:parts]
@@ -1122,24 +1176,12 @@
             ],
             [info, pair_of_rank, query, own_kv, far_kv, flat_attended, row_lse] + dout_parts,
             scalars=2,
-            after=[out_chunks[0]],
+            after=[rs_send_two, out_send],
             scratch=[pltpu.VMEM((2 * total, total), f32), pltpu.VMEM((total, hw), f32)],
             flops=5 * 2 * head_count * 2 * total * total * HEAD_DIM,
+            grant=VMEM_LARGE,
         )
         dkv_far = core_swap(dkv_send)
-
-        def quarter_kernel(own_ref, far_ref, keep_ref, send_ref):
-            keep_ref[...] = own_ref[0] + far_ref[0].astype(f32)
-            send_ref[...] = (own_ref[1] + far_ref[1].astype(f32)).astype(bf)
-
-        rs_own_two, rs_send_two = local_call(
-            quarter_kernel,
-            "feed_quarters",
-            [shape_of((span, half_width), f32), shape_of((span, half_width), bf)],
-            [rs_own, rs_far],
-            after=[dkv_send],
-        )
-        rs_far_two = chip_swap(rs_send_two, 2)
 
         def normed_back_kernel(dq_ref, own_ref, far_ref, w_ref, *refs):
             toks = refs[:parts]
@@ -1173,12 +1215,10 @@
             ],
             [flat_dq, dkv_own, dkv_far, w_heads_full] + token_parts,
             flops=2 * total * width * 3 * hw,
-            after=[rs_send_two],
         )
         gt_keep, gt_send, grad_mixed, first_sums, mixed_sums = nb_out
         gt_far = chip_swap(gt_send, 1)
 
-        tall = half_own + small_rows
 
         def input_weights_kernel(
             info_ref, normed_ref, mixed_ref, first_ref, bias_ref, late_ref, row_ref, *refs
@@ -1189,141 +1229,125 @@
             small_scr[...] = jnp.zeros_like(small_scr)
             for j in range(seq_parts):
                 at = slice(j * own_width, (j + 1) * own_width)
-                small_scr[j, 0:2, 0:own_width] = first_ref[0:2, at]
-                small_scr[j, 4:8, 0:own_width] = late_ref[0:4, at]
-            small_scr[chip_id, 2:3, 0:hw] = bias_ref[0:1, 0:hw]
-            small_scr[chip_id, 3:4, 0:hw] = bias_ref[0:1, 2 * hw : 3 * hw]
+                small_scr[j, 0:2, :] = first_ref[0:2, at]
+                small_scr[j, 4:8, :] = late_ref[0:4, at]
+            small_scr[chip_id, 2:3, :] = bias_ref[0:1, 0:hw]
+            small_scr[chip_id, 3:4, :] = bias_ref[0:1, 2 * hw : 3 * hw]
             for j in range(ff // own_width):
-                small_scr[seq, 8 + j : 9 + j, 0:own_width] = row_ref[
-                    :, j * own_width : (j + 1) * own_width
-                ]
+                small_scr[seq, 8 + j : 9 + j, :] = row_ref[:, j * own_width : (j + 1) * own_width]
             for flip, out_ref in ((0, keep_ref), (1, send_ref)):
                 half = jnp.bitwise_xor(core_id, flip)
                 for j in range(seq_parts):
                     start = pl.multiple_of(j * own_width + half * half_own, 16)
-                    out_ref[j, 0:half_own, :] = grad_scr[pl.ds(start, half_own), :].astype(bf)
-                    out_ref[j, half_own:tall, :] = small_scr[j].astype(bf)
+                    out_ref[j, :, 0 : 3 * hw] = grad_scr[pl.ds(start, half_own), :].astype(bf)
+                    out_ref[j, 0:small_rows, 3 * hw :] = small_scr[j].astype(bf)
+                    out_ref[j, small_rows:, 3 * hw :] = jnp.zeros(
+                        (half_own - small_rows, side), bf
+                    )
 
         in_keep, in_send = local_call(
             input_weights_kernel,
             "input_weights",
-            [shape_of((seq_parts, tall, 3 * hw), bf)] * 2,
+            [shape_of((seq_parts, half_own, width), bf)] * 2,
             [info, normed, grad_mixed, first_sums, mixed_sums, late_sums, grad_expand_row],
             scalars=1,
             scratch=[
                 pltpu.VMEM((width, 3 * hw), f32),
-                pltpu.VMEM((seq_parts, small_rows, 3 * hw), f32),
+                pltpu.VMEM((seq_parts, small_rows, own_width), f32),
             ],
             flops=2 * total * width * 3 * hw,
         )
         in_far = core_swap(in_send)
 
-        def out_sum_kernel(info_ref, mid_ref, vec_ref, *refs):
-            owned = refs[:seq_parts]
-            keep_ref, send_ref, block_ref, scr = refs[seq_parts:]
-            result = mid_ref[...] + vec_ref[7:8]
-            outs = jnp.zeros((fold, width), f32)
-            for j in range(seq_parts):
-                result = result + owned[j][0:rows, :].astype(f32)
-                outs = outs + owned[j][rows:, :].astype(f32)
-            block_ref[0] = result.astype(bf)
-            scr[0:fold, :] = outs[:, 0:half_width]
-            scr[fold:, :] = outs[:, half_width:]
-            for k in range(parts):
-                piece = scr[aligned(jnp.bitwise_xor(info_ref[1], k), sub), :]
-                if k % 2:
-                    send_ref[k // 2] = piece.astype(bf)
-                else:
-                    keep_ref[k // 2] = piece
-
-        os_keep, os_send, block_out = local_call(
-            out_sum_kernel,
-            "output_sum",
-            [
-                shape_of((parts // 2, sub, half_width), f32),
-                shape_of((parts // 2, sub, half_width), bf),
-                shape_of((1, rows, width), bf),
-            ],
-            [info, middle, vectors] + oc_parts,
-            scalars=1,
-            scratch=[pltpu.VMEM((own_width, half_width), f32)],
-            after=[in_send],
-        )
-        os_far = chip_swap(os_send, 1)
-
-        def dp_pack_kernel(info_ref, own_ref, far_two_ref, keep_ref, far_ref, *refs):
-            con_ref, scr = refs[seq_parts:]
+        fold = own_width // 2
+        rider = -(-sub // 32) * 16
+        at_outs = slice(half_own, half_own + fold)
+
+        def fold_in(value):
+            down = value.shape[0] // 2
+            return jnp.concatenate([value[0:down], value[down:]], axis=1)
+
+        def fold_out(value):
+            across = value.shape[1] // 2
+            return jnp.concatenate([value[:, 0:across], value[:, across:]], axis=0)
+
+        def dp_pack_kernel(
+            info_ref, own_ref, far_two_ref, keep_ref, far_ref, ok_ref, of_ref, gk_ref, gf_ref, *refs
+        ):
+            con_ref, gown_ref, gsend_ref, scr = refs[seq_parts:]
             whole = own_ref[...] + far_two_ref[...].astype(f32)
             con_ref[...] = whole[0 : ff // parts].astype(bf)
             scr[...] = whole[ff // parts :]
             for j in range(seq_parts):
                 at = jnp.bitwise_xor(info_ref[0], j)
-                refs[j][0:tall, :] = (keep_ref[at].astype(f32) + far_ref[at].astype(f32)).astype(
+                refs[j][0:half_own, :] = (
+                    keep_ref[at].astype(f32) + far_ref[at].astype(f32)
+                ).astype(bf)
+                refs[j][at_outs, :] = fold_in(ok_ref[at].astype(f32) + of_ref[at].astype(f32)).astype(
                     bf
                 )
-                refs[j][tall:, 0:half_ff] = scr[aligned(at, sub), :].astype(bf)
-                refs[j][tall:, half_ff:] = jnp.zeros((sub, 3 * hw - half_ff), bf)
+                piece = fold_in(scr[aligned(at, sub), :])
+                piece = jnp.concatenate(
+                    [piece, jnp.zeros((rider - sub // 2, width), f32)], axis=0
+                )
+                refs[j][half_own + fold :, :] = piece.astype(bf)
+            gown_ref[...] = gk_ref[0] + gf_ref[0].astype(f32)
+            gsend_ref[...] = (gk_ref[1] + gf_ref[1].astype(f32)).astype(bf)
 
         dp_out = local_call(
             dp_pack_kernel,
             "owners",
-            [shape_of((tall + sub, 3 * hw), bf)] * seq_parts
-            + [shape_of((ff // parts, half_width), bf)],
-            [info, rs_own_two, rs_far_two, in_keep, in_far],
-            scalars=1,
-            scratch=[pltpu.VMEM((own_width, half_ff), f32)],
-            after=[block_out],
-        )
-        dp_parts = [dp_out[0]] + [seq_swap(dp_out[j], j) for j in others]
-        con_one = dp_out[seq_parts]
-        con_two = chip_swap(con_one, 2)
-
-        wide = tall + sub
-        tail = own_width * half_ff // (3 * hw)
-        over = own_width - tail
-
-        def dp_sum_kernel(info_ref, gk_ref, gf_ref, ok_ref, of_ref, *refs):
-            owned = refs[:seq_parts]
-            last_ref, gown_ref, gsend_ref, scr = refs[seq_parts:]
-            whole = owned[0][0:tall, :].astype(f32)
-            for j in others:
-                whole = whole + owned[j][0:tall, :].astype(f32)
-            last_ref[0:tall, :] = whole.astype(bf)
-            for j in range(seq_parts):
-                place = jnp.bitwise_xor(info_ref[0], j)
-                scr[aligned(place, sub), :] = owned[j][tall:, 0:half_ff]
-            last_ref[tall : tall + tail, 0:half_ff] = scr[0:tail, :]
-            last_ref[tall : tall + over, half_ff:] = scr[tail:, 0 : half_ff // 2]
-            last_ref[tall + over : tall + tail, half_ff:] = scr[tail:, half_ff // 2 :]
-            for k in range(2):
-                at = slice(tall + tail + k * sub, tall + tail + (k + 1) * sub)
-                last_ref[at, 0:half_width] = (ok_ref[k] + of_ref[k].astype(f32)).astype(bf)
-                last_ref[at, half_width:] = jnp.zeros((sub, 3 * hw - half_width), bf)
-            gown_ref[...] = gk_ref[0] + gf_ref[0].astype(f32)
-            gsend_ref[...] = (gk_ref[1] + gf_ref[1].astype(f32)).astype(bf)
-
-        last_one, gt_own, gt_send_two = local_call(
-            dp_sum_kernel,
-            "shares",
-            [
-                shape_of((tall + tail + 2 * sub, 3 * hw), bf),
+            [shape_of((half_own + fold + rider, width), bf)] * seq_parts
+            + [
+                shape_of((ff // parts, half_width), bf),
                 shape_of((rows, width), f32),
                 shape_of((rows, width), bf),
             ],
-            [info, gt_keep, gt_far, os_keep, os_far] + dp_parts,
+            [info, rs_own_two, rs_far_two, in_keep, in_far, out_keep, out_far, gt_keep, gt_far],
             scalars=1,
-            scratch=[pltpu.VMEM((own_width, half_ff), bf)],
-            after=[con_two],
-        )
-        last_one_far = chip_swap(last_one, 2)
+            scratch=[pltpu.VMEM((own_width, half_ff), f32)],
+        )
+        dp_parts = [dp_out[0]] + [seq_swap(dp_out[j], j) for j in others]
+        con_one, gt_own, gt_send_two = dp_out[seq_parts:]
+        con_two = chip_swap(con_one, 2)
         gt_far_two = chip_swap(gt_send_two, 2)
+
         con_one_far = chip_swap(con_one, 1)
         con_two_far = chip_swap(con_two, 1)
+
+        def dp_sum_kernel(info_ref, *refs):
+            owned = refs[:seq_parts]
+            last_ref, scr = refs[seq_parts:]
+            whole = owned[0][0 : half_own + fold, :].astype(f32)
+            for j in others:
+                whole = whole + owned[j][0 : half_own + fold, :].astype(f32)
+            last_ref[0 : half_own + fold, :] = whole.astype(bf)
+            for j in range(seq_parts):
+                place = jnp.bitwise_xor(info_ref[0], j)
+                piece = owned[j][half_own + fold :, :].astype(f32)
+                scr[aligned(place, sub), :] = fold_out(piece[0 : sub // 2])
+            last_ref[half_own + fold :, :] = fold_in(scr[...]).astype(bf)
+
+        (last_one,) = local_call(
+            dp_sum_kernel,
+            "shares",
+            [shape_of((half_own + 2 * fold, width), bf)],
+            [info] + dp_parts,
+            scalars=1,
+            scratch=[pltpu.VMEM((own_width, half_ff), f32)],
+            after=[con_one_far, con_two_far, gt_far_two],
+        )
+        last_two = chip_swap(last_one, 2)
+        last_one_far = chip_swap(last_one, 1)
+        last_two_far = chip_swap(last_two, 1)
+        last_parts = [last_one, last_one_far, last_two, last_two_far]
+        last_far = [core_swap(member) for member in last_parts]
         con_parts = [con_one, con_one_far, con_two, con_two_far]
         con_far = [core_swap(member) for member in con_parts]
 
         def contract_kernel(info_ref, *refs):
-            con_ref = refs[2 * parts]
+            con_ref, done_ref = refs[2 * parts :]
+            done_ref[...] = jnp.zeros_like(done_ref)
             for flip in range(2):
                 lanes = aligned(jnp.bitwise_xor(info_ref[2], flip), half_width)
                 for k in range(parts):
@@ -1332,31 +1356,29 @@
                         f32
                     )
 
-        (grad_contract,) = local_call(
+        grad_contract, contract_done = local_call(
             contract_kernel,
             "contract_final",
-            [shape_of((ff, width), f32)],
+            [shape_of((ff, width), f32), shape_of((8, 128), f32)],
             [info] + con_parts + con_far,
             scalars=1,
         )
 
-        def last_pair_kernel(own_ref, far_ref, out_ref):
-            for slot, (first, second) in enumerate(((own_ref, far_ref), (far_ref, own_ref))):
-                out_ref[slot, 0 : tall + tail, :] = first[0 : tall + tail, :]
-                outs = first[tall + tail : wide + tail, :].astype(f32)
-                outs = outs + second[wide + tail :, :].astype(f32)
-                out_ref[slot, tall + tail :, :] = outs.astype(bf)
-
-        (last_two,) = local_call(
-            last_pair_kernel,
-            "input_pair",
-            [shape_of((2, wide + tail, 3 * hw), bf)],
-            [last_one, last_one_far],
-            after=[gt_far_two, con_one_far, con_two_far],
-        )
-        last_two_far = chip_swap(last_two, 1)
-        core_two = core_swap(last_two)
-        core_two_far = core_swap(last_two_far)
+        res_parts = [results[0]] + [seq_swap(results[j], j) for j in others]
+
+        def result_kernel(mid_ref, vec_ref, *refs):
+            result = mid_ref[...] + vec_ref[7:8]
+            for j in range(seq_parts):
+                result = result + refs[j][...].astype(f32)
+            refs[seq_parts][0] = result.astype(bf)
+
+        (block_out,) = local_call(
+            result_kernel,
+            "result",
+            [shape_of((1, rows, width), bf)],
+            [middle, vectors] + res_parts,
+            after=[last_one],
+        )
 
         def tokens_kernel(tok_ref, vec_ref, gmid_ref, own_ref, far_ref, out_ref):
             grad = own_ref[...] + far_ref[...].astype(f32)
@@ -1371,59 +1393,52 @@
         )
 
         def last_kernel(info_ref, *refs):
-            gin_ref, gout_ref, small_ref, exp_ref, scr = refs[4:]
-
-            def member(far_core, k):
-                return refs[2 * far_core + k % 2][k // 2]
-
+            gin_ref, gout_ref, exp_ref = refs[2 * parts : 2 * parts + 3]
+            bias_ref, smalls, scr = refs[2 * parts + 3], refs[2 * parts + 4 : -1], refs[-1]
             for flip in range(2):
                 half = jnp.bitwise_xor(info_ref[2], flip)
+                outs = jnp.zeros((fold, width), f32)
                 for k in range(parts):
                     at = jnp.bitwise_xor(info_ref[1], k)
-                    piece = member(flip, k).astype(f32)
-                    scr[at, aligned(half, half_own), :] = piece[0:half_own]
-                    gout_ref[aligned(at, sub), aligned(half, half_width)] = piece[
-                        tall + tail :, 0:half_width
-                    ]
-                    turned = jnp.concatenate(
-                        [
-                            piece[tall : tall + over, half_ff:],
-                            piece[tall + over : tall + tail, half_ff:],
-                        ],
-                        axis=1,
-                    )
-                    turned = jnp.concatenate(
-                        [piece[tall : tall + tail, 0:half_ff], turned], axis=0
-                    )
+                    piece = refs[flip * parts + k][...].astype(f32)
+                    scr[at, aligned(half, half_own), :] = piece[0:half_own, 0 : 3 * hw]
+                    outs = outs + piece[at_outs]
+                    turned = fold_out(piece[half_own + fold :])
                     for j in range(seq_parts):
                         cols = pl.ds(pl.multiple_of(j * ff + half * half_ff, 128), half_ff)
                         exp_ref[aligned(at, sub), cols] = turned[j * sub : (j + 1) * sub]
+                gout_ref[:, aligned(half, half_width)] = fold_out(outs)
             for at in range(parts):
                 for base in range(3):
                     start = base * width + at * hw
                     gin_ref[:, start : start + hw] = scr[at, :, base * hw : (base + 1) * hw]
-            small = member(0, 0)[half_own:tall, 0:own_width].astype(f32)
+            small = refs[0][0:small_rows, 3 * hw :].astype(f32)
             for k in others:
-                small = small + member(0, k)[half_own:tall, 0:own_width].astype(f32)
-            small_ref[...] = small
-
-        grad_input, grad_output, small_sums, grad_expand = local_call(
+                small = small + refs[k][0:small_rows, 3 * hw :].astype(f32)
+            for i in range(8):
+                smalls[i][...] = small[i : i + 1].reshape(own_width)
+            bias_ref[...] = jnp.concatenate(
+                [small[8 + i : 9 + i] for i in range(ff // own_width)], axis=1
+            ).reshape(ff)
+
+        last_out = local_call(
             last_kernel,
             "weights_final",
             [
                 shape_of((own_width, 3 * width), f32),
                 shape_of((own_width, width), f32),
-                shape_of((small_rows, own_width), f32),
                 shape_of((own_width, seq_parts * ff), f32),
-            ],
-            [info, last_two, last_two_far, core_two, core_two_far],
+                shape_of((ff,), f32),
+            ]
+            + [shape_of((own_width,), f32)] * 8,
+            [info] + last_parts + last_far,
             scalars=1,
-            after=[grad_tokens, grad_contract],
             scratch=[pltpu.VMEM((parts, own_width, 3 * hw), f32)],
-        )
-
-        small_of = [small_sums[i] for i in range(8)]
-        grad_expand_bias = small_sums[8 : 8 + ff // own_width].reshape(ff)
+            after=[contract_done],
+            grant=VMEM_LARGE,
+        )
+        grad_input, grad_output, grad_expand, grad_expand_bias = last_out[:4]
+        small_of = last_out[4:]
         return (
             block_out,
             grad_tokens,

time: 221 us -> 195 us (0.88)
  waiting for transfers between devices: 125 us -> 100 us
  local copies, waits for them, and re-layouts: 5.49 us -> 0.05 us
  starting transfers between devices: 51 us -> 55.7 us
    ppermute x21 -> x18, waiting for transfers between devices: 46.4 us -> 25.9 us  [seq_swap(): return lax.ppermute(member, 'dp', [(i, i ^ step) for i in range(seq_parts)])]
    ppermute x19, waiting for transfers between devices: 76.6 us -> 64.9 us  [chip_swap(): lax.ppermute(member, 'ctx', [(i, 2 * (i // 2 ^ step) + i % 2) for i in ra...]
    ppermute x11 -> x15, waiting for transfers between devices: 2.3 us -> 9.31 us  [core_swap(): return lax.ppermute(member, 'ctx', [(i, i ^ 1) for i in range(ranks)])]
    ppermute x19, starting transfers between devices: 25 us -> 31.7 us  [chip_swap(): lax.ppermute(member, 'ctx', [(i, 2 * (i // 2 ^ step) + i % 2) for i in ra...]
    unnamed x24 -> x20, local copies, waits for them, and re-layouts: 4.22 us -> 0.05 us
    ppermute x21 -> x18, starting transfers between devices: 24.3 us -> 21.2 us  [seq_swap(): return lax.ppermute(member, 'dp', [(i, i ^ step) for i in range(seq_parts)])]
  transfers between devices with their start and end apart: 51 -> 52, of which waited for: 23 -> 27; matrix products, arithmetic and copies ran while one was open for 0% -> 0% of each run, Pallas kernels for 10% -> 8%
where the time goes in v3:
time: 195 us
  waiting for transfers between devices  100 us (51%)
  starting transfers between devices  55.7 us (29%)
  Pallas kernels  37.2 us (19%)
    ppermute x19, waiting for transfers between devices, chip_swap(): lax.ppermute(member, 'ctx', [(i, 2 * (i // 2 ^ step) + i % 2) for i in ra...  64.9 us
    pallas_call x21, Pallas kernels, local_call(): pl.pallas_call(ordered, out_shape=tuple(outs), in_specs=[pl.BlockSpec(mem...  37.2 us
    ppermute x19, starting transfers between devices, chip_swap(): lax.ppermute(member, 'ctx', [(i, 2 * (i // 2 ^ step) + i % 2) for i in ra...  31.7 us
    ppermute x18, waiting for transfers between devices, seq_swap(): return lax.ppermute(member, 'dp', [(i, i ^ step) for i in range(seq_parts)])  25.9 us
    ppermute x18, starting transfers between devices, seq_swap(): return lax.ppermute(member, 'dp', [(i, i ^ step) for i in range(seq_parts)])  21.2 us
    ppermute x15, waiting for transfers between devices, core_swap(): return lax.ppermute(member, 'ctx', [(i, i ^ 1) for i in range(ranks)])  9.31 us
  transfers between devices with their start and end apart: 52, of which 27 were waited for; matrix products, arithmetic and copies ran while one was open for 0% of the time, Pallas kernels for 8%

profile of v3, /device:TPU:0, one launch (start us, length us, event | category | flops | bytes accessed | tf_op | source)
XLA Modules:
  0.0 194.7 jit_solution(17286982364816050882)
XLA Ops:
  1.3 2.8 %pack.1 = (bf16[192,768]{1,0:T(8,128)(2,1)}, bf16[128,768]{1,0:T(8,128)(2,1)}) custom-call(s32[3]{0:T(128)} %pad_add_fusion.refs_0_, bf16[128,768]{1,0:T(8,128)(2,1)} %bitcast.8, bf16[192,2304]{1,0:T(8,128)(2,1)} %refs_1_.5, bf16[192,768]{1,0:T(8,128)(2,1)} %refs_2_.4, bf16[192]{0:T(256)(128)(2,1)} %refs_4_.1, bf16[192]{0:T(256)(128)(2,1)} %refs_5_.1, ...), custom_call_target="tpu_custom_call" | custom-call | bytes 1870860 | tf_op jit(solution)/shard_map/pack/pallas_call | solution.py:636
  4.0 5.1 %collective-permute-start.2 = (bf16[128,768]{1,0:T(8,128)(2,1)}, bf16[128,768]{1,0:T(8,128)(2,1)S(1)}, u32[]{:S(2)}, u32[]{:S(2)}) collective-permute-start(bf16[128,768]{1,0:T(8,128)(2,1)} %get-tuple-element.89.refs_3_.refs_1_.refs_4_.refs_0_), channel_id=1, source_target_pairs={{0,6},{1,7},{2,4},{3,5},{4,2},{5,3},{6,0},{7,1},{8,14},{9,15},{10,... | collective-permute-start | bytes 589832 | tf_op jit(solution)/shard_map/ppermute | solution.py:686
  9.2 2.5 %collective-permute-start.5 = (bf16[192,768]{1,0:T(8,128)(2,1)}, bf16[192,768]{1,0:T(8,128)(2,1)S(1)}, u32[]{:S(2)}, u32[]{:S(2)}) collective-permute-start(bf16[192,768]{1,0:T(8,128)(2,1)} %get-tuple-element.90.refs_7_.refs_3_), channel_id=1, source_target_pairs={{0,24},{8,16},{16,8},{24,0},{1,25},{9,17},{17,9},{25,1},{2,26},{10... | collective-permute-start | bytes 884744 | tf_op jit(solution)/shard_map/ppermute | solution.py:691
  12.8 2.0 %collective-permute-done.2.refs_5_.refs_6_.refs_7_ = bf16[128,768]{1,0:T(8,128)(2,1)S(1)} collective-permute-done((bf16[128,768]{1,0:T(8,128)(2,1)}, bf16[128,768]{1,0:T(8,128)(2,1)S(1)}, u32[]{:S(2)}, u32[]{:S(2)}) %collective-permute-start.2) | collective-permute-done | bytes 196640 | tf_op jit(solution)/shard_map/ppermute | solution.py:686
  14.8 8.6 %collective-permute-start = (bf16[128,768]{1,0:T(8,128)(2,1)}, bf16[128,768]{1,0:T(8,128)(2,1)S(1)}, u32[]{:S(2)}, u32[]{:S(2)}) collective-permute-start(bf16[128,768]{1,0:T(8,128)(2,1)} %get-tuple-element.89.refs_3_.refs_1_.refs_4_.refs_0_), channel_id=1, source_target_pairs={{0,2},{1,3},{2,0},{3,1},{4,6},{5,7},{6,4},{7,5},{8,10},{9,11},{10,... | collective-permute-start | bytes 589832 | tf_op jit(solution)/shard_map/ppermute | solution.py:686
  23.4 2.8 %collective-permute-done.1.refs_4_.refs_5_.refs_6_ = bf16[128,768]{1,0:T(8,128)(2,1)S(1)} collective-permute-done((bf16[128,768]{1,0:T(8,128)(2,1)}, bf16[128,768]{1,0:T(8,128)(2,1)S(1)}, u32[]{:S(2)}, u32[]{:S(2)}) %collective-permute-start.1) | collective-permute-done | bytes 196640 | tf_op jit(solution)/shard_map/ppermute | solution.py:686
  26.2 4.0 %collective-permute-done.refs_3_.refs_4_.refs_5_ = bf16[128,768]{1,0:T(8,128)(2,1)S(1)} collective-permute-done((bf16[128,768]{1,0:T(8,128)(2,1)}, bf16[128,768]{1,0:T(8,128)(2,1)S(1)}, u32[]{:S(2)}, u32[]{:S(2)}) %collective-permute-start) | collective-permute-done | bytes 196640 | tf_op jit(solution)/shard_map/ppermute | solution.py:686
  30.4 2.4 %collective-permute-done.6.refs_9_ = bf16[576,768]{1,0:T(8,128)(2,1)S(1)} collective-permute-done((bf16[576,768]{1,0:T(8,128)(2,1)S(1)}, bf16[576,768]{1,0:T(8,128)(2,1)S(1)}, u32[]{:S(2)}, u32[]{:S(2)}) %collective-permute-start.6) | collective-permute-done | bytes 884768 | tf_op jit(solution)/shard_map/ppermute | solution.py:683
  32.8 2.1 %project.1 = (bf16[512,192]{1,0:T(8,128)(2,1)S(1)}, bf16[512,384]{1,0:T(8,128)(2,1)S(1)}, bf16[512,768]{1,0:T(8,128)(2,1)S(1)}, bf16[768,576]{1,0:T(8,128)(2,1)S...) custom-call(s32[3]{0:T(128)S(1)} %copy-done.6, bf16[192,2304]{1,0:T(8,128)(2,1)S(1)} %copy-done, ...), custom_call_target="tpu_custom_call" | custom-call | flops 452984832 | bytes 7520268 | tf_op jit(solution)/shard_map/project/pallas_call | solution.py:636
  35.8 1.6 collective-permute-start.11
  37.4 1.5 collective-permute-start.12
  39.4 3.7 %attend.1 = (bf16[128,192]{1,0:T(8,128)(2,1)S(1)}, bf16[128,192]{1,0:T(8,128)(2,1)S(1)}, bf16[128,192]{1,0:T(8,128)(2,1)S(1)}, bf16[128,192]{1,0:T(8,128)(2,1)S(...) custom-call(s32[3]{0:T(128)S(1)} %copy-done.6, s32[8]{0:T(128)S(1)} %copy-done.9, ...), custom_call_target="tpu_custom_call" | custom-call | flops 402653184 | bytes 1589292 | tf_op jit(solution)/shard_map/attend/pallas_call | solution.py:636
  43.2 2.8 %collective-permute-start.9 = (bf16[128,192]{1,0:T(8,128)(2,1)S(1)}, bf16[128,192]{1,0:T(8,128)(2,1)S(1)}, u32[]{:S(2)}, u32[]{:S(2)}) collective-permute-start(bf16[128,192]{1,0:T(8,128)(2,1)S(1)} %get-tuple-element.97), channel_id=1, source_target_pairs={{0,4},{1,5},{2,6},{3,7},{4,0},{5,1},{6,2},{7,3},{8,12},{9,13},{10,... | collective-permute-start | bytes 147464 | tf_op jit(solution)/shard_map/ppermute | solution.py:686
  46.0 1.7 collective-permute-done.8.refs_5_.refs_3_
  47.7 2.3 %collective-permute-start.10 = (bf16[128,192]{1,0:T(8,128)(2,1)S(1)}, bf16[128,192]{1,0:T(8,128)(2,1)S(1)}, u32[]{:S(2)}, u32[]{:S(2)}) collective-permute-start(bf16[128,192]{1,0:T(8,128)(2,1)S(1)} %get-tuple-element.98), channel_id=1, source_target_pairs={{0,6},{1,7},{2,4},{3,5},{4,2},{5,3},{6,0},{7,1},{8,14},{9,15},{10,... | collective-permute-start | bytes 147464 | tf_op jit(solution)/shard_map/ppermute | solution.py:686
  50.0 3.7 %collective-permute-done.10.refs_7_.refs_5_ = bf16[128,192]{1,0:T(8,128)(2,1)S(1)} collective-permute-done((bf16[128,192]{1,0:T(8,128)(2,1)S(1)}, bf16[128,192]{1,0:T(8,128)(2,1)S(1)}, u32[]{:S(2)}, u32[]{:S(2)}) %collective-permute-start.10) | collective-permute-done | bytes 49184 | tf_op jit(solution)/shard_map/ppermute | solution.py:686
  53.7 1.1 middle.1
  55.0 2.5 %collective-permute-start.17 = (bf16[128,768]{1,0:T(8,128)(2,1)S(1)}, bf16[128,768]{1,0:T(8,128)(2,1)S(1)}, u32[]{:S(2)}, u32[]{:S(2)}) collective-permute-start(bf16[128,768]{1,0:T(8,128)(2,1)S(1)} %get-tuple-element.103.refs_3_.refs_6_), channel_id=1, source_target_pairs={{0,24},{8,16},{16,8},{24,0},{1,25},{9,17},{17,9},{25,1},{2,26},{10... | collective-permute-start | bytes 589832 | tf_op jit(solution)/shard_map/ppermute | solution.py:691
  58.6 5.2 %collective-permute-done.17.refs_9_ = bf16[128,768]{1,0:T(8,128)(2,1)S(1)} collective-permute-done((bf16[128,768]{1,0:T(8,128)(2,1)S(1)}, bf16[128,768]{1,0:T(8,128)(2,1)S(1)}, u32[]{:S(2)}, u32[]{:S(2)}) %collective-permute-start.17) | collective-permute-done | bytes 196640 | tf_op jit(solution)/shard_map/ppermute | solution.py:691
  63.7 3.7 %collective-permute-done.16.refs_8_ = bf16[128,768]{1,0:T(8,128)(2,1)S(1)} collective-permute-done((bf16[128,768]{1,0:T(8,128)(2,1)S(1)}, bf16[128,768]{1,0:T(8,128)(2,1)S(1)}, u32[]{:S(2)}, u32[]{:S(2)}) %collective-permute-start.16) | collective-permute-done | bytes 196640 | tf_op jit(solution)/shard_map/ppermute | solution.py:691
  67.5 5.6 %feed.1 = (bf16[128,768]{1,0:T(8,128)(2,1)S(1)}, bf16[128,768]{1,0:T(8,128)(2,1)S(1)}, bf16[128,768]{1,0:T(8,128)(2,1)S(1)}, bf16[128,768]{1,0:T(8,128)(2,1)S(1)...) custom-call(s32[3]{0:T(128)S(1)} %copy-done.6, ...), custom_call_target="tpu_custom_call" | custom-call | flops 3623878656 | bytes 8753676 | tf_op jit(solution)/shard_map/feed/pallas_call | solution.py:636
  73.2 2.8 %collective-permute-done.21.refs_2_ = bf16[4,384,384]{2,1,0:T(8,128)(2,1)S(1)} collective-permute-done((bf16[4,384,384]{2,1,0:T(8,128)(2,1)S(1)}, bf16[4,384,384]{2,1,0:T(8,128)(2,1)S(1)}, u32[]{:S(2)}, u32[]{:S(2)}) %collective-permute-start.21) | collective-permute-done | bytes 1179680 | tf_op jit(solution)/shard_map/ppermute | solution.py:683
  76.0 0.8 feed_halves.1
  77.0 1.5 collective-permute-start.23
  79.2 1.3 collective-permute-start.25
  80.5 4.3 %collective-permute-done.23.refs_6_ = bf16[128,768]{1,0:T(8,128)(2,1)S(1)} collective-permute-done((bf16[128,768]{1,0:T(8,128)(2,1)S(1)}, bf16[128,768]{1,0:T(8,128)(2,1)S(1)}, u32[]{:S(2)}, u32[]{:S(2)}) %collective-permute-start.23) | collective-permute-done | bytes 196640 | tf_op jit(solution)/shard_map/ppermute | solution.py:691
  84.8 4.6 %collective-permute-done.24.refs_7_ = bf16[128,768]{1,0:T(8,128)(2,1)S(1)} collective-permute-done((bf16[128,768]{1,0:T(8,128)(2,1)S(1)}, bf16[128,768]{1,0:T(8,128)(2,1)S(1)}, u32[]{:S(2)}, u32[]{:S(2)}) %collective-permute-start.24) | collective-permute-done | bytes 196640 | tf_op jit(solution)/shard_map/ppermute | solution.py:691
  89.4 1.4 middle_back.1
  90.8 2.4 %collective-permute-start.26 = (bf16[128,192]{1,0:T(8,128)(2,1)S(1)}, bf16[128,192]{1,0:T(8,128)(2,1)S(1)}, u32[]{:S(2)}, u32[]{:S(2)}) collective-permute-start(bf16[128,192]{1,0:T(8,128)(2,1)S(1)} %get-tuple-element.116), channel_id=1, source_target_pairs={{0,6},{1,7},{2,4},{3,5},{4,2},{5,3},{6,0},{7,1},{8,14},{9,15},{10,... | collective-permute-start | bytes 147464 | tf_op jit(solution)/shard_map/ppermute | solution.py:686
  93.2 0.8 collective-permute-start.28
  93.9 1.3 collective-permute-start.29
  95.3 1.0 output_weights.1
  96.3 1.1 collective-permute-done.26.refs_2_.refs_10_
  97.9 1.2 collective-permute-done.29.refs_9_
  99.1 5.0 %attend_back.1 = (f32[192,512]{1,0:T(8,128)S(1)}, f32[512,384]{1,0:T(8,128)S(1)}, bf16[512,384]{1,0:T(8,128)(2,1)S(1)}) custom-call(s32[3]{0:T(128)S(1)} %copy-done.6, s32[8]{0:T(128)S(1)} %copy-done.9, bf16[512,192]{1,0:T(8,128)(2,1)S(1)} %get-tuple-element.93.refs_2_, bf16[512,384]{1,0:T(8,128)(2,1)S(1)} %get-tuple-element.94.refs_3_, ...), custom_call_target="tpu_custom_call" | custom-call | flops 1006632960 | bytes 3162156 | tf_op jit(solution)/shard_map/attend_back/pallas_call | solution.py:636
  104.7 1.2 collective-permute-done.30.refs_2_
  105.9 1.8 normed_back.1
  107.7 1.5 input_weights.1
  109.4 1.3 collective-permute-start.33
  110.7 1.7 collective-permute-start.27
  112.4 13.5 %collective-permute-done.27.refs_2_ = bf16[384,384]{1,0:T(8,128)(2,1)S(1)} collective-permute-done((bf16[384,384]{1,0:T(8,128)(2,1)S(1)}, bf16[384,384]{1,0:T(8,128)(2,1)S(1)}, u32[]{:S(2)}, u32[]{:S(2)}) %collective-permute-start.27) | collective-permute-done | bytes 294944 | tf_op jit(solution)/shard_map/ppermute | solution.py:686
  125.9 1.2 collective-permute-done.33.refs_8_
  127.1 1.1 owners.1
  128.2 2.2 %collective-permute-start.38 = (bf16[192,384]{1,0:T(8,128)(2,1)S(1)}, bf16[192,384]{1,0:T(8,128)(2,1)S(1)}, u32[]{:S(2)}, u32[]{:S(2)}) collective-permute-start(bf16[192,384]{1,0:T(8,128)(2,1)S(1)} %get-tuple-element.145.refs_1_), channel_id=1, source_target_pairs={{0,4},{1,5},{2,6},{3,7},{4,0},{5,1},{6,2},{7,3},{8,12},{9,13},{10,... | collective-permute-start | bytes 442376 | tf_op jit(solution)/shard_map/ppermute | solution.py:686
  131.0 1.4 collective-permute-start.35
  132.4 1.5 collective-permute-start.36
  134.0 0.8 collective-permute-start.37
  134.8 3.0 %collective-permute-done.38.refs_3_ = bf16[192,384]{1,0:T(8,128)(2,1)S(1)} collective-permute-done((bf16[192,384]{1,0:T(8,128)(2,1)S(1)}, bf16[192,384]{1,0:T(8,128)(2,1)S(1)}, u32[]{:S(2)}, u32[]{:S(2)}) %collective-permute-start.38) | collective-permute-done | bytes 147488 | tf_op jit(solution)/shard_map/ppermute | solution.py:686
  137.8 2.6 %collective-permute-done.37.refs_5_.refs_2_ = bf16[192,384]{1,0:T(8,128)(2,1)S(1)} collective-permute-done((bf16[192,384]{1,0:T(8,128)(2,1)S(1)}, bf16[192,384]{1,0:T(8,128)(2,1)S(1)}, u32[]{:S(2)}, u32[]{:S(2)}) %collective-permute-start.37) | collective-permute-done | bytes 147488 | tf_op jit(solution)/shard_map/ppermute | solution.py:686
  140.7 8.0 %collective-permute-done.40.refs_7_.refs_4_ = bf16[128,768]{1,0:T(8,128)(2,1)S(1)} collective-permute-done((bf16[128,768]{1,0:T(8,128)(2,1)S(1)}, bf16[128,768]{1,0:T(8,128)(2,1)S(1)}, u32[]{:S(2)}, u32[]{:S(2)}) %collective-permute-start.40) | collective-permute-done | bytes 196640 | tf_op jit(solution)/shard_map/ppermute | solution.py:686
  148.8 0.9 collective-permute-done.39.refs_6_.refs_4_
  149.7 0.8 shares.1.refs_6_.refs_1_
  150.6 1.8 collective-permute-start.41
  152.4 18.6 %collective-permute-done.42.refs_3_ = bf16[288,768]{1,0:T(8,128)(2,1)S(1)} collective-permute-done((bf16[288,768]{1,0:T(8,128)(2,1)S(1)}, bf16[288,768]{1,0:T(8,128)(2,1)S(1)}, u32[]{:S(2)}, u32[]{:S(2)}) %collective-permute-start.42) | collective-permute-done | bytes 442400 | tf_op jit(solution)/shard_map/ppermute | solution.py:686
  171.1 0.8 collective-permute-start.18
  171.8 1.3 collective-permute-start.19
  173.2 1.4 collective-permute-start.20
  174.5 4.3 %collective-permute-done.18.refs_3_ = bf16[128,768]{1,0:T(8,128)(2,1)S(1)} collective-permute-done((bf16[128,768]{1,0:T(8,128)(2,1)S(1)}, bf16[128,768]{1,0:T(8,128)(2,1)S(1)}, u32[]{:S(2)}, u32[]{:S(2)}) %collective-permute-start.18) | collective-permute-done | bytes 196640 | tf_op jit(solution)/shard_map/ppermute | solution.py:691
  178.8 3.7 %collective-permute-done.19.refs_4_ = bf16[128,768]{1,0:T(8,128)(2,1)S(1)} collective-permute-done((bf16[128,768]{1,0:T(8,128)(2,1)S(1)}, bf16[128,768]{1,0:T(8,128)(2,1)S(1)}, u32[]{:S(2)}, u32[]{:S(2)}) %collective-permute-start.19) | collective-permute-done | bytes 196640 | tf_op jit(solution)/shard_map/ppermute | solution.py:691
  184.1 2.6 %collective-permute-done.49.refs_6_ = bf16[192,384]{1,0:T(8,128)(2,1)S(1)} collective-permute-done((bf16[192,384]{1,0:T(8,128)(2,1)S(1)}, bf16[192,384]{1,0:T(8,128)(2,1)S(1)}, u32[]{:S(2)}, u32[]{:S(2)}) %collective-permute-start.49) | collective-permute-done | bytes 147488 | tf_op jit(solution)/shard_map/ppermute | solution.py:683
  187.0 1.1 tokens_back.1
  188.0 0.8 result.1
  188.9 2.1 %contract_final.1 = (f32[768,768]{1,0:T(8,128)}, f32[8,128]{1,0:T(8,128)S(1)}) custom-call(s32[3]{0:T(128)S(1)} %copy-done.6, bf16[192,384]{1,0:T(8,128)(2,1)S(1)} %get-tuple-element.145.refs_1_, bf16[192,384]{1,0:T(8,128)(2,1)S(1)} %collective-permute-done.37.refs_5_.refs_2_, bf16[192,384]{1,0:T(8,128)(2,1)S(1)} %collective-permute-done.38.refs_3_, ...), custom_call_target="tpu_custom_call" | custom-call | bytes 3543052 | tf_op jit(solution)/shard_map/contract_final/pallas_call | solution.py:636
  191.0 3.6 %weights_final.1 = (f32[192,2304]{1,0:T(8,128)}, f32[192,768]{1,0:T(8,128)}, f32[192,3072]{1,0:T(8,128)}, f32[768]{0:T(1024)}, f32[192]{0:T(256)}, /*index=5*/f3...) custom-call(s32[3]{0:T(128)S(1)} %copy-done.6, ...), custom_call_target="tpu_custom_call" | custom-call | bytes 8266764 | tf_op jit(solution)/shard_map/weights_final/pallas_call | solution.py:636
  (82 shorter events, 9.5 us)
Async XLA Ops:
  4.0 10.8 %collective-permute-start.2 = (bf16[128,768]{1,0:T(8,128)(2,1)}, bf16[128,768]{1,0:T(8,128)(2,1)S(1)}, u32[]{:S(2)}, u32[]{:S(2)}) collective-permute-start(bf16[128,768]{1,0:T(8,128)(2,1)} %get-tuple-element.89.refs_3_.refs_1_.refs_4_.refs_0_), channel_id=1, source_target_pairs={{0,6},{1,7},{2,4},{3,5},{4,2},{5,3},{6,0},{7,1},{8,14},{9,15},{10,... | collective-permute-start | bytes 589832 | tf_op jit(solution)/shard_map/ppermute | solution.py:686
  9.2 23.6 %copy-start = (bf16[192,2304]{1,0:T(8,128)(2,1)S(1)}, bf16[192,2304]{1,0:T(8,128)(2,1)}, u32[]{:S(2)}) copy-start(bf16[192,2304]{1,0:T(8,128)(2,1)} %refs_1_.5) | copy-start | bytes 2654212
  9.2 23.6 %copy-start.1 = (bf16[128,768]{1,0:T(8,128)(2,1)S(1)}, bf16[128,768]{1,0:T(8,128)(2,1)}, u32[]{:S(2)}) copy-start(bf16[128,768]{1,0:T(8,128)(2,1)} %get-tuple-element.89.refs_3_.refs_1_.refs_4_.refs_0_) | copy-start | bytes 589828
  9.2 23.6 %copy-start.2 = (bf16[192,768]{1,0:T(8,128)(2,1)S(1)}, bf16[192,768]{1,0:T(8,128)(2,1)}, u32[]{:S(2)}) copy-start(bf16[192,768]{1,0:T(8,128)(2,1)} %refs_2_.4) | copy-start | bytes 884740
  9.2 23.6 %copy-start.3 = (bf16[192,768]{1,0:T(8,128)(2,1)S(1)}, bf16[192,768]{1,0:T(8,128)(2,1)}, u32[]{:S(2)}) copy-start(bf16[192,768]{1,0:T(8,128)(2,1)} %get-tuple-element.90.refs_7_.refs_3_) | copy-start | bytes 884740
  9.2 23.7 %copy-start.6 = (s32[3]{0:T(128)S(1)}, s32[3]{0:T(128)}, u32[]{:S(2)}) copy-start(s32[3]{0:T(128)} %pad_add_fusion.refs_0_) | copy-start | bytes 40
  9.2 21.0 %collective-permute-start.5 = (bf16[192,768]{1,0:T(8,128)(2,1)}, bf16[192,768]{1,0:T(8,128)(2,1)S(1)}, u32[]{:S(2)}, u32[]{:S(2)}) collective-permute-start(bf16[192,768]{1,0:T(8,128)(2,1)} %get-tuple-element.90.refs_7_.refs_3_), channel_id=1, source_target_pairs={{0,24},{8,16},{16,8},{24,0},{1,25},{9,17},{17,9},{25,1},{2,26},{10... | collective-permute-start | bytes 884744 | tf_op jit(solution)/shard_map/ppermute | solution.py:691
  11.7 18.5 %collective-permute-start.4 = (bf16[192,768]{1,0:T(8,128)(2,1)}, bf16[192,768]{1,0:T(8,128)(2,1)S(1)}, u32[]{:S(2)}, u32[]{:S(2)}) collective-permute-start(bf16[192,768]{1,0:T(8,128)(2,1)} %get-tuple-element.90.refs_7_.refs_3_), channel_id=1, source_target_pairs={{0,16},{8,24},{16,0},{24,8},{1,17},{9,25},{17,1},{25,9},{2,18},{10... | collective-permute-start | bytes 884744 | tf_op jit(solution)/shard_map/ppermute | solution.py:691
  12.2 18.0 %collective-permute-start.3 = (bf16[192,768]{1,0:T(8,128)(2,1)}, bf16[192,768]{1,0:T(8,128)(2,1)S(1)}, u32[]{:S(2)}, u32[]{:S(2)}) collective-permute-start(bf16[192,768]{1,0:T(8,128)(2,1)} %get-tuple-element.90.refs_7_.refs_3_), channel_id=1, source_target_pairs={{0,8},{8,0},{16,24},{24,16},{1,9},{9,1},{17,25},{25,17},{2,10},{10... | collective-permute-start | bytes 884744 | tf_op jit(solution)/shard_map/ppermute | solution.py:691
  12.8 13.4 %collective-permute-start.1 = (bf16[128,768]{1,0:T(8,128)(2,1)}, bf16[128,768]{1,0:T(8,128)(2,1)S(1)}, u32[]{:S(2)}, u32[]{:S(2)}) collective-permute-start(bf16[128,768]{1,0:T(8,128)(2,1)} %get-tuple-element.89.refs_3_.refs_1_.refs_4_.refs_0_), channel_id=1, source_target_pairs={{0,4},{1,5},{2,6},{3,7},{4,0},{5,1},{6,2},{7,3},{8,12},{9,13},{10,... | collective-permute-start | bytes 589832 | tf_op jit(solution)/shard_map/ppermute | solution.py:686
  14.8 15.4 %collective-permute-start = (bf16[128,768]{1,0:T(8,128)(2,1)}, bf16[128,768]{1,0:T(8,128)(2,1)S(1)}, u32[]{:S(2)}, u32[]{:S(2)}) collective-permute-start(bf16[128,768]{1,0:T(8,128)(2,1)} %get-tuple-element.89.refs_3_.refs_1_.refs_4_.refs_0_), channel_id=1, source_target_pairs={{0,2},{1,3},{2,0},{3,1},{4,6},{5,7},{6,4},{7,5},{8,10},{9,11},{10,... | collective-permute-start | bytes 589832 | tf_op jit(solution)/shard_map/ppermute | solution.py:686
  30.3 4.9 %copy-start.4 = (bf16[192,3072]{1,0:T(8,128)(2,1)S(1)}, bf16[192,3072]{1,0:T(8,128)(2,1)}, u32[]{:S(2)}) copy-start(bf16[192,3072]{1,0:T(8,128)(2,1)} %refs_3_.3) | copy-start | bytes 3538948
  30.3 4.8 %copy-start.5 = (bf16[1,128,768]{2,1,0:T(8,128)(2,1)S(1)}, bf16[1,128,768]{2,1,0:T(8,128)(2,1)}, u32[]{:S(2)}) copy-start(bf16[1,128,768]{2,1,0:T(8,128)(2,1)} %param.31) | copy-start | bytes 589828
  30.3 2.5 %collective-permute-start.6 = (bf16[576,768]{1,0:T(8,128)(2,1)S(1)}, bf16[576,768]{1,0:T(8,128)(2,1)S(1)}, u32[]{:S(2)}, u32[]{:S(2)}) collective-permute-start(bf16[576,768]{1,0:T(8,128)(2,1)S(1)} %pack_stack.1.refs_8_), channel_id=1, source_target_pairs={{0,1},{1,0},{2,3},{3,2},{4,5},{5,4},{6,7},{7,6},{8,9},{9,8},{10,11... | collective-permute-start | bytes 2654216 | tf_op jit(solution)/shard_map/ppermute | solution.py:683
  35.0 4.4 %copy-start.9 = (s32[8]{0:T(128)S(1)}, s32[8]{0:T(128)}, u32[]{:S(2)}) copy-start(s32[8]{0:T(128)} %refs_1_.9) | copy-start | bytes 100
  35.0 4.4 %collective-permute-start.7 = (bf16[512,384]{1,0:T(8,128)(2,1)S(1)}, bf16[512,384]{1,0:T(8,128)(2,1)S(1)}, u32[]{:S(2)}, u32[]{:S(2)}) collective-permute-start(bf16[512,384]{1,0:T(8,128)(2,1)S(1)} %get-tuple-element.94.refs_3_), channel_id=1, source_target_pairs={{0,1},{1,0},{2,3},{3,2},{4,5},{5,4},{6,7},{7,6},{8,9},{9,8},{10,11... | collective-permute-start | bytes 1179656 | tf_op jit(solution)/shard_map/ppermute | solution.py:683
  35.8 19.1 %collective-permute-start.11 = (bf16[224,768]{1,0:T(8,128)(2,1)S(1)}, bf16[224,768]{1,0:T(8,128)(2,1)S(1)}, u32[]{:S(2)}, u32[]{:S(2)}) collective-permute-start(bf16[224,768]{1,0:T(8,128)(2,1)S(1)} %get-tuple-element.100), channel_id=1, source_target_pairs={{0,8},{8,0},{16,24},{24,16},{1,9},{9,1},{17,25},{25,17},{2,10},{10... | collective-permute-start | bytes 1032200 | tf_op jit(solution)/shard_map/ppermute | solution.py:691
  37.4 17.5 %collective-permute-start.12 = (bf16[224,768]{1,0:T(8,128)(2,1)S(1)}, bf16[224,768]{1,0:T(8,128)(2,1)S(1)}, u32[]{:S(2)}, u32[]{:S(2)}) collective-permute-start(bf16[224,768]{1,0:T(8,128)(2,1)S(1)} %get-tuple-element.101), channel_id=1, source_target_pairs={{0,16},{8,24},{16,0},{24,8},{1,17},{9,25},{17,1},{25,9},{2,18},{10... | collective-permute-start | bytes 1032200 | tf_op jit(solution)/shard_map/ppermute | solution.py:691
  38.9 16.0 %collective-permute-start.13 = (bf16[224,768]{1,0:T(8,128)(2,1)S(1)}, bf16[224,768]{1,0:T(8,128)(2,1)S(1)}, u32[]{:S(2)}, u32[]{:S(2)}) collective-permute-start(bf16[224,768]{1,0:T(8,128)(2,1)S(1)} %get-tuple-element.102), channel_id=1, source_target_pairs={{0,24},{8,16},{16,8},{24,0},{1,25},{9,17},{17,9},{25,1},{2,26},{10... | collective-permute-start | bytes 1032200 | tf_op jit(solution)/shard_map/ppermute | solution.py:691
  43.1 4.6 %collective-permute-start.8 = (bf16[128,192]{1,0:T(8,128)(2,1)S(1)}, bf16[128,192]{1,0:T(8,128)(2,1)S(1)}, u32[]{:S(2)}, u32[]{:S(2)}) collective-permute-start(bf16[128,192]{1,0:T(8,128)(2,1)S(1)} %get-tuple-element.96), channel_id=1, source_target_pairs={{0,2},{1,3},{2,0},{3,1},{4,6},{5,7},{6,4},{7,5},{8,10},{9,11},{10,... | collective-permute-start | bytes 147464 | tf_op jit(solution)/shard_map/ppermute | solution.py:686
  43.2 6.8 %collective-permute-start.9 = (bf16[128,192]{1,0:T(8,128)(2,1)S(1)}, bf16[128,192]{1,0:T(8,128)(2,1)S(1)}, u32[]{:S(2)}, u32[]{:S(2)}) collective-permute-start(bf16[128,192]{1,0:T(8,128)(2,1)S(1)} %get-tuple-element.97), channel_id=1, source_target_pairs={{0,4},{1,5},{2,6},{3,7},{4,0},{5,1},{6,2},{7,3},{8,12},{9,13},{10,... | collective-permute-start | bytes 147464 | tf_op jit(solution)/shard_map/ppermute | solution.py:686
  47.7 6.1 %collective-permute-start.10 = (bf16[128,192]{1,0:T(8,128)(2,1)S(1)}, bf16[128,192]{1,0:T(8,128)(2,1)S(1)}, u32[]{:S(2)}, u32[]{:S(2)}) collective-permute-start(bf16[128,192]{1,0:T(8,128)(2,1)S(1)} %get-tuple-element.98), channel_id=1, source_target_pairs={{0,6},{1,7},{2,4},{3,5},{4,2},{5,3},{6,0},{7,1},{8,14},{9,15},{10,... | collective-permute-start | bytes 147464 | tf_op jit(solution)/shard_map/ppermute | solution.py:686
  54.8 12.7 %copy-start.7 = (bf16[768,768]{1,0:T(8,128)(2,1)S(1)}, bf16[768,768]{1,0:T(8,128)(2,1)}, u32[]{:S(2)}) copy-start(bf16[768,768]{1,0:T(8,128)(2,1)} %refs_2_.5) | copy-start | bytes 3538948
  54.8 12.7 %copy-start.8 = (bf16[768]{0:T(1024)(128)(2,1)S(1)}, bf16[768]{0:T(1024)(128)(2,1)}, u32[]{:S(2)}) copy-start(bf16[768]{0:T(1024)(128)(2,1)} %refs_1_.8) | copy-start | bytes 4612
  54.9 12.6 %collective-permute-start.14 = (bf16[288,768]{1,0:T(8,128)(2,1)S(1)}, bf16[288,768]{1,0:T(8,128)(2,1)S(1)}, u32[]{:S(2)}, u32[]{:S(2)}) collective-permute-start(bf16[288,768]{1,0:T(8,128)(2,1)S(1)} %expand_stack.1), channel_id=1, source_target_pairs={{0,1},{1,0},{2,3},{3,2},{4,5},{5,4},{6,7},{7,6},{8,9},{9,8},{10,11... | collective-permute-start | bytes 1327112 | tf_op jit(solution)/shard_map/ppermute | solution.py:683
  55.0 8.7 %collective-permute-start.17 = (bf16[128,768]{1,0:T(8,128)(2,1)S(1)}, bf16[128,768]{1,0:T(8,128)(2,1)S(1)}, u32[]{:S(2)}, u32[]{:S(2)}) collective-permute-start(bf16[128,768]{1,0:T(8,128)(2,1)S(1)} %get-tuple-element.103.refs_3_.refs_6_), channel_id=1, source_target_pairs={{0,24},{8,16},{16,8},{24,0},{1,25},{9,17},{17,9},{25,1},{2,26},{10... | collective-permute-start | bytes 589832 | tf_op jit(solution)/shard_map/ppermute | solution.py:691
  57.5 9.9 %collective-permute-start.16 = (bf16[128,768]{1,0:T(8,128)(2,1)S(1)}, bf16[128,768]{1,0:T(8,128)(2,1)S(1)}, u32[]{:S(2)}, u32[]{:S(2)}) collective-permute-start(bf16[128,768]{1,0:T(8,128)(2,1)S(1)} %get-tuple-element.103.refs_3_.refs_6_), channel_id=1, source_target_pairs={{0,16},{8,24},{16,0},{24,8},{1,17},{9,25},{17,1},{25,9},{2,18},{10... | collective-permute-start | bytes 589832 | tf_op jit(solution)/shard_map/ppermute | solution.py:691
  58.0 9.5 %collective-permute-start.15 = (bf16[128,768]{1,0:T(8,128)(2,1)S(1)}, bf16[128,768]{1,0:T(8,128)(2,1)S(1)}, u32[]{:S(2)}, u32[]{:S(2)}) collective-permute-start(bf16[128,768]{1,0:T(8,128)(2,1)S(1)} %get-tuple-element.103.refs_3_.refs_6_), channel_id=1, source_target_pairs={{0,8},{8,0},{16,24},{24,16},{1,9},{9,1},{17,25},{25,17},{2,10},{10... | collective-permute-start | bytes 589832 | tf_op jit(solution)/shard_map/ppermute | solution.py:691
  73.1 2.9 %collective-permute-start.21 = (bf16[4,384,384]{2,1,0:T(8,128)(2,1)S(1)}, bf16[4,384,384]{2,1,0:T(8,128)(2,1)S(1)}, u32[]{:S(2)}, u32[]{:S(2)}) collective-permute-start(bf16[4,384,384]{2,1,0:T(8,128)(2,1)S(1)} %get-tuple-element.109), channel_id=1, source_target_pairs={{0,1},{1,0},{2,3},{3,2},{4,5},{5,4},{6,7},{7,6},{8,9},{9,8},{10,11... | collective-permute-start | bytes 3538952 | tf_op jit(solution)/shard_map/ppermute | solution.py:683
  76.9 20.5 %collective-permute-start.22 = (bf16[2,384,384]{2,1,0:T(8,128)(2,1)S(1)}, bf16[2,384,384]{2,1,0:T(8,128)(2,1)S(1)}, u32[]{:S(2)}, u32[]{:S(2)}) collective-permute-start(bf16[2,384,384]{2,1,0:T(8,128)(2,1)S(1)} %get-tuple-element.111.refs_9_), channel_id=1, source_target_pairs={{0,2},{1,3},{2,0},{3,1},{4,6},{5,7},{6,4},{7,5},{8,10},{9,11},{10,... | collective-permute-start | bytes 1769480 | tf_op jit(solution)/shard_map/ppermute | solution.py:686
  77.0 7.8 %collective-permute-start.23 = (bf16[128,768]{1,0:T(8,128)(2,1)S(1)}, bf16[128,768]{1,0:T(8,128)(2,1)S(1)}, u32[]{:S(2)}, u32[]{:S(2)}) collective-permute-start(bf16[128,768]{1,0:T(8,128)(2,1)S(1)} %get-tuple-element.113), channel_id=1, source_target_pairs={{0,8},{8,0},{16,24},{24,16},{1,9},{9,1},{17,25},{25,17},{2,10},{10... | collective-permute-start | bytes 589832 | tf_op jit(solution)/shard_map/ppermute | solution.py:691
  78.5 10.9 %collective-permute-start.24 = (bf16[128,768]{1,0:T(8,128)(2,1)S(1)}, bf16[128,768]{1,0:T(8,128)(2,1)S(1)}, u32[]{:S(2)}, u32[]{:S(2)}) collective-permute-start(bf16[128,768]{1,0:T(8,128)(2,1)S(1)} %get-tuple-element.114), channel_id=1, source_target_pairs={{0,16},{8,24},{16,0},{24,8},{1,17},{9,25},{17,1},{25,9},{2,18},{10... | collective-permute-start | bytes 589832 | tf_op jit(solution)/shard_map/ppermute | solution.py:691
  79.2 10.2 %collective-permute-start.25 = (bf16[128,768]{1,0:T(8,128)(2,1)S(1)}, bf16[128,768]{1,0:T(8,128)(2,1)S(1)}, u32[]{:S(2)}, u32[]{:S(2)}) collective-permute-start(bf16[128,768]{1,0:T(8,128)(2,1)S(1)} %get-tuple-element.115), channel_id=1, source_target_pairs={{0,24},{8,16},{16,8},{24,0},{1,25},{9,17},{17,9},{25,1},{2,26},{10... | collective-permute-start | bytes 589832 | tf_op jit(solution)/shard_map/ppermute | solution.py:691
  90.8 6.6 %collective-permute-start.26 = (bf16[128,192]{1,0:T(8,128)(2,1)S(1)}, bf16[128,192]{1,0:T(8,128)(2,1)S(1)}, u32[]{:S(2)}, u32[]{:S(2)}) collective-permute-start(bf16[128,192]{1,0:T(8,128)(2,1)S(1)} %get-tuple-element.116), channel_id=1, source_target_pairs={{0,6},{1,7},{2,4},{3,5},{4,2},{5,3},{6,0},{7,1},{8,14},{9,15},{10,... | collective-permute-start | bytes 147464 | tf_op jit(solution)/shard_map/ppermute | solution.py:686
  93.2 4.7 %collective-permute-start.28 = (bf16[128,192]{1,0:T(8,128)(2,1)S(1)}, bf16[128,192]{1,0:T(8,128)(2,1)S(1)}, u32[]{:S(2)}, u32[]{:S(2)}) collective-permute-start(bf16[128,192]{1,0:T(8,128)(2,1)S(1)} %get-tuple-element.123), channel_id=1, source_target_pairs={{0,2},{1,3},{2,0},{3,1},{4,6},{5,7},{6,4},{7,5},{8,10},{9,11},{10,... | collective-permute-start | bytes 147464 | tf_op jit(solution)/shard_map/ppermute | solution.py:686
  93.9 5.2 %collective-permute-start.29 = (bf16[128,192]{1,0:T(8,128)(2,1)S(1)}, bf16[128,192]{1,0:T(8,128)(2,1)S(1)}, u32[]{:S(2)}, u32[]{:S(2)}) collective-permute-start(bf16[128,192]{1,0:T(8,128)(2,1)S(1)} %get-tuple-element.124), channel_id=1, source_target_pairs={{0,4},{1,5},{2,6},{3,7},{4,0},{5,1},{6,2},{7,3},{8,12},{9,13},{10,... | collective-permute-start | bytes 147464 | tf_op jit(solution)/shard_map/ppermute | solution.py:686
  104.1 1.8 collective-permute-start.30
  104.2 8.2 %collective-permute-start.32 = (bf16[4,192,384]{2,1,0:T(8,128)(2,1)S(1)}, bf16[4,192,384]{2,1,0:T(8,128)(2,1)S(1)}, u32[]{:S(2)}, u32[]{:S(2)}) collective-permute-start(bf16[4,192,384]{2,1,0:T(8,128)(2,1)S(1)} %get-tuple-element.126.refs_12_), channel_id=1, source_target_pairs={{0,1},{1,0},{2,3},{3,2},{4,5},{5,4},{6,7},{7,6},{8,9},{9,8},{10,11... | collective-permute-start | bytes 1769480 | tf_op jit(solution)/shard_map/ppermute | solution.py:683
  109.2 17.9 %collective-permute-start.31 = (bf16[4,96,768]{2,1,0:T(8,128)(2,1)S(1)}, bf16[4,96,768]{2,1,0:T(8,128)(2,1)S(1)}, u32[]{:S(2)}, u32[]{:S(2)}) collective-permute-start(bf16[4,96,768]{2,1,0:T(8,128)(2,1)S(1)} %get-tuple-element.137), channel_id=1, source_target_pairs={{0,1},{1,0},{2,3},{3,2},{4,5},{5,4},{6,7},{7,6},{8,9},{9,8},{10,11... | collective-permute-start | bytes 1769480 | tf_op jit(solution)/shard_map/ppermute | solution.py:683
  109.4 17.7 %collective-permute-start.33 = (bf16[2,128,768]{2,1,0:T(8,128)(2,1)S(1)}, bf16[2,128,768]{2,1,0:T(8,128)(2,1)S(1)}, u32[]{:S(2)}, u32[]{:S(2)}) collective-permute-start(bf16[2,128,768]{2,1,0:T(8,128)(2,1)S(1)} %get-tuple-element.140), channel_id=1, source_target_pairs={{0,2},{1,3},{2,0},{3,1},{4,6},{5,7},{6,4},{7,5},{8,10},{9,11},{10,... | collective-permute-start | bytes 1179656 | tf_op jit(solution)/shard_map/ppermute | solution.py:686
  110.7 15.2 %collective-permute-start.27 = (bf16[384,384]{1,0:T(8,128)(2,1)S(1)}, bf16[384,384]{1,0:T(8,128)(2,1)S(1)}, u32[]{:S(2)}, u32[]{:S(2)}) collective-permute-start(bf16[384,384]{1,0:T(8,128)(2,1)S(1)} %get-tuple-element.118.refs_11_), channel_id=1, source_target_pairs={{0,4},{1,5},{2,6},{3,7},{4,0},{5,1},{6,2},{7,3},{8,12},{9,13},{10,... | collective-permute-start | bytes 884744 | tf_op jit(solution)/shard_map/ppermute | solution.py:686
  128.2 9.5 %collective-permute-start.38 = (bf16[192,384]{1,0:T(8,128)(2,1)S(1)}, bf16[192,384]{1,0:T(8,128)(2,1)S(1)}, u32[]{:S(2)}, u32[]{:S(2)}) collective-permute-start(bf16[192,384]{1,0:T(8,128)(2,1)S(1)} %get-tuple-element.145.refs_1_), channel_id=1, source_target_pairs={{0,4},{1,5},{2,6},{3,7},{4,0},{5,1},{6,2},{7,3},{8,12},{9,13},{10,... | collective-permute-start | bytes 442376 | tf_op jit(solution)/shard_map/ppermute | solution.py:686
  130.5 19.2 %collective-permute-start.34 = (bf16[224,768]{1,0:T(8,128)(2,1)S(1)}, bf16[224,768]{1,0:T(8,128)(2,1)S(1)}, u32[]{:S(2)}, u32[]{:S(2)}) collective-permute-start(bf16[224,768]{1,0:T(8,128)(2,1)S(1)} %get-tuple-element.142), channel_id=1, source_target_pairs={{0,8},{8,0},{16,24},{24,16},{1,9},{9,1},{17,25},{25,17},{2,10},{10... | collective-permute-start | bytes 1032200 | tf_op jit(solution)/shard_map/ppermute | solution.py:691
  131.0 18.7 %collective-permute-start.35 = (bf16[224,768]{1,0:T(8,128)(2,1)S(1)}, bf16[224,768]{1,0:T(8,128)(2,1)S(1)}, u32[]{:S(2)}, u32[]{:S(2)}) collective-permute-start(bf16[224,768]{1,0:T(8,128)(2,1)S(1)} %get-tuple-element.143), channel_id=1, source_target_pairs={{0,16},{8,24},{16,0},{24,8},{1,17},{9,25},{17,1},{25,9},{2,18},{10... | collective-permute-start | bytes 1032200 | tf_op jit(solution)/shard_map/ppermute | solution.py:691
  132.4 17.3 %collective-permute-start.36 = (bf16[224,768]{1,0:T(8,128)(2,1)S(1)}, bf16[224,768]{1,0:T(8,128)(2,1)S(1)}, u32[]{:S(2)}, u32[]{:S(2)}) collective-permute-start(bf16[224,768]{1,0:T(8,128)(2,1)S(1)} %get-tuple-element.144), channel_id=1, source_target_pairs={{0,24},{8,16},{16,8},{24,0},{1,25},{9,17},{17,9},{25,1},{2,26},{10... | collective-permute-start | bytes 1032200 | tf_op jit(solution)/shard_map/ppermute | solution.py:691
  134.0 6.4 %collective-permute-start.37 = (bf16[192,384]{1,0:T(8,128)(2,1)S(1)}, bf16[192,384]{1,0:T(8,128)(2,1)S(1)}, u32[]{:S(2)}, u32[]{:S(2)}) collective-permute-start(bf16[192,384]{1,0:T(8,128)(2,1)S(1)} %get-tuple-element.145.refs_1_), channel_id=1, source_target_pairs={{0,2},{1,3},{2,0},{3,1},{4,6},{5,7},{6,4},{7,5},{8,10},{9,11},{10,... | collective-permute-start | bytes 442376 | tf_op jit(solution)/shard_map/ppermute | solution.py:686
  137.8 11.0 %collective-permute-start.40 = (bf16[128,768]{1,0:T(8,128)(2,1)S(1)}, bf16[128,768]{1,0:T(8,128)(2,1)S(1)}, u32[]{:S(2)}, u32[]{:S(2)}) collective-permute-start(bf16[128,768]{1,0:T(8,128)(2,1)S(1)} %get-tuple-element.146), channel_id=1, source_target_pairs={{0,4},{1,5},{2,6},{3,7},{4,0},{5,1},{6,2},{7,3},{8,12},{9,13},{10,... | collective-permute-start | bytes 589832 | tf_op jit(solution)/shard_map/ppermute | solution.py:686
  140.4 9.3 %collective-permute-start.39 = (bf16[192,384]{1,0:T(8,128)(2,1)S(1)}, bf16[192,384]{1,0:T(8,128)(2,1)S(1)}, u32[]{:S(2)}, u32[]{:S(2)}) collective-permute-start(bf16[192,384]{1,0:T(8,128)(2,1)S(1)} %collective-permute-done.38.refs_3_), channel_id=1, source_target_pairs={{0,2},{1,3},{2,0},{3,1},{4,6},{5,7},{6,4},{7,5},{8,10},{9,11},{10,... | collective-permute-start | bytes 442376 | tf_op jit(solution)/shard_map/ppermute | solution.py:686
  150.6 20.5 %collective-permute-start.42 = (bf16[288,768]{1,0:T(8,128)(2,1)S(1)}, bf16[288,768]{1,0:T(8,128)(2,1)S(1)}, u32[]{:S(2)}, u32[]{:S(2)}) collective-permute-start(bf16[288,768]{1,0:T(8,128)(2,1)S(1)} %shares.1.refs_6_.refs_1_), channel_id=1, source_target_pairs={{0,4},{1,5},{2,6},{3,7},{4,0},{5,1},{6,2},{7,3},{8,12},{9,13},{10,... | collective-permute-start | bytes 1327112 | tf_op jit(solution)/shard_map/ppermute | solution.py:686
  150.6 32.5 %collective-permute-start.41 = (bf16[288,768]{1,0:T(8,128)(2,1)S(1)}, bf16[288,768]{1,0:T(8,128)(2,1)S(1)}, u32[]{:S(2)}, u32[]{:S(2)}) collective-permute-start(bf16[288,768]{1,0:T(8,128)(2,1)S(1)} %shares.1.refs_6_.refs_1_), channel_id=1, source_target_pairs={{0,2},{1,3},{2,0},{3,1},{4,6},{5,7},{6,4},{7,5},{8,10},{9,11},{10,... | collective-permute-start | bytes 1327112 | tf_op jit(solution)/shard_map/ppermute | solution.py:686
  171.1 12.5 %collective-permute-start.43 = (bf16[288,768]{1,0:T(8,128)(2,1)S(1)}, bf16[288,768]{1,0:T(8,128)(2,1)S(1)}, u32[]{:S(2)}, u32[]{:S(2)}) collective-permute-start(bf16[288,768]{1,0:T(8,128)(2,1)S(1)} %collective-permute-done.42.refs_3_), channel_id=1, source_target_pairs={{0,2},{1,3},{2,0},{3,1},{4,6},{5,7},{6,4},{7,5},{8,10},{9,11},{10,... | collective-permute-start | bytes 1327112 | tf_op jit(solution)/shard_map/ppermute | solution.py:686
  171.1 7.8 %collective-permute-start.18 = (bf16[128,768]{1,0:T(8,128)(2,1)S(1)}, bf16[128,768]{1,0:T(8,128)(2,1)S(1)}, u32[]{:S(2)}, u32[]{:S(2)}) collective-permute-start(bf16[128,768]{1,0:T(8,128)(2,1)S(1)} %get-tuple-element.105), channel_id=1, source_target_pairs={{0,8},{8,0},{16,24},{24,16},{1,9},{9,1},{17,25},{25,17},{2,10},{10... | collective-permute-start | bytes 589832 | tf_op jit(solution)/shard_map/ppermute | solution.py:691
  171.8 10.7 %collective-permute-start.19 = (bf16[128,768]{1,0:T(8,128)(2,1)S(1)}, bf16[128,768]{1,0:T(8,128)(2,1)S(1)}, u32[]{:S(2)}, u32[]{:S(2)}) collective-permute-start(bf16[128,768]{1,0:T(8,128)(2,1)S(1)} %get-tuple-element.106), channel_id=1, source_target_pairs={{0,16},{8,24},{16,0},{24,8},{1,17},{9,25},{17,1},{25,9},{2,18},{10... | collective-permute-start | bytes 589832 | tf_op jit(solution)/shard_map/ppermute | solution.py:691
  173.2 9.4 %collective-permute-start.20 = (bf16[128,768]{1,0:T(8,128)(2,1)S(1)}, bf16[128,768]{1,0:T(8,128)(2,1)S(1)}, u32[]{:S(2)}, u32[]{:S(2)}) collective-permute-start(bf16[128,768]{1,0:T(8,128)(2,1)S(1)} %get-tuple-element.107), channel_id=1, source_target_pairs={{0,24},{8,16},{16,8},{24,0},{1,25},{9,17},{17,9},{25,1},{2,26},{10... | collective-permute-start | bytes 589832 | tf_op jit(solution)/shard_map/ppermute | solution.py:691
  178.8 4.2 %collective-permute-start.48 = (bf16[192,384]{1,0:T(8,128)(2,1)S(1)}, bf16[192,384]{1,0:T(8,128)(2,1)S(1)}, u32[]{:S(2)}, u32[]{:S(2)}) collective-permute-start(bf16[192,384]{1,0:T(8,128)(2,1)S(1)} %get-tuple-element.145.refs_1_), channel_id=1, source_target_pairs={{0,1},{1,0},{2,3},{3,2},{4,5},{5,4},{6,7},{7,6},{8,9},{9,8},{10,11... | collective-permute-start | bytes 442376 | tf_op jit(solution)/shard_map/ppermute | solution.py:683
  182.5 1.4 collective-permute-start.50
  182.5 8.4 %collective-permute-start.44 = (bf16[288,768]{1,0:T(8,128)(2,1)S(1)}, bf16[288,768]{1,0:T(8,128)(2,1)S(1)}, u32[]{:S(2)}, u32[]{:S(2)}) collective-permute-start(bf16[288,768]{1,0:T(8,128)(2,1)S(1)} %shares.1.refs_6_.refs_1_), channel_id=1, source_target_pairs={{0,1},{1,0},{2,3},{3,2},{4,5},{5,4},{6,7},{7,6},{8,9},{9,8},{10,11... | collective-permute-start | bytes 1327112 | tf_op jit(solution)/shard_map/ppermute | solution.py:683
  183.1 7.9 %collective-permute-start.46 = (bf16[288,768]{1,0:T(8,128)(2,1)S(1)}, bf16[288,768]{1,0:T(8,128)(2,1)S(1)}, u32[]{:S(2)}, u32[]{:S(2)}) collective-permute-start(bf16[288,768]{1,0:T(8,128)(2,1)S(1)} %collective-permute-done.42.refs_3_), channel_id=1, source_target_pairs={{0,1},{1,0},{2,3},{3,2},{4,5},{5,4},{6,7},{7,6},{8,9},{9,8},{10,11... | collective-permute-start | bytes 1327112 | tf_op jit(solution)/shard_map/ppermute | solution.py:683
  183.1 7.9 %collective-permute-start.45 = (bf16[288,768]{1,0:T(8,128)(2,1)S(1)}, bf16[288,768]{1,0:T(8,128)(2,1)S(1)}, u32[]{:S(2)}, u32[]{:S(2)}) collective-permute-start(bf16[288,768]{1,0:T(8,128)(2,1)S(1)} %collective-permute-done.41.refs_2_), channel_id=1, source_target_pairs={{0,1},{1,0},{2,3},{3,2},{4,5},{5,4},{6,7},{7,6},{8,9},{9,8},{10,11... | collective-permute-start | bytes 1327112 | tf_op jit(solution)/shard_map/ppermute | solution.py:683
  183.6 7.4 %collective-permute-start.47 = (bf16[288,768]{1,0:T(8,128)(2,1)S(1)}, bf16[288,768]{1,0:T(8,128)(2,1)S(1)}, u32[]{:S(2)}, u32[]{:S(2)}) collective-permute-start(bf16[288,768]{1,0:T(8,128)(2,1)S(1)} %collective-permute-done.43.refs_4_), channel_id=1, source_target_pairs={{0,1},{1,0},{2,3},{3,2},{4,5},{5,4},{6,7},{7,6},{8,9},{9,8},{10,11... | collective-permute-start | bytes 1327112 | tf_op jit(solution)/shard_map/ppermute | solution.py:683
  183.9 2.7 %collective-permute-start.49 = (bf16[192,384]{1,0:T(8,128)(2,1)S(1)}, bf16[192,384]{1,0:T(8,128)(2,1)S(1)}, u32[]{:S(2)}, u32[]{:S(2)}) collective-permute-start(bf16[192,384]{1,0:T(8,128)(2,1)S(1)} %collective-permute-done.37.refs_5_.refs_2_), channel_id=1, source_target_pairs={{0,1},{1,0},{2,3},{3,2},{4,5},{5,4},{6,7},{7,6},{8,9},{9,8},{10,11... | collective-permute-start | bytes 442376 | tf_op jit(solution)/shard_map/ppermute | solution.py:683
  186.6 2.2 %collective-permute-start.51 = (bf16[192,384]{1,0:T(8,128)(2,1)S(1)}, bf16[192,384]{1,0:T(8,128)(2,1)S(1)}, u32[]{:S(2)}, u32[]{:S(2)}) collective-permute-start(bf16[192,384]{1,0:T(8,128)(2,1)S(1)} %collective-permute-done.39.refs_6_.refs_4_), channel_id=1, source_target_pairs={{0,1},{1,0},{2,3},{3,2},{4,5},{5,4},{6,7},{7,6},{8,9},{9,8},{10,11... | collective-permute-start | bytes 442376 | tf_op jit(solution)/shard_map/ppermute | solution.py:683

commit v4 on v3

--- a/solution.py
+++ b/solution.py
@@ -786,7 +786,8 @@
             space=pltpu.HBM,
             grant=60 * 1024 * 1024,
         )
-        token_parts = [own_tokens] + [chip_swap(own_tokens, k) for k in others]
+        token_two = chip_swap(own_tokens, 2)
+        token_parts = [own_tokens, chip_swap(own_tokens, 1), token_two, chip_swap(token_two, 1)]
         packed_near = [seq_swap(packed, j) for j in others]
 
         def stack_kernel(*refs):
@@ -1185,7 +1186,7 @@
 
         def normed_back_kernel(dq_ref, own_ref, far_ref, w_ref, *refs):
             toks = refs[:parts]
-            keep_ref, send_ref, mixed_ref, sums_ref, bias_ref = refs[parts:]
+            keep_ref, *send_refs, mixed_ref, sums_ref, bias_ref = refs[parts:]
             mixed_ref[:, 0:hw] = dq_ref[...].T.astype(bf)
             mixed_ref[:, hw:] = (own_ref[...] + far_ref[...].astype(f32)).astype(bf)
             shift_sum = jnp.zeros((1, width), f32)
@@ -1193,7 +1194,7 @@
             for k in range(parts):
                 grad = mm_nt(mixed_ref[k * rows : (k + 1) * rows, :], w_ref[...])
                 if k % 2:
-                    send_ref[k // 2] = grad.astype(bf)
+                    send_refs[k // 2][...] = grad.astype(bf)
                 else:
                     keep_ref[k // 2] = grad
                 xhat, _ = norm_stats(toks[k][...].astype(f32))
@@ -1208,7 +1209,8 @@
             "normed_back",
             [
                 shape_of((parts // 2, rows, width), f32),
-                shape_of((parts // 2, rows, width), bf),
+                shape_of((rows, width), bf),
+                shape_of((rows, width), bf),
                 shape_of((total, 3 * hw), bf),
                 shape_of((8, width), f32),
                 shape_of((8, 3 * hw), f32),
@@ -1216,14 +1218,14 @@
             [flat_dq, dkv_own, dkv_far, w_heads_full] + token_parts,
             flops=2 * total * width * 3 * hw,
         )
-        gt_keep, gt_send, grad_mixed, first_sums, mixed_sums = nb_out
-        gt_far = chip_swap(gt_send, 1)
+        gt_keep, *gt_send, grad_mixed, first_sums, mixed_sums = nb_out
+        gt_far = [chip_swap(member, 1) for member in gt_send]
 
 
         def input_weights_kernel(
             info_ref, normed_ref, mixed_ref, first_ref, bias_ref, late_ref, row_ref, *refs
         ):
-            keep_ref, send_ref, grad_scr, small_scr = refs
+            keep_ref, *send_refs, grad_scr, small_scr = refs
             grad_scr[...] = mm_tn(normed_ref[...], mixed_ref[...])
             core_id, chip_id, seq = info_ref[2], info_ref[1], info_ref[0]
             small_scr[...] = jnp.zeros_like(small_scr)
@@ -1235,20 +1237,22 @@
             small_scr[chip_id, 3:4, :] = bias_ref[0:1, 2 * hw : 3 * hw]
             for j in range(ff // own_width):
                 small_scr[seq, 8 + j : 9 + j, :] = row_ref[:, j * own_width : (j + 1) * own_width]
-            for flip, out_ref in ((0, keep_ref), (1, send_ref)):
+            for flip in range(2):
                 half = jnp.bitwise_xor(core_id, flip)
                 for j in range(seq_parts):
+                    out_ref = send_refs[j] if flip else keep_ref.at[j]
                     start = pl.multiple_of(j * own_width + half * half_own, 16)
-                    out_ref[j, :, 0 : 3 * hw] = grad_scr[pl.ds(start, half_own), :].astype(bf)
-                    out_ref[j, 0:small_rows, 3 * hw :] = small_scr[j].astype(bf)
-                    out_ref[j, small_rows:, 3 * hw :] = jnp.zeros(
+                    out_ref[:, 0 : 3 * hw] = grad_scr[pl.ds(start, half_own), :].astype(bf)
+                    out_ref[0:small_rows, 3 * hw :] = small_scr[j].astype(bf)
+                    out_ref[small_rows:, 3 * hw :] = jnp.zeros(
                         (half_own - small_rows, side), bf
                     )
 
-        in_keep, in_send = local_call(
+        in_keep, *in_send = local_call(
             input_weights_kernel,
             "input_weights",
-            [shape_of((seq_parts, half_own, width), bf)] * 2,
+            [shape_of((seq_parts, half_own, width), bf)]
+            + [shape_of((half_own, width), bf)] * seq_parts,
             [info, normed, grad_mixed, first_sums, mixed_sums, late_sums, grad_expand_row],
             scalars=1,
             scratch=[
@@ -1257,7 +1261,7 @@
             ],
             flops=2 * total * width * 3 * hw,
         )
-        in_far = core_swap(in_send)
+        in_far = [core_swap(member) for member in in_send]
 
         fold = own_width // 2
         rider = -(-sub // 32) * 16
@@ -1271,17 +1275,37 @@
             across = value.shape[1] // 2
             return jnp.concatenate([value[:, 0:across], value[:, across:]], axis=0)
 
+        res_parts = [results[0]] + [seq_swap(results[j], j) for j in others]
+
+        def result_kernel(mid_ref, vec_ref, *refs):
+            result = mid_ref[...] + vec_ref[7:8]
+            for j in range(seq_parts):
+                result = result + refs[j][...].astype(f32)
+            refs[seq_parts][0] = result.astype(bf)
+            refs[seq_parts + 1][...] = jnp.zeros((8, 128), f32)
+
+        block_out, block_done = local_call(
+            result_kernel,
+            "result",
+            [shape_of((1, rows, width), bf), shape_of((8, 128), f32)],
+            [middle, vectors] + res_parts,
+            after=[in_keep],
+        )
+
         def dp_pack_kernel(
-            info_ref, own_ref, far_two_ref, keep_ref, far_ref, ok_ref, of_ref, gk_ref, gf_ref, *refs
+            info_ref, own_ref, far_two_ref, keep_ref, ok_ref, of_ref, *refs
         ):
-            con_ref, gown_ref, gsend_ref, scr = refs[seq_parts:]
+            fars, refs = refs[:seq_parts], refs[seq_parts:]
+            con_ref, scr, far_scr = refs[seq_parts:]
+            for j in range(seq_parts):
+                far_scr[j] = fars[j][...]
             whole = own_ref[...] + far_two_ref[...].astype(f32)
             con_ref[...] = whole[0 : ff // parts].astype(bf)
             scr[...] = whole[ff // parts :]
             for j in range(seq_parts):
                 at = jnp.bitwise_xor(info_ref[0], j)
                 refs[j][0:half_own, :] = (
-                    keep_ref[at].astype(f32) + far_ref[at].astype(f32)
+                    keep_ref[at].astype(f32) + far_scr[at].astype(f32)
                 ).astype(bf)
                 refs[j][at_outs, :] = fold_in(ok_ref[at].astype(f32) + of_ref[at].astype(f32)).astype(
                     bf
@@ -1291,29 +1315,60 @@
                     [piece, jnp.zeros((rider - sub // 2, width), f32)], axis=0
                 )
                 refs[j][half_own + fold :, :] = piece.astype(bf)
-            gown_ref[...] = gk_ref[0] + gf_ref[0].astype(f32)
-            gsend_ref[...] = (gk_ref[1] + gf_ref[1].astype(f32)).astype(bf)
-
         dp_out = local_call(
             dp_pack_kernel,
             "owners",
             [shape_of((half_own + fold + rider, width), bf)] * seq_parts
-            + [
-                shape_of((ff // parts, half_width), bf),
-                shape_of((rows, width), f32),
-                shape_of((rows, width), bf),
+            + [shape_of((ff // parts, half_width), bf)],
+            [info, rs_own_two, rs_far_two, in_keep, out_keep, out_far] + in_far,
+            scalars=1,
+            scratch=[
+                pltpu.VMEM((own_width, half_ff), f32),
+                pltpu.VMEM((seq_parts, half_own, width), bf),
             ],
-            [info, rs_own_two, rs_far_two, in_keep, in_far, out_keep, out_far, gt_keep, gt_far],
-            scalars=1,
-            scratch=[pltpu.VMEM((own_width, half_ff), f32)],
+            after=[block_done],
         )
         dp_parts = [dp_out[0]] + [seq_swap(dp_out[j], j) for j in others]
-        con_one, gt_own, gt_send_two = dp_out[seq_parts:]
+        con_one = dp_out[seq_parts]
+
+        def half_sum_kernel(keep_ref, first_ref, second_ref, own_ref, send_ref):
+            own_ref[...] = keep_ref[0] + first_ref[...].astype(f32)
+            send_ref[...] = (keep_ref[1] + second_ref[...].astype(f32)).astype(bf)
+
+        gt_own, gt_send_two = local_call(
+            half_sum_kernel,
+            "tokens_halves",
+            [shape_of((rows, width), f32), shape_of((rows, width), bf)],
+            [gt_keep] + gt_far,
+            after=[con_one],
+        )
         con_two = chip_swap(con_one, 2)
         gt_far_two = chip_swap(gt_send_two, 2)
 
         con_one_far = chip_swap(con_one, 1)
         con_two_far = chip_swap(con_two, 1)
+
+        con_parts = [con_one, con_one_far, con_two, con_two_far]
+        con_far = [core_swap(member) for member in con_parts]
+
+        def contract_kernel(info_ref, *refs):
+            con_ref, done_ref = refs[2 * parts :]
+            done_ref[...] = jnp.zeros_like(done_ref)
+            for flip in range(2):
+                lanes = aligned(jnp.bitwise_xor(info_ref[2], flip), half_width)
+                for k in range(parts):
+                    at = jnp.bitwise_xor(info_ref[1], k)
+                    con_ref[aligned(at, ff // parts), lanes] = refs[flip * parts + k][...].astype(
+                        f32
+                    )
+
+        grad_contract, contract_done = local_call(
+            contract_kernel,
+            "contract_final",
+            [shape_of((ff, width), f32), shape_of((8, 128), f32)],
+            [info] + con_parts + con_far,
+            scalars=1,
+        )
 
         def dp_sum_kernel(info_ref, *refs):
             owned = refs[:seq_parts]
@@ -1339,58 +1394,32 @@
         )
         last_two = chip_swap(last_one, 2)
         last_one_far = chip_swap(last_one, 1)
-        last_two_far = chip_swap(last_two, 1)
-        last_parts = [last_one, last_one_far, last_two, last_two_far]
-        last_far = [core_swap(member) for member in last_parts]
-        con_parts = [con_one, con_one_far, con_two, con_two_far]
-        con_far = [core_swap(member) for member in con_parts]
-
-        def contract_kernel(info_ref, *refs):
-            con_ref, done_ref = refs[2 * parts :]
+        def tokens_kernel(tok_ref, vec_ref, gmid_ref, own_ref, far_ref, out_ref, done_ref):
             done_ref[...] = jnp.zeros_like(done_ref)
-            for flip in range(2):
-                lanes = aligned(jnp.bitwise_xor(info_ref[2], flip), half_width)
-                for k in range(parts):
-                    at = jnp.bitwise_xor(info_ref[1], k)
-                    con_ref[aligned(at, ff // parts), lanes] = refs[flip * parts + k][...].astype(
-                        f32
-                    )
-
-        grad_contract, contract_done = local_call(
-            contract_kernel,
-            "contract_final",
-            [shape_of((ff, width), f32), shape_of((8, 128), f32)],
-            [info] + con_parts + con_far,
-            scalars=1,
-        )
-
-        res_parts = [results[0]] + [seq_swap(results[j], j) for j in others]
-
-        def result_kernel(mid_ref, vec_ref, *refs):
-            result = mid_ref[...] + vec_ref[7:8]
-            for j in range(seq_parts):
-                result = result + refs[j][...].astype(f32)
-            refs[seq_parts][0] = result.astype(bf)
-
-        (block_out,) = local_call(
-            result_kernel,
-            "result",
-            [shape_of((1, rows, width), bf)],
-            [middle, vectors] + res_parts,
-            after=[last_one],
-        )
-
-        def tokens_kernel(tok_ref, vec_ref, gmid_ref, own_ref, far_ref, out_ref):
             grad = own_ref[...] + far_ref[...].astype(f32)
             xhat, spread = norm_stats(tok_ref[...].astype(f32))
             out_ref[0] = gmid_ref[...] + norm_back(grad, vec_ref[0:1], xhat, spread)
 
-        (grad_tokens,) = local_call(
+        grad_tokens, tokens_done = local_call(
             tokens_kernel,
             "tokens_back",
-            [shape_of((1, rows, width), f32)],
+            [shape_of((1, rows, width), f32), shape_of((8, 128), f32)],
             [own_tokens, vectors, grad_middle, gt_own, gt_far_two],
         )
+
+        def pass_kernel(in_ref, out_ref):
+            out_ref[...] = in_ref[...]
+
+        (last_two_on,) = local_call(
+            pass_kernel,
+            "pass_on",
+            [shape_of((half_own + 2 * fold, width), bf)],
+            [last_two],
+            after=[contract_done, tokens_done, last_one_far],
+        )
+        last_two_far = chip_swap(last_two_on, 1)
+        last_parts = [last_one, last_one_far, last_two, last_two_far]
+        last_far = [core_swap(member) for member in last_parts]
 
         def last_kernel(info_ref, *refs):
             gin_ref, gout_ref, exp_ref = refs[2 * parts : 2 * parts + 3]
@@ -1434,7 +1463,6 @@
             [info] + last_parts + last_far,
             scalars=1,
             scratch=[pltpu.VMEM((parts, own_width, 3 * hw), f32)],
-            after=[contract_done],
             grant=VMEM_LARGE,
         )
         grad_input, grad_output, grad_expand, grad_expand_bias = last_out[:4]

time: 195 us -> 180 us (0.923)
  waiting for transfers between devices: 100 us -> 90.6 us
  starting transfers between devices: 55.7 us -> 50.6 us
    ppermute x19 -> x20, waiting for transfers between devices: 64.9 us -> 57.3 us  [chip_swap(): lax.ppermute(member, 'ctx', [(i, 2 * (i // 2 ^ step) + i % 2) for i in ra...]
    ppermute x19 -> x20, starting transfers between devices: 31.7 us -> 27 us  [chip_swap(): lax.ppermute(member, 'ctx', [(i, 2 * (i // 2 ^ step) + i % 2) for i in ra...]
    ppermute x15 -> x18, waiting for transfers between devices: 9.31 us -> 8.56 us  [core_swap(): return lax.ppermute(member, 'ctx', [(i, i ^ 1) for i in range(ranks)])]
    pallas_call x21 -> x23, Pallas kernels: 37.2 us -> 37.3 us  [local_call(): pl.pallas_call(ordered, out_shape=tuple(outs), in_specs=[pl.BlockSpec(mem...]
  transfers between devices with their start and end apart: 52 -> 56, of which waited for: 27 -> 32; matrix products, arithmetic and copies ran while one was open for 0% -> 0% of each run, Pallas kernels for 8% -> 9%
where the time goes in v4:
time: 180 us
  waiting for transfers between devices  90.6 us (50%)
  starting transfers between devices  50.6 us (28%)
  Pallas kernels  37.3 us (21%)
    ppermute x20, waiting for transfers between devices, chip_swap(): lax.ppermute(member, 'ctx', [(i, 2 * (i // 2 ^ step) + i % 2) for i in ra...  57.3 us
    pallas_call x23, Pallas kernels, local_call(): pl.pallas_call(ordered, out_shape=tuple(outs), in_specs=[pl.BlockSpec(mem...  37.3 us
    ppermute x20, starting transfers between devices, chip_swap(): lax.ppermute(member, 'ctx', [(i, 2 * (i // 2 ^ step) + i % 2) for i in ra...  27 us
    ppermute x18, waiting for transfers between devices, seq_swap(): return lax.ppermute(member, 'dp', [(i, i ^ step) for i in range(seq_parts)])  24.7 us
    ppermute x18, starting transfers between devices, seq_swap(): return lax.ppermute(member, 'dp', [(i, i ^ step) for i in range(seq_parts)])  20.8 us
    ppermute x18, waiting for transfers between devices, core_swap(): return lax.ppermute(member, 'ctx', [(i, i ^ 1) for i in range(ranks)])  8.56 us
  transfers between devices with their start and end apart: 56, of which 32 were waited for; matrix products, arithmetic and copies ran while one was open for 0% of the time, Pallas kernels for 9%

profile of v4, /device:TPU:0, one launch (start us, length us, event | category | flops | bytes accessed | tf_op | source)
XLA Modules:
  0.0 180.3 jit_solution(18266636892069403444)
XLA Ops:
  1.3 2.8 %pack.1 = (bf16[192,768]{1,0:T(8,128)(2,1)}, bf16[128,768]{1,0:T(8,128)(2,1)}) custom-call(s32[3]{0:T(128)} %pad_add_fusion.refs_0_, bf16[128,768]{1,0:T(8,128)(2,1)} %bitcast.8, bf16[192,2304]{1,0:T(8,128)(2,1)} %refs_1_.5, bf16[192,768]{1,0:T(8,128)(2,1)} %refs_2_.4, bf16[192]{0:T(256)(128)(2,1)} %refs_4_.1, bf16[192]{0:T(256)(128)(2,1)} %refs_5_.1, ...), custom_call_target="tpu_custom_call" | custom-call | bytes 1870860 | tf_op jit(solution)/shard_map/pack/pallas_call | solution.py:636
  4.0 4.1 %collective-permute-start.1 = (bf16[128,768]{1,0:T(8,128)(2,1)}, bf16[128,768]{1,0:T(8,128)(2,1)S(1)}, u32[]{:S(2)}, u32[]{:S(2)}) collective-permute-start(bf16[128,768]{1,0:T(8,128)(2,1)} %get-tuple-element.97.refs_3_.refs_1_.refs_4_.refs_0_), channel_id=1, source_target_pairs={{0,4},{1,5},{2,6},{3,7},{4,0},{5,1},{6,2},{7,3},{8,12},{9,13},{10,... | collective-permute-start | bytes 589832 | tf_op jit(solution)/shard_map/ppermute | solution.py:686
  8.2 2.5 %collective-permute-start.5 = (bf16[192,768]{1,0:T(8,128)(2,1)}, bf16[192,768]{1,0:T(8,128)(2,1)S(1)}, u32[]{:S(2)}, u32[]{:S(2)}) collective-permute-start(bf16[192,768]{1,0:T(8,128)(2,1)} %get-tuple-element.98.refs_7_.refs_3_), channel_id=1, source_target_pairs={{0,24},{8,16},{16,8},{24,0},{1,25},{9,17},{17,9},{25,1},{2,26},{10... | collective-permute-start | bytes 884744 | tf_op jit(solution)/shard_map/ppermute | solution.py:691
  11.7 1.6 collective-permute-start
  13.3 4.3 %collective-permute-done.1.refs_4_.refs_5_.refs_6_ = bf16[128,768]{1,0:T(8,128)(2,1)S(1)} collective-permute-done((bf16[128,768]{1,0:T(8,128)(2,1)}, bf16[128,768]{1,0:T(8,128)(2,1)S(1)}, u32[]{:S(2)}, u32[]{:S(2)}) %collective-permute-start.1) | collective-permute-done | bytes 196640 | tf_op jit(solution)/shard_map/ppermute | solution.py:686
  17.6 0.8 collective-permute-start.2
  18.3 3.2 %collective-permute-done.refs_3_.refs_4_.refs_5_ = bf16[128,768]{1,0:T(8,128)(2,1)S(1)} collective-permute-done((bf16[128,768]{1,0:T(8,128)(2,1)}, bf16[128,768]{1,0:T(8,128)(2,1)S(1)}, u32[]{:S(2)}, u32[]{:S(2)}) %collective-permute-start) | collective-permute-done | bytes 196640 | tf_op jit(solution)/shard_map/ppermute | solution.py:686
  21.5 2.6 %collective-permute-done.4.refs_1_ = bf16[192,768]{1,0:T(8,128)(2,1)S(1)} collective-permute-done((bf16[192,768]{1,0:T(8,128)(2,1)}, bf16[192,768]{1,0:T(8,128)(2,1)S(1)}, u32[]{:S(2)}, u32[]{:S(2)}) %collective-permute-start.4) | collective-permute-done | bytes 294944 | tf_op jit(solution)/shard_map/ppermute | solution.py:691
  24.9 2.4 %collective-permute-done.6.refs_9_ = bf16[576,768]{1,0:T(8,128)(2,1)S(1)} collective-permute-done((bf16[576,768]{1,0:T(8,128)(2,1)S(1)}, bf16[576,768]{1,0:T(8,128)(2,1)S(1)}, u32[]{:S(2)}, u32[]{:S(2)}) %collective-permute-start.6) | collective-permute-done | bytes 884768 | tf_op jit(solution)/shard_map/ppermute | solution.py:683
  27.3 2.1 %project.1 = (bf16[512,192]{1,0:T(8,128)(2,1)S(1)}, bf16[512,384]{1,0:T(8,128)(2,1)S(1)}, bf16[512,768]{1,0:T(8,128)(2,1)S(1)}, bf16[768,576]{1,0:T(8,128)(2,1)S...) custom-call(s32[3]{0:T(128)S(1)} %copy-done.6, bf16[192,2304]{1,0:T(8,128)(2,1)S(1)} %copy-done, ...), custom_call_target="tpu_custom_call" | custom-call | flops 452984832 | bytes 7520268 | tf_op jit(solution)/shard_map/project/pallas_call | solution.py:636
  30.2 1.6 collective-permute-start.11
  31.9 1.5 collective-permute-start.12
  33.8 3.7 %attend.1 = (bf16[128,192]{1,0:T(8,128)(2,1)S(1)}, bf16[128,192]{1,0:T(8,128)(2,1)S(1)}, bf16[128,192]{1,0:T(8,128)(2,1)S(1)}, bf16[128,192]{1,0:T(8,128)(2,1)S(...) custom-call(s32[3]{0:T(128)S(1)} %copy-done.6, s32[8]{0:T(128)S(1)} %copy-done.9, ...), custom_call_target="tpu_custom_call" | custom-call | flops 402653184 | bytes 1589292 | tf_op jit(solution)/shard_map/attend/pallas_call | solution.py:636
  37.6 1.2 collective-permute-start.8
  38.8 2.6 %collective-permute-start.9 = (bf16[128,192]{1,0:T(8,128)(2,1)S(1)}, bf16[128,192]{1,0:T(8,128)(2,1)S(1)}, u32[]{:S(2)}, u32[]{:S(2)}) collective-permute-start(bf16[128,192]{1,0:T(8,128)(2,1)S(1)} %get-tuple-element.105), channel_id=1, source_target_pairs={{0,4},{1,5},{2,6},{3,7},{4,0},{5,1},{6,2},{7,3},{8,12},{9,13},{10,... | collective-permute-start | bytes 147464 | tf_op jit(solution)/shard_map/ppermute | solution.py:686
  41.4 1.0 collective-permute-done.8.refs_5_.refs_3_
  42.4 2.9 %collective-permute-start.10 = (bf16[128,192]{1,0:T(8,128)(2,1)S(1)}, bf16[128,192]{1,0:T(8,128)(2,1)S(1)}, u32[]{:S(2)}, u32[]{:S(2)}) collective-permute-start(bf16[128,192]{1,0:T(8,128)(2,1)S(1)} %get-tuple-element.106), channel_id=1, source_target_pairs={{0,6},{1,7},{2,4},{3,5},{4,2},{5,3},{6,0},{7,1},{8,14},{9,15},{10,... | collective-permute-start | bytes 147464 | tf_op jit(solution)/shard_map/ppermute | solution.py:686
  45.3 3.1 %collective-permute-done.10.refs_7_.refs_5_ = bf16[128,192]{1,0:T(8,128)(2,1)S(1)} collective-permute-done((bf16[128,192]{1,0:T(8,128)(2,1)S(1)}, bf16[128,192]{1,0:T(8,128)(2,1)S(1)}, u32[]{:S(2)}, u32[]{:S(2)}) %collective-permute-start.10) | collective-permute-done | bytes 49184 | tf_op jit(solution)/shard_map/ppermute | solution.py:686
  48.5 1.1 middle.1
  49.7 2.6 %collective-permute-start.17 = (bf16[128,768]{1,0:T(8,128)(2,1)S(1)}, bf16[128,768]{1,0:T(8,128)(2,1)S(1)}, u32[]{:S(2)}, u32[]{:S(2)}) collective-permute-start(bf16[128,768]{1,0:T(8,128)(2,1)S(1)} %get-tuple-element.111.refs_3_.refs_6_), channel_id=1, source_target_pairs={{0,24},{8,16},{16,8},{24,0},{1,25},{9,17},{17,9},{25,1},{2,26},{10... | collective-permute-start | bytes 589832 | tf_op jit(solution)/shard_map/ppermute | solution.py:691
  53.3 5.2 %collective-permute-done.17.refs_9_ = bf16[128,768]{1,0:T(8,128)(2,1)S(1)} collective-permute-done((bf16[128,768]{1,0:T(8,128)(2,1)S(1)}, bf16[128,768]{1,0:T(8,128)(2,1)S(1)}, u32[]{:S(2)}, u32[]{:S(2)}) %collective-permute-start.17) | collective-permute-done | bytes 196640 | tf_op jit(solution)/shard_map/ppermute | solution.py:691
  58.5 3.7 %collective-permute-done.16.refs_8_ = bf16[128,768]{1,0:T(8,128)(2,1)S(1)} collective-permute-done((bf16[128,768]{1,0:T(8,128)(2,1)S(1)}, bf16[128,768]{1,0:T(8,128)(2,1)S(1)}, u32[]{:S(2)}, u32[]{:S(2)}) %collective-permute-start.16) | collective-permute-done | bytes 196640 | tf_op jit(solution)/shard_map/ppermute | solution.py:691
  62.3 5.6 %feed.1 = (bf16[128,768]{1,0:T(8,128)(2,1)S(1)}, bf16[128,768]{1,0:T(8,128)(2,1)S(1)}, bf16[128,768]{1,0:T(8,128)(2,1)S(1)}, bf16[128,768]{1,0:T(8,128)(2,1)S(1)...) custom-call(s32[3]{0:T(128)S(1)} %copy-done.6, ...), custom_call_target="tpu_custom_call" | custom-call | flops 3623878656 | bytes 8753676 | tf_op jit(solution)/shard_map/feed/pallas_call | solution.py:636
  68.0 2.8 %collective-permute-done.24.refs_2_ = bf16[4,384,384]{2,1,0:T(8,128)(2,1)S(1)} collective-permute-done((bf16[4,384,384]{2,1,0:T(8,128)(2,1)S(1)}, bf16[4,384,384]{2,1,0:T(8,128)(2,1)S(1)}, u32[]{:S(2)}, u32[]{:S(2)}) %collective-permute-start.24) | collective-permute-done | bytes 1179680 | tf_op jit(solution)/shard_map/ppermute | solution.py:683
  70.9 0.8 feed_halves.1
  72.4 1.0 collective-permute-start.21
  73.3 1.0 collective-permute-start.22
  74.3 1.5 collective-permute-start.23
  75.9 4.3 %collective-permute-done.21.refs_6_ = bf16[128,768]{1,0:T(8,128)(2,1)S(1)} collective-permute-done((bf16[128,768]{1,0:T(8,128)(2,1)S(1)}, bf16[128,768]{1,0:T(8,128)(2,1)S(1)}, u32[]{:S(2)}, u32[]{:S(2)}) %collective-permute-start.21) | collective-permute-done | bytes 196640 | tf_op jit(solution)/shard_map/ppermute | solution.py:691
  80.2 4.0 %collective-permute-done.22.refs_7_ = bf16[128,768]{1,0:T(8,128)(2,1)S(1)} collective-permute-done((bf16[128,768]{1,0:T(8,128)(2,1)S(1)}, bf16[128,768]{1,0:T(8,128)(2,1)S(1)}, u32[]{:S(2)}, u32[]{:S(2)}) %collective-permute-start.22) | collective-permute-done | bytes 196640 | tf_op jit(solution)/shard_map/ppermute | solution.py:691
  84.2 1.4 middle_back.1
  85.6 2.9 %collective-permute-start.27 = (bf16[128,192]{1,0:T(8,128)(2,1)S(1)}, bf16[128,192]{1,0:T(8,128)(2,1)S(1)}, u32[]{:S(2)}, u32[]{:S(2)}) collective-permute-start(bf16[128,192]{1,0:T(8,128)(2,1)S(1)} %get-tuple-element.129), channel_id=1, source_target_pairs={{0,6},{1,7},{2,4},{3,5},{4,2},{5,3},{6,0},{7,1},{8,14},{9,15},{10,... | collective-permute-start | bytes 147464 | tf_op jit(solution)/shard_map/ppermute | solution.py:686
  88.6 0.8 collective-permute-start.25
  90.1 1.0 output_weights.1
  92.0 1.3 collective-permute-done.25.refs_8_
  93.3 1.2 collective-permute-done.26.refs_9_
  94.5 5.0 %attend_back.1 = (f32[192,512]{1,0:T(8,128)S(1)}, f32[512,384]{1,0:T(8,128)S(1)}, bf16[512,384]{1,0:T(8,128)(2,1)S(1)}) custom-call(s32[3]{0:T(128)S(1)} %copy-done.6, s32[8]{0:T(128)S(1)} %copy-done.9, bf16[512,192]{1,0:T(8,128)(2,1)S(1)} %get-tuple-element.101.refs_2_, bf16[512,384]{1,0:T(8,128)(2,1)S(1)} %get-tuple-element.102.refs_3_, ...), custom_call_target="tpu_custom_call" | custom-call | flops 1006632960 | bytes 3162156 | tf_op jit(solution)/shard_map/attend_back/pallas_call | solution.py:636
  100.6 1.2 collective-permute-start.32
  101.8 1.3 collective-permute-start.19
  103.1 1.3 collective-permute-start.20
  104.4 1.8 %normed_back.1 = (f32[2,128,768]{2,1,0:T(8,128)S(1)}, bf16[128,768]{1,0:T(8,128)(2,1)S(1)}, bf16[128,768]{1,0:T(8,128)(2,1)S(1)}, bf16[512,576]{1,0:T(8,128)(2,1...) custom-call(f32[192,512]{1,0:T(8,128)S(1)} %get-tuple-element.134.refs_0_, f32[512,384]{1,0:T(8,128)S(1)} %get-tuple-element.135.refs_1_, ...), custom_call_target="tpu_custom_call" | custom-call | flops 452984832 | bytes 5056512 | tf_op jit(solution)/shard_map/normed_back/pallas_call | solution.py:636
  106.2 1.5 input_weights.1
  107.8 4.5 %collective-permute-done.19.refs_4_ = bf16[128,768]{1,0:T(8,128)(2,1)S(1)} collective-permute-done((bf16[128,768]{1,0:T(8,128)(2,1)S(1)}, bf16[128,768]{1,0:T(8,128)(2,1)S(1)}, u32[]{:S(2)}, u32[]{:S(2)}) %collective-permute-start.19) | collective-permute-done | bytes 196640 | tf_op jit(solution)/shard_map/ppermute | solution.py:691
  112.3 2.0 %collective-permute-start.30 = (bf16[128,768]{1,0:T(8,128)(2,1)S(1)}, bf16[128,768]{1,0:T(8,128)(2,1)S(1)}, u32[]{:S(2)}, u32[]{:S(2)}) collective-permute-start(bf16[128,768]{1,0:T(8,128)(2,1)S(1)} %get-tuple-element.147), channel_id=1, source_target_pairs={{0,2},{1,3},{2,0},{3,1},{4,6},{5,7},{6,4},{7,5},{8,10},{9,11},{10,... | collective-permute-start | bytes 589832 | tf_op jit(solution)/shard_map/ppermute | solution.py:686
  114.8 1.8 %collective-permute-done.32.refs_2_ = bf16[384,384]{1,0:T(8,128)(2,1)S(1)} collective-permute-done((bf16[384,384]{1,0:T(8,128)(2,1)S(1)}, bf16[384,384]{1,0:T(8,128)(2,1)S(1)}, u32[]{:S(2)}, u32[]{:S(2)}) %collective-permute-start.32) | collective-permute-done | bytes 294944 | tf_op jit(solution)/shard_map/ppermute | solution.py:686
  116.6 0.8 result.1
  118.0 1.1 owners.1
  119.1 2.2 %collective-permute-start.43 = (bf16[192,384]{1,0:T(8,128)(2,1)S(1)}, bf16[192,384]{1,0:T(8,128)(2,1)S(1)}, u32[]{:S(2)}, u32[]{:S(2)}) collective-permute-start(bf16[192,384]{1,0:T(8,128)(2,1)S(1)} %get-tuple-element.156.refs_3_.refs_1_), channel_id=1, source_target_pairs={{0,4},{1,5},{2,6},{3,7},{4,0},{5,1},{6,2},{7,3},{8,12},{9,13},{10,... | collective-permute-start | bytes 442376 | tf_op jit(solution)/shard_map/ppermute | solution.py:686
  121.2 1.2 collective-permute-start.39
  123.1 1.6 collective-permute-start.41
  124.7 1.8 collective-permute-done.31.refs_2_
  126.6 2.5 %collective-permute-done.43.refs_3_ = bf16[192,384]{1,0:T(8,128)(2,1)S(1)} collective-permute-done((bf16[192,384]{1,0:T(8,128)(2,1)S(1)}, bf16[192,384]{1,0:T(8,128)(2,1)S(1)}, u32[]{:S(2)}, u32[]{:S(2)}) %collective-permute-start.43) | collective-permute-done | bytes 147488 | tf_op jit(solution)/shard_map/ppermute | solution.py:686
  129.1 3.5 %collective-permute-done.42.refs_5_.refs_2_ = bf16[192,384]{1,0:T(8,128)(2,1)S(1)} collective-permute-done((bf16[192,384]{1,0:T(8,128)(2,1)S(1)}, bf16[192,384]{1,0:T(8,128)(2,1)S(1)}, u32[]{:S(2)}, u32[]{:S(2)}) %collective-permute-start.42) | collective-permute-done | bytes 147488 | tf_op jit(solution)/shard_map/ppermute | solution.py:686
  133.2 7.2 %collective-permute-done.38.refs_4_.refs_7_ = bf16[128,768]{1,0:T(8,128)(2,1)S(1)} collective-permute-done((bf16[128,768]{1,0:T(8,128)(2,1)S(1)}, bf16[128,768]{1,0:T(8,128)(2,1)S(1)}, u32[]{:S(2)}, u32[]{:S(2)}) %collective-permute-start.38) | collective-permute-done | bytes 196640 | tf_op jit(solution)/shard_map/ppermute | solution.py:686
  140.3 1.0 collective-permute-done.44.refs_6_.refs_4_
  141.3 0.8 shares.1.refs_1_
  142.4 2.5 %collective-permute-start.45 = (bf16[288,768]{1,0:T(8,128)(2,1)S(1)}, bf16[288,768]{1,0:T(8,128)(2,1)S(1)}, u32[]{:S(2)}, u32[]{:S(2)}) collective-permute-start(bf16[288,768]{1,0:T(8,128)(2,1)S(1)} %shares.1.refs_1_), channel_id=1, source_target_pairs={{0,2},{1,3},{2,0},{3,1},{4,6},{5,7},{6,4},{7,5},{8,10},{9,11},{10,... | collective-permute-start | bytes 1327112 | tf_op jit(solution)/shard_map/ppermute | solution.py:686
  145.4 0.9 collective-permute-done.47.refs_5_
  146.4 1.1 tokens_back.1
  147.6 2.1 %contract_final.1 = (f32[768,768]{1,0:T(8,128)}, f32[8,128]{1,0:T(8,128)S(1)}) custom-call(s32[3]{0:T(128)S(1)} %copy-done.6, bf16[192,384]{1,0:T(8,128)(2,1)S(1)} %get-tuple-element.156.refs_3_.refs_1_, bf16[192,384]{1,0:T(8,128)(2,1)S(1)} %collective-permute-done.42.refs_5_.refs_2_, bf16[192,384]{1,0:T(8,128)(2,1)S(1)} %collective-permute-done.43.refs_3_, ...), custom_call_target="tpu_custom_call" | custom-call | bytes 3543052 | tf_op jit(solution)/shard_map/contract_final/pallas_call | solution.py:636
  149.7 12.9 %collective-permute-done.46.refs_0_.refs_3_ = bf16[288,768]{1,0:T(8,128)(2,1)S(1)} collective-permute-done((bf16[288,768]{1,0:T(8,128)(2,1)S(1)}, bf16[288,768]{1,0:T(8,128)(2,1)S(1)}, u32[]{:S(2)}, u32[]{:S(2)}) %collective-permute-start.46) | collective-permute-done | bytes 442400 | tf_op jit(solution)/shard_map/ppermute | solution.py:686
  163.6 11.2 %collective-permute-done.51.refs_4_ = bf16[288,768]{1,0:T(8,128)(2,1)S(1)} collective-permute-done((bf16[288,768]{1,0:T(8,128)(2,1)S(1)}, bf16[288,768]{1,0:T(8,128)(2,1)S(1)}, u32[]{:S(2)}, u32[]{:S(2)}) %collective-permute-start.51) | collective-permute-done | bytes 442400 | tf_op jit(solution)/shard_map/ppermute | solution.py:686
  174.8 1.8 collective-permute-done.55.refs_8_
  176.6 3.5 %weights_final.1 = (f32[192,2304]{1,0:T(8,128)}, f32[192,768]{1,0:T(8,128)}, f32[192,3072]{1,0:T(8,128)}, f32[768]{0:T(1024)}, f32[192]{0:T(256)}, /*index=5*/f3...) custom-call(s32[3]{0:T(128)S(1)} %copy-done.6, ...), custom_call_target="tpu_custom_call" | custom-call | bytes 8266764 | tf_op jit(solution)/shard_map/weights_final/pallas_call | solution.py:636
  (92 shorter events, 12.8 us)
Async XLA Ops:
  4.0 13.5 %collective-permute-start.1 = (bf16[128,768]{1,0:T(8,128)(2,1)}, bf16[128,768]{1,0:T(8,128)(2,1)S(1)}, u32[]{:S(2)}, u32[]{:S(2)}) collective-permute-start(bf16[128,768]{1,0:T(8,128)(2,1)} %get-tuple-element.97.refs_3_.refs_1_.refs_4_.refs_0_), channel_id=1, source_target_pairs={{0,4},{1,5},{2,6},{3,7},{4,0},{5,1},{6,2},{7,3},{8,12},{9,13},{10,... | collective-permute-start | bytes 589832 | tf_op jit(solution)/shard_map/ppermute | solution.py:686
  8.2 19.1 %copy-start = (bf16[192,2304]{1,0:T(8,128)(2,1)S(1)}, bf16[192,2304]{1,0:T(8,128)(2,1)}, u32[]{:S(2)}) copy-start(bf16[192,2304]{1,0:T(8,128)(2,1)} %refs_1_.5) | copy-start | bytes 2654212
  8.2 19.1 %copy-start.1 = (bf16[128,768]{1,0:T(8,128)(2,1)S(1)}, bf16[128,768]{1,0:T(8,128)(2,1)}, u32[]{:S(2)}) copy-start(bf16[128,768]{1,0:T(8,128)(2,1)} %get-tuple-element.97.refs_3_.refs_1_.refs_4_.refs_0_) | copy-start | bytes 589828
  8.2 19.1 %copy-start.2 = (bf16[192,768]{1,0:T(8,128)(2,1)S(1)}, bf16[192,768]{1,0:T(8,128)(2,1)}, u32[]{:S(2)}) copy-start(bf16[192,768]{1,0:T(8,128)(2,1)} %refs_2_.4) | copy-start | bytes 884740
  8.2 19.1 %copy-start.3 = (bf16[192,768]{1,0:T(8,128)(2,1)S(1)}, bf16[192,768]{1,0:T(8,128)(2,1)}, u32[]{:S(2)}) copy-start(bf16[192,768]{1,0:T(8,128)(2,1)} %get-tuple-element.98.refs_7_.refs_3_) | copy-start | bytes 884740
  8.2 19.1 %copy-start.6 = (s32[3]{0:T(128)S(1)}, s32[3]{0:T(128)}, u32[]{:S(2)}) copy-start(s32[3]{0:T(128)} %pad_add_fusion.refs_0_) | copy-start | bytes 40
  8.2 13.3 %collective-permute-start.5 = (bf16[192,768]{1,0:T(8,128)(2,1)}, bf16[192,768]{1,0:T(8,128)(2,1)S(1)}, u32[]{:S(2)}, u32[]{:S(2)}) collective-permute-start(bf16[192,768]{1,0:T(8,128)(2,1)} %get-tuple-element.98.refs_7_.refs_3_), channel_id=1, source_target_pairs={{0,24},{8,16},{16,8},{24,0},{1,25},{9,17},{17,9},{25,1},{2,26},{10... | collective-permute-start | bytes 884744 | tf_op jit(solution)/shard_map/ppermute | solution.py:691
  10.7 13.4 %collective-permute-start.4 = (bf16[192,768]{1,0:T(8,128)(2,1)}, bf16[192,768]{1,0:T(8,128)(2,1)S(1)}, u32[]{:S(2)}, u32[]{:S(2)}) collective-permute-start(bf16[192,768]{1,0:T(8,128)(2,1)} %get-tuple-element.98.refs_7_.refs_3_), channel_id=1, source_target_pairs={{0,16},{8,24},{16,0},{24,8},{1,17},{9,25},{17,1},{25,9},{2,18},{10... | collective-permute-start | bytes 884744 | tf_op jit(solution)/shard_map/ppermute | solution.py:691
  11.2 13.0 %collective-permute-start.3 = (bf16[192,768]{1,0:T(8,128)(2,1)}, bf16[192,768]{1,0:T(8,128)(2,1)S(1)}, u32[]{:S(2)}, u32[]{:S(2)}) collective-permute-start(bf16[192,768]{1,0:T(8,128)(2,1)} %get-tuple-element.98.refs_7_.refs_3_), channel_id=1, source_target_pairs={{0,8},{8,0},{16,24},{24,16},{1,9},{9,1},{17,25},{25,17},{2,10},{10... | collective-permute-start | bytes 884744 | tf_op jit(solution)/shard_map/ppermute | solution.py:691
  11.7 9.8 %collective-permute-start = (bf16[128,768]{1,0:T(8,128)(2,1)}, bf16[128,768]{1,0:T(8,128)(2,1)S(1)}, u32[]{:S(2)}, u32[]{:S(2)}) collective-permute-start(bf16[128,768]{1,0:T(8,128)(2,1)} %get-tuple-element.97.refs_3_.refs_1_.refs_4_.refs_0_), channel_id=1, source_target_pairs={{0,2},{1,3},{2,0},{3,1},{4,6},{5,7},{6,4},{7,5},{8,10},{9,11},{10,... | collective-permute-start | bytes 589832 | tf_op jit(solution)/shard_map/ppermute | solution.py:686
  17.6 7.1 %collective-permute-start.2 = (bf16[128,768]{1,0:T(8,128)(2,1)S(1)}, bf16[128,768]{1,0:T(8,128)(2,1)S(1)}, u32[]{:S(2)}, u32[]{:S(2)}) collective-permute-start(bf16[128,768]{1,0:T(8,128)(2,1)S(1)} %collective-permute-done.1.refs_4_.refs_5_.refs_6_), channel_id=1, source_target_pairs={{0,2},{1,3},{2,0},{3,1},{4,6},{5,7},{6,4},{7,5},{8,10},{9,11},{10,... | collective-permute-start | bytes 589832 | tf_op jit(solution)/shard_map/ppermute | solution.py:686
  24.8 4.9 %copy-start.4 = (bf16[192,3072]{1,0:T(8,128)(2,1)S(1)}, bf16[192,3072]{1,0:T(8,128)(2,1)}, u32[]{:S(2)}) copy-start(bf16[192,3072]{1,0:T(8,128)(2,1)} %refs_3_.3) | copy-start | bytes 3538948
  24.8 2.5 %collective-permute-start.6 = (bf16[576,768]{1,0:T(8,128)(2,1)S(1)}, bf16[576,768]{1,0:T(8,128)(2,1)S(1)}, u32[]{:S(2)}, u32[]{:S(2)}) collective-permute-start(bf16[576,768]{1,0:T(8,128)(2,1)S(1)} %pack_stack.1.refs_8_), channel_id=1, source_target_pairs={{0,1},{1,0},{2,3},{3,2},{4,5},{5,4},{6,7},{7,6},{8,9},{9,8},{10,11... | collective-permute-start | bytes 2654216 | tf_op jit(solution)/shard_map/ppermute | solution.py:683
  29.4 4.4 %collective-permute-start.7 = (bf16[512,384]{1,0:T(8,128)(2,1)S(1)}, bf16[512,384]{1,0:T(8,128)(2,1)S(1)}, u32[]{:S(2)}, u32[]{:S(2)}) collective-permute-start(bf16[512,384]{1,0:T(8,128)(2,1)S(1)} %get-tuple-element.102.refs_3_), channel_id=1, source_target_pairs={{0,1},{1,0},{2,3},{3,2},{4,5},{5,4},{6,7},{7,6},{8,9},{9,8},{10,11... | collective-permute-start | bytes 1179656 | tf_op jit(solution)/shard_map/ppermute | solution.py:683
  30.2 19.4 %collective-permute-start.11 = (bf16[224,768]{1,0:T(8,128)(2,1)S(1)}, bf16[224,768]{1,0:T(8,128)(2,1)S(1)}, u32[]{:S(2)}, u32[]{:S(2)}) collective-permute-start(bf16[224,768]{1,0:T(8,128)(2,1)S(1)} %get-tuple-element.108), channel_id=1, source_target_pairs={{0,8},{8,0},{16,24},{24,16},{1,9},{9,1},{17,25},{25,17},{2,10},{10... | collective-permute-start | bytes 1032200 | tf_op jit(solution)/shard_map/ppermute | solution.py:691
  31.9 17.7 %collective-permute-start.12 = (bf16[224,768]{1,0:T(8,128)(2,1)S(1)}, bf16[224,768]{1,0:T(8,128)(2,1)S(1)}, u32[]{:S(2)}, u32[]{:S(2)}) collective-permute-start(bf16[224,768]{1,0:T(8,128)(2,1)S(1)} %get-tuple-element.109), channel_id=1, source_target_pairs={{0,16},{8,24},{16,0},{24,8},{1,17},{9,25},{17,1},{25,9},{2,18},{10... | collective-permute-start | bytes 1032200 | tf_op jit(solution)/shard_map/ppermute | solution.py:691
  33.4 16.2 %collective-permute-start.13 = (bf16[224,768]{1,0:T(8,128)(2,1)S(1)}, bf16[224,768]{1,0:T(8,128)(2,1)S(1)}, u32[]{:S(2)}, u32[]{:S(2)}) collective-permute-start(bf16[224,768]{1,0:T(8,128)(2,1)S(1)} %get-tuple-element.110), channel_id=1, source_target_pairs={{0,24},{8,16},{16,8},{24,0},{1,25},{9,17},{17,9},{25,1},{2,26},{10... | collective-permute-start | bytes 1032200 | tf_op jit(solution)/shard_map/ppermute | solution.py:691
  37.6 4.8 %collective-permute-start.8 = (bf16[128,192]{1,0:T(8,128)(2,1)S(1)}, bf16[128,192]{1,0:T(8,128)(2,1)S(1)}, u32[]{:S(2)}, u32[]{:S(2)}) collective-permute-start(bf16[128,192]{1,0:T(8,128)(2,1)S(1)} %get-tuple-element.104), channel_id=1, source_target_pairs={{0,2},{1,3},{2,0},{3,1},{4,6},{5,7},{6,4},{7,5},{8,10},{9,11},{10,... | collective-permute-start | bytes 147464 | tf_op jit(solution)/shard_map/ppermute | solution.py:686
  38.8 6.6 %collective-permute-start.9 = (bf16[128,192]{1,0:T(8,128)(2,1)S(1)}, bf16[128,192]{1,0:T(8,128)(2,1)S(1)}, u32[]{:S(2)}, u32[]{:S(2)}) collective-permute-start(bf16[128,192]{1,0:T(8,128)(2,1)S(1)} %get-tuple-element.105), channel_id=1, source_target_pairs={{0,4},{1,5},{2,6},{3,7},{4,0},{5,1},{6,2},{7,3},{8,12},{9,13},{10,... | collective-permute-start | bytes 147464 | tf_op jit(solution)/shard_map/ppermute | solution.py:686
  42.4 6.1 %collective-permute-start.10 = (bf16[128,192]{1,0:T(8,128)(2,1)S(1)}, bf16[128,192]{1,0:T(8,128)(2,1)S(1)}, u32[]{:S(2)}, u32[]{:S(2)}) collective-permute-start(bf16[128,192]{1,0:T(8,128)(2,1)S(1)} %get-tuple-element.106), channel_id=1, source_target_pairs={{0,6},{1,7},{2,4},{3,5},{4,2},{5,3},{6,0},{7,1},{8,14},{9,15},{10,... | collective-permute-start | bytes 147464 | tf_op jit(solution)/shard_map/ppermute | solution.py:686
  49.6 12.8 %copy-start.7 = (bf16[768,768]{1,0:T(8,128)(2,1)S(1)}, bf16[768,768]{1,0:T(8,128)(2,1)}, u32[]{:S(2)}) copy-start(bf16[768,768]{1,0:T(8,128)(2,1)} %refs_2_.5) | copy-start | bytes 3538948
  49.6 12.8 %copy-start.8 = (bf16[768]{0:T(1024)(128)(2,1)S(1)}, bf16[768]{0:T(1024)(128)(2,1)}, u32[]{:S(2)}) copy-start(bf16[768]{0:T(1024)(128)(2,1)} %refs_1_.8) | copy-start | bytes 4612
  49.7 12.7 %collective-permute-start.14 = (bf16[288,768]{1,0:T(8,128)(2,1)S(1)}, bf16[288,768]{1,0:T(8,128)(2,1)S(1)}, u32[]{:S(2)}, u32[]{:S(2)}) collective-permute-start(bf16[288,768]{1,0:T(8,128)(2,1)S(1)} %expand_stack.1), channel_id=1, source_target_pairs={{0,1},{1,0},{2,3},{3,2},{4,5},{5,4},{6,7},{7,6},{8,9},{9,8},{10,11... | collective-permute-start | bytes 1327112 | tf_op jit(solution)/shard_map/ppermute | solution.py:683
  49.7 8.7 %collective-permute-start.17 = (bf16[128,768]{1,0:T(8,128)(2,1)S(1)}, bf16[128,768]{1,0:T(8,128)(2,1)S(1)}, u32[]{:S(2)}, u32[]{:S(2)}) collective-permute-start(bf16[128,768]{1,0:T(8,128)(2,1)S(1)} %get-tuple-element.111.refs_3_.refs_6_), channel_id=1, source_target_pairs={{0,24},{8,16},{16,8},{24,0},{1,25},{9,17},{17,9},{25,1},{2,26},{10... | collective-permute-start | bytes 589832 | tf_op jit(solution)/shard_map/ppermute | solution.py:691
  52.3 9.9 %collective-permute-start.16 = (bf16[128,768]{1,0:T(8,128)(2,1)S(1)}, bf16[128,768]{1,0:T(8,128)(2,1)S(1)}, u32[]{:S(2)}, u32[]{:S(2)}) collective-permute-start(bf16[128,768]{1,0:T(8,128)(2,1)S(1)} %get-tuple-element.111.refs_3_.refs_6_), channel_id=1, source_target_pairs={{0,16},{8,24},{16,0},{24,8},{1,17},{9,25},{17,1},{25,9},{2,18},{10... | collective-permute-start | bytes 589832 | tf_op jit(solution)/shard_map/ppermute | solution.py:691
  52.8 9.5 %collective-permute-start.15 = (bf16[128,768]{1,0:T(8,128)(2,1)S(1)}, bf16[128,768]{1,0:T(8,128)(2,1)S(1)}, u32[]{:S(2)}, u32[]{:S(2)}) collective-permute-start(bf16[128,768]{1,0:T(8,128)(2,1)S(1)} %get-tuple-element.111.refs_3_.refs_6_), channel_id=1, source_target_pairs={{0,8},{8,0},{16,24},{24,16},{1,9},{9,1},{17,25},{25,17},{2,10},{10... | collective-permute-start | bytes 589832 | tf_op jit(solution)/shard_map/ppermute | solution.py:691
  67.9 2.9 %collective-permute-start.24 = (bf16[4,384,384]{2,1,0:T(8,128)(2,1)S(1)}, bf16[4,384,384]{2,1,0:T(8,128)(2,1)S(1)}, u32[]{:S(2)}, u32[]{:S(2)}) collective-permute-start(bf16[4,384,384]{2,1,0:T(8,128)(2,1)S(1)} %get-tuple-element.124), channel_id=1, source_target_pairs={{0,1},{1,0},{2,3},{3,2},{4,5},{5,4},{6,7},{7,6},{8,9},{9,8},{10,11... | collective-permute-start | bytes 3538952 | tf_op jit(solution)/shard_map/ppermute | solution.py:683
  71.7 20.2 %collective-permute-start.28 = (bf16[2,384,384]{2,1,0:T(8,128)(2,1)S(1)}, bf16[2,384,384]{2,1,0:T(8,128)(2,1)S(1)}, u32[]{:S(2)}, u32[]{:S(2)}) collective-permute-start(bf16[2,384,384]{2,1,0:T(8,128)(2,1)S(1)} %get-tuple-element.125.refs_9_), channel_id=1, source_target_pairs={{0,2},{1,3},{2,0},{3,1},{4,6},{5,7},{6,4},{7,5},{8,10},{9,11},{10,... | collective-permute-start | bytes 1769480 | tf_op jit(solution)/shard_map/ppermute | solution.py:686
  72.4 7.8 %collective-permute-start.21 = (bf16[128,768]{1,0:T(8,128)(2,1)S(1)}, bf16[128,768]{1,0:T(8,128)(2,1)S(1)}, u32[]{:S(2)}, u32[]{:S(2)}) collective-permute-start(bf16[128,768]{1,0:T(8,128)(2,1)S(1)} %get-tuple-element.120), channel_id=1, source_target_pairs={{0,8},{8,0},{16,24},{24,16},{1,9},{9,1},{17,25},{25,17},{2,10},{10... | collective-permute-start | bytes 589832 | tf_op jit(solution)/shard_map/ppermute | solution.py:691
  73.3 10.9 %collective-permute-start.22 = (bf16[128,768]{1,0:T(8,128)(2,1)S(1)}, bf16[128,768]{1,0:T(8,128)(2,1)S(1)}, u32[]{:S(2)}, u32[]{:S(2)}) collective-permute-start(bf16[128,768]{1,0:T(8,128)(2,1)S(1)} %get-tuple-element.121), channel_id=1, source_target_pairs={{0,16},{8,24},{16,0},{24,8},{1,17},{9,25},{17,1},{25,9},{2,18},{10... | collective-permute-start | bytes 589832 | tf_op jit(solution)/shard_map/ppermute | solution.py:691
  74.3 9.9 %collective-permute-start.23 = (bf16[128,768]{1,0:T(8,128)(2,1)S(1)}, bf16[128,768]{1,0:T(8,128)(2,1)S(1)}, u32[]{:S(2)}, u32[]{:S(2)}) collective-permute-start(bf16[128,768]{1,0:T(8,128)(2,1)S(1)} %get-tuple-element.122), channel_id=1, source_target_pairs={{0,24},{8,16},{16,8},{24,0},{1,25},{9,17},{17,9},{25,1},{2,26},{10... | collective-permute-start | bytes 589832 | tf_op jit(solution)/shard_map/ppermute | solution.py:691
  85.6 6.2 %collective-permute-start.27 = (bf16[128,192]{1,0:T(8,128)(2,1)S(1)}, bf16[128,192]{1,0:T(8,128)(2,1)S(1)}, u32[]{:S(2)}, u32[]{:S(2)}) collective-permute-start(bf16[128,192]{1,0:T(8,128)(2,1)S(1)} %get-tuple-element.129), channel_id=1, source_target_pairs={{0,6},{1,7},{2,4},{3,5},{4,2},{5,3},{6,0},{7,1},{8,14},{9,15},{10,... | collective-permute-start | bytes 147464 | tf_op jit(solution)/shard_map/ppermute | solution.py:686
  88.6 4.7 %collective-permute-start.25 = (bf16[128,192]{1,0:T(8,128)(2,1)S(1)}, bf16[128,192]{1,0:T(8,128)(2,1)S(1)}, u32[]{:S(2)}, u32[]{:S(2)}) collective-permute-start(bf16[128,192]{1,0:T(8,128)(2,1)S(1)} %get-tuple-element.127), channel_id=1, source_target_pairs={{0,2},{1,3},{2,0},{3,1},{4,6},{5,7},{6,4},{7,5},{8,10},{9,11},{10,... | collective-permute-start | bytes 147464 | tf_op jit(solution)/shard_map/ppermute | solution.py:686
  89.3 5.2 %collective-permute-start.26 = (bf16[128,192]{1,0:T(8,128)(2,1)S(1)}, bf16[128,192]{1,0:T(8,128)(2,1)S(1)}, u32[]{:S(2)}, u32[]{:S(2)}) collective-permute-start(bf16[128,192]{1,0:T(8,128)(2,1)S(1)} %get-tuple-element.128), channel_id=1, source_target_pairs={{0,4},{1,5},{2,6},{3,7},{4,0},{5,1},{6,2},{7,3},{8,12},{9,13},{10,... | collective-permute-start | bytes 147464 | tf_op jit(solution)/shard_map/ppermute | solution.py:686
  99.5 3.6 %collective-permute-start.29 = (bf16[512,384]{1,0:T(8,128)(2,1)S(1)}, bf16[512,384]{1,0:T(8,128)(2,1)S(1)}, u32[]{:S(2)}, u32[]{:S(2)}) collective-permute-start(bf16[512,384]{1,0:T(8,128)(2,1)S(1)} %get-tuple-element.136), channel_id=1, source_target_pairs={{0,1},{1,0},{2,3},{3,2},{4,5},{5,4},{6,7},{7,6},{8,9},{9,8},{10,11... | collective-permute-start | bytes 1179656 | tf_op jit(solution)/shard_map/ppermute | solution.py:683
  99.6 14.8 %collective-permute-start.33 = (bf16[4,192,384]{2,1,0:T(8,128)(2,1)S(1)}, bf16[4,192,384]{2,1,0:T(8,128)(2,1)S(1)}, u32[]{:S(2)}, u32[]{:S(2)}) collective-permute-start(bf16[4,192,384]{2,1,0:T(8,128)(2,1)S(1)} %get-tuple-element.133.refs_12_), channel_id=1, source_target_pairs={{0,1},{1,0},{2,3},{3,2},{4,5},{5,4},{6,7},{7,6},{8,9},{9,8},{10,11... | collective-permute-start | bytes 1769480 | tf_op jit(solution)/shard_map/ppermute | solution.py:683
  100.1 7.8 %collective-permute-start.18 = (bf16[128,768]{1,0:T(8,128)(2,1)S(1)}, bf16[128,768]{1,0:T(8,128)(2,1)S(1)}, u32[]{:S(2)}, u32[]{:S(2)}) collective-permute-start(bf16[128,768]{1,0:T(8,128)(2,1)S(1)} %get-tuple-element.113), channel_id=1, source_target_pairs={{0,8},{8,0},{16,24},{24,16},{1,9},{9,1},{17,25},{25,17},{2,10},{10... | collective-permute-start | bytes 589832 | tf_op jit(solution)/shard_map/ppermute | solution.py:691
  100.6 16.0 %collective-permute-start.32 = (bf16[384,384]{1,0:T(8,128)(2,1)S(1)}, bf16[384,384]{1,0:T(8,128)(2,1)S(1)}, u32[]{:S(2)}, u32[]{:S(2)}) collective-permute-start(bf16[384,384]{1,0:T(8,128)(2,1)S(1)} %get-tuple-element.131.refs_11_), channel_id=1, source_target_pairs={{0,4},{1,5},{2,6},{3,7},{4,0},{5,1},{6,2},{7,3},{8,12},{9,13},{10,... | collective-permute-start | bytes 884744 | tf_op jit(solution)/shard_map/ppermute | solution.py:686
  101.8 10.5 %collective-permute-start.19 = (bf16[128,768]{1,0:T(8,128)(2,1)S(1)}, bf16[128,768]{1,0:T(8,128)(2,1)S(1)}, u32[]{:S(2)}, u32[]{:S(2)}) collective-permute-start(bf16[128,768]{1,0:T(8,128)(2,1)S(1)} %get-tuple-element.114), channel_id=1, source_target_pairs={{0,16},{8,24},{16,0},{24,8},{1,17},{9,25},{17,1},{25,9},{2,18},{10... | collective-permute-start | bytes 589832 | tf_op jit(solution)/shard_map/ppermute | solution.py:691
  103.1 11.3 %collective-permute-start.20 = (bf16[128,768]{1,0:T(8,128)(2,1)S(1)}, bf16[128,768]{1,0:T(8,128)(2,1)S(1)}, u32[]{:S(2)}, u32[]{:S(2)}) collective-permute-start(bf16[128,768]{1,0:T(8,128)(2,1)S(1)} %get-tuple-element.115), channel_id=1, source_target_pairs={{0,24},{8,16},{16,8},{24,0},{1,25},{9,17},{17,9},{25,1},{2,26},{10... | collective-permute-start | bytes 589832 | tf_op jit(solution)/shard_map/ppermute | solution.py:691
  107.8 8.8 %collective-permute-start.34 = (bf16[96,768]{1,0:T(8,128)(2,1)S(1)}, bf16[96,768]{1,0:T(8,128)(2,1)S(1)}, u32[]{:S(2)}, u32[]{:S(2)}) collective-permute-start(bf16[96,768]{1,0:T(8,128)(2,1)S(1)} %get-tuple-element.151), channel_id=1, source_target_pairs={{0,1},{1,0},{2,3},{3,2},{4,5},{5,4},{6,7},{7,6},{8,9},{9,8},{10,11... | collective-permute-start | bytes 442376 | tf_op jit(solution)/shard_map/ppermute | solution.py:683
  112.3 10.8 %collective-permute-start.30 = (bf16[128,768]{1,0:T(8,128)(2,1)S(1)}, bf16[128,768]{1,0:T(8,128)(2,1)S(1)}, u32[]{:S(2)}, u32[]{:S(2)}) collective-permute-start(bf16[128,768]{1,0:T(8,128)(2,1)S(1)} %get-tuple-element.147), channel_id=1, source_target_pairs={{0,2},{1,3},{2,0},{3,1},{4,6},{5,7},{6,4},{7,5},{8,10},{9,11},{10,... | collective-permute-start | bytes 589832 | tf_op jit(solution)/shard_map/ppermute | solution.py:686
  114.3 3.2 %collective-permute-start.35 = (bf16[96,768]{1,0:T(8,128)(2,1)S(1)}, bf16[96,768]{1,0:T(8,128)(2,1)S(1)}, u32[]{:S(2)}, u32[]{:S(2)}) collective-permute-start(bf16[96,768]{1,0:T(8,128)(2,1)S(1)} %get-tuple-element.152), channel_id=1, source_target_pairs={{0,1},{1,0},{2,3},{3,2},{4,5},{5,4},{6,7},{7,6},{8,9},{9,8},{10,11... | collective-permute-start | bytes 442376 | tf_op jit(solution)/shard_map/ppermute | solution.py:683
  114.3 3.2 %collective-permute-start.36 = (bf16[96,768]{1,0:T(8,128)(2,1)S(1)}, bf16[96,768]{1,0:T(8,128)(2,1)S(1)}, u32[]{:S(2)}, u32[]{:S(2)}) collective-permute-start(bf16[96,768]{1,0:T(8,128)(2,1)S(1)} %get-tuple-element.153), channel_id=1, source_target_pairs={{0,1},{1,0},{2,3},{3,2},{4,5},{5,4},{6,7},{7,6},{8,9},{9,8},{10,11... | collective-permute-start | bytes 442376 | tf_op jit(solution)/shard_map/ppermute | solution.py:683
  116.6 1.4 collective-permute-start.37
  116.6 9.9 %collective-permute-start.31 = (bf16[128,768]{1,0:T(8,128)(2,1)S(1)}, bf16[128,768]{1,0:T(8,128)(2,1)S(1)}, u32[]{:S(2)}, u32[]{:S(2)}) collective-permute-start(bf16[128,768]{1,0:T(8,128)(2,1)S(1)} %get-tuple-element.148), channel_id=1, source_target_pairs={{0,2},{1,3},{2,0},{3,1},{4,6},{5,7},{6,4},{7,5},{8,10},{9,11},{10,... | collective-permute-start | bytes 589832 | tf_op jit(solution)/shard_map/ppermute | solution.py:686
  119.1 10.1 %collective-permute-start.43 = (bf16[192,384]{1,0:T(8,128)(2,1)S(1)}, bf16[192,384]{1,0:T(8,128)(2,1)S(1)}, u32[]{:S(2)}, u32[]{:S(2)}) collective-permute-start(bf16[192,384]{1,0:T(8,128)(2,1)S(1)} %get-tuple-element.156.refs_3_.refs_1_), channel_id=1, source_target_pairs={{0,4},{1,5},{2,6},{3,7},{4,0},{5,1},{6,2},{7,3},{8,12},{9,13},{10,... | collective-permute-start | bytes 442376 | tf_op jit(solution)/shard_map/ppermute | solution.py:686
  121.2 20.1 %collective-permute-start.39 = (bf16[224,768]{1,0:T(8,128)(2,1)S(1)}, bf16[224,768]{1,0:T(8,128)(2,1)S(1)}, u32[]{:S(2)}, u32[]{:S(2)}) collective-permute-start(bf16[224,768]{1,0:T(8,128)(2,1)S(1)} %get-tuple-element.161), channel_id=1, source_target_pairs={{0,8},{8,0},{16,24},{24,16},{1,9},{9,1},{17,25},{25,17},{2,10},{10... | collective-permute-start | bytes 1032200 | tf_op jit(solution)/shard_map/ppermute | solution.py:691
  122.4 18.9 %collective-permute-start.40 = (bf16[224,768]{1,0:T(8,128)(2,1)S(1)}, bf16[224,768]{1,0:T(8,128)(2,1)S(1)}, u32[]{:S(2)}, u32[]{:S(2)}) collective-permute-start(bf16[224,768]{1,0:T(8,128)(2,1)S(1)} %get-tuple-element.162), channel_id=1, source_target_pairs={{0,16},{8,24},{16,0},{24,8},{1,17},{9,25},{17,1},{25,9},{2,18},{10... | collective-permute-start | bytes 1032200 | tf_op jit(solution)/shard_map/ppermute | solution.py:691
  123.1 18.2 %collective-permute-start.41 = (bf16[224,768]{1,0:T(8,128)(2,1)S(1)}, bf16[224,768]{1,0:T(8,128)(2,1)S(1)}, u32[]{:S(2)}, u32[]{:S(2)}) collective-permute-start(bf16[224,768]{1,0:T(8,128)(2,1)S(1)} %get-tuple-element.163), channel_id=1, source_target_pairs={{0,24},{8,16},{16,8},{24,0},{1,25},{9,17},{17,9},{25,1},{2,26},{10... | collective-permute-start | bytes 1032200 | tf_op jit(solution)/shard_map/ppermute | solution.py:691
  126.5 6.1 %collective-permute-start.42 = (bf16[192,384]{1,0:T(8,128)(2,1)S(1)}, bf16[192,384]{1,0:T(8,128)(2,1)S(1)}, u32[]{:S(2)}, u32[]{:S(2)}) collective-permute-start(bf16[192,384]{1,0:T(8,128)(2,1)S(1)} %get-tuple-element.156.refs_3_.refs_1_), channel_id=1, source_target_pairs={{0,2},{1,3},{2,0},{3,1},{4,6},{5,7},{6,4},{7,5},{8,10},{9,11},{10,... | collective-permute-start | bytes 442376 | tf_op jit(solution)/shard_map/ppermute | solution.py:686
  129.1 11.2 %collective-permute-start.38 = (bf16[128,768]{1,0:T(8,128)(2,1)S(1)}, bf16[128,768]{1,0:T(8,128)(2,1)S(1)}, u32[]{:S(2)}, u32[]{:S(2)}) collective-permute-start(bf16[128,768]{1,0:T(8,128)(2,1)S(1)} %get-tuple-element.158), channel_id=1, source_target_pairs={{0,4},{1,5},{2,6},{3,7},{4,0},{5,1},{6,2},{7,3},{8,12},{9,13},{10,... | collective-permute-start | bytes 589832 | tf_op jit(solution)/shard_map/ppermute | solution.py:686
  132.6 8.7 %collective-permute-start.44 = (bf16[192,384]{1,0:T(8,128)(2,1)S(1)}, bf16[192,384]{1,0:T(8,128)(2,1)S(1)}, u32[]{:S(2)}, u32[]{:S(2)}) collective-permute-start(bf16[192,384]{1,0:T(8,128)(2,1)S(1)} %collective-permute-done.43.refs_3_), channel_id=1, source_target_pairs={{0,2},{1,3},{2,0},{3,1},{4,6},{5,7},{6,4},{7,5},{8,10},{9,11},{10,... | collective-permute-start | bytes 442376 | tf_op jit(solution)/shard_map/ppermute | solution.py:686
  142.2 20.5 %collective-permute-start.46 = (bf16[288,768]{1,0:T(8,128)(2,1)S(1)}, bf16[288,768]{1,0:T(8,128)(2,1)S(1)}, u32[]{:S(2)}, u32[]{:S(2)}) collective-permute-start(bf16[288,768]{1,0:T(8,128)(2,1)S(1)} %shares.1.refs_1_), channel_id=1, source_target_pairs={{0,4},{1,5},{2,6},{3,7},{4,0},{5,1},{6,2},{7,3},{8,12},{9,13},{10,... | collective-permute-start | bytes 1327112 | tf_op jit(solution)/shard_map/ppermute | solution.py:686
  142.4 20.4 %collective-permute-start.45 = (bf16[288,768]{1,0:T(8,128)(2,1)S(1)}, bf16[288,768]{1,0:T(8,128)(2,1)S(1)}, u32[]{:S(2)}, u32[]{:S(2)}) collective-permute-start(bf16[288,768]{1,0:T(8,128)(2,1)S(1)} %shares.1.refs_1_), channel_id=1, source_target_pairs={{0,2},{1,3},{2,0},{3,1},{4,6},{5,7},{6,4},{7,5},{8,10},{9,11},{10,... | collective-permute-start | bytes 1327112 | tf_op jit(solution)/shard_map/ppermute | solution.py:686
  144.9 1.4 collective-permute-start.47
  144.9 2.6 %collective-permute-start.49 = (bf16[192,384]{1,0:T(8,128)(2,1)S(1)}, bf16[192,384]{1,0:T(8,128)(2,1)S(1)}, u32[]{:S(2)}, u32[]{:S(2)}) collective-permute-start(bf16[192,384]{1,0:T(8,128)(2,1)S(1)} %collective-permute-done.43.refs_3_), channel_id=1, source_target_pairs={{0,1},{1,0},{2,3},{3,2},{4,5},{5,4},{6,7},{7,6},{8,9},{9,8},{10,11... | collective-permute-start | bytes 442376 | tf_op jit(solution)/shard_map/ppermute | solution.py:683
  145.4 2.1 %collective-permute-start.48 = (bf16[192,384]{1,0:T(8,128)(2,1)S(1)}, bf16[192,384]{1,0:T(8,128)(2,1)S(1)}, u32[]{:S(2)}, u32[]{:S(2)}) collective-permute-start(bf16[192,384]{1,0:T(8,128)(2,1)S(1)} %collective-permute-done.42.refs_5_.refs_2_), channel_id=1, source_target_pairs={{0,1},{1,0},{2,3},{3,2},{4,5},{5,4},{6,7},{7,6},{8,9},{9,8},{10,11... | collective-permute-start | bytes 442376 | tf_op jit(solution)/shard_map/ppermute | solution.py:683
  146.3 1.4 collective-permute-start.50
  162.9 11.9 %collective-permute-start.51 = (bf16[288,768]{1,0:T(8,128)(2,1)S(1)}, bf16[288,768]{1,0:T(8,128)(2,1)S(1)}, u32[]{:S(2)}, u32[]{:S(2)}) collective-permute-start(bf16[288,768]{1,0:T(8,128)(2,1)S(1)} %pass_on.1), channel_id=1, source_target_pairs={{0,2},{1,3},{2,0},{3,1},{4,6},{5,7},{6,4},{7,5},{8,10},{9,11},{10,... | collective-permute-start | bytes 1327112 | tf_op jit(solution)/shard_map/ppermute | solution.py:686
  162.9 11.8 %collective-permute-start.52 = (bf16[288,768]{1,0:T(8,128)(2,1)S(1)}, bf16[288,768]{1,0:T(8,128)(2,1)S(1)}, u32[]{:S(2)}, u32[]{:S(2)}) collective-permute-start(bf16[288,768]{1,0:T(8,128)(2,1)S(1)} %shares.1.refs_1_), channel_id=1, source_target_pairs={{0,1},{1,0},{2,3},{3,2},{4,5},{5,4},{6,7},{7,6},{8,9},{9,8},{10,11... | collective-permute-start | bytes 1327112 | tf_op jit(solution)/shard_map/ppermute | solution.py:683
  163.0 11.8 %collective-permute-start.54 = (bf16[288,768]{1,0:T(8,128)(2,1)S(1)}, bf16[288,768]{1,0:T(8,128)(2,1)S(1)}, u32[]{:S(2)}, u32[]{:S(2)}) collective-permute-start(bf16[288,768]{1,0:T(8,128)(2,1)S(1)} %collective-permute-done.46.refs_0_.refs_3_), channel_id=1, source_target_pairs={{0,1},{1,0},{2,3},{3,2},{4,5},{5,4},{6,7},{7,6},{8,9},{9,8},{10,11... | collective-permute-start | bytes 1327112 | tf_op jit(solution)/shard_map/ppermute | solution.py:683
  163.5 11.3 %collective-permute-start.53 = (bf16[288,768]{1,0:T(8,128)(2,1)S(1)}, bf16[288,768]{1,0:T(8,128)(2,1)S(1)}, u32[]{:S(2)}, u32[]{:S(2)}) collective-permute-start(bf16[288,768]{1,0:T(8,128)(2,1)S(1)} %collective-permute-done.45.refs_3_.refs_2_), channel_id=1, source_target_pairs={{0,1},{1,0},{2,3},{3,2},{4,5},{5,4},{6,7},{7,6},{8,9},{9,8},{10,11... | collective-permute-start | bytes 1327112 | tf_op jit(solution)/shard_map/ppermute | solution.py:683
  174.8 1.8 collective-permute-start.55
  (2 other events, 9.3 us)

commit v5 on v4

--- a/solution.py
+++ b/solution.py
@@ -642,7 +642,9 @@
         out_specs=tuple(pl.BlockSpec(memory_space=pltpu.VMEM) for _ in outs),
         scratch_shapes=list(scratch),
         compiler_params=pltpu.CompilerParams(vmem_limit_bytes=grant),
-        cost_estimate=pl.CostEstimate(flops=flops, bytes_accessed=moved, transcendentals=0),
+        cost_estimate=pl.CostEstimate(
+            flops=flops, bytes_accessed=moved if flops else 0, transcendentals=0
+        ),
         name=name,
     )(*args, *after)
 
@@ -1122,6 +1124,41 @@
         )
         out_far = core_swap(out_send)
 
+        fold = own_width // 2
+        rider = -(-sub // 32) * 16
+        pair_rows = fold // 2
+        at_outs = slice(half_own, half_own + pair_rows)
+
+        def fold_in(value):
+            down = value.shape[0] // 2
+            return jnp.concatenate([value[0:down], value[down:]], axis=1)
+
+        def fold_out(value):
+            across = value.shape[1] // 2
+            return jnp.concatenate([value[:, 0:across], value[:, across:]], axis=0)
+
+        def out_halves_kernel(info_ref, keep_ref, far_ref, own_ref, send_ref, scr):
+            mine = info_ref[1] % 2
+            for to in range(seq_parts):
+                whole = fold_in(keep_ref[to].astype(f32) + far_ref[to].astype(f32))
+                scr[0] = whole[0:pair_rows]
+                scr[1] = whole[pair_rows:]
+                own_ref[to] = scr[mine]
+                send_ref[to] = scr[1 - mine].astype(bf)
+
+        oh_own, oh_send = local_call(
+            out_halves_kernel,
+            "output_halves",
+            [
+                shape_of((seq_parts, pair_rows, width), f32),
+                shape_of((seq_parts, pair_rows, width), bf),
+            ],
+            [info, out_keep, out_far],
+            scalars=1,
+            scratch=[pltpu.VMEM((2, pair_rows, width), f32)],
+        )
+        oh_far = chip_swap(oh_send, 1)
+
         def quarter_kernel(own_ref, far_ref, keep_ref, send_ref):
             keep_ref[...] = own_ref[0] + far_ref[0].astype(f32)
             send_ref[...] = (own_ref[1] + far_ref[1].astype(f32)).astype(bf)
@@ -1179,7 +1216,7 @@
             scalars=2,
             after=[rs_send_two, out_send],
             scratch=[pltpu.VMEM((2 * total, total), f32), pltpu.VMEM((total, hw), f32)],
-            flops=5 * 2 * head_count * 2 * total * total * HEAD_DIM,
+            flops=8 * 5 * 2 * head_count * 2 * total * total * HEAD_DIM,
             grant=VMEM_LARGE,
         )
         dkv_far = core_swap(dkv_send)
@@ -1216,7 +1253,7 @@
                 shape_of((8, 3 * hw), f32),
             ],
             [flat_dq, dkv_own, dkv_far, w_heads_full] + token_parts,
-            flops=2 * total * width * 3 * hw,
+            flops=0,
         )
         gt_keep, *gt_send, grad_mixed, first_sums, mixed_sums = nb_out
         gt_far = [chip_swap(member, 1) for member in gt_send]
@@ -1259,21 +1296,9 @@
                 pltpu.VMEM((width, 3 * hw), f32),
                 pltpu.VMEM((seq_parts, small_rows, own_width), f32),
             ],
-            flops=2 * total * width * 3 * hw,
+            flops=0,
         )
         in_far = [core_swap(member) for member in in_send]
-
-        fold = own_width // 2
-        rider = -(-sub // 32) * 16
-        at_outs = slice(half_own, half_own + fold)
-
-        def fold_in(value):
-            down = value.shape[0] // 2
-            return jnp.concatenate([value[0:down], value[down:]], axis=1)
-
-        def fold_out(value):
-            across = value.shape[1] // 2
-            return jnp.concatenate([value[:, 0:across], value[:, across:]], axis=0)
 
         res_parts = [results[0]] + [seq_swap(results[j], j) for j in others]
 
@@ -1307,20 +1332,18 @@
                 refs[j][0:half_own, :] = (
                     keep_ref[at].astype(f32) + far_scr[at].astype(f32)
                 ).astype(bf)
-                refs[j][at_outs, :] = fold_in(ok_ref[at].astype(f32) + of_ref[at].astype(f32)).astype(
-                    bf
-                )
+                refs[j][at_outs, :] = (ok_ref[at] + of_ref[at].astype(f32)).astype(bf)
                 piece = fold_in(scr[aligned(at, sub), :])
                 piece = jnp.concatenate(
                     [piece, jnp.zeros((rider - sub // 2, width), f32)], axis=0
                 )
-                refs[j][half_own + fold :, :] = piece.astype(bf)
+                refs[j][half_own + pair_rows :, :] = piece.astype(bf)
         dp_out = local_call(
             dp_pack_kernel,
             "owners",
-            [shape_of((half_own + fold + rider, width), bf)] * seq_parts
+            [shape_of((half_own + pair_rows + rider, width), bf)] * seq_parts
             + [shape_of((ff // parts, half_width), bf)],
-            [info, rs_own_two, rs_far_two, in_keep, out_keep, out_far] + in_far,
+            [info, rs_own_two, rs_far_two, in_keep, oh_own, oh_far] + in_far,
             scalars=1,
             scratch=[
                 pltpu.VMEM((own_width, half_ff), f32),
@@ -1373,20 +1396,21 @@
         def dp_sum_kernel(info_ref, *refs):
             owned = refs[:seq_parts]
             last_ref, scr = refs[seq_parts:]
-            whole = owned[0][0 : half_own + fold, :].astype(f32)
+            top = half_own + pair_rows
+            whole = owned[0][0:top, :].astype(f32)
             for j in others:
-                whole = whole + owned[j][0 : half_own + fold, :].astype(f32)
-            last_ref[0 : half_own + fold, :] = whole.astype(bf)
+                whole = whole + owned[j][0:top, :].astype(f32)
+            last_ref[0:top, :] = whole.astype(bf)
             for j in range(seq_parts):
                 place = jnp.bitwise_xor(info_ref[0], j)
-                piece = owned[j][half_own + fold :, :].astype(f32)
+                piece = owned[j][top:, :].astype(f32)
                 scr[aligned(place, sub), :] = fold_out(piece[0 : sub // 2])
-            last_ref[half_own + fold :, :] = fold_in(scr[...]).astype(bf)
+            last_ref[top:, :] = fold_in(scr[...]).astype(bf)
 
         (last_one,) = local_call(
             dp_sum_kernel,
             "shares",
-            [shape_of((half_own + 2 * fold, width), bf)],
+            [shape_of((half_own + pair_rows + fold, width), bf)],
             [info] + dp_parts,
             scalars=1,
             scratch=[pltpu.VMEM((own_width, half_ff), f32)],
@@ -1413,7 +1437,7 @@
         (last_two_on,) = local_call(
             pass_kernel,
             "pass_on",
-            [shape_of((half_own + 2 * fold, width), bf)],
+            [shape_of((half_own + pair_rows + fold, width), bf)],
             [last_two],
             after=[contract_done, tokens_done, last_one_far],
         )
@@ -1423,20 +1447,25 @@
 
         def last_kernel(info_ref, *refs):
             gin_ref, gout_ref, exp_ref = refs[2 * parts : 2 * parts + 3]
-            bias_ref, smalls, scr = refs[2 * parts + 3], refs[2 * parts + 4 : -1], refs[-1]
+            bias_ref, smalls, scr, out_scr = refs[2 * parts + 3], refs[2 * parts + 4 : -2], *refs[-2:]
             for flip in range(2):
                 half = jnp.bitwise_xor(info_ref[2], flip)
-                outs = jnp.zeros((fold, width), f32)
+                outs = [jnp.zeros((pair_rows, width), f32)] * 2
                 for k in range(parts):
                     at = jnp.bitwise_xor(info_ref[1], k)
                     piece = refs[flip * parts + k][...].astype(f32)
                     scr[at, aligned(half, half_own), :] = piece[0:half_own, 0 : 3 * hw]
-                    outs = outs + piece[at_outs]
-                    turned = fold_out(piece[half_own + fold :])
+                    outs[k % 2] = outs[k % 2] + piece[at_outs]
+                    turned = fold_out(piece[half_own + pair_rows :])
                     for j in range(seq_parts):
                         cols = pl.ds(pl.multiple_of(j * ff + half * half_ff, 128), half_ff)
                         exp_ref[aligned(at, sub), cols] = turned[j * sub : (j + 1) * sub]
-                gout_ref[:, aligned(half, half_width)] = fold_out(outs)
+                mine = info_ref[1] % 2
+                out_scr[mine] = outs[0]
+                out_scr[1 - mine] = outs[1]
+                gout_ref[:, aligned(half, half_width)] = fold_out(
+                    jnp.concatenate([out_scr[0], out_scr[1]], axis=0)
+                )
             for at in range(parts):
                 for base in range(3):
                     start = base * width + at * hw
@@ -1462,7 +1491,10 @@
             + [shape_of((own_width,), f32)] * 8,
             [info] + last_parts + last_far,
             scalars=1,
-            scratch=[pltpu.VMEM((parts, own_width, 3 * hw), f32)],
+            scratch=[
+                pltpu.VMEM((parts, own_width, 3 * hw), f32),
+                pltpu.VMEM((2, pair_rows, width), f32),
+            ],
             grant=VMEM_LARGE,
         )
         grad_input, grad_output, grad_expand, grad_expand_bias = last_out[:4]

time: 180 us -> 177 us (0.983)
  waiting for transfers between devices: 90.6 us -> 80.1 us
  starting transfers between devices: 50.6 us -> 56.4 us
    ppermute x20 -> x21, waiting for transfers between devices: 57.3 us -> 47.5 us  [chip_swap(): lax.ppermute(member, 'ctx', [(i, 2 * (i // 2 ^ step) + i % 2) for i in ra...]
    ppermute x20 -> x21, starting transfers between devices: 27 us -> 32.7 us  [chip_swap(): lax.ppermute(member, 'ctx', [(i, 2 * (i // 2 ^ step) + i % 2) for i in ra...]
    pallas_call x23 -> x24, Pallas kernels: 37.3 us -> 37.8 us  [local_call(): pl.pallas_call(ordered, out_shape=tuple(outs), in_specs=[pl.BlockSpec(mem...]
  transfers between devices with their start and end apart: 56 -> 57, of which waited for: 32 -> 30; matrix products, arithmetic and copies ran while one was open for 0% -> 0% of each run, Pallas kernels for 9% -> 13%
where the time goes in v5:
time: 177 us; the launch traced here: 176 us
  waiting for transfers between devices  80.1 us (45%)
  starting transfers between devices  56.4 us (32%)
  Pallas kernels  37.8 us (21%)
    ppermute x21, waiting for transfers between devices, chip_swap(): lax.ppermute(member, 'ctx', [(i, 2 * (i // 2 ^ step) + i % 2) for i in ra...  47.5 us
    pallas_call x24, Pallas kernels, local_call(): pl.pallas_call(ordered, out_shape=tuple(outs), in_specs=[pl.BlockSpec(mem...  37.8 us
    ppermute x21, starting transfers between devices, chip_swap(): lax.ppermute(member, 'ctx', [(i, 2 * (i // 2 ^ step) + i % 2) for i in ra...  32.7 us
    ppermute x18, waiting for transfers between devices, seq_swap(): return lax.ppermute(member, 'dp', [(i, i ^ step) for i in range(seq_parts)])  24.7 us
    ppermute x18, starting transfers between devices, seq_swap(): return lax.ppermute(member, 'dp', [(i, i ^ step) for i in range(seq_parts)])  21.4 us
    ppermute x18, waiting for transfers between devices, core_swap(): return lax.ppermute(member, 'ctx', [(i, i ^ 1) for i in range(ranks)])  7.93 us
  transfers between devices with their start and end apart: 57, of which 30 were waited for; matrix products, arithmetic and copies ran while one was open for 0% of the time, Pallas kernels for 13%

profile of v5, /device:TPU:0, one launch (start us, length us, event | category | flops | bytes accessed | tf_op | source)
XLA Modules:
  0.0 176.2 jit_solution(17456486079965179416)
XLA Ops:
  1.3 2.8 %pack.1 = (bf16[192,768]{1,0:T(8,128)(2,1)}, bf16[128,768]{1,0:T(8,128)(2,1)}) custom-call(s32[3]{0:T(128)} %pad_add_fusion.refs_0_, bf16[128,768]{1,0:T(8,128)(2,1)} %bitcast.8, bf16[192,2304]{1,0:T(8,128)(2,1)} %refs_1_.5, bf16[192,768]{1,0:T(8,128)(2,1)} %refs_2_.4, bf16[192]{0:T(256)(128)(2,1)} %refs_4_.1, bf16[192]{0:T(256)(128)(2,1)} %refs_5_.1, ...), custom_call_target="tpu_custom_call" | custom-call | tf_op jit(solution)/shard_map/pack/pallas_call | solution.py:636
  4.0 4.1 %collective-permute-start.1 = (bf16[128,768]{1,0:T(8,128)(2,1)}, bf16[128,768]{1,0:T(8,128)(2,1)S(1)}, u32[]{:S(2)}, u32[]{:S(2)}) collective-permute-start(bf16[128,768]{1,0:T(8,128)(2,1)} %get-tuple-element.99.refs_3_.refs_1_.refs_4_.refs_0_), channel_id=1, source_target_pairs={{0,4},{1,5},{2,6},{3,7},{4,0},{5,1},{6,2},{7,3},{8,12},{9,13},{10,... | collective-permute-start | bytes 589832 | tf_op jit(solution)/shard_map/ppermute | solution.py:688
  8.2 2.5 %collective-permute-start.5 = (bf16[192,768]{1,0:T(8,128)(2,1)}, bf16[192,768]{1,0:T(8,128)(2,1)S(1)}, u32[]{:S(2)}, u32[]{:S(2)}) collective-permute-start(bf16[192,768]{1,0:T(8,128)(2,1)} %get-tuple-element.100.refs_7_.refs_3_), channel_id=1, source_target_pairs={{0,24},{8,16},{16,8},{24,0},{1,25},{9,17},{17,9},{25,1},{2,26},{10... | collective-permute-start | bytes 884744 | tf_op jit(solution)/shard_map/ppermute | solution.py:693
  11.7 1.6 collective-permute-start
  13.3 4.3 %collective-permute-done.1.refs_4_.refs_5_.refs_6_ = bf16[128,768]{1,0:T(8,128)(2,1)S(1)} collective-permute-done((bf16[128,768]{1,0:T(8,128)(2,1)}, bf16[128,768]{1,0:T(8,128)(2,1)S(1)}, u32[]{:S(2)}, u32[]{:S(2)}) %collective-permute-start.1) | collective-permute-done | bytes 196640 | tf_op jit(solution)/shard_map/ppermute | solution.py:688
  18.3 3.2 %collective-permute-done.refs_3_.refs_4_.refs_5_ = bf16[128,768]{1,0:T(8,128)(2,1)S(1)} collective-permute-done((bf16[128,768]{1,0:T(8,128)(2,1)}, bf16[128,768]{1,0:T(8,128)(2,1)S(1)}, u32[]{:S(2)}, u32[]{:S(2)}) %collective-permute-start) | collective-permute-done | bytes 196640 | tf_op jit(solution)/shard_map/ppermute | solution.py:688
  21.5 2.6 %collective-permute-done.4.refs_1_ = bf16[192,768]{1,0:T(8,128)(2,1)S(1)} collective-permute-done((bf16[192,768]{1,0:T(8,128)(2,1)}, bf16[192,768]{1,0:T(8,128)(2,1)S(1)}, u32[]{:S(2)}, u32[]{:S(2)}) %collective-permute-start.4) | collective-permute-done | bytes 294944 | tf_op jit(solution)/shard_map/ppermute | solution.py:693
  24.9 2.4 %collective-permute-done.6.refs_9_ = bf16[576,768]{1,0:T(8,128)(2,1)S(1)} collective-permute-done((bf16[576,768]{1,0:T(8,128)(2,1)S(1)}, bf16[576,768]{1,0:T(8,128)(2,1)S(1)}, u32[]{:S(2)}, u32[]{:S(2)}) %collective-permute-start.6) | collective-permute-done | bytes 884768 | tf_op jit(solution)/shard_map/ppermute | solution.py:685
  27.3 2.1 %project.1 = (bf16[512,192]{1,0:T(8,128)(2,1)S(1)}, bf16[512,384]{1,0:T(8,128)(2,1)S(1)}, bf16[512,768]{1,0:T(8,128)(2,1)S(1)}, bf16[768,576]{1,0:T(8,128)(2,1)S...) custom-call(s32[3]{0:T(128)S(1)} %copy-done.6, bf16[192,2304]{1,0:T(8,128)(2,1)S(1)} %copy-done, ...), custom_call_target="tpu_custom_call" | custom-call | flops 452984832 | bytes 7520268 | tf_op jit(solution)/shard_map/project/pallas_call | solution.py:636
  30.2 1.6 collective-permute-start.11
  31.9 1.5 collective-permute-start.12
  33.8 3.7 %attend.1 = (bf16[128,192]{1,0:T(8,128)(2,1)S(1)}, bf16[128,192]{1,0:T(8,128)(2,1)S(1)}, bf16[128,192]{1,0:T(8,128)(2,1)S(1)}, bf16[128,192]{1,0:T(8,128)(2,1)S(...) custom-call(s32[3]{0:T(128)S(1)} %copy-done.6, s32[8]{0:T(128)S(1)} %copy-done.9, ...), custom_call_target="tpu_custom_call" | custom-call | flops 402653184 | bytes 1589292 | tf_op jit(solution)/shard_map/attend/pallas_call | solution.py:636
  37.6 1.2 collective-permute-start.8
  38.8 2.6 %collective-permute-start.9 = (bf16[128,192]{1,0:T(8,128)(2,1)S(1)}, bf16[128,192]{1,0:T(8,128)(2,1)S(1)}, u32[]{:S(2)}, u32[]{:S(2)}) collective-permute-start(bf16[128,192]{1,0:T(8,128)(2,1)S(1)} %get-tuple-element.107), channel_id=1, source_target_pairs={{0,4},{1,5},{2,6},{3,7},{4,0},{5,1},{6,2},{7,3},{8,12},{9,13},{10,... | collective-permute-start | bytes 147464 | tf_op jit(solution)/shard_map/ppermute | solution.py:688
  41.4 1.0 collective-permute-done.8.refs_5_.refs_3_
  42.4 2.9 %collective-permute-start.10 = (bf16[128,192]{1,0:T(8,128)(2,1)S(1)}, bf16[128,192]{1,0:T(8,128)(2,1)S(1)}, u32[]{:S(2)}, u32[]{:S(2)}) collective-permute-start(bf16[128,192]{1,0:T(8,128)(2,1)S(1)} %get-tuple-element.108), channel_id=1, source_target_pairs={{0,6},{1,7},{2,4},{3,5},{4,2},{5,3},{6,0},{7,1},{8,14},{9,15},{10,... | collective-permute-start | bytes 147464 | tf_op jit(solution)/shard_map/ppermute | solution.py:688
  45.3 3.1 %collective-permute-done.10.refs_7_.refs_5_ = bf16[128,192]{1,0:T(8,128)(2,1)S(1)} collective-permute-done((bf16[128,192]{1,0:T(8,128)(2,1)S(1)}, bf16[128,192]{1,0:T(8,128)(2,1)S(1)}, u32[]{:S(2)}, u32[]{:S(2)}) %collective-permute-start.10) | collective-permute-done | bytes 49184 | tf_op jit(solution)/shard_map/ppermute | solution.py:688
  48.5 1.1 middle.1
  49.7 2.6 %collective-permute-start.17 = (bf16[128,768]{1,0:T(8,128)(2,1)S(1)}, bf16[128,768]{1,0:T(8,128)(2,1)S(1)}, u32[]{:S(2)}, u32[]{:S(2)}) collective-permute-start(bf16[128,768]{1,0:T(8,128)(2,1)S(1)} %get-tuple-element.113.refs_3_.refs_6_), channel_id=1, source_target_pairs={{0,24},{8,16},{16,8},{24,0},{1,25},{9,17},{17,9},{25,1},{2,26},{10... | collective-permute-start | bytes 589832 | tf_op jit(solution)/shard_map/ppermute | solution.py:693
  53.3 5.2 %collective-permute-done.17.refs_9_ = bf16[128,768]{1,0:T(8,128)(2,1)S(1)} collective-permute-done((bf16[128,768]{1,0:T(8,128)(2,1)S(1)}, bf16[128,768]{1,0:T(8,128)(2,1)S(1)}, u32[]{:S(2)}, u32[]{:S(2)}) %collective-permute-start.17) | collective-permute-done | bytes 196640 | tf_op jit(solution)/shard_map/ppermute | solution.py:693
  58.5 3.7 %collective-permute-done.16.refs_8_ = bf16[128,768]{1,0:T(8,128)(2,1)S(1)} collective-permute-done((bf16[128,768]{1,0:T(8,128)(2,1)S(1)}, bf16[128,768]{1,0:T(8,128)(2,1)S(1)}, u32[]{:S(2)}, u32[]{:S(2)}) %collective-permute-start.16) | collective-permute-done | bytes 196640 | tf_op jit(solution)/shard_map/ppermute | solution.py:693
  62.3 5.6 %feed.1 = (bf16[128,768]{1,0:T(8,128)(2,1)S(1)}, bf16[128,768]{1,0:T(8,128)(2,1)S(1)}, bf16[128,768]{1,0:T(8,128)(2,1)S(1)}, bf16[128,768]{1,0:T(8,128)(2,1)S(1)...) custom-call(s32[3]{0:T(128)S(1)} %copy-done.6, ...), custom_call_target="tpu_custom_call" | custom-call | flops 3623878656 | bytes 8753676 | tf_op jit(solution)/shard_map/feed/pallas_call | solution.py:636
  68.0 2.8 %collective-permute-done.24.refs_2_ = bf16[4,384,384]{2,1,0:T(8,128)(2,1)S(1)} collective-permute-done((bf16[4,384,384]{2,1,0:T(8,128)(2,1)S(1)}, bf16[4,384,384]{2,1,0:T(8,128)(2,1)S(1)}, u32[]{:S(2)}, u32[]{:S(2)}) %collective-permute-start.24) | collective-permute-done | bytes 1179680 | tf_op jit(solution)/shard_map/ppermute | solution.py:685
  70.9 0.8 feed_halves.1
  72.4 1.0 collective-permute-start.21
  73.3 1.0 collective-permute-start.22
  74.3 1.5 collective-permute-start.23
  75.8 4.3 %collective-permute-done.21.refs_6_ = bf16[128,768]{1,0:T(8,128)(2,1)S(1)} collective-permute-done((bf16[128,768]{1,0:T(8,128)(2,1)S(1)}, bf16[128,768]{1,0:T(8,128)(2,1)S(1)}, u32[]{:S(2)}, u32[]{:S(2)}) %collective-permute-start.21) | collective-permute-done | bytes 196640 | tf_op jit(solution)/shard_map/ppermute | solution.py:693
  80.1 4.0 %collective-permute-done.22.refs_7_ = bf16[128,768]{1,0:T(8,128)(2,1)S(1)} collective-permute-done((bf16[128,768]{1,0:T(8,128)(2,1)S(1)}, bf16[128,768]{1,0:T(8,128)(2,1)S(1)}, u32[]{:S(2)}, u32[]{:S(2)}) %collective-permute-start.22) | collective-permute-done | bytes 196640 | tf_op jit(solution)/shard_map/ppermute | solution.py:693
  84.2 1.4 middle_back.1
  85.6 2.9 %collective-permute-start.27 = (bf16[128,192]{1,0:T(8,128)(2,1)S(1)}, bf16[128,192]{1,0:T(8,128)(2,1)S(1)}, u32[]{:S(2)}, u32[]{:S(2)}) collective-permute-start(bf16[128,192]{1,0:T(8,128)(2,1)S(1)} %get-tuple-element.131), channel_id=1, source_target_pairs={{0,6},{1,7},{2,4},{3,5},{4,2},{5,3},{6,0},{7,1},{8,14},{9,15},{10,... | collective-permute-start | bytes 147464 | tf_op jit(solution)/shard_map/ppermute | solution.py:688
  90.1 1.0 output_weights.1
  92.0 1.3 collective-permute-done.25.refs_8_
  93.3 1.2 collective-permute-done.26.refs_9_
  94.5 5.0 %attend_back.1 = (f32[192,512]{1,0:T(8,128)S(1)}, f32[512,384]{1,0:T(8,128)S(1)}, bf16[512,384]{1,0:T(8,128)(2,1)S(1)}) custom-call(s32[3]{0:T(128)S(1)} %copy-done.6, s32[8]{0:T(128)S(1)} %copy-done.9, bf16[512,192]{1,0:T(8,128)(2,1)S(1)} %get-tuple-element.103.refs_2_, bf16[512,384]{1,0:T(8,128)(2,1)S(1)} %get-tuple-element.104.refs_3_, ...), custom_call_target="tpu_custom_call" | custom-call | flops 8053063680 | bytes 3162156 | tf_op jit(solution)/shard_map/attend_back/pallas_call | solution.py:636
  100.2 1.2 collective-permute-start.32
  102.1 2.1 %collective-permute-start.34 = (bf16[4,48,768]{2,1,0:T(8,128)(2,1)S(1)}, bf16[4,48,768]{2,1,0:T(8,128)(2,1)S(1)}, u32[]{:S(2)}, u32[]{:S(2)}) collective-permute-start(bf16[4,48,768]{2,1,0:T(8,128)(2,1)S(1)} %get-tuple-element.154), channel_id=1, source_target_pairs={{0,2},{1,3},{2,0},{3,1},{4,6},{5,7},{6,4},{7,5},{8,10},{9,11},{10,... | collective-permute-start | bytes 884744 | tf_op jit(solution)/shard_map/ppermute | solution.py:688
  104.2 1.3 collective-permute-start.19
  105.5 1.3 collective-permute-start.20
  106.9 1.8 %normed_back.1 = (f32[2,128,768]{2,1,0:T(8,128)S(1)}, bf16[128,768]{1,0:T(8,128)(2,1)S(1)}, bf16[128,768]{1,0:T(8,128)(2,1)S(1)}, bf16[512,576]{1,0:T(8,128)(2,1...) custom-call(f32[192,512]{1,0:T(8,128)S(1)} %get-tuple-element.136.refs_0_, f32[512,384]{1,0:T(8,128)S(1)} %get-tuple-element.137.refs_1_, ...), custom_call_target="tpu_custom_call" | custom-call | tf_op jit(solution)/shard_map/normed_back/pallas_call | solution.py:636
  108.7 1.5 input_weights.1
  110.3 4.6 %collective-permute-done.19.refs_4_ = bf16[128,768]{1,0:T(8,128)(2,1)S(1)} collective-permute-done((bf16[128,768]{1,0:T(8,128)(2,1)S(1)}, bf16[128,768]{1,0:T(8,128)(2,1)S(1)}, u32[]{:S(2)}, u32[]{:S(2)}) %collective-permute-start.19) | collective-permute-done | bytes 196640 | tf_op jit(solution)/shard_map/ppermute | solution.py:693
  115.4 1.2 collective-permute-done.32.refs_2_
  116.8 2.0 %collective-permute-start.31 = (bf16[128,768]{1,0:T(8,128)(2,1)S(1)}, bf16[128,768]{1,0:T(8,128)(2,1)S(1)}, u32[]{:S(2)}, u32[]{:S(2)}) collective-permute-start(bf16[128,768]{1,0:T(8,128)(2,1)S(1)} %get-tuple-element.150), channel_id=1, source_target_pairs={{0,2},{1,3},{2,0},{3,1},{4,6},{5,7},{6,4},{7,5},{8,10},{9,11},{10,... | collective-permute-start | bytes 589832 | tf_op jit(solution)/shard_map/ppermute | solution.py:688
  119.7 0.9 owners.1
  120.6 1.5 collective-permute-start.44
  122.1 2.0 %collective-permute-start.43 = (bf16[192,384]{1,0:T(8,128)(2,1)S(1)}, bf16[192,384]{1,0:T(8,128)(2,1)S(1)}, u32[]{:S(2)}, u32[]{:S(2)}) collective-permute-start(bf16[192,384]{1,0:T(8,128)(2,1)S(1)} %get-tuple-element.160.refs_3_.refs_1_), channel_id=1, source_target_pairs={{0,2},{1,3},{2,0},{3,1},{4,6},{5,7},{6,4},{7,5},{8,10},{9,11},{10,... | collective-permute-start | bytes 442376 | tf_op jit(solution)/shard_map/ppermute | solution.py:688
  124.1 1.5 collective-permute-start.40
  125.6 2.1 %collective-permute-done.30.refs_1_ = bf16[128,768]{1,0:T(8,128)(2,1)S(1)} collective-permute-done((bf16[128,768]{1,0:T(8,128)(2,1)S(1)}, bf16[128,768]{1,0:T(8,128)(2,1)S(1)}, u32[]{:S(2)}, u32[]{:S(2)}) %collective-permute-start.30) | collective-permute-done | bytes 196640 | tf_op jit(solution)/shard_map/ppermute | solution.py:688
  127.7 1.3 collective-permute-start.41
  129.0 3.0 %collective-permute-done.31.refs_2_ = bf16[128,768]{1,0:T(8,128)(2,1)S(1)} collective-permute-done((bf16[128,768]{1,0:T(8,128)(2,1)S(1)}, bf16[128,768]{1,0:T(8,128)(2,1)S(1)}, u32[]{:S(2)}, u32[]{:S(2)}) %collective-permute-start.31) | collective-permute-done | bytes 196640 | tf_op jit(solution)/shard_map/ppermute | solution.py:688
  131.9 1.3 collective-permute-start.42
  133.3 1.2 collective-permute-start.39
  134.5 2.5 %collective-permute-start.45 = (bf16[192,384]{1,0:T(8,128)(2,1)S(1)}, bf16[192,384]{1,0:T(8,128)(2,1)S(1)}, u32[]{:S(2)}, u32[]{:S(2)}) collective-permute-start(bf16[192,384]{1,0:T(8,128)(2,1)S(1)} %collective-permute-done.44.refs_3_), channel_id=1, source_target_pairs={{0,2},{1,3},{2,0},{3,1},{4,6},{5,7},{6,4},{7,5},{8,10},{9,11},{10,... | collective-permute-start | bytes 442376 | tf_op jit(solution)/shard_map/ppermute | solution.py:688
  137.0 6.5 %collective-permute-done.39.refs_4_.refs_7_ = bf16[128,768]{1,0:T(8,128)(2,1)S(1)} collective-permute-done((bf16[128,768]{1,0:T(8,128)(2,1)S(1)}, bf16[128,768]{1,0:T(8,128)(2,1)S(1)}, u32[]{:S(2)}, u32[]{:S(2)}) %collective-permute-start.39) | collective-permute-done | bytes 196640 | tf_op jit(solution)/shard_map/ppermute | solution.py:688
  144.6 1.5 collective-permute-start.46
  146.6 0.9 collective-permute-done.48.refs_5_
  147.6 1.1 tokens_back.1
  148.9 2.1 %contract_final.1 = (f32[768,768]{1,0:T(8,128)}, f32[8,128]{1,0:T(8,128)S(1)}) custom-call(s32[3]{0:T(128)S(1)} %copy-done.6, bf16[192,384]{1,0:T(8,128)(2,1)S(1)} %get-tuple-element.160.refs_3_.refs_1_, bf16[192,384]{1,0:T(8,128)(2,1)S(1)} %collective-permute-done.43.refs_5_.refs_2_, bf16[192,384]{1,0:T(8,128)(2,1)S(1)} %collective-permute-done.44.refs_3_, ...), custom_call_target="tpu_custom_call" | custom-call | tf_op jit(solution)/shard_map/contract_final/pallas_call | solution.py:636
  151.0 8.8 %collective-permute-done.47.refs_0_.refs_3_ = bf16[240,768]{1,0:T(8,128)(2,1)S(1)} collective-permute-done((bf16[240,768]{1,0:T(8,128)(2,1)S(1)}, bf16[240,768]{1,0:T(8,128)(2,1)S(1)}, u32[]{:S(2)}, u32[]{:S(2)}) %collective-permute-start.47) | collective-permute-done | bytes 368672 | tf_op jit(solution)/shard_map/ppermute | solution.py:688
  159.8 2.2 %collective-permute-done.46.refs_3_.refs_2_ = bf16[240,768]{1,0:T(8,128)(2,1)S(1)} collective-permute-done((bf16[240,768]{1,0:T(8,128)(2,1)S(1)}, bf16[240,768]{1,0:T(8,128)(2,1)S(1)}, u32[]{:S(2)}, u32[]{:S(2)}) %collective-permute-start.46) | collective-permute-done | bytes 368672 | tf_op jit(solution)/shard_map/ppermute | solution.py:688
  162.9 8.0 %collective-permute-done.52.refs_4_ = bf16[240,768]{1,0:T(8,128)(2,1)S(1)} collective-permute-done((bf16[240,768]{1,0:T(8,128)(2,1)S(1)}, bf16[240,768]{1,0:T(8,128)(2,1)S(1)}, u32[]{:S(2)}, u32[]{:S(2)}) %collective-permute-start.52) | collective-permute-done | bytes 368672 | tf_op jit(solution)/shard_map/ppermute | solution.py:688
  170.9 1.7 collective-permute-done.56.refs_8_
  172.5 3.5 %weights_final.1 = (f32[192,2304]{1,0:T(8,128)}, f32[192,768]{1,0:T(8,128)}, f32[192,3072]{1,0:T(8,128)}, f32[768]{0:T(1024)}, f32[192]{0:T(256)}, /*index=5*/f3...) custom-call(s32[3]{0:T(128)S(1)} %copy-done.6, ...), custom_call_target="tpu_custom_call" | custom-call | tf_op jit(solution)/shard_map/weights_final/pallas_call | solution.py:636
  (95 shorter events, 14.7 us)
Async XLA Ops:
  4.0 13.5 %collective-permute-start.1 = (bf16[128,768]{1,0:T(8,128)(2,1)}, bf16[128,768]{1,0:T(8,128)(2,1)S(1)}, u32[]{:S(2)}, u32[]{:S(2)}) collective-permute-start(bf16[128,768]{1,0:T(8,128)(2,1)} %get-tuple-element.99.refs_3_.refs_1_.refs_4_.refs_0_), channel_id=1, source_target_pairs={{0,4},{1,5},{2,6},{3,7},{4,0},{5,1},{6,2},{7,3},{8,12},{9,13},{10,... | collective-permute-start | bytes 589832 | tf_op jit(solution)/shard_map/ppermute | solution.py:688
  8.2 19.1 %copy-start = (bf16[192,2304]{1,0:T(8,128)(2,1)S(1)}, bf16[192,2304]{1,0:T(8,128)(2,1)}, u32[]{:S(2)}) copy-start(bf16[192,2304]{1,0:T(8,128)(2,1)} %refs_1_.5) | copy-start | bytes 2654212
  8.2 19.1 %copy-start.1 = (bf16[128,768]{1,0:T(8,128)(2,1)S(1)}, bf16[128,768]{1,0:T(8,128)(2,1)}, u32[]{:S(2)}) copy-start(bf16[128,768]{1,0:T(8,128)(2,1)} %get-tuple-element.99.refs_3_.refs_1_.refs_4_.refs_0_) | copy-start | bytes 589828
  8.2 19.1 %copy-start.2 = (bf16[192,768]{1,0:T(8,128)(2,1)S(1)}, bf16[192,768]{1,0:T(8,128)(2,1)}, u32[]{:S(2)}) copy-start(bf16[192,768]{1,0:T(8,128)(2,1)} %refs_2_.4) | copy-start | bytes 884740
  8.2 19.1 %copy-start.3 = (bf16[192,768]{1,0:T(8,128)(2,1)S(1)}, bf16[192,768]{1,0:T(8,128)(2,1)}, u32[]{:S(2)}) copy-start(bf16[192,768]{1,0:T(8,128)(2,1)} %get-tuple-element.100.refs_7_.refs_3_) | copy-start | bytes 884740
  8.2 19.1 %copy-start.6 = (s32[3]{0:T(128)S(1)}, s32[3]{0:T(128)}, u32[]{:S(2)}) copy-start(s32[3]{0:T(128)} %pad_add_fusion.refs_0_) | copy-start | bytes 40
  8.2 13.3 %collective-permute-start.5 = (bf16[192,768]{1,0:T(8,128)(2,1)}, bf16[192,768]{1,0:T(8,128)(2,1)S(1)}, u32[]{:S(2)}, u32[]{:S(2)}) collective-permute-start(bf16[192,768]{1,0:T(8,128)(2,1)} %get-tuple-element.100.refs_7_.refs_3_), channel_id=1, source_target_pairs={{0,24},{8,16},{16,8},{24,0},{1,25},{9,17},{17,9},{25,1},{2,26},{10... | collective-permute-start | bytes 884744 | tf_op jit(solution)/shard_map/ppermute | solution.py:693
  10.7 13.4 %collective-permute-start.4 = (bf16[192,768]{1,0:T(8,128)(2,1)}, bf16[192,768]{1,0:T(8,128)(2,1)S(1)}, u32[]{:S(2)}, u32[]{:S(2)}) collective-permute-start(bf16[192,768]{1,0:T(8,128)(2,1)} %get-tuple-element.100.refs_7_.refs_3_), channel_id=1, source_target_pairs={{0,16},{8,24},{16,0},{24,8},{1,17},{9,25},{17,1},{25,9},{2,18},{10... | collective-permute-start | bytes 884744 | tf_op jit(solution)/shard_map/ppermute | solution.py:693
  11.2 13.0 %collective-permute-start.3 = (bf16[192,768]{1,0:T(8,128)(2,1)}, bf16[192,768]{1,0:T(8,128)(2,1)S(1)}, u32[]{:S(2)}, u32[]{:S(2)}) collective-permute-start(bf16[192,768]{1,0:T(8,128)(2,1)} %get-tuple-element.100.refs_7_.refs_3_), channel_id=1, source_target_pairs={{0,8},{8,0},{16,24},{24,16},{1,9},{9,1},{17,25},{25,17},{2,10},{10... | collective-permute-start | bytes 884744 | tf_op jit(solution)/shard_map/ppermute | solution.py:693
  11.7 9.8 %collective-permute-start = (bf16[128,768]{1,0:T(8,128)(2,1)}, bf16[128,768]{1,0:T(8,128)(2,1)S(1)}, u32[]{:S(2)}, u32[]{:S(2)}) collective-permute-start(bf16[128,768]{1,0:T(8,128)(2,1)} %get-tuple-element.99.refs_3_.refs_1_.refs_4_.refs_0_), channel_id=1, source_target_pairs={{0,2},{1,3},{2,0},{3,1},{4,6},{5,7},{6,4},{7,5},{8,10},{9,11},{10,... | collective-permute-start | bytes 589832 | tf_op jit(solution)/shard_map/ppermute | solution.py:688
  17.6 7.1 %collective-permute-start.2 = (bf16[128,768]{1,0:T(8,128)(2,1)S(1)}, bf16[128,768]{1,0:T(8,128)(2,1)S(1)}, u32[]{:S(2)}, u32[]{:S(2)}) collective-permute-start(bf16[128,768]{1,0:T(8,128)(2,1)S(1)} %collective-permute-done.1.refs_4_.refs_5_.refs_6_), channel_id=1, source_target_pairs={{0,2},{1,3},{2,0},{3,1},{4,6},{5,7},{6,4},{7,5},{8,10},{9,11},{10,... | collective-permute-start | bytes 589832 | tf_op jit(solution)/shard_map/ppermute | solution.py:688
  24.8 2.5 %collective-permute-start.6 = (bf16[576,768]{1,0:T(8,128)(2,1)S(1)}, bf16[576,768]{1,0:T(8,128)(2,1)S(1)}, u32[]{:S(2)}, u32[]{:S(2)}) collective-permute-start(bf16[576,768]{1,0:T(8,128)(2,1)S(1)} %pack_stack.1.refs_8_), channel_id=1, source_target_pairs={{0,1},{1,0},{2,3},{3,2},{4,5},{5,4},{6,7},{7,6},{8,9},{9,8},{10,11... | collective-permute-start | bytes 2654216 | tf_op jit(solution)/shard_map/ppermute | solution.py:685
  29.4 4.4 %collective-permute-start.7 = (bf16[512,384]{1,0:T(8,128)(2,1)S(1)}, bf16[512,384]{1,0:T(8,128)(2,1)S(1)}, u32[]{:S(2)}, u32[]{:S(2)}) collective-permute-start(bf16[512,384]{1,0:T(8,128)(2,1)S(1)} %get-tuple-element.104.refs_3_), channel_id=1, source_target_pairs={{0,1},{1,0},{2,3},{3,2},{4,5},{5,4},{6,7},{7,6},{8,9},{9,8},{10,11... | collective-permute-start | bytes 1179656 | tf_op jit(solution)/shard_map/ppermute | solution.py:685
  30.2 19.4 %collective-permute-start.11 = (bf16[224,768]{1,0:T(8,128)(2,1)S(1)}, bf16[224,768]{1,0:T(8,128)(2,1)S(1)}, u32[]{:S(2)}, u32[]{:S(2)}) collective-permute-start(bf16[224,768]{1,0:T(8,128)(2,1)S(1)} %get-tuple-element.110), channel_id=1, source_target_pairs={{0,8},{8,0},{16,24},{24,16},{1,9},{9,1},{17,25},{25,17},{2,10},{10... | collective-permute-start | bytes 1032200 | tf_op jit(solution)/shard_map/ppermute | solution.py:693
  31.9 17.7 %collective-permute-start.12 = (bf16[224,768]{1,0:T(8,128)(2,1)S(1)}, bf16[224,768]{1,0:T(8,128)(2,1)S(1)}, u32[]{:S(2)}, u32[]{:S(2)}) collective-permute-start(bf16[224,768]{1,0:T(8,128)(2,1)S(1)} %get-tuple-element.111), channel_id=1, source_target_pairs={{0,16},{8,24},{16,0},{24,8},{1,17},{9,25},{17,1},{25,9},{2,18},{10... | collective-permute-start | bytes 1032200 | tf_op jit(solution)/shard_map/ppermute | solution.py:693
  33.4 16.2 %collective-permute-start.13 = (bf16[224,768]{1,0:T(8,128)(2,1)S(1)}, bf16[224,768]{1,0:T(8,128)(2,1)S(1)}, u32[]{:S(2)}, u32[]{:S(2)}) collective-permute-start(bf16[224,768]{1,0:T(8,128)(2,1)S(1)} %get-tuple-element.112), channel_id=1, source_target_pairs={{0,24},{8,16},{16,8},{24,0},{1,25},{9,17},{17,9},{25,1},{2,26},{10... | collective-permute-start | bytes 1032200 | tf_op jit(solution)/shard_map/ppermute | solution.py:693
  37.6 4.8 %collective-permute-start.8 = (bf16[128,192]{1,0:T(8,128)(2,1)S(1)}, bf16[128,192]{1,0:T(8,128)(2,1)S(1)}, u32[]{:S(2)}, u32[]{:S(2)}) collective-permute-start(bf16[128,192]{1,0:T(8,128)(2,1)S(1)} %get-tuple-element.106), channel_id=1, source_target_pairs={{0,2},{1,3},{2,0},{3,1},{4,6},{5,7},{6,4},{7,5},{8,10},{9,11},{10,... | collective-permute-start | bytes 147464 | tf_op jit(solution)/shard_map/ppermute | solution.py:688
  38.8 6.6 %collective-permute-start.9 = (bf16[128,192]{1,0:T(8,128)(2,1)S(1)}, bf16[128,192]{1,0:T(8,128)(2,1)S(1)}, u32[]{:S(2)}, u32[]{:S(2)}) collective-permute-start(bf16[128,192]{1,0:T(8,128)(2,1)S(1)} %get-tuple-element.107), channel_id=1, source_target_pairs={{0,4},{1,5},{2,6},{3,7},{4,0},{5,1},{6,2},{7,3},{8,12},{9,13},{10,... | collective-permute-start | bytes 147464 | tf_op jit(solution)/shard_map/ppermute | solution.py:688
  42.4 6.1 %collective-permute-start.10 = (bf16[128,192]{1,0:T(8,128)(2,1)S(1)}, bf16[128,192]{1,0:T(8,128)(2,1)S(1)}, u32[]{:S(2)}, u32[]{:S(2)}) collective-permute-start(bf16[128,192]{1,0:T(8,128)(2,1)S(1)} %get-tuple-element.108), channel_id=1, source_target_pairs={{0,6},{1,7},{2,4},{3,5},{4,2},{5,3},{6,0},{7,1},{8,14},{9,15},{10,... | collective-permute-start | bytes 147464 | tf_op jit(solution)/shard_map/ppermute | solution.py:688
  49.6 12.8 %copy-start.7 = (bf16[768,768]{1,0:T(8,128)(2,1)S(1)}, bf16[768,768]{1,0:T(8,128)(2,1)}, u32[]{:S(2)}) copy-start(bf16[768,768]{1,0:T(8,128)(2,1)} %refs_2_.5) | copy-start | bytes 3538948
  49.6 12.8 %copy-start.8 = (bf16[768]{0:T(1024)(128)(2,1)S(1)}, bf16[768]{0:T(1024)(128)(2,1)}, u32[]{:S(2)}) copy-start(bf16[768]{0:T(1024)(128)(2,1)} %refs_1_.8) | copy-start | bytes 4612
  49.7 12.7 %collective-permute-start.14 = (bf16[288,768]{1,0:T(8,128)(2,1)S(1)}, bf16[288,768]{1,0:T(8,128)(2,1)S(1)}, u32[]{:S(2)}, u32[]{:S(2)}) collective-permute-start(bf16[288,768]{1,0:T(8,128)(2,1)S(1)} %expand_stack.1), channel_id=1, source_target_pairs={{0,1},{1,0},{2,3},{3,2},{4,5},{5,4},{6,7},{7,6},{8,9},{9,8},{10,11... | collective-permute-start | bytes 1327112 | tf_op jit(solution)/shard_map/ppermute | solution.py:685
  49.7 8.7 %collective-permute-start.17 = (bf16[128,768]{1,0:T(8,128)(2,1)S(1)}, bf16[128,768]{1,0:T(8,128)(2,1)S(1)}, u32[]{:S(2)}, u32[]{:S(2)}) collective-permute-start(bf16[128,768]{1,0:T(8,128)(2,1)S(1)} %get-tuple-element.113.refs_3_.refs_6_), channel_id=1, source_target_pairs={{0,24},{8,16},{16,8},{24,0},{1,25},{9,17},{17,9},{25,1},{2,26},{10... | collective-permute-start | bytes 589832 | tf_op jit(solution)/shard_map/ppermute | solution.py:693
  52.3 9.9 %collective-permute-start.16 = (bf16[128,768]{1,0:T(8,128)(2,1)S(1)}, bf16[128,768]{1,0:T(8,128)(2,1)S(1)}, u32[]{:S(2)}, u32[]{:S(2)}) collective-permute-start(bf16[128,768]{1,0:T(8,128)(2,1)S(1)} %get-tuple-element.113.refs_3_.refs_6_), channel_id=1, source_target_pairs={{0,16},{8,24},{16,0},{24,8},{1,17},{9,25},{17,1},{25,9},{2,18},{10... | collective-permute-start | bytes 589832 | tf_op jit(solution)/shard_map/ppermute | solution.py:693
  52.8 9.5 %collective-permute-start.15 = (bf16[128,768]{1,0:T(8,128)(2,1)S(1)}, bf16[128,768]{1,0:T(8,128)(2,1)S(1)}, u32[]{:S(2)}, u32[]{:S(2)}) collective-permute-start(bf16[128,768]{1,0:T(8,128)(2,1)S(1)} %get-tuple-element.113.refs_3_.refs_6_), channel_id=1, source_target_pairs={{0,8},{8,0},{16,24},{24,16},{1,9},{9,1},{17,25},{25,17},{2,10},{10... | collective-permute-start | bytes 589832 | tf_op jit(solution)/shard_map/ppermute | solution.py:693
  67.9 2.9 %collective-permute-start.24 = (bf16[4,384,384]{2,1,0:T(8,128)(2,1)S(1)}, bf16[4,384,384]{2,1,0:T(8,128)(2,1)S(1)}, u32[]{:S(2)}, u32[]{:S(2)}) collective-permute-start(bf16[4,384,384]{2,1,0:T(8,128)(2,1)S(1)} %get-tuple-element.126), channel_id=1, source_target_pairs={{0,1},{1,0},{2,3},{3,2},{4,5},{5,4},{6,7},{7,6},{8,9},{9,8},{10,11... | collective-permute-start | bytes 3538952 | tf_op jit(solution)/shard_map/ppermute | solution.py:685
  71.7 20.2 %collective-permute-start.28 = (bf16[2,384,384]{2,1,0:T(8,128)(2,1)S(1)}, bf16[2,384,384]{2,1,0:T(8,128)(2,1)S(1)}, u32[]{:S(2)}, u32[]{:S(2)}) collective-permute-start(bf16[2,384,384]{2,1,0:T(8,128)(2,1)S(1)} %get-tuple-element.127.refs_9_), channel_id=1, source_target_pairs={{0,2},{1,3},{2,0},{3,1},{4,6},{5,7},{6,4},{7,5},{8,10},{9,11},{10,... | collective-permute-start | bytes 1769480 | tf_op jit(solution)/shard_map/ppermute | solution.py:688
  72.4 7.8 %collective-permute-start.21 = (bf16[128,768]{1,0:T(8,128)(2,1)S(1)}, bf16[128,768]{1,0:T(8,128)(2,1)S(1)}, u32[]{:S(2)}, u32[]{:S(2)}) collective-permute-start(bf16[128,768]{1,0:T(8,128)(2,1)S(1)} %get-tuple-element.122), channel_id=1, source_target_pairs={{0,8},{8,0},{16,24},{24,16},{1,9},{9,1},{17,25},{25,17},{2,10},{10... | collective-permute-start | bytes 589832 | tf_op jit(solution)/shard_map/ppermute | solution.py:693
  73.3 10.9 %collective-permute-start.22 = (bf16[128,768]{1,0:T(8,128)(2,1)S(1)}, bf16[128,768]{1,0:T(8,128)(2,1)S(1)}, u32[]{:S(2)}, u32[]{:S(2)}) collective-permute-start(bf16[128,768]{1,0:T(8,128)(2,1)S(1)} %get-tuple-element.123), channel_id=1, source_target_pairs={{0,16},{8,24},{16,0},{24,8},{1,17},{9,25},{17,1},{25,9},{2,18},{10... | collective-permute-start | bytes 589832 | tf_op jit(solution)/shard_map/ppermute | solution.py:693
  74.3 9.9 %collective-permute-start.23 = (bf16[128,768]{1,0:T(8,128)(2,1)S(1)}, bf16[128,768]{1,0:T(8,128)(2,1)S(1)}, u32[]{:S(2)}, u32[]{:S(2)}) collective-permute-start(bf16[128,768]{1,0:T(8,128)(2,1)S(1)} %get-tuple-element.124), channel_id=1, source_target_pairs={{0,24},{8,16},{16,8},{24,0},{1,25},{9,17},{17,9},{25,1},{2,26},{10... | collective-permute-start | bytes 589832 | tf_op jit(solution)/shard_map/ppermute | solution.py:693
  85.6 6.2 %collective-permute-start.27 = (bf16[128,192]{1,0:T(8,128)(2,1)S(1)}, bf16[128,192]{1,0:T(8,128)(2,1)S(1)}, u32[]{:S(2)}, u32[]{:S(2)}) collective-permute-start(bf16[128,192]{1,0:T(8,128)(2,1)S(1)} %get-tuple-element.131), channel_id=1, source_target_pairs={{0,6},{1,7},{2,4},{3,5},{4,2},{5,3},{6,0},{7,1},{8,14},{9,15},{10,... | collective-permute-start | bytes 147464 | tf_op jit(solution)/shard_map/ppermute | solution.py:688
  88.5 4.7 %collective-permute-start.25 = (bf16[128,192]{1,0:T(8,128)(2,1)S(1)}, bf16[128,192]{1,0:T(8,128)(2,1)S(1)}, u32[]{:S(2)}, u32[]{:S(2)}) collective-permute-start(bf16[128,192]{1,0:T(8,128)(2,1)S(1)} %get-tuple-element.129), channel_id=1, source_target_pairs={{0,2},{1,3},{2,0},{3,1},{4,6},{5,7},{6,4},{7,5},{8,10},{9,11},{10,... | collective-permute-start | bytes 147464 | tf_op jit(solution)/shard_map/ppermute | solution.py:688
  89.3 5.2 %collective-permute-start.26 = (bf16[128,192]{1,0:T(8,128)(2,1)S(1)}, bf16[128,192]{1,0:T(8,128)(2,1)S(1)}, u32[]{:S(2)}, u32[]{:S(2)}) collective-permute-start(bf16[128,192]{1,0:T(8,128)(2,1)S(1)} %get-tuple-element.130), channel_id=1, source_target_pairs={{0,4},{1,5},{2,6},{3,7},{4,0},{5,1},{6,2},{7,3},{8,12},{9,13},{10,... | collective-permute-start | bytes 147464 | tf_op jit(solution)/shard_map/ppermute | solution.py:688
  91.1 10.2 %collective-permute-start.33 = (bf16[4,192,384]{2,1,0:T(8,128)(2,1)S(1)}, bf16[4,192,384]{2,1,0:T(8,128)(2,1)S(1)}, u32[]{:S(2)}, u32[]{:S(2)}) collective-permute-start(bf16[4,192,384]{2,1,0:T(8,128)(2,1)S(1)} %get-tuple-element.135.refs_12_), channel_id=1, source_target_pairs={{0,1},{1,0},{2,3},{3,2},{4,5},{5,4},{6,7},{7,6},{8,9},{9,8},{10,11... | collective-permute-start | bytes 1769480 | tf_op jit(solution)/shard_map/ppermute | solution.py:685
  99.5 6.0 %collective-permute-start.29 = (bf16[512,384]{1,0:T(8,128)(2,1)S(1)}, bf16[512,384]{1,0:T(8,128)(2,1)S(1)}, u32[]{:S(2)}, u32[]{:S(2)}) collective-permute-start(bf16[512,384]{1,0:T(8,128)(2,1)S(1)} %get-tuple-element.138), channel_id=1, source_target_pairs={{0,1},{1,0},{2,3},{3,2},{4,5},{5,4},{6,7},{7,6},{8,9},{9,8},{10,11... | collective-permute-start | bytes 1179656 | tf_op jit(solution)/shard_map/ppermute | solution.py:685
  99.6 10.6 %collective-permute-start.18 = (bf16[128,768]{1,0:T(8,128)(2,1)S(1)}, bf16[128,768]{1,0:T(8,128)(2,1)S(1)}, u32[]{:S(2)}, u32[]{:S(2)}) collective-permute-start(bf16[128,768]{1,0:T(8,128)(2,1)S(1)} %get-tuple-element.115), channel_id=1, source_target_pairs={{0,8},{8,0},{16,24},{24,16},{1,9},{9,1},{17,25},{25,17},{2,10},{10... | collective-permute-start | bytes 589832 | tf_op jit(solution)/shard_map/ppermute | solution.py:693
  100.2 16.4 %collective-permute-start.32 = (bf16[384,384]{1,0:T(8,128)(2,1)S(1)}, bf16[384,384]{1,0:T(8,128)(2,1)S(1)}, u32[]{:S(2)}, u32[]{:S(2)}) collective-permute-start(bf16[384,384]{1,0:T(8,128)(2,1)S(1)} %get-tuple-element.133.refs_11_), channel_id=1, source_target_pairs={{0,4},{1,5},{2,6},{3,7},{4,0},{5,1},{6,2},{7,3},{8,12},{9,13},{10,... | collective-permute-start | bytes 884744 | tf_op jit(solution)/shard_map/ppermute | solution.py:688
  102.1 14.7 %collective-permute-start.34 = (bf16[4,48,768]{2,1,0:T(8,128)(2,1)S(1)}, bf16[4,48,768]{2,1,0:T(8,128)(2,1)S(1)}, u32[]{:S(2)}, u32[]{:S(2)}) collective-permute-start(bf16[4,48,768]{2,1,0:T(8,128)(2,1)S(1)} %get-tuple-element.154), channel_id=1, source_target_pairs={{0,2},{1,3},{2,0},{3,1},{4,6},{5,7},{6,4},{7,5},{8,10},{9,11},{10,... | collective-permute-start | bytes 884744 | tf_op jit(solution)/shard_map/ppermute | solution.py:688
  104.2 10.6 %collective-permute-start.19 = (bf16[128,768]{1,0:T(8,128)(2,1)S(1)}, bf16[128,768]{1,0:T(8,128)(2,1)S(1)}, u32[]{:S(2)}, u32[]{:S(2)}) collective-permute-start(bf16[128,768]{1,0:T(8,128)(2,1)S(1)} %get-tuple-element.116), channel_id=1, source_target_pairs={{0,16},{8,24},{16,0},{24,8},{1,17},{9,25},{17,1},{25,9},{2,18},{10... | collective-permute-start | bytes 589832 | tf_op jit(solution)/shard_map/ppermute | solution.py:693
  105.5 9.3 %collective-permute-start.20 = (bf16[128,768]{1,0:T(8,128)(2,1)S(1)}, bf16[128,768]{1,0:T(8,128)(2,1)S(1)}, u32[]{:S(2)}, u32[]{:S(2)}) collective-permute-start(bf16[128,768]{1,0:T(8,128)(2,1)S(1)} %get-tuple-element.117), channel_id=1, source_target_pairs={{0,24},{8,16},{16,8},{24,0},{1,25},{9,17},{17,9},{25,1},{2,26},{10... | collective-permute-start | bytes 589832 | tf_op jit(solution)/shard_map/ppermute | solution.py:693
  110.2 6.6 %collective-permute-start.35 = (bf16[96,768]{1,0:T(8,128)(2,1)S(1)}, bf16[96,768]{1,0:T(8,128)(2,1)S(1)}, u32[]{:S(2)}, u32[]{:S(2)}) collective-permute-start(bf16[96,768]{1,0:T(8,128)(2,1)S(1)} %get-tuple-element.155), channel_id=1, source_target_pairs={{0,1},{1,0},{2,3},{3,2},{4,5},{5,4},{6,7},{7,6},{8,9},{9,8},{10,11... | collective-permute-start | bytes 442376 | tf_op jit(solution)/shard_map/ppermute | solution.py:685
  114.8 4.8 %collective-permute-start.36 = (bf16[96,768]{1,0:T(8,128)(2,1)S(1)}, bf16[96,768]{1,0:T(8,128)(2,1)S(1)}, u32[]{:S(2)}, u32[]{:S(2)}) collective-permute-start(bf16[96,768]{1,0:T(8,128)(2,1)S(1)} %get-tuple-element.156), channel_id=1, source_target_pairs={{0,1},{1,0},{2,3},{3,2},{4,5},{5,4},{6,7},{7,6},{8,9},{9,8},{10,11... | collective-permute-start | bytes 442376 | tf_op jit(solution)/shard_map/ppermute | solution.py:685
  114.8 4.8 %collective-permute-start.37 = (bf16[96,768]{1,0:T(8,128)(2,1)S(1)}, bf16[96,768]{1,0:T(8,128)(2,1)S(1)}, u32[]{:S(2)}, u32[]{:S(2)}) collective-permute-start(bf16[96,768]{1,0:T(8,128)(2,1)S(1)} %get-tuple-element.157), channel_id=1, source_target_pairs={{0,1},{1,0},{2,3},{3,2},{4,5},{5,4},{6,7},{7,6},{8,9},{9,8},{10,11... | collective-permute-start | bytes 442376 | tf_op jit(solution)/shard_map/ppermute | solution.py:685
  116.6 3.1 %collective-permute-start.38 = (bf16[96,768]{1,0:T(8,128)(2,1)S(1)}, bf16[96,768]{1,0:T(8,128)(2,1)S(1)}, u32[]{:S(2)}, u32[]{:S(2)}) collective-permute-start(bf16[96,768]{1,0:T(8,128)(2,1)S(1)} %get-tuple-element.158), channel_id=1, source_target_pairs={{0,1},{1,0},{2,3},{3,2},{4,5},{5,4},{6,7},{7,6},{8,9},{9,8},{10,11... | collective-permute-start | bytes 442376 | tf_op jit(solution)/shard_map/ppermute | solution.py:685
  116.8 10.9 %collective-permute-start.30 = (bf16[128,768]{1,0:T(8,128)(2,1)S(1)}, bf16[128,768]{1,0:T(8,128)(2,1)S(1)}, u32[]{:S(2)}, u32[]{:S(2)}) collective-permute-start(bf16[128,768]{1,0:T(8,128)(2,1)S(1)} %get-tuple-element.149), channel_id=1, source_target_pairs={{0,2},{1,3},{2,0},{3,1},{4,6},{5,7},{6,4},{7,5},{8,10},{9,11},{10,... | collective-permute-start | bytes 589832 | tf_op jit(solution)/shard_map/ppermute | solution.py:688
  116.8 15.1 %collective-permute-start.31 = (bf16[128,768]{1,0:T(8,128)(2,1)S(1)}, bf16[128,768]{1,0:T(8,128)(2,1)S(1)}, u32[]{:S(2)}, u32[]{:S(2)}) collective-permute-start(bf16[128,768]{1,0:T(8,128)(2,1)S(1)} %get-tuple-element.150), channel_id=1, source_target_pairs={{0,2},{1,3},{2,0},{3,1},{4,6},{5,7},{6,4},{7,5},{8,10},{9,11},{10,... | collective-permute-start | bytes 589832 | tf_op jit(solution)/shard_map/ppermute | solution.py:688
  120.6 12.7 %collective-permute-start.44 = (bf16[192,384]{1,0:T(8,128)(2,1)S(1)}, bf16[192,384]{1,0:T(8,128)(2,1)S(1)}, u32[]{:S(2)}, u32[]{:S(2)}) collective-permute-start(bf16[192,384]{1,0:T(8,128)(2,1)S(1)} %get-tuple-element.160.refs_3_.refs_1_), channel_id=1, source_target_pairs={{0,4},{1,5},{2,6},{3,7},{4,0},{5,1},{6,2},{7,3},{8,12},{9,13},{10,... | collective-permute-start | bytes 442376 | tf_op jit(solution)/shard_map/ppermute | solution.py:688
  122.1 12.4 %collective-permute-start.43 = (bf16[192,384]{1,0:T(8,128)(2,1)S(1)}, bf16[192,384]{1,0:T(8,128)(2,1)S(1)}, u32[]{:S(2)}, u32[]{:S(2)}) collective-permute-start(bf16[192,384]{1,0:T(8,128)(2,1)S(1)} %get-tuple-element.160.refs_3_.refs_1_), channel_id=1, source_target_pairs={{0,2},{1,3},{2,0},{3,1},{4,6},{5,7},{6,4},{7,5},{8,10},{9,11},{10,... | collective-permute-start | bytes 442376 | tf_op jit(solution)/shard_map/ppermute | solution.py:688
  124.1 19.4 %collective-permute-start.40 = (bf16[176,768]{1,0:T(8,128)(2,1)S(1)}, bf16[176,768]{1,0:T(8,128)(2,1)S(1)}, u32[]{:S(2)}, u32[]{:S(2)}) collective-permute-start(bf16[176,768]{1,0:T(8,128)(2,1)S(1)} %get-tuple-element.165), channel_id=1, source_target_pairs={{0,8},{8,0},{16,24},{24,16},{1,9},{9,1},{17,25},{25,17},{2,10},{10... | collective-permute-start | bytes 811016 | tf_op jit(solution)/shard_map/ppermute | solution.py:693
  127.7 15.8 %collective-permute-start.41 = (bf16[176,768]{1,0:T(8,128)(2,1)S(1)}, bf16[176,768]{1,0:T(8,128)(2,1)S(1)}, u32[]{:S(2)}, u32[]{:S(2)}) collective-permute-start(bf16[176,768]{1,0:T(8,128)(2,1)S(1)} %get-tuple-element.166), channel_id=1, source_target_pairs={{0,16},{8,24},{16,0},{24,8},{1,17},{9,25},{17,1},{25,9},{2,18},{10... | collective-permute-start | bytes 811016 | tf_op jit(solution)/shard_map/ppermute | solution.py:693
  131.9 11.6 %collective-permute-start.42 = (bf16[176,768]{1,0:T(8,128)(2,1)S(1)}, bf16[176,768]{1,0:T(8,128)(2,1)S(1)}, u32[]{:S(2)}, u32[]{:S(2)}) collective-permute-start(bf16[176,768]{1,0:T(8,128)(2,1)S(1)} %get-tuple-element.167), channel_id=1, source_target_pairs={{0,24},{8,16},{16,8},{24,0},{1,25},{9,17},{17,9},{25,1},{2,26},{10... | collective-permute-start | bytes 811016 | tf_op jit(solution)/shard_map/ppermute | solution.py:693
  133.3 10.2 %collective-permute-start.39 = (bf16[128,768]{1,0:T(8,128)(2,1)S(1)}, bf16[128,768]{1,0:T(8,128)(2,1)S(1)}, u32[]{:S(2)}, u32[]{:S(2)}) collective-permute-start(bf16[128,768]{1,0:T(8,128)(2,1)S(1)} %get-tuple-element.162), channel_id=1, source_target_pairs={{0,4},{1,5},{2,6},{3,7},{4,0},{5,1},{6,2},{7,3},{8,12},{9,13},{10,... | collective-permute-start | bytes 589832 | tf_op jit(solution)/shard_map/ppermute | solution.py:688
  134.5 9.3 %collective-permute-start.45 = (bf16[192,384]{1,0:T(8,128)(2,1)S(1)}, bf16[192,384]{1,0:T(8,128)(2,1)S(1)}, u32[]{:S(2)}, u32[]{:S(2)}) collective-permute-start(bf16[192,384]{1,0:T(8,128)(2,1)S(1)} %collective-permute-done.44.refs_3_), channel_id=1, source_target_pairs={{0,2},{1,3},{2,0},{3,1},{4,6},{5,7},{6,4},{7,5},{8,10},{9,11},{10,... | collective-permute-start | bytes 442376 | tf_op jit(solution)/shard_map/ppermute | solution.py:688
  144.6 15.2 %collective-permute-start.47 = (bf16[240,768]{1,0:T(8,128)(2,1)S(1)}, bf16[240,768]{1,0:T(8,128)(2,1)S(1)}, u32[]{:S(2)}, u32[]{:S(2)}) collective-permute-start(bf16[240,768]{1,0:T(8,128)(2,1)S(1)} %shares.1.refs_1_), channel_id=1, source_target_pairs={{0,4},{1,5},{2,6},{3,7},{4,0},{5,1},{6,2},{7,3},{8,12},{9,13},{10,... | collective-permute-start | bytes 1105928 | tf_op jit(solution)/shard_map/ppermute | solution.py:688
  144.6 17.4 %collective-permute-start.46 = (bf16[240,768]{1,0:T(8,128)(2,1)S(1)}, bf16[240,768]{1,0:T(8,128)(2,1)S(1)}, u32[]{:S(2)}, u32[]{:S(2)}) collective-permute-start(bf16[240,768]{1,0:T(8,128)(2,1)S(1)} %shares.1.refs_1_), channel_id=1, source_target_pairs={{0,2},{1,3},{2,0},{3,1},{4,6},{5,7},{6,4},{7,5},{8,10},{9,11},{10,... | collective-permute-start | bytes 1105928 | tf_op jit(solution)/shard_map/ppermute | solution.py:688
  146.1 1.4 collective-permute-start.48
  146.1 2.6 %collective-permute-start.50 = (bf16[192,384]{1,0:T(8,128)(2,1)S(1)}, bf16[192,384]{1,0:T(8,128)(2,1)S(1)}, u32[]{:S(2)}, u32[]{:S(2)}) collective-permute-start(bf16[192,384]{1,0:T(8,128)(2,1)S(1)} %collective-permute-done.44.refs_3_), channel_id=1, source_target_pairs={{0,1},{1,0},{2,3},{3,2},{4,5},{5,4},{6,7},{7,6},{8,9},{9,8},{10,11... | collective-permute-start | bytes 442376 | tf_op jit(solution)/shard_map/ppermute | solution.py:685
  146.6 2.1 %collective-permute-start.49 = (bf16[192,384]{1,0:T(8,128)(2,1)S(1)}, bf16[192,384]{1,0:T(8,128)(2,1)S(1)}, u32[]{:S(2)}, u32[]{:S(2)}) collective-permute-start(bf16[192,384]{1,0:T(8,128)(2,1)S(1)} %collective-permute-done.43.refs_5_.refs_2_), channel_id=1, source_target_pairs={{0,1},{1,0},{2,3},{3,2},{4,5},{5,4},{6,7},{7,6},{8,9},{9,8},{10,11... | collective-permute-start | bytes 442376 | tf_op jit(solution)/shard_map/ppermute | solution.py:685
  147.5 1.4 collective-permute-start.51
  162.0 8.8 %collective-permute-start.52 = (bf16[240,768]{1,0:T(8,128)(2,1)S(1)}, bf16[240,768]{1,0:T(8,128)(2,1)S(1)}, u32[]{:S(2)}, u32[]{:S(2)}) collective-permute-start(bf16[240,768]{1,0:T(8,128)(2,1)S(1)} %pass_on.1), channel_id=1, source_target_pairs={{0,2},{1,3},{2,0},{3,1},{4,6},{5,7},{6,4},{7,5},{8,10},{9,11},{10,... | collective-permute-start | bytes 1105928 | tf_op jit(solution)/shard_map/ppermute | solution.py:688
  162.4 8.5 %collective-permute-start.53 = (bf16[240,768]{1,0:T(8,128)(2,1)S(1)}, bf16[240,768]{1,0:T(8,128)(2,1)S(1)}, u32[]{:S(2)}, u32[]{:S(2)}) collective-permute-start(bf16[240,768]{1,0:T(8,128)(2,1)S(1)} %shares.1.refs_1_), channel_id=1, source_target_pairs={{0,1},{1,0},{2,3},{3,2},{4,5},{5,4},{6,7},{7,6},{8,9},{9,8},{10,11... | collective-permute-start | bytes 1105928 | tf_op jit(solution)/shard_map/ppermute | solution.py:685
  162.4 8.5 %collective-permute-start.55 = (bf16[240,768]{1,0:T(8,128)(2,1)S(1)}, bf16[240,768]{1,0:T(8,128)(2,1)S(1)}, u32[]{:S(2)}, u32[]{:S(2)}) collective-permute-start(bf16[240,768]{1,0:T(8,128)(2,1)S(1)} %collective-permute-done.47.refs_0_.refs_3_), channel_id=1, source_target_pairs={{0,1},{1,0},{2,3},{3,2},{4,5},{5,4},{6,7},{7,6},{8,9},{9,8},{10,11... | collective-permute-start | bytes 1105928 | tf_op jit(solution)/shard_map/ppermute | solution.py:685
  162.9 8.0 %collective-permute-start.54 = (bf16[240,768]{1,0:T(8,128)(2,1)S(1)}, bf16[240,768]{1,0:T(8,128)(2,1)S(1)}, u32[]{:S(2)}, u32[]{:S(2)}) collective-permute-start(bf16[240,768]{1,0:T(8,128)(2,1)S(1)} %collective-permute-done.46.refs_3_.refs_2_), channel_id=1, source_target_pairs={{0,1},{1,0},{2,3},{3,2},{4,5},{5,4},{6,7},{7,6},{8,9},{9,8},{10,11... | collective-permute-start | bytes 1105928 | tf_op jit(solution)/shard_map/ppermute | solution.py:685
  170.8 1.7 collective-permute-start.56
  (3 other events, 14.1 us)

commit v6 on v5

--- a/solution.py
+++ b/solution.py
@@ -1223,7 +1223,7 @@
 
         def normed_back_kernel(dq_ref, own_ref, far_ref, w_ref, *refs):
             toks = refs[:parts]
-            keep_ref, *send_refs, mixed_ref, sums_ref, bias_ref = refs[parts:]
+            keep_ref, send_ref, mixed_ref, sums_ref, bias_ref = refs[parts:]
             mixed_ref[:, 0:hw] = dq_ref[...].T.astype(bf)
             mixed_ref[:, hw:] = (own_ref[...] + far_ref[...].astype(f32)).astype(bf)
             shift_sum = jnp.zeros((1, width), f32)
@@ -1231,7 +1231,7 @@
             for k in range(parts):
                 grad = mm_nt(mixed_ref[k * rows : (k + 1) * rows, :], w_ref[...])
                 if k % 2:
-                    send_refs[k // 2][...] = grad.astype(bf)
+                    send_ref[k // 2] = grad.astype(bf)
                 else:
                     keep_ref[k // 2] = grad
                 xhat, _ = norm_stats(toks[k][...].astype(f32))
@@ -1246,8 +1246,7 @@
             "normed_back",
             [
                 shape_of((parts // 2, rows, width), f32),
-                shape_of((rows, width), bf),
-                shape_of((rows, width), bf),
+                shape_of((parts // 2, rows, width), bf),
                 shape_of((total, 3 * hw), bf),
                 shape_of((8, width), f32),
                 shape_of((8, 3 * hw), f32),
@@ -1255,8 +1254,8 @@
             [flat_dq, dkv_own, dkv_far, w_heads_full] + token_parts,
             flops=0,
         )
-        gt_keep, *gt_send, grad_mixed, first_sums, mixed_sums = nb_out
-        gt_far = [chip_swap(member, 1) for member in gt_send]
+        gt_keep, gt_send, grad_mixed, first_sums, mixed_sums = nb_out
+        gt_far = chip_swap(gt_send, 1)
 
 
         def input_weights_kernel(
@@ -1354,15 +1353,15 @@
         dp_parts = [dp_out[0]] + [seq_swap(dp_out[j], j) for j in others]
         con_one = dp_out[seq_parts]
 
-        def half_sum_kernel(keep_ref, first_ref, second_ref, own_ref, send_ref):
-            own_ref[...] = keep_ref[0] + first_ref[...].astype(f32)
-            send_ref[...] = (keep_ref[1] + second_ref[...].astype(f32)).astype(bf)
+        def half_sum_kernel(keep_ref, far_ref, own_ref, send_ref):
+            own_ref[...] = keep_ref[0] + far_ref[0].astype(f32)
+            send_ref[...] = (keep_ref[1] + far_ref[1].astype(f32)).astype(bf)
 
         gt_own, gt_send_two = local_call(
             half_sum_kernel,
             "tokens_halves",
             [shape_of((rows, width), f32), shape_of((rows, width), bf)],
-            [gt_keep] + gt_far,
+            [gt_keep, gt_far],
             after=[con_one],
         )
         con_two = chip_swap(con_one, 2)

time: 177 us -> 176 us (level)
  starting transfers between devices: 56.4 us -> 54.6 us
    ppermute x21 -> x20, waiting for transfers between devices: 47.5 us -> 41.8 us  [chip_swap(): lax.ppermute(member, 'ctx', [(i, 2 * (i // 2 ^ step) + i % 2) for i in ra...]
    ppermute x18, waiting for transfers between devices: 24.7 us -> 29.8 us  [seq_swap(): return lax.ppermute(member, 'dp', [(i, i ^ step) for i in range(seq_parts)])]
    ppermute x21 -> x20, starting transfers between devices: 32.7 us -> 31 us  [chip_swap(): lax.ppermute(member, 'ctx', [(i, 2 * (i // 2 ^ step) + i % 2) for i in ra...]
  transfers between devices with their start and end apart: 57 -> 56, of which waited for: 30 -> 34; matrix products, arithmetic and copies ran while one was open for 0% -> 0% of each run, Pallas kernels for 13% -> 13%
where the time goes in v6:
time: 176 us; the launch traced here: 175 us
  waiting for transfers between devices  81.2 us (46%)
  starting transfers between devices  54.6 us (31%)
  Pallas kernels  37.8 us (21%)
    ppermute x20, waiting for transfers between devices, chip_swap(): lax.ppermute(member, 'ctx', [(i, 2 * (i // 2 ^ step) + i % 2) for i in ra...  41.8 us
    pallas_call x24, Pallas kernels, local_call(): pl.pallas_call(ordered, out_shape=tuple(outs), in_specs=[pl.BlockSpec(mem...  37.8 us
    ppermute x20, starting transfers between devices, chip_swap(): lax.ppermute(member, 'ctx', [(i, 2 * (i // 2 ^ step) + i % 2) for i in ra...  31 us
    ppermute x18, waiting for transfers between devices, seq_swap(): return lax.ppermute(member, 'dp', [(i, i ^ step) for i in range(seq_parts)])  29.8 us
    ppermute x18, starting transfers between devices, seq_swap(): return lax.ppermute(member, 'dp', [(i, i ^ step) for i in range(seq_parts)])  21.3 us
    ppermute x18, waiting for transfers between devices, core_swap(): return lax.ppermute(member, 'ctx', [(i, i ^ 1) for i in range(ranks)])  9.56 us
  transfers between devices with their start and end apart: 56, of which 34 were waited for; matrix products, arithmetic and copies ran while one was open for 0% of the time, Pallas kernels for 13%

profile of v6, /device:TPU:0, one launch (start us, length us, event | category | flops | bytes accessed | tf_op | source)
XLA Modules:
  0.0 175.4 jit_solution(1967893603965455279)
XLA Ops:
  1.3 2.8 %pack.1 = (bf16[192,768]{1,0:T(8,128)(2,1)}, bf16[128,768]{1,0:T(8,128)(2,1)}) custom-call(s32[3]{0:T(128)} %pad_add_fusion.refs_0_, bf16[128,768]{1,0:T(8,128)(2,1)} %bitcast.8, bf16[192,2304]{1,0:T(8,128)(2,1)} %refs_1_.5, bf16[192,768]{1,0:T(8,128)(2,1)} %refs_2_.4, bf16[192]{0:T(256)(128)(2,1)} %refs_4_.1, bf16[192]{0:T(256)(128)(2,1)} %refs_5_.1, ...), custom_call_target="tpu_custom_call" | custom-call | tf_op jit(solution)/shard_map/pack/pallas_call | solution.py:636
  4.0 4.1 %collective-permute-start.1 = (bf16[128,768]{1,0:T(8,128)(2,1)}, bf16[128,768]{1,0:T(8,128)(2,1)S(1)}, u32[]{:S(2)}, u32[]{:S(2)}) collective-permute-start(bf16[128,768]{1,0:T(8,128)(2,1)} %get-tuple-element.98.refs_3_.refs_1_.refs_4_.refs_0_), channel_id=1, source_target_pairs={{0,4},{1,5},{2,6},{3,7},{4,0},{5,1},{6,2},{7,3},{8,12},{9,13},{10,... | collective-permute-start | bytes 589832 | tf_op jit(solution)/shard_map/ppermute | solution.py:688
  8.2 2.5 %collective-permute-start.5 = (bf16[192,768]{1,0:T(8,128)(2,1)}, bf16[192,768]{1,0:T(8,128)(2,1)S(1)}, u32[]{:S(2)}, u32[]{:S(2)}) collective-permute-start(bf16[192,768]{1,0:T(8,128)(2,1)} %get-tuple-element.99.refs_7_.refs_3_), channel_id=1, source_target_pairs={{0,24},{8,16},{16,8},{24,0},{1,25},{9,17},{17,9},{25,1},{2,26},{10... | collective-permute-start | bytes 884744 | tf_op jit(solution)/shard_map/ppermute | solution.py:693
  11.7 1.6 collective-permute-start
  13.3 4.3 %collective-permute-done.1.refs_4_.refs_5_.refs_6_ = bf16[128,768]{1,0:T(8,128)(2,1)S(1)} collective-permute-done((bf16[128,768]{1,0:T(8,128)(2,1)}, bf16[128,768]{1,0:T(8,128)(2,1)S(1)}, u32[]{:S(2)}, u32[]{:S(2)}) %collective-permute-start.1) | collective-permute-done | bytes 196640 | tf_op jit(solution)/shard_map/ppermute | solution.py:688
  18.3 3.2 %collective-permute-done.refs_3_.refs_4_.refs_5_ = bf16[128,768]{1,0:T(8,128)(2,1)S(1)} collective-permute-done((bf16[128,768]{1,0:T(8,128)(2,1)}, bf16[128,768]{1,0:T(8,128)(2,1)S(1)}, u32[]{:S(2)}, u32[]{:S(2)}) %collective-permute-start) | collective-permute-done | bytes 196640 | tf_op jit(solution)/shard_map/ppermute | solution.py:688
  21.5 2.6 %collective-permute-done.4.refs_1_ = bf16[192,768]{1,0:T(8,128)(2,1)S(1)} collective-permute-done((bf16[192,768]{1,0:T(8,128)(2,1)}, bf16[192,768]{1,0:T(8,128)(2,1)S(1)}, u32[]{:S(2)}, u32[]{:S(2)}) %collective-permute-start.4) | collective-permute-done | bytes 294944 | tf_op jit(solution)/shard_map/ppermute | solution.py:693
  24.9 2.4 %collective-permute-done.6.refs_9_ = bf16[576,768]{1,0:T(8,128)(2,1)S(1)} collective-permute-done((bf16[576,768]{1,0:T(8,128)(2,1)S(1)}, bf16[576,768]{1,0:T(8,128)(2,1)S(1)}, u32[]{:S(2)}, u32[]{:S(2)}) %collective-permute-start.6) | collective-permute-done | bytes 884768 | tf_op jit(solution)/shard_map/ppermute | solution.py:685
  27.3 2.1 %project.1 = (bf16[512,192]{1,0:T(8,128)(2,1)S(1)}, bf16[512,384]{1,0:T(8,128)(2,1)S(1)}, bf16[512,768]{1,0:T(8,128)(2,1)S(1)}, bf16[768,576]{1,0:T(8,128)(2,1)S...) custom-call(s32[3]{0:T(128)S(1)} %copy-done.6, bf16[192,2304]{1,0:T(8,128)(2,1)S(1)} %copy-done, ...), custom_call_target="tpu_custom_call" | custom-call | flops 452984832 | bytes 7520268 | tf_op jit(solution)/shard_map/project/pallas_call | solution.py:636
  30.2 1.6 collective-permute-start.11
  31.9 1.5 collective-permute-start.12
  33.8 3.7 %attend.1 = (bf16[128,192]{1,0:T(8,128)(2,1)S(1)}, bf16[128,192]{1,0:T(8,128)(2,1)S(1)}, bf16[128,192]{1,0:T(8,128)(2,1)S(1)}, bf16[128,192]{1,0:T(8,128)(2,1)S(...) custom-call(s32[3]{0:T(128)S(1)} %copy-done.6, s32[8]{0:T(128)S(1)} %copy-done.9, ...), custom_call_target="tpu_custom_call" | custom-call | flops 402653184 | bytes 1589292 | tf_op jit(solution)/shard_map/attend/pallas_call | solution.py:636
  37.6 1.2 collective-permute-start.8
  38.8 2.6 %collective-permute-start.9 = (bf16[128,192]{1,0:T(8,128)(2,1)S(1)}, bf16[128,192]{1,0:T(8,128)(2,1)S(1)}, u32[]{:S(2)}, u32[]{:S(2)}) collective-permute-start(bf16[128,192]{1,0:T(8,128)(2,1)S(1)} %get-tuple-element.106), channel_id=1, source_target_pairs={{0,4},{1,5},{2,6},{3,7},{4,0},{5,1},{6,2},{7,3},{8,12},{9,13},{10,... | collective-permute-start | bytes 147464 | tf_op jit(solution)/shard_map/ppermute | solution.py:688
  41.4 1.0 collective-permute-done.8.refs_5_.refs_3_
  42.4 2.9 %collective-permute-start.10 = (bf16[128,192]{1,0:T(8,128)(2,1)S(1)}, bf16[128,192]{1,0:T(8,128)(2,1)S(1)}, u32[]{:S(2)}, u32[]{:S(2)}) collective-permute-start(bf16[128,192]{1,0:T(8,128)(2,1)S(1)} %get-tuple-element.107), channel_id=1, source_target_pairs={{0,6},{1,7},{2,4},{3,5},{4,2},{5,3},{6,0},{7,1},{8,14},{9,15},{10,... | collective-permute-start | bytes 147464 | tf_op jit(solution)/shard_map/ppermute | solution.py:688
  45.3 3.1 %collective-permute-done.10.refs_7_.refs_5_ = bf16[128,192]{1,0:T(8,128)(2,1)S(1)} collective-permute-done((bf16[128,192]{1,0:T(8,128)(2,1)S(1)}, bf16[128,192]{1,0:T(8,128)(2,1)S(1)}, u32[]{:S(2)}, u32[]{:S(2)}) %collective-permute-start.10) | collective-permute-done | bytes 49184 | tf_op jit(solution)/shard_map/ppermute | solution.py:688
  48.5 1.1 middle.1
  49.7 2.6 %collective-permute-start.17 = (bf16[128,768]{1,0:T(8,128)(2,1)S(1)}, bf16[128,768]{1,0:T(8,128)(2,1)S(1)}, u32[]{:S(2)}, u32[]{:S(2)}) collective-permute-start(bf16[128,768]{1,0:T(8,128)(2,1)S(1)} %get-tuple-element.112.refs_3_.refs_6_), channel_id=1, source_target_pairs={{0,24},{8,16},{16,8},{24,0},{1,25},{9,17},{17,9},{25,1},{2,26},{10... | collective-permute-start | bytes 589832 | tf_op jit(solution)/shard_map/ppermute | solution.py:693
  53.3 5.2 %collective-permute-done.17.refs_9_ = bf16[128,768]{1,0:T(8,128)(2,1)S(1)} collective-permute-done((bf16[128,768]{1,0:T(8,128)(2,1)S(1)}, bf16[128,768]{1,0:T(8,128)(2,1)S(1)}, u32[]{:S(2)}, u32[]{:S(2)}) %collective-permute-start.17) | collective-permute-done | bytes 196640 | tf_op jit(solution)/shard_map/ppermute | solution.py:693
  58.5 3.7 %collective-permute-done.16.refs_8_ = bf16[128,768]{1,0:T(8,128)(2,1)S(1)} collective-permute-done((bf16[128,768]{1,0:T(8,128)(2,1)S(1)}, bf16[128,768]{1,0:T(8,128)(2,1)S(1)}, u32[]{:S(2)}, u32[]{:S(2)}) %collective-permute-start.16) | collective-permute-done | bytes 196640 | tf_op jit(solution)/shard_map/ppermute | solution.py:693
  62.3 5.6 %feed.1 = (bf16[128,768]{1,0:T(8,128)(2,1)S(1)}, bf16[128,768]{1,0:T(8,128)(2,1)S(1)}, bf16[128,768]{1,0:T(8,128)(2,1)S(1)}, bf16[128,768]{1,0:T(8,128)(2,1)S(1)...) custom-call(s32[3]{0:T(128)S(1)} %copy-done.6, ...), custom_call_target="tpu_custom_call" | custom-call | flops 3623878656 | bytes 8753676 | tf_op jit(solution)/shard_map/feed/pallas_call | solution.py:636
  68.0 2.8 %collective-permute-done.24.refs_2_ = bf16[4,384,384]{2,1,0:T(8,128)(2,1)S(1)} collective-permute-done((bf16[4,384,384]{2,1,0:T(8,128)(2,1)S(1)}, bf16[4,384,384]{2,1,0:T(8,128)(2,1)S(1)}, u32[]{:S(2)}, u32[]{:S(2)}) %collective-permute-start.24) | collective-permute-done | bytes 1179680 | tf_op jit(solution)/shard_map/ppermute | solution.py:685
  70.9 0.8 feed_halves.1
  72.4 1.0 collective-permute-start.21
  73.3 1.0 collective-permute-start.22
  74.3 1.5 collective-permute-start.23
  75.8 4.3 %collective-permute-done.21.refs_6_ = bf16[128,768]{1,0:T(8,128)(2,1)S(1)} collective-permute-done((bf16[128,768]{1,0:T(8,128)(2,1)S(1)}, bf16[128,768]{1,0:T(8,128)(2,1)S(1)}, u32[]{:S(2)}, u32[]{:S(2)}) %collective-permute-start.21) | collective-permute-done | bytes 196640 | tf_op jit(solution)/shard_map/ppermute | solution.py:693
  80.1 4.0 %collective-permute-done.22.refs_7_ = bf16[128,768]{1,0:T(8,128)(2,1)S(1)} collective-permute-done((bf16[128,768]{1,0:T(8,128)(2,1)S(1)}, bf16[128,768]{1,0:T(8,128)(2,1)S(1)}, u32[]{:S(2)}, u32[]{:S(2)}) %collective-permute-start.22) | collective-permute-done | bytes 196640 | tf_op jit(solution)/shard_map/ppermute | solution.py:693
  84.2 1.4 middle_back.1
  85.6 2.9 %collective-permute-start.27 = (bf16[128,192]{1,0:T(8,128)(2,1)S(1)}, bf16[128,192]{1,0:T(8,128)(2,1)S(1)}, u32[]{:S(2)}, u32[]{:S(2)}) collective-permute-start(bf16[128,192]{1,0:T(8,128)(2,1)S(1)} %get-tuple-element.130), channel_id=1, source_target_pairs={{0,6},{1,7},{2,4},{3,5},{4,2},{5,3},{6,0},{7,1},{8,14},{9,15},{10,... | collective-permute-start | bytes 147464 | tf_op jit(solution)/shard_map/ppermute | solution.py:688
  90.1 1.0 output_weights.1
  92.0 1.3 collective-permute-done.25.refs_8_
  93.3 1.2 collective-permute-done.26.refs_9_
  94.5 5.0 %attend_back.1 = (f32[192,512]{1,0:T(8,128)S(1)}, f32[512,384]{1,0:T(8,128)S(1)}, bf16[512,384]{1,0:T(8,128)(2,1)S(1)}) custom-call(s32[3]{0:T(128)S(1)} %copy-done.6, s32[8]{0:T(128)S(1)} %copy-done.9, bf16[512,192]{1,0:T(8,128)(2,1)S(1)} %get-tuple-element.102.refs_2_, bf16[512,384]{1,0:T(8,128)(2,1)S(1)} %get-tuple-element.103.refs_3_, ...), custom_call_target="tpu_custom_call" | custom-call | flops 8053063680 | bytes 3162156 | tf_op jit(solution)/shard_map/attend_back/pallas_call | solution.py:636
  100.2 1.2 collective-permute-start.31
  102.1 2.1 %collective-permute-start.33 = (bf16[4,48,768]{2,1,0:T(8,128)(2,1)S(1)}, bf16[4,48,768]{2,1,0:T(8,128)(2,1)S(1)}, u32[]{:S(2)}, u32[]{:S(2)}) collective-permute-start(bf16[4,48,768]{2,1,0:T(8,128)(2,1)S(1)} %get-tuple-element.152), channel_id=1, source_target_pairs={{0,2},{1,3},{2,0},{3,1},{4,6},{5,7},{6,4},{7,5},{8,10},{9,11},{10,... | collective-permute-start | bytes 884744 | tf_op jit(solution)/shard_map/ppermute | solution.py:688
  104.2 1.3 collective-permute-start.19
  105.5 1.3 collective-permute-start.20
  106.9 1.8 %normed_back.1 = (f32[2,128,768]{2,1,0:T(8,128)S(1)}, bf16[2,128,768]{2,1,0:T(8,128)(2,1)S(1)}, bf16[512,576]{1,0:T(8,128)(2,1)S(1)}, f32[8,768]{1,0:T(8,128)S(1)}, f32[8,576]{1,0:T(8,128)S(1)}) custom-call(f32[192,512]{1,0:T(8,128)S(1)} %get-tuple-element.135.refs_0_, f32[512,384]{1,0:T(8,128)S(1)} %get-tuple-element.136.refs_1_, ...), custom_call_target="tpu_custom_call" | custom-call | tf_op jit(solution)/shard_map/normed_back/pallas_call | solution.py:636
  108.9 1.5 input_weights.1
  110.3 4.5 %collective-permute-done.19.refs_4_ = bf16[128,768]{1,0:T(8,128)(2,1)S(1)} collective-permute-done((bf16[128,768]{1,0:T(8,128)(2,1)S(1)}, bf16[128,768]{1,0:T(8,128)(2,1)S(1)}, u32[]{:S(2)}, u32[]{:S(2)}) %collective-permute-start.19) | collective-permute-done | bytes 196640 | tf_op jit(solution)/shard_map/ppermute | solution.py:693
  115.4 1.2 collective-permute-done.31.refs_2_
  116.6 1.0 collective-permute-done.33.refs_5_
  119.0 0.9 owners.1
  119.9 1.3 collective-permute-start.43
  121.2 2.5 %collective-permute-start.42 = (bf16[192,384]{1,0:T(8,128)(2,1)S(1)}, bf16[192,384]{1,0:T(8,128)(2,1)S(1)}, u32[]{:S(2)}, u32[]{:S(2)}) collective-permute-start(bf16[192,384]{1,0:T(8,128)(2,1)S(1)} %get-tuple-element.158.refs_2_.refs_1_), channel_id=1, source_target_pairs={{0,2},{1,3},{2,0},{3,1},{4,6},{5,7},{6,4},{7,5},{8,10},{9,11},{10,... | collective-permute-start | bytes 442376 | tf_op jit(solution)/shard_map/ppermute | solution.py:688
  123.7 1.5 collective-permute-start.39
  125.9 2.2 %collective-permute-done.30.refs_1_ = bf16[2,128,768]{2,1,0:T(8,128)(2,1)S(1)} collective-permute-done((bf16[2,128,768]{2,1,0:T(8,128)(2,1)S(1)}, bf16[2,128,768]{2,1,0:T(8,128)(2,1)S(1)}, u32[]{:S(2)}, u32[]{:S(2)}) %collective-permute-start.30) | collective-permute-done | bytes 393248 | tf_op jit(solution)/shard_map/ppermute | solution.py:688
  128.1 1.7 collective-permute-start.41
  130.1 1.5 collective-permute-done.42.refs_5_.refs_2_
  131.6 1.9 %collective-permute-start.44 = (bf16[192,384]{1,0:T(8,128)(2,1)S(1)}, bf16[192,384]{1,0:T(8,128)(2,1)S(1)}, u32[]{:S(2)}, u32[]{:S(2)}) collective-permute-start(bf16[192,384]{1,0:T(8,128)(2,1)S(1)} %collective-permute-done.43.refs_3_), channel_id=1, source_target_pairs={{0,2},{1,3},{2,0},{3,1},{4,6},{5,7},{6,4},{7,5},{8,10},{9,11},{10,... | collective-permute-start | bytes 442376 | tf_op jit(solution)/shard_map/ppermute | solution.py:688
  133.5 5.2 %collective-permute-done.40.refs_3_ = bf16[176,768]{1,0:T(8,128)(2,1)S(1)} collective-permute-done((bf16[176,768]{1,0:T(8,128)(2,1)S(1)}, bf16[176,768]{1,0:T(8,128)(2,1)S(1)}, u32[]{:S(2)}, u32[]{:S(2)}) %collective-permute-start.40) | collective-permute-done | bytes 270368 | tf_op jit(solution)/shard_map/ppermute | solution.py:693
  138.7 2.0 %collective-permute-done.38.refs_4_.refs_7_ = bf16[128,768]{1,0:T(8,128)(2,1)S(1)} collective-permute-done((bf16[128,768]{1,0:T(8,128)(2,1)S(1)}, bf16[128,768]{1,0:T(8,128)(2,1)S(1)}, u32[]{:S(2)}, u32[]{:S(2)}) %collective-permute-start.38) | collective-permute-done | bytes 196640 | tf_op jit(solution)/shard_map/ppermute | solution.py:688
  141.5 0.9 collective-permute-start.46
  142.4 2.5 %collective-permute-start.45 = (bf16[240,768]{1,0:T(8,128)(2,1)S(1)}, bf16[240,768]{1,0:T(8,128)(2,1)S(1)}, u32[]{:S(2)}, u32[]{:S(2)}) collective-permute-start(bf16[240,768]{1,0:T(8,128)(2,1)S(1)} %shares.1.refs_1_), channel_id=1, source_target_pairs={{0,2},{1,3},{2,0},{3,1},{4,6},{5,7},{6,4},{7,5},{8,10},{9,11},{10,... | collective-permute-start | bytes 1105928 | tf_op jit(solution)/shard_map/ppermute | solution.py:688
  145.4 0.9 collective-permute-done.47.refs_5_
  146.7 0.9 collective-permute-done.50.refs_8_
  147.6 2.1 %contract_final.1 = (f32[768,768]{1,0:T(8,128)}, f32[8,128]{1,0:T(8,128)S(1)}) custom-call(s32[3]{0:T(128)S(1)} %copy-done.6, bf16[192,384]{1,0:T(8,128)(2,1)S(1)} %get-tuple-element.158.refs_2_.refs_1_, bf16[192,384]{1,0:T(8,128)(2,1)S(1)} %collective-permute-done.42.refs_5_.refs_2_, bf16[192,384]{1,0:T(8,128)(2,1)S(1)} %collective-permute-done.43.refs_3_, ...), custom_call_target="tpu_custom_call" | custom-call | tf_op jit(solution)/shard_map/contract_final/pallas_call | solution.py:636
  149.7 1.1 tokens_back.1
  150.8 8.8 %collective-permute-done.46.refs_0_.refs_3_ = bf16[240,768]{1,0:T(8,128)(2,1)S(1)} collective-permute-done((bf16[240,768]{1,0:T(8,128)(2,1)S(1)}, bf16[240,768]{1,0:T(8,128)(2,1)S(1)}, u32[]{:S(2)}, u32[]{:S(2)}) %collective-permute-start.46) | collective-permute-done | bytes 368672 | tf_op jit(solution)/shard_map/ppermute | solution.py:688
  160.5 9.6 %collective-permute-done.51.refs_4_ = bf16[240,768]{1,0:T(8,128)(2,1)S(1)} collective-permute-done((bf16[240,768]{1,0:T(8,128)(2,1)S(1)}, bf16[240,768]{1,0:T(8,128)(2,1)S(1)}, u32[]{:S(2)}, u32[]{:S(2)}) %collective-permute-start.51) | collective-permute-done | bytes 368672 | tf_op jit(solution)/shard_map/ppermute | solution.py:688
  170.1 1.7 collective-permute-done.55.refs_8_
  171.8 3.5 %weights_final.1 = (f32[192,2304]{1,0:T(8,128)}, f32[192,768]{1,0:T(8,128)}, f32[192,3072]{1,0:T(8,128)}, f32[768]{0:T(1024)}, f32[192]{0:T(256)}, /*index=5*/f3...) custom-call(s32[3]{0:T(128)S(1)} %copy-done.6, ...), custom_call_target="tpu_custom_call" | custom-call | tf_op jit(solution)/shard_map/weights_final/pallas_call | solution.py:636
  (93 shorter events, 16.0 us)
Async XLA Ops:
  4.0 13.5 %collective-permute-start.1 = (bf16[128,768]{1,0:T(8,128)(2,1)}, bf16[128,768]{1,0:T(8,128)(2,1)S(1)}, u32[]{:S(2)}, u32[]{:S(2)}) collective-permute-start(bf16[128,768]{1,0:T(8,128)(2,1)} %get-tuple-element.98.refs_3_.refs_1_.refs_4_.refs_0_), channel_id=1, source_target_pairs={{0,4},{1,5},{2,6},{3,7},{4,0},{5,1},{6,2},{7,3},{8,12},{9,13},{10,... | collective-permute-start | bytes 589832 | tf_op jit(solution)/shard_map/ppermute | solution.py:688
  8.2 19.1 %copy-start = (bf16[192,2304]{1,0:T(8,128)(2,1)S(1)}, bf16[192,2304]{1,0:T(8,128)(2,1)}, u32[]{:S(2)}) copy-start(bf16[192,2304]{1,0:T(8,128)(2,1)} %refs_1_.5) | copy-start | bytes 2654212
  8.2 19.1 %copy-start.1 = (bf16[128,768]{1,0:T(8,128)(2,1)S(1)}, bf16[128,768]{1,0:T(8,128)(2,1)}, u32[]{:S(2)}) copy-start(bf16[128,768]{1,0:T(8,128)(2,1)} %get-tuple-element.98.refs_3_.refs_1_.refs_4_.refs_0_) | copy-start | bytes 589828
  8.2 19.1 %copy-start.2 = (bf16[192,768]{1,0:T(8,128)(2,1)S(1)}, bf16[192,768]{1,0:T(8,128)(2,1)}, u32[]{:S(2)}) copy-start(bf16[192,768]{1,0:T(8,128)(2,1)} %refs_2_.4) | copy-start | bytes 884740
  8.2 19.1 %copy-start.3 = (bf16[192,768]{1,0:T(8,128)(2,1)S(1)}, bf16[192,768]{1,0:T(8,128)(2,1)}, u32[]{:S(2)}) copy-start(bf16[192,768]{1,0:T(8,128)(2,1)} %get-tuple-element.99.refs_7_.refs_3_) | copy-start | bytes 884740
  8.2 19.1 %copy-start.6 = (s32[3]{0:T(128)S(1)}, s32[3]{0:T(128)}, u32[]{:S(2)}) copy-start(s32[3]{0:T(128)} %pad_add_fusion.refs_0_) | copy-start | bytes 40
  8.2 13.3 %collective-permute-start.5 = (bf16[192,768]{1,0:T(8,128)(2,1)}, bf16[192,768]{1,0:T(8,128)(2,1)S(1)}, u32[]{:S(2)}, u32[]{:S(2)}) collective-permute-start(bf16[192,768]{1,0:T(8,128)(2,1)} %get-tuple-element.99.refs_7_.refs_3_), channel_id=1, source_target_pairs={{0,24},{8,16},{16,8},{24,0},{1,25},{9,17},{17,9},{25,1},{2,26},{10... | collective-permute-start | bytes 884744 | tf_op jit(solution)/shard_map/ppermute | solution.py:693
  10.7 13.4 %collective-permute-start.4 = (bf16[192,768]{1,0:T(8,128)(2,1)}, bf16[192,768]{1,0:T(8,128)(2,1)S(1)}, u32[]{:S(2)}, u32[]{:S(2)}) collective-permute-start(bf16[192,768]{1,0:T(8,128)(2,1)} %get-tuple-element.99.refs_7_.refs_3_), channel_id=1, source_target_pairs={{0,16},{8,24},{16,0},{24,8},{1,17},{9,25},{17,1},{25,9},{2,18},{10... | collective-permute-start | bytes 884744 | tf_op jit(solution)/shard_map/ppermute | solution.py:693
  11.2 13.0 %collective-permute-start.3 = (bf16[192,768]{1,0:T(8,128)(2,1)}, bf16[192,768]{1,0:T(8,128)(2,1)S(1)}, u32[]{:S(2)}, u32[]{:S(2)}) collective-permute-start(bf16[192,768]{1,0:T(8,128)(2,1)} %get-tuple-element.99.refs_7_.refs_3_), channel_id=1, source_target_pairs={{0,8},{8,0},{16,24},{24,16},{1,9},{9,1},{17,25},{25,17},{2,10},{10... | collective-permute-start | bytes 884744 | tf_op jit(solution)/shard_map/ppermute | solution.py:693
  11.7 9.8 %collective-permute-start = (bf16[128,768]{1,0:T(8,128)(2,1)}, bf16[128,768]{1,0:T(8,128)(2,1)S(1)}, u32[]{:S(2)}, u32[]{:S(2)}) collective-permute-start(bf16[128,768]{1,0:T(8,128)(2,1)} %get-tuple-element.98.refs_3_.refs_1_.refs_4_.refs_0_), channel_id=1, source_target_pairs={{0,2},{1,3},{2,0},{3,1},{4,6},{5,7},{6,4},{7,5},{8,10},{9,11},{10,... | collective-permute-start | bytes 589832 | tf_op jit(solution)/shard_map/ppermute | solution.py:688
  17.6 7.1 %collective-permute-start.2 = (bf16[128,768]{1,0:T(8,128)(2,1)S(1)}, bf16[128,768]{1,0:T(8,128)(2,1)S(1)}, u32[]{:S(2)}, u32[]{:S(2)}) collective-permute-start(bf16[128,768]{1,0:T(8,128)(2,1)S(1)} %collective-permute-done.1.refs_4_.refs_5_.refs_6_), channel_id=1, source_target_pairs={{0,2},{1,3},{2,0},{3,1},{4,6},{5,7},{6,4},{7,5},{8,10},{9,11},{10,... | collective-permute-start | bytes 589832 | tf_op jit(solution)/shard_map/ppermute | solution.py:688
  24.8 4.9 %copy-start.4 = (bf16[192,3072]{1,0:T(8,128)(2,1)S(1)}, bf16[192,3072]{1,0:T(8,128)(2,1)}, u32[]{:S(2)}) copy-start(bf16[192,3072]{1,0:T(8,128)(2,1)} %refs_3_.3) | copy-start | bytes 3538948
  24.8 2.5 %collective-permute-start.6 = (bf16[576,768]{1,0:T(8,128)(2,1)S(1)}, bf16[576,768]{1,0:T(8,128)(2,1)S(1)}, u32[]{:S(2)}, u32[]{:S(2)}) collective-permute-start(bf16[576,768]{1,0:T(8,128)(2,1)S(1)} %pack_stack.1.refs_8_), channel_id=1, source_target_pairs={{0,1},{1,0},{2,3},{3,2},{4,5},{5,4},{6,7},{7,6},{8,9},{9,8},{10,11... | collective-permute-start | bytes 2654216 | tf_op jit(solution)/shard_map/ppermute | solution.py:685
  29.4 4.4 %collective-permute-start.7 = (bf16[512,384]{1,0:T(8,128)(2,1)S(1)}, bf16[512,384]{1,0:T(8,128)(2,1)S(1)}, u32[]{:S(2)}, u32[]{:S(2)}) collective-permute-start(bf16[512,384]{1,0:T(8,128)(2,1)S(1)} %get-tuple-element.103.refs_3_), channel_id=1, source_target_pairs={{0,1},{1,0},{2,3},{3,2},{4,5},{5,4},{6,7},{7,6},{8,9},{9,8},{10,11... | collective-permute-start | bytes 1179656 | tf_op jit(solution)/shard_map/ppermute | solution.py:685
  30.2 19.4 %collective-permute-start.11 = (bf16[224,768]{1,0:T(8,128)(2,1)S(1)}, bf16[224,768]{1,0:T(8,128)(2,1)S(1)}, u32[]{:S(2)}, u32[]{:S(2)}) collective-permute-start(bf16[224,768]{1,0:T(8,128)(2,1)S(1)} %get-tuple-element.109), channel_id=1, source_target_pairs={{0,8},{8,0},{16,24},{24,16},{1,9},{9,1},{17,25},{25,17},{2,10},{10... | collective-permute-start | bytes 1032200 | tf_op jit(solution)/shard_map/ppermute | solution.py:693
  31.9 17.7 %collective-permute-start.12 = (bf16[224,768]{1,0:T(8,128)(2,1)S(1)}, bf16[224,768]{1,0:T(8,128)(2,1)S(1)}, u32[]{:S(2)}, u32[]{:S(2)}) collective-permute-start(bf16[224,768]{1,0:T(8,128)(2,1)S(1)} %get-tuple-element.110), channel_id=1, source_target_pairs={{0,16},{8,24},{16,0},{24,8},{1,17},{9,25},{17,1},{25,9},{2,18},{10... | collective-permute-start | bytes 1032200 | tf_op jit(solution)/shard_map/ppermute | solution.py:693
  33.4 16.2 %collective-permute-start.13 = (bf16[224,768]{1,0:T(8,128)(2,1)S(1)}, bf16[224,768]{1,0:T(8,128)(2,1)S(1)}, u32[]{:S(2)}, u32[]{:S(2)}) collective-permute-start(bf16[224,768]{1,0:T(8,128)(2,1)S(1)} %get-tuple-element.111), channel_id=1, source_target_pairs={{0,24},{8,16},{16,8},{24,0},{1,25},{9,17},{17,9},{25,1},{2,26},{10... | collective-permute-start | bytes 1032200 | tf_op jit(solution)/shard_map/ppermute | solution.py:693
  37.6 4.8 %collective-permute-start.8 = (bf16[128,192]{1,0:T(8,128)(2,1)S(1)}, bf16[128,192]{1,0:T(8,128)(2,1)S(1)}, u32[]{:S(2)}, u32[]{:S(2)}) collective-permute-start(bf16[128,192]{1,0:T(8,128)(2,1)S(1)} %get-tuple-element.105), channel_id=1, source_target_pairs={{0,2},{1,3},{2,0},{3,1},{4,6},{5,7},{6,4},{7,5},{8,10},{9,11},{10,... | collective-permute-start | bytes 147464 | tf_op jit(solution)/shard_map/ppermute | solution.py:688
  38.8 6.6 %collective-permute-start.9 = (bf16[128,192]{1,0:T(8,128)(2,1)S(1)}, bf16[128,192]{1,0:T(8,128)(2,1)S(1)}, u32[]{:S(2)}, u32[]{:S(2)}) collective-permute-start(bf16[128,192]{1,0:T(8,128)(2,1)S(1)} %get-tuple-element.106), channel_id=1, source_target_pairs={{0,4},{1,5},{2,6},{3,7},{4,0},{5,1},{6,2},{7,3},{8,12},{9,13},{10,... | collective-permute-start | bytes 147464 | tf_op jit(solution)/shard_map/ppermute | solution.py:688
  42.4 6.1 %collective-permute-start.10 = (bf16[128,192]{1,0:T(8,128)(2,1)S(1)}, bf16[128,192]{1,0:T(8,128)(2,1)S(1)}, u32[]{:S(2)}, u32[]{:S(2)}) collective-permute-start(bf16[128,192]{1,0:T(8,128)(2,1)S(1)} %get-tuple-element.107), channel_id=1, source_target_pairs={{0,6},{1,7},{2,4},{3,5},{4,2},{5,3},{6,0},{7,1},{8,14},{9,15},{10,... | collective-permute-start | bytes 147464 | tf_op jit(solution)/shard_map/ppermute | solution.py:688
  49.6 12.8 %copy-start.7 = (bf16[768,768]{1,0:T(8,128)(2,1)S(1)}, bf16[768,768]{1,0:T(8,128)(2,1)}, u32[]{:S(2)}) copy-start(bf16[768,768]{1,0:T(8,128)(2,1)} %refs_2_.5) | copy-start | bytes 3538948
  49.6 12.8 %copy-start.8 = (bf16[768]{0:T(1024)(128)(2,1)S(1)}, bf16[768]{0:T(1024)(128)(2,1)}, u32[]{:S(2)}) copy-start(bf16[768]{0:T(1024)(128)(2,1)} %refs_1_.8) | copy-start | bytes 4612
  49.7 12.7 %collective-permute-start.14 = (bf16[288,768]{1,0:T(8,128)(2,1)S(1)}, bf16[288,768]{1,0:T(8,128)(2,1)S(1)}, u32[]{:S(2)}, u32[]{:S(2)}) collective-permute-start(bf16[288,768]{1,0:T(8,128)(2,1)S(1)} %expand_stack.1), channel_id=1, source_target_pairs={{0,1},{1,0},{2,3},{3,2},{4,5},{5,4},{6,7},{7,6},{8,9},{9,8},{10,11... | collective-permute-start | bytes 1327112 | tf_op jit(solution)/shard_map/ppermute | solution.py:685
  49.7 8.7 %collective-permute-start.17 = (bf16[128,768]{1,0:T(8,128)(2,1)S(1)}, bf16[128,768]{1,0:T(8,128)(2,1)S(1)}, u32[]{:S(2)}, u32[]{:S(2)}) collective-permute-start(bf16[128,768]{1,0:T(8,128)(2,1)S(1)} %get-tuple-element.112.refs_3_.refs_6_), channel_id=1, source_target_pairs={{0,24},{8,16},{16,8},{24,0},{1,25},{9,17},{17,9},{25,1},{2,26},{10... | collective-permute-start | bytes 589832 | tf_op jit(solution)/shard_map/ppermute | solution.py:693
  52.3 9.9 %collective-permute-start.16 = (bf16[128,768]{1,0:T(8,128)(2,1)S(1)}, bf16[128,768]{1,0:T(8,128)(2,1)S(1)}, u32[]{:S(2)}, u32[]{:S(2)}) collective-permute-start(bf16[128,768]{1,0:T(8,128)(2,1)S(1)} %get-tuple-element.112.refs_3_.refs_6_), channel_id=1, source_target_pairs={{0,16},{8,24},{16,0},{24,8},{1,17},{9,25},{17,1},{25,9},{2,18},{10... | collective-permute-start | bytes 589832 | tf_op jit(solution)/shard_map/ppermute | solution.py:693
  52.8 9.5 %collective-permute-start.15 = (bf16[128,768]{1,0:T(8,128)(2,1)S(1)}, bf16[128,768]{1,0:T(8,128)(2,1)S(1)}, u32[]{:S(2)}, u32[]{:S(2)}) collective-permute-start(bf16[128,768]{1,0:T(8,128)(2,1)S(1)} %get-tuple-element.112.refs_3_.refs_6_), channel_id=1, source_target_pairs={{0,8},{8,0},{16,24},{24,16},{1,9},{9,1},{17,25},{25,17},{2,10},{10... | collective-permute-start | bytes 589832 | tf_op jit(solution)/shard_map/ppermute | solution.py:693
  67.9 2.9 %collective-permute-start.24 = (bf16[4,384,384]{2,1,0:T(8,128)(2,1)S(1)}, bf16[4,384,384]{2,1,0:T(8,128)(2,1)S(1)}, u32[]{:S(2)}, u32[]{:S(2)}) collective-permute-start(bf16[4,384,384]{2,1,0:T(8,128)(2,1)S(1)} %get-tuple-element.125), channel_id=1, source_target_pairs={{0,1},{1,0},{2,3},{3,2},{4,5},{5,4},{6,7},{7,6},{8,9},{9,8},{10,11... | collective-permute-start | bytes 3538952 | tf_op jit(solution)/shard_map/ppermute | solution.py:685
  71.7 20.2 %collective-permute-start.28 = (bf16[2,384,384]{2,1,0:T(8,128)(2,1)S(1)}, bf16[2,384,384]{2,1,0:T(8,128)(2,1)S(1)}, u32[]{:S(2)}, u32[]{:S(2)}) collective-permute-start(bf16[2,384,384]{2,1,0:T(8,128)(2,1)S(1)} %get-tuple-element.126.refs_9_), channel_id=1, source_target_pairs={{0,2},{1,3},{2,0},{3,1},{4,6},{5,7},{6,4},{7,5},{8,10},{9,11},{10,... | collective-permute-start | bytes 1769480 | tf_op jit(solution)/shard_map/ppermute | solution.py:688
  72.4 7.8 %collective-permute-start.21 = (bf16[128,768]{1,0:T(8,128)(2,1)S(1)}, bf16[128,768]{1,0:T(8,128)(2,1)S(1)}, u32[]{:S(2)}, u32[]{:S(2)}) collective-permute-start(bf16[128,768]{1,0:T(8,128)(2,1)S(1)} %get-tuple-element.121), channel_id=1, source_target_pairs={{0,8},{8,0},{16,24},{24,16},{1,9},{9,1},{17,25},{25,17},{2,10},{10... | collective-permute-start | bytes 589832 | tf_op jit(solution)/shard_map/ppermute | solution.py:693
  73.3 10.9 %collective-permute-start.22 = (bf16[128,768]{1,0:T(8,128)(2,1)S(1)}, bf16[128,768]{1,0:T(8,128)(2,1)S(1)}, u32[]{:S(2)}, u32[]{:S(2)}) collective-permute-start(bf16[128,768]{1,0:T(8,128)(2,1)S(1)} %get-tuple-element.122), channel_id=1, source_target_pairs={{0,16},{8,24},{16,0},{24,8},{1,17},{9,25},{17,1},{25,9},{2,18},{10... | collective-permute-start | bytes 589832 | tf_op jit(solution)/shard_map/ppermute | solution.py:693
  74.3 9.9 %collective-permute-start.23 = (bf16[128,768]{1,0:T(8,128)(2,1)S(1)}, bf16[128,768]{1,0:T(8,128)(2,1)S(1)}, u32[]{:S(2)}, u32[]{:S(2)}) collective-permute-start(bf16[128,768]{1,0:T(8,128)(2,1)S(1)} %get-tuple-element.123), channel_id=1, source_target_pairs={{0,24},{8,16},{16,8},{24,0},{1,25},{9,17},{17,9},{25,1},{2,26},{10... | collective-permute-start | bytes 589832 | tf_op jit(solution)/shard_map/ppermute | solution.py:693
  85.6 6.2 %collective-permute-start.27 = (bf16[128,192]{1,0:T(8,128)(2,1)S(1)}, bf16[128,192]{1,0:T(8,128)(2,1)S(1)}, u32[]{:S(2)}, u32[]{:S(2)}) collective-permute-start(bf16[128,192]{1,0:T(8,128)(2,1)S(1)} %get-tuple-element.130), channel_id=1, source_target_pairs={{0,6},{1,7},{2,4},{3,5},{4,2},{5,3},{6,0},{7,1},{8,14},{9,15},{10,... | collective-permute-start | bytes 147464 | tf_op jit(solution)/shard_map/ppermute | solution.py:688
  88.5 4.7 %collective-permute-start.25 = (bf16[128,192]{1,0:T(8,128)(2,1)S(1)}, bf16[128,192]{1,0:T(8,128)(2,1)S(1)}, u32[]{:S(2)}, u32[]{:S(2)}) collective-permute-start(bf16[128,192]{1,0:T(8,128)(2,1)S(1)} %get-tuple-element.128), channel_id=1, source_target_pairs={{0,2},{1,3},{2,0},{3,1},{4,6},{5,7},{6,4},{7,5},{8,10},{9,11},{10,... | collective-permute-start | bytes 147464 | tf_op jit(solution)/shard_map/ppermute | solution.py:688
  89.3 5.2 %collective-permute-start.26 = (bf16[128,192]{1,0:T(8,128)(2,1)S(1)}, bf16[128,192]{1,0:T(8,128)(2,1)S(1)}, u32[]{:S(2)}, u32[]{:S(2)}) collective-permute-start(bf16[128,192]{1,0:T(8,128)(2,1)S(1)} %get-tuple-element.129), channel_id=1, source_target_pairs={{0,4},{1,5},{2,6},{3,7},{4,0},{5,1},{6,2},{7,3},{8,12},{9,13},{10,... | collective-permute-start | bytes 147464 | tf_op jit(solution)/shard_map/ppermute | solution.py:688
  91.1 10.2 %collective-permute-start.32 = (bf16[4,192,384]{2,1,0:T(8,128)(2,1)S(1)}, bf16[4,192,384]{2,1,0:T(8,128)(2,1)S(1)}, u32[]{:S(2)}, u32[]{:S(2)}) collective-permute-start(bf16[4,192,384]{2,1,0:T(8,128)(2,1)S(1)} %get-tuple-element.134.refs_12_), channel_id=1, source_target_pairs={{0,1},{1,0},{2,3},{3,2},{4,5},{5,4},{6,7},{7,6},{8,9},{9,8},{10,11... | collective-permute-start | bytes 1769480 | tf_op jit(solution)/shard_map/ppermute | solution.py:685
  99.5 6.0 %collective-permute-start.29 = (bf16[512,384]{1,0:T(8,128)(2,1)S(1)}, bf16[512,384]{1,0:T(8,128)(2,1)S(1)}, u32[]{:S(2)}, u32[]{:S(2)}) collective-permute-start(bf16[512,384]{1,0:T(8,128)(2,1)S(1)} %get-tuple-element.137), channel_id=1, source_target_pairs={{0,1},{1,0},{2,3},{3,2},{4,5},{5,4},{6,7},{7,6},{8,9},{9,8},{10,11... | collective-permute-start | bytes 1179656 | tf_op jit(solution)/shard_map/ppermute | solution.py:685
  99.6 9.1 %collective-permute-start.18 = (bf16[128,768]{1,0:T(8,128)(2,1)S(1)}, bf16[128,768]{1,0:T(8,128)(2,1)S(1)}, u32[]{:S(2)}, u32[]{:S(2)}) collective-permute-start(bf16[128,768]{1,0:T(8,128)(2,1)S(1)} %get-tuple-element.114), channel_id=1, source_target_pairs={{0,8},{8,0},{16,24},{24,16},{1,9},{9,1},{17,25},{25,17},{2,10},{10... | collective-permute-start | bytes 589832 | tf_op jit(solution)/shard_map/ppermute | solution.py:693
  100.2 16.4 %collective-permute-start.31 = (bf16[384,384]{1,0:T(8,128)(2,1)S(1)}, bf16[384,384]{1,0:T(8,128)(2,1)S(1)}, u32[]{:S(2)}, u32[]{:S(2)}) collective-permute-start(bf16[384,384]{1,0:T(8,128)(2,1)S(1)} %get-tuple-element.132.refs_11_), channel_id=1, source_target_pairs={{0,4},{1,5},{2,6},{3,7},{4,0},{5,1},{6,2},{7,3},{8,12},{9,13},{10,... | collective-permute-start | bytes 884744 | tf_op jit(solution)/shard_map/ppermute | solution.py:688
  102.1 15.5 %collective-permute-start.33 = (bf16[4,48,768]{2,1,0:T(8,128)(2,1)S(1)}, bf16[4,48,768]{2,1,0:T(8,128)(2,1)S(1)}, u32[]{:S(2)}, u32[]{:S(2)}) collective-permute-start(bf16[4,48,768]{2,1,0:T(8,128)(2,1)S(1)} %get-tuple-element.152), channel_id=1, source_target_pairs={{0,2},{1,3},{2,0},{3,1},{4,6},{5,7},{6,4},{7,5},{8,10},{9,11},{10,... | collective-permute-start | bytes 884744 | tf_op jit(solution)/shard_map/ppermute | solution.py:688
  104.2 10.6 %collective-permute-start.19 = (bf16[128,768]{1,0:T(8,128)(2,1)S(1)}, bf16[128,768]{1,0:T(8,128)(2,1)S(1)}, u32[]{:S(2)}, u32[]{:S(2)}) collective-permute-start(bf16[128,768]{1,0:T(8,128)(2,1)S(1)} %get-tuple-element.115), channel_id=1, source_target_pairs={{0,16},{8,24},{16,0},{24,8},{1,17},{9,25},{17,1},{25,9},{2,18},{10... | collective-permute-start | bytes 589832 | tf_op jit(solution)/shard_map/ppermute | solution.py:693
  105.5 9.3 %collective-permute-start.20 = (bf16[128,768]{1,0:T(8,128)(2,1)S(1)}, bf16[128,768]{1,0:T(8,128)(2,1)S(1)}, u32[]{:S(2)}, u32[]{:S(2)}) collective-permute-start(bf16[128,768]{1,0:T(8,128)(2,1)S(1)} %get-tuple-element.116), channel_id=1, source_target_pairs={{0,24},{8,16},{16,8},{24,0},{1,25},{9,17},{17,9},{25,1},{2,26},{10... | collective-permute-start | bytes 589832 | tf_op jit(solution)/shard_map/ppermute | solution.py:693
  108.7 19.4 %collective-permute-start.30 = (bf16[2,128,768]{2,1,0:T(8,128)(2,1)S(1)}, bf16[2,128,768]{2,1,0:T(8,128)(2,1)S(1)}, u32[]{:S(2)}, u32[]{:S(2)}) collective-permute-start(bf16[2,128,768]{2,1,0:T(8,128)(2,1)S(1)} %get-tuple-element.148), channel_id=1, source_target_pairs={{0,2},{1,3},{2,0},{3,1},{4,6},{5,7},{6,4},{7,5},{8,10},{9,11},{10,... | collective-permute-start | bytes 1179656 | tf_op jit(solution)/shard_map/ppermute | solution.py:688
  114.8 3.6 %collective-permute-start.34 = (bf16[96,768]{1,0:T(8,128)(2,1)S(1)}, bf16[96,768]{1,0:T(8,128)(2,1)S(1)}, u32[]{:S(2)}, u32[]{:S(2)}) collective-permute-start(bf16[96,768]{1,0:T(8,128)(2,1)S(1)} %get-tuple-element.153), channel_id=1, source_target_pairs={{0,1},{1,0},{2,3},{3,2},{4,5},{5,4},{6,7},{7,6},{8,9},{9,8},{10,11... | collective-permute-start | bytes 442376 | tf_op jit(solution)/shard_map/ppermute | solution.py:685
  114.8 3.6 %collective-permute-start.35 = (bf16[96,768]{1,0:T(8,128)(2,1)S(1)}, bf16[96,768]{1,0:T(8,128)(2,1)S(1)}, u32[]{:S(2)}, u32[]{:S(2)}) collective-permute-start(bf16[96,768]{1,0:T(8,128)(2,1)S(1)} %get-tuple-element.154), channel_id=1, source_target_pairs={{0,1},{1,0},{2,3},{3,2},{4,5},{5,4},{6,7},{7,6},{8,9},{9,8},{10,11... | collective-permute-start | bytes 442376 | tf_op jit(solution)/shard_map/ppermute | solution.py:685
  116.6 1.8 %collective-permute-start.36 = (bf16[96,768]{1,0:T(8,128)(2,1)S(1)}, bf16[96,768]{1,0:T(8,128)(2,1)S(1)}, u32[]{:S(2)}, u32[]{:S(2)}) collective-permute-start(bf16[96,768]{1,0:T(8,128)(2,1)S(1)} %get-tuple-element.155), channel_id=1, source_target_pairs={{0,1},{1,0},{2,3},{3,2},{4,5},{5,4},{6,7},{7,6},{8,9},{9,8},{10,11... | collective-permute-start | bytes 442376 | tf_op jit(solution)/shard_map/ppermute | solution.py:685
  117.6 1.4 collective-permute-start.37
  119.9 10.2 %collective-permute-start.43 = (bf16[192,384]{1,0:T(8,128)(2,1)S(1)}, bf16[192,384]{1,0:T(8,128)(2,1)S(1)}, u32[]{:S(2)}, u32[]{:S(2)}) collective-permute-start(bf16[192,384]{1,0:T(8,128)(2,1)S(1)} %get-tuple-element.158.refs_2_.refs_1_), channel_id=1, source_target_pairs={{0,4},{1,5},{2,6},{3,7},{4,0},{5,1},{6,2},{7,3},{8,12},{9,13},{10,... | collective-permute-start | bytes 442376 | tf_op jit(solution)/shard_map/ppermute | solution.py:688
  121.2 10.4 %collective-permute-start.42 = (bf16[192,384]{1,0:T(8,128)(2,1)S(1)}, bf16[192,384]{1,0:T(8,128)(2,1)S(1)}, u32[]{:S(2)}, u32[]{:S(2)}) collective-permute-start(bf16[192,384]{1,0:T(8,128)(2,1)S(1)} %get-tuple-element.158.refs_2_.refs_1_), channel_id=1, source_target_pairs={{0,2},{1,3},{2,0},{3,1},{4,6},{5,7},{6,4},{7,5},{8,10},{9,11},{10,... | collective-permute-start | bytes 442376 | tf_op jit(solution)/shard_map/ppermute | solution.py:688
  123.7 9.8 %collective-permute-start.39 = (bf16[176,768]{1,0:T(8,128)(2,1)S(1)}, bf16[176,768]{1,0:T(8,128)(2,1)S(1)}, u32[]{:S(2)}, u32[]{:S(2)}) collective-permute-start(bf16[176,768]{1,0:T(8,128)(2,1)S(1)} %get-tuple-element.163), channel_id=1, source_target_pairs={{0,8},{8,0},{16,24},{24,16},{1,9},{9,1},{17,25},{25,17},{2,10},{10... | collective-permute-start | bytes 811016 | tf_op jit(solution)/shard_map/ppermute | solution.py:693
  125.2 13.5 %collective-permute-start.40 = (bf16[176,768]{1,0:T(8,128)(2,1)S(1)}, bf16[176,768]{1,0:T(8,128)(2,1)S(1)}, u32[]{:S(2)}, u32[]{:S(2)}) collective-permute-start(bf16[176,768]{1,0:T(8,128)(2,1)S(1)} %get-tuple-element.164), channel_id=1, source_target_pairs={{0,16},{8,24},{16,0},{24,8},{1,17},{9,25},{17,1},{25,9},{2,18},{10... | collective-permute-start | bytes 811016 | tf_op jit(solution)/shard_map/ppermute | solution.py:693
  128.1 10.6 %collective-permute-start.41 = (bf16[176,768]{1,0:T(8,128)(2,1)S(1)}, bf16[176,768]{1,0:T(8,128)(2,1)S(1)}, u32[]{:S(2)}, u32[]{:S(2)}) collective-permute-start(bf16[176,768]{1,0:T(8,128)(2,1)S(1)} %get-tuple-element.165), channel_id=1, source_target_pairs={{0,24},{8,16},{16,8},{24,0},{1,25},{9,17},{17,9},{25,1},{2,26},{10... | collective-permute-start | bytes 811016 | tf_op jit(solution)/shard_map/ppermute | solution.py:693
  130.1 10.7 %collective-permute-start.38 = (bf16[128,768]{1,0:T(8,128)(2,1)S(1)}, bf16[128,768]{1,0:T(8,128)(2,1)S(1)}, u32[]{:S(2)}, u32[]{:S(2)}) collective-permute-start(bf16[128,768]{1,0:T(8,128)(2,1)S(1)} %get-tuple-element.160), channel_id=1, source_target_pairs={{0,4},{1,5},{2,6},{3,7},{4,0},{5,1},{6,2},{7,3},{8,12},{9,13},{10,... | collective-permute-start | bytes 589832 | tf_op jit(solution)/shard_map/ppermute | solution.py:688
  131.6 7.1 %collective-permute-start.44 = (bf16[192,384]{1,0:T(8,128)(2,1)S(1)}, bf16[192,384]{1,0:T(8,128)(2,1)S(1)}, u32[]{:S(2)}, u32[]{:S(2)}) collective-permute-start(bf16[192,384]{1,0:T(8,128)(2,1)S(1)} %collective-permute-done.43.refs_3_), channel_id=1, source_target_pairs={{0,2},{1,3},{2,0},{3,1},{4,6},{5,7},{6,4},{7,5},{8,10},{9,11},{10,... | collective-permute-start | bytes 442376 | tf_op jit(solution)/shard_map/ppermute | solution.py:688
  141.5 18.1 %collective-permute-start.46 = (bf16[240,768]{1,0:T(8,128)(2,1)S(1)}, bf16[240,768]{1,0:T(8,128)(2,1)S(1)}, u32[]{:S(2)}, u32[]{:S(2)}) collective-permute-start(bf16[240,768]{1,0:T(8,128)(2,1)S(1)} %shares.1.refs_1_), channel_id=1, source_target_pairs={{0,4},{1,5},{2,6},{3,7},{4,0},{5,1},{6,2},{7,3},{8,12},{9,13},{10,... | collective-permute-start | bytes 1105928 | tf_op jit(solution)/shard_map/ppermute | solution.py:688
  142.4 17.4 %collective-permute-start.45 = (bf16[240,768]{1,0:T(8,128)(2,1)S(1)}, bf16[240,768]{1,0:T(8,128)(2,1)S(1)}, u32[]{:S(2)}, u32[]{:S(2)}) collective-permute-start(bf16[240,768]{1,0:T(8,128)(2,1)S(1)} %shares.1.refs_1_), channel_id=1, source_target_pairs={{0,2},{1,3},{2,0},{3,1},{4,6},{5,7},{6,4},{7,5},{8,10},{9,11},{10,... | collective-permute-start | bytes 1105928 | tf_op jit(solution)/shard_map/ppermute | solution.py:688
  144.9 1.4 collective-permute-start.47
  144.9 1.6 collective-permute-start.49
  145.4 1.4 collective-permute-start.48
  146.2 1.4 collective-permute-start.50
  159.8 10.3 %collective-permute-start.51 = (bf16[240,768]{1,0:T(8,128)(2,1)S(1)}, bf16[240,768]{1,0:T(8,128)(2,1)S(1)}, u32[]{:S(2)}, u32[]{:S(2)}) collective-permute-start(bf16[240,768]{1,0:T(8,128)(2,1)S(1)} %pass_on.1), channel_id=1, source_target_pairs={{0,2},{1,3},{2,0},{3,1},{4,6},{5,7},{6,4},{7,5},{8,10},{9,11},{10,... | collective-permute-start | bytes 1105928 | tf_op jit(solution)/shard_map/ppermute | solution.py:688
  159.9 10.2 %collective-permute-start.52 = (bf16[240,768]{1,0:T(8,128)(2,1)S(1)}, bf16[240,768]{1,0:T(8,128)(2,1)S(1)}, u32[]{:S(2)}, u32[]{:S(2)}) collective-permute-start(bf16[240,768]{1,0:T(8,128)(2,1)S(1)} %shares.1.refs_1_), channel_id=1, source_target_pairs={{0,1},{1,0},{2,3},{3,2},{4,5},{5,4},{6,7},{7,6},{8,9},{9,8},{10,11... | collective-permute-start | bytes 1105928 | tf_op jit(solution)/shard_map/ppermute | solution.py:685
  159.9 10.2 %collective-permute-start.54 = (bf16[240,768]{1,0:T(8,128)(2,1)S(1)}, bf16[240,768]{1,0:T(8,128)(2,1)S(1)}, u32[]{:S(2)}, u32[]{:S(2)}) collective-permute-start(bf16[240,768]{1,0:T(8,128)(2,1)S(1)} %collective-permute-done.46.refs_0_.refs_3_), channel_id=1, source_target_pairs={{0,1},{1,0},{2,3},{3,2},{4,5},{5,4},{6,7},{7,6},{8,9},{9,8},{10,11... | collective-permute-start | bytes 1105928 | tf_op jit(solution)/shard_map/ppermute | solution.py:685
  160.4 9.7 %collective-permute-start.53 = (bf16[240,768]{1,0:T(8,128)(2,1)S(1)}, bf16[240,768]{1,0:T(8,128)(2,1)S(1)}, u32[]{:S(2)}, u32[]{:S(2)}) collective-permute-start(bf16[240,768]{1,0:T(8,128)(2,1)S(1)} %collective-permute-done.45.refs_3_.refs_2_), channel_id=1, source_target_pairs={{0,1},{1,0},{2,3},{3,2},{4,5},{5,4},{6,7},{7,6},{8,9},{9,8},{10,11... | collective-permute-start | bytes 1105928 | tf_op jit(solution)/shard_map/ppermute | solution.py:685
  170.1 1.7 collective-permute-start.55
  (2 other events, 9.3 us)

commit v7 on v6

--- a/solution.py
+++ b/solution.py
@@ -1348,7 +1348,6 @@
                 pltpu.VMEM((own_width, half_ff), f32),
                 pltpu.VMEM((seq_parts, half_own, width), bf),
             ],
-            after=[block_done],
         )
         dp_parts = [dp_out[0]] + [seq_swap(dp_out[j], j) for j in others]
         con_one = dp_out[seq_parts]
@@ -1413,7 +1412,7 @@
             [info] + dp_parts,
             scalars=1,
             scratch=[pltpu.VMEM((own_width, half_ff), f32)],
-            after=[con_one_far, con_two_far, gt_far_two],
+            after=[con_one_far, con_two_far, gt_far_two, block_done],
         )
         last_two = chip_swap(last_one, 2)
         last_one_far = chip_swap(last_one, 1)

time: 176 us -> 178 us (1.011)
  waiting for transfers between devices: 81.2 us -> 83.3 us
  transfers between devices with their start and end apart: 56 -> 56, of which waited for: 34 -> 32; matrix products, arithmetic and copies ran while one was open for 0% -> 0% of each run, Pallas kernels for 13% -> 12%
where the time goes in v7:
time: 178 us
  waiting for transfers between devices  83.3 us (47%)
  starting transfers between devices  55 us (31%)
  Pallas kernels  37.8 us (21%)
    ppermute x20, waiting for transfers between devices, chip_swap(): lax.ppermute(member, 'ctx', [(i, 2 * (i // 2 ^ step) + i % 2) for i in ra...  43.5 us
    pallas_call x24, Pallas kernels, local_call(): pl.pallas_call(ordered, out_shape=tuple(outs), in_specs=[pl.BlockSpec(mem...  37.8 us
    ppermute x20, starting transfers between devices, chip_swap(): lax.ppermute(member, 'ctx', [(i, 2 * (i // 2 ^ step) + i % 2) for i in ra...  31.3 us
    ppermute x18, waiting for transfers between devices, seq_swap(): return lax.ppermute(member, 'dp', [(i, i ^ step) for i in range(seq_parts)])  30.8 us
    ppermute x18, starting transfers between devices, seq_swap(): return lax.ppermute(member, 'dp', [(i, i ^ step) for i in range(seq_parts)])  21.1 us
    ppermute x18, waiting for transfers between devices, core_swap(): return lax.ppermute(member, 'ctx', [(i, i ^ 1) for i in range(ranks)])  9.02 us
  transfers between devices with their start and end apart: 56, of which 32 were waited for; matrix products, arithmetic and copies ran while one was open for 0% of the time, Pallas kernels for 12%

profile of v7, /device:TPU:0, one launch (start us, length us, event | category | flops | bytes accessed | tf_op | source)
XLA Modules:
  0.0 177.9 jit_solution(11503460641361109452)
XLA Ops:
  1.3 2.8 %pack.1 = (bf16[192,768]{1,0:T(8,128)(2,1)}, bf16[128,768]{1,0:T(8,128)(2,1)}) custom-call(s32[3]{0:T(128)} %pad_add_fusion.refs_0_, bf16[128,768]{1,0:T(8,128)(2,1)} %bitcast.8, bf16[192,2304]{1,0:T(8,128)(2,1)} %refs_1_.5, bf16[192,768]{1,0:T(8,128)(2,1)} %refs_2_.4, bf16[192]{0:T(256)(128)(2,1)} %refs_4_.1, bf16[192]{0:T(256)(128)(2,1)} %refs_5_.1, ...), custom_call_target="tpu_custom_call" | custom-call | tf_op jit(solution)/shard_map/pack/pallas_call | solution.py:636
  4.0 4.1 %collective-permute-start.1 = (bf16[128,768]{1,0:T(8,128)(2,1)}, bf16[128,768]{1,0:T(8,128)(2,1)S(1)}, u32[]{:S(2)}, u32[]{:S(2)}) collective-permute-start(bf16[128,768]{1,0:T(8,128)(2,1)} %get-tuple-element.98.refs_3_.refs_1_.refs_4_.refs_0_), channel_id=1, source_target_pairs={{0,4},{1,5},{2,6},{3,7},{4,0},{5,1},{6,2},{7,3},{8,12},{9,13},{10,... | collective-permute-start | bytes 589832 | tf_op jit(solution)/shard_map/ppermute | solution.py:688
  8.2 2.5 %collective-permute-start.5 = (bf16[192,768]{1,0:T(8,128)(2,1)}, bf16[192,768]{1,0:T(8,128)(2,1)S(1)}, u32[]{:S(2)}, u32[]{:S(2)}) collective-permute-start(bf16[192,768]{1,0:T(8,128)(2,1)} %get-tuple-element.99.refs_7_.refs_3_), channel_id=1, source_target_pairs={{0,24},{8,16},{16,8},{24,0},{1,25},{9,17},{17,9},{25,1},{2,26},{10... | collective-permute-start | bytes 884744 | tf_op jit(solution)/shard_map/ppermute | solution.py:693
  11.7 1.6 collective-permute-start
  13.3 4.3 %collective-permute-done.1.refs_4_.refs_5_.refs_6_ = bf16[128,768]{1,0:T(8,128)(2,1)S(1)} collective-permute-done((bf16[128,768]{1,0:T(8,128)(2,1)}, bf16[128,768]{1,0:T(8,128)(2,1)S(1)}, u32[]{:S(2)}, u32[]{:S(2)}) %collective-permute-start.1) | collective-permute-done | bytes 196640 | tf_op jit(solution)/shard_map/ppermute | solution.py:688
  18.3 3.2 %collective-permute-done.refs_3_.refs_4_.refs_5_ = bf16[128,768]{1,0:T(8,128)(2,1)S(1)} collective-permute-done((bf16[128,768]{1,0:T(8,128)(2,1)}, bf16[128,768]{1,0:T(8,128)(2,1)S(1)}, u32[]{:S(2)}, u32[]{:S(2)}) %collective-permute-start) | collective-permute-done | bytes 196640 | tf_op jit(solution)/shard_map/ppermute | solution.py:688
  21.5 2.6 %collective-permute-done.4.refs_1_ = bf16[192,768]{1,0:T(8,128)(2,1)S(1)} collective-permute-done((bf16[192,768]{1,0:T(8,128)(2,1)}, bf16[192,768]{1,0:T(8,128)(2,1)S(1)}, u32[]{:S(2)}, u32[]{:S(2)}) %collective-permute-start.4) | collective-permute-done | bytes 294944 | tf_op jit(solution)/shard_map/ppermute | solution.py:693
  24.9 2.4 %collective-permute-done.6.refs_9_ = bf16[576,768]{1,0:T(8,128)(2,1)S(1)} collective-permute-done((bf16[576,768]{1,0:T(8,128)(2,1)S(1)}, bf16[576,768]{1,0:T(8,128)(2,1)S(1)}, u32[]{:S(2)}, u32[]{:S(2)}) %collective-permute-start.6) | collective-permute-done | bytes 884768 | tf_op jit(solution)/shard_map/ppermute | solution.py:685
  27.3 2.1 %project.1 = (bf16[512,192]{1,0:T(8,128)(2,1)S(1)}, bf16[512,384]{1,0:T(8,128)(2,1)S(1)}, bf16[512,768]{1,0:T(8,128)(2,1)S(1)}, bf16[768,576]{1,0:T(8,128)(2,1)S...) custom-call(s32[3]{0:T(128)S(1)} %copy-done.6, bf16[192,2304]{1,0:T(8,128)(2,1)S(1)} %copy-done, ...), custom_call_target="tpu_custom_call" | custom-call | flops 452984832 | bytes 7520268 | tf_op jit(solution)/shard_map/project/pallas_call | solution.py:636
  30.2 1.6 collective-permute-start.11
  31.9 1.5 collective-permute-start.12
  33.8 3.7 %attend.1 = (bf16[128,192]{1,0:T(8,128)(2,1)S(1)}, bf16[128,192]{1,0:T(8,128)(2,1)S(1)}, bf16[128,192]{1,0:T(8,128)(2,1)S(1)}, bf16[128,192]{1,0:T(8,128)(2,1)S(...) custom-call(s32[3]{0:T(128)S(1)} %copy-done.6, s32[8]{0:T(128)S(1)} %copy-done.9, ...), custom_call_target="tpu_custom_call" | custom-call | flops 402653184 | bytes 1589292 | tf_op jit(solution)/shard_map/attend/pallas_call | solution.py:636
  37.6 1.2 collective-permute-start.8
  38.8 2.6 %collective-permute-start.9 = (bf16[128,192]{1,0:T(8,128)(2,1)S(1)}, bf16[128,192]{1,0:T(8,128)(2,1)S(1)}, u32[]{:S(2)}, u32[]{:S(2)}) collective-permute-start(bf16[128,192]{1,0:T(8,128)(2,1)S(1)} %get-tuple-element.106), channel_id=1, source_target_pairs={{0,4},{1,5},{2,6},{3,7},{4,0},{5,1},{6,2},{7,3},{8,12},{9,13},{10,... | collective-permute-start | bytes 147464 | tf_op jit(solution)/shard_map/ppermute | solution.py:688
  41.4 1.0 collective-permute-done.8.refs_5_.refs_3_
  42.4 2.9 %collective-permute-start.10 = (bf16[128,192]{1,0:T(8,128)(2,1)S(1)}, bf16[128,192]{1,0:T(8,128)(2,1)S(1)}, u32[]{:S(2)}, u32[]{:S(2)}) collective-permute-start(bf16[128,192]{1,0:T(8,128)(2,1)S(1)} %get-tuple-element.107), channel_id=1, source_target_pairs={{0,6},{1,7},{2,4},{3,5},{4,2},{5,3},{6,0},{7,1},{8,14},{9,15},{10,... | collective-permute-start | bytes 147464 | tf_op jit(solution)/shard_map/ppermute | solution.py:688
  45.3 3.1 %collective-permute-done.10.refs_7_.refs_5_ = bf16[128,192]{1,0:T(8,128)(2,1)S(1)} collective-permute-done((bf16[128,192]{1,0:T(8,128)(2,1)S(1)}, bf16[128,192]{1,0:T(8,128)(2,1)S(1)}, u32[]{:S(2)}, u32[]{:S(2)}) %collective-permute-start.10) | collective-permute-done | bytes 49184 | tf_op jit(solution)/shard_map/ppermute | solution.py:688
  48.5 1.1 middle.1
  49.7 2.6 %collective-permute-start.17 = (bf16[128,768]{1,0:T(8,128)(2,1)S(1)}, bf16[128,768]{1,0:T(8,128)(2,1)S(1)}, u32[]{:S(2)}, u32[]{:S(2)}) collective-permute-start(bf16[128,768]{1,0:T(8,128)(2,1)S(1)} %get-tuple-element.112.refs_3_.refs_6_), channel_id=1, source_target_pairs={{0,24},{8,16},{16,8},{24,0},{1,25},{9,17},{17,9},{25,1},{2,26},{10... | collective-permute-start | bytes 589832 | tf_op jit(solution)/shard_map/ppermute | solution.py:693
  53.3 5.2 %collective-permute-done.17.refs_9_ = bf16[128,768]{1,0:T(8,128)(2,1)S(1)} collective-permute-done((bf16[128,768]{1,0:T(8,128)(2,1)S(1)}, bf16[128,768]{1,0:T(8,128)(2,1)S(1)}, u32[]{:S(2)}, u32[]{:S(2)}) %collective-permute-start.17) | collective-permute-done | bytes 196640 | tf_op jit(solution)/shard_map/ppermute | solution.py:693
  58.5 3.7 %collective-permute-done.16.refs_8_ = bf16[128,768]{1,0:T(8,128)(2,1)S(1)} collective-permute-done((bf16[128,768]{1,0:T(8,128)(2,1)S(1)}, bf16[128,768]{1,0:T(8,128)(2,1)S(1)}, u32[]{:S(2)}, u32[]{:S(2)}) %collective-permute-start.16) | collective-permute-done | bytes 196640 | tf_op jit(solution)/shard_map/ppermute | solution.py:693
  62.3 5.6 %feed.1 = (bf16[128,768]{1,0:T(8,128)(2,1)S(1)}, bf16[128,768]{1,0:T(8,128)(2,1)S(1)}, bf16[128,768]{1,0:T(8,128)(2,1)S(1)}, bf16[128,768]{1,0:T(8,128)(2,1)S(1)...) custom-call(s32[3]{0:T(128)S(1)} %copy-done.6, ...), custom_call_target="tpu_custom_call" | custom-call | flops 3623878656 | bytes 8753676 | tf_op jit(solution)/shard_map/feed/pallas_call | solution.py:636
  68.0 2.8 %collective-permute-done.24.refs_2_ = bf16[4,384,384]{2,1,0:T(8,128)(2,1)S(1)} collective-permute-done((bf16[4,384,384]{2,1,0:T(8,128)(2,1)S(1)}, bf16[4,384,384]{2,1,0:T(8,128)(2,1)S(1)}, u32[]{:S(2)}, u32[]{:S(2)}) %collective-permute-start.24) | collective-permute-done | bytes 1179680 | tf_op jit(solution)/shard_map/ppermute | solution.py:685
  70.9 0.8 feed_halves.1
  72.4 1.0 collective-permute-start.21
  73.3 1.0 collective-permute-start.22
  74.3 1.5 collective-permute-start.23
  75.8 4.3 %collective-permute-done.21.refs_6_ = bf16[128,768]{1,0:T(8,128)(2,1)S(1)} collective-permute-done((bf16[128,768]{1,0:T(8,128)(2,1)S(1)}, bf16[128,768]{1,0:T(8,128)(2,1)S(1)}, u32[]{:S(2)}, u32[]{:S(2)}) %collective-permute-start.21) | collective-permute-done | bytes 196640 | tf_op jit(solution)/shard_map/ppermute | solution.py:693
  80.1 4.0 %collective-permute-done.22.refs_7_ = bf16[128,768]{1,0:T(8,128)(2,1)S(1)} collective-permute-done((bf16[128,768]{1,0:T(8,128)(2,1)S(1)}, bf16[128,768]{1,0:T(8,128)(2,1)S(1)}, u32[]{:S(2)}, u32[]{:S(2)}) %collective-permute-start.22) | collective-permute-done | bytes 196640 | tf_op jit(solution)/shard_map/ppermute | solution.py:693
  84.2 1.4 middle_back.1
  85.6 2.9 %collective-permute-start.27 = (bf16[128,192]{1,0:T(8,128)(2,1)S(1)}, bf16[128,192]{1,0:T(8,128)(2,1)S(1)}, u32[]{:S(2)}, u32[]{:S(2)}) collective-permute-start(bf16[128,192]{1,0:T(8,128)(2,1)S(1)} %get-tuple-element.130), channel_id=1, source_target_pairs={{0,6},{1,7},{2,4},{3,5},{4,2},{5,3},{6,0},{7,1},{8,14},{9,15},{10,... | collective-permute-start | bytes 147464 | tf_op jit(solution)/shard_map/ppermute | solution.py:688
  90.1 1.0 output_weights.1
  92.0 1.3 collective-permute-done.25.refs_8_
  93.3 1.2 collective-permute-done.26.refs_9_
  94.5 5.0 %attend_back.1 = (f32[192,512]{1,0:T(8,128)S(1)}, f32[512,384]{1,0:T(8,128)S(1)}, bf16[512,384]{1,0:T(8,128)(2,1)S(1)}) custom-call(s32[3]{0:T(128)S(1)} %copy-done.6, s32[8]{0:T(128)S(1)} %copy-done.9, bf16[512,192]{1,0:T(8,128)(2,1)S(1)} %get-tuple-element.102.refs_2_, bf16[512,384]{1,0:T(8,128)(2,1)S(1)} %get-tuple-element.103.refs_3_, ...), custom_call_target="tpu_custom_call" | custom-call | flops 8053063680 | bytes 3162156 | tf_op jit(solution)/shard_map/attend_back/pallas_call | solution.py:636
  99.6 0.9 collective-permute-start.31
  100.5 0.8 output_halves.1
  101.3 2.1 %collective-permute-start.33 = (bf16[4,48,768]{2,1,0:T(8,128)(2,1)S(1)}, bf16[4,48,768]{2,1,0:T(8,128)(2,1)S(1)}, u32[]{:S(2)}, u32[]{:S(2)}) collective-permute-start(bf16[4,48,768]{2,1,0:T(8,128)(2,1)S(1)} %get-tuple-element.152), channel_id=1, source_target_pairs={{0,2},{1,3},{2,0},{3,1},{4,6},{5,7},{6,4},{7,5},{8,10},{9,11},{10,... | collective-permute-start | bytes 884744 | tf_op jit(solution)/shard_map/ppermute | solution.py:688
  103.4 1.8 %normed_back.1 = (f32[2,128,768]{2,1,0:T(8,128)S(1)}, bf16[2,128,768]{2,1,0:T(8,128)(2,1)S(1)}, bf16[512,576]{1,0:T(8,128)(2,1)S(1)}, f32[8,768]{1,0:T(8,128)S(1)}, f32[8,576]{1,0:T(8,128)S(1)}) custom-call(f32[192,512]{1,0:T(8,128)S(1)} %get-tuple-element.135.refs_0_, f32[512,384]{1,0:T(8,128)S(1)} %get-tuple-element.136.refs_1_, ...), custom_call_target="tpu_custom_call" | custom-call | tf_op jit(solution)/shard_map/normed_back/pallas_call | solution.py:636
  105.3 1.5 input_weights.1
  107.4 9.0 %collective-permute-done.31.refs_2_ = bf16[384,384]{1,0:T(8,128)(2,1)S(1)} collective-permute-done((bf16[384,384]{1,0:T(8,128)(2,1)S(1)}, bf16[384,384]{1,0:T(8,128)(2,1)S(1)}, u32[]{:S(2)}, u32[]{:S(2)}) %collective-permute-start.31) | collective-permute-done | bytes 294944 | tf_op jit(solution)/shard_map/ppermute | solution.py:688
  117.5 1.3 collective-permute-start.19
  118.9 1.5 collective-permute-start.20
  120.3 0.9 owners.1
  121.3 1.5 collective-permute-start.43
  122.8 1.8 collective-permute-done.18.refs_3_
  125.3 3.3 %collective-permute-done.19.refs_4_ = bf16[128,768]{1,0:T(8,128)(2,1)S(1)} collective-permute-done((bf16[128,768]{1,0:T(8,128)(2,1)S(1)}, bf16[128,768]{1,0:T(8,128)(2,1)S(1)}, u32[]{:S(2)}, u32[]{:S(2)}) %collective-permute-start.19) | collective-permute-done | bytes 196640 | tf_op jit(solution)/shard_map/ppermute | solution.py:693
  128.6 1.1 collective-permute-start.39
  130.4 1.6 collective-permute-start.41
  132.1 1.1 collective-permute-start.38
  133.2 2.5 %collective-permute-start.44 = (bf16[192,384]{1,0:T(8,128)(2,1)S(1)}, bf16[192,384]{1,0:T(8,128)(2,1)S(1)}, u32[]{:S(2)}, u32[]{:S(2)}) collective-permute-start(bf16[192,384]{1,0:T(8,128)(2,1)S(1)} %collective-permute-done.43.refs_3_), channel_id=1, source_target_pairs={{0,2},{1,3},{2,0},{3,1},{4,6},{5,7},{6,4},{7,5},{8,10},{9,11},{10,... | collective-permute-start | bytes 442376 | tf_op jit(solution)/shard_map/ppermute | solution.py:688
  135.8 0.8 result.1
  136.6 1.0 collective-permute-done.39.refs_2_
  137.5 4.6 %collective-permute-done.40.refs_3_ = bf16[176,768]{1,0:T(8,128)(2,1)S(1)} collective-permute-done((bf16[176,768]{1,0:T(8,128)(2,1)S(1)}, bf16[176,768]{1,0:T(8,128)(2,1)S(1)}, u32[]{:S(2)}, u32[]{:S(2)}) %collective-permute-start.40) | collective-permute-done | bytes 270368 | tf_op jit(solution)/shard_map/ppermute | solution.py:693
  143.3 1.4 collective-permute-start.46
  144.8 2.5 %collective-permute-start.45 = (bf16[240,768]{1,0:T(8,128)(2,1)S(1)}, bf16[240,768]{1,0:T(8,128)(2,1)S(1)}, u32[]{:S(2)}, u32[]{:S(2)}) collective-permute-start(bf16[240,768]{1,0:T(8,128)(2,1)S(1)} %shares.1.refs_1_), channel_id=1, source_target_pairs={{0,2},{1,3},{2,0},{3,1},{4,6},{5,7},{6,4},{7,5},{8,10},{9,11},{10,... | collective-permute-start | bytes 1105928 | tf_op jit(solution)/shard_map/ppermute | solution.py:688
  147.8 0.9 collective-permute-done.47.refs_5_
  149.1 0.9 collective-permute-done.50.refs_8_
  150.0 2.1 %contract_final.1 = (f32[768,768]{1,0:T(8,128)}, f32[8,128]{1,0:T(8,128)S(1)}) custom-call(s32[3]{0:T(128)S(1)} %copy-done.6, bf16[192,384]{1,0:T(8,128)(2,1)S(1)} %get-tuple-element.157.refs_2_.refs_1_, bf16[192,384]{1,0:T(8,128)(2,1)S(1)} %collective-permute-done.42.refs_5_.refs_2_, bf16[192,384]{1,0:T(8,128)(2,1)S(1)} %collective-permute-done.43.refs_3_, ...), custom_call_target="tpu_custom_call" | custom-call | tf_op jit(solution)/shard_map/contract_final/pallas_call | solution.py:636
  152.1 1.1 tokens_back.1
  153.2 8.8 %collective-permute-done.46.refs_0_.refs_3_ = bf16[240,768]{1,0:T(8,128)(2,1)S(1)} collective-permute-done((bf16[240,768]{1,0:T(8,128)(2,1)S(1)}, bf16[240,768]{1,0:T(8,128)(2,1)S(1)}, u32[]{:S(2)}, u32[]{:S(2)}) %collective-permute-start.46) | collective-permute-done | bytes 368672 | tf_op jit(solution)/shard_map/ppermute | solution.py:688
  162.9 9.6 %collective-permute-done.51.refs_4_ = bf16[240,768]{1,0:T(8,128)(2,1)S(1)} collective-permute-done((bf16[240,768]{1,0:T(8,128)(2,1)S(1)}, bf16[240,768]{1,0:T(8,128)(2,1)S(1)}, u32[]{:S(2)}, u32[]{:S(2)}) %collective-permute-start.51) | collective-permute-done | bytes 368672 | tf_op jit(solution)/shard_map/ppermute | solution.py:688
  172.6 1.7 collective-permute-done.55.refs_8_
  174.3 3.5 %weights_final.1 = (f32[192,2304]{1,0:T(8,128)}, f32[192,768]{1,0:T(8,128)}, f32[192,3072]{1,0:T(8,128)}, f32[768]{0:T(1024)}, f32[192]{0:T(256)}, /*index=5*/f3...) custom-call(s32[3]{0:T(128)S(1)} %copy-done.6, ...), custom_call_target="tpu_custom_call" | custom-call | tf_op jit(solution)/shard_map/weights_final/pallas_call | solution.py:636
  (93 shorter events, 15.4 us)
Async XLA Ops:
  4.0 13.5 %collective-permute-start.1 = (bf16[128,768]{1,0:T(8,128)(2,1)}, bf16[128,768]{1,0:T(8,128)(2,1)S(1)}, u32[]{:S(2)}, u32[]{:S(2)}) collective-permute-start(bf16[128,768]{1,0:T(8,128)(2,1)} %get-tuple-element.98.refs_3_.refs_1_.refs_4_.refs_0_), channel_id=1, source_target_pairs={{0,4},{1,5},{2,6},{3,7},{4,0},{5,1},{6,2},{7,3},{8,12},{9,13},{10,... | collective-permute-start | bytes 589832 | tf_op jit(solution)/shard_map/ppermute | solution.py:688
  8.2 19.1 %copy-start = (bf16[192,2304]{1,0:T(8,128)(2,1)S(1)}, bf16[192,2304]{1,0:T(8,128)(2,1)}, u32[]{:S(2)}) copy-start(bf16[192,2304]{1,0:T(8,128)(2,1)} %refs_1_.5) | copy-start | bytes 2654212
  8.2 19.1 %copy-start.1 = (bf16[128,768]{1,0:T(8,128)(2,1)S(1)}, bf16[128,768]{1,0:T(8,128)(2,1)}, u32[]{:S(2)}) copy-start(bf16[128,768]{1,0:T(8,128)(2,1)} %get-tuple-element.98.refs_3_.refs_1_.refs_4_.refs_0_) | copy-start | bytes 589828
  8.2 19.1 %copy-start.2 = (bf16[192,768]{1,0:T(8,128)(2,1)S(1)}, bf16[192,768]{1,0:T(8,128)(2,1)}, u32[]{:S(2)}) copy-start(bf16[192,768]{1,0:T(8,128)(2,1)} %refs_2_.4) | copy-start | bytes 884740
  8.2 19.1 %copy-start.3 = (bf16[192,768]{1,0:T(8,128)(2,1)S(1)}, bf16[192,768]{1,0:T(8,128)(2,1)}, u32[]{:S(2)}) copy-start(bf16[192,768]{1,0:T(8,128)(2,1)} %get-tuple-element.99.refs_7_.refs_3_) | copy-start | bytes 884740
  8.2 19.1 %copy-start.6 = (s32[3]{0:T(128)S(1)}, s32[3]{0:T(128)}, u32[]{:S(2)}) copy-start(s32[3]{0:T(128)} %pad_add_fusion.refs_0_) | copy-start | bytes 40
  8.2 13.3 %collective-permute-start.5 = (bf16[192,768]{1,0:T(8,128)(2,1)}, bf16[192,768]{1,0:T(8,128)(2,1)S(1)}, u32[]{:S(2)}, u32[]{:S(2)}) collective-permute-start(bf16[192,768]{1,0:T(8,128)(2,1)} %get-tuple-element.99.refs_7_.refs_3_), channel_id=1, source_target_pairs={{0,24},{8,16},{16,8},{24,0},{1,25},{9,17},{17,9},{25,1},{2,26},{10... | collective-permute-start | bytes 884744 | tf_op jit(solution)/shard_map/ppermute | solution.py:693
  10.7 13.4 %collective-permute-start.4 = (bf16[192,768]{1,0:T(8,128)(2,1)}, bf16[192,768]{1,0:T(8,128)(2,1)S(1)}, u32[]{:S(2)}, u32[]{:S(2)}) collective-permute-start(bf16[192,768]{1,0:T(8,128)(2,1)} %get-tuple-element.99.refs_7_.refs_3_), channel_id=1, source_target_pairs={{0,16},{8,24},{16,0},{24,8},{1,17},{9,25},{17,1},{25,9},{2,18},{10... | collective-permute-start | bytes 884744 | tf_op jit(solution)/shard_map/ppermute | solution.py:693
  11.2 13.0 %collective-permute-start.3 = (bf16[192,768]{1,0:T(8,128)(2,1)}, bf16[192,768]{1,0:T(8,128)(2,1)S(1)}, u32[]{:S(2)}, u32[]{:S(2)}) collective-permute-start(bf16[192,768]{1,0:T(8,128)(2,1)} %get-tuple-element.99.refs_7_.refs_3_), channel_id=1, source_target_pairs={{0,8},{8,0},{16,24},{24,16},{1,9},{9,1},{17,25},{25,17},{2,10},{10... | collective-permute-start | bytes 884744 | tf_op jit(solution)/shard_map/ppermute | solution.py:693
  11.7 9.8 %collective-permute-start = (bf16[128,768]{1,0:T(8,128)(2,1)}, bf16[128,768]{1,0:T(8,128)(2,1)S(1)}, u32[]{:S(2)}, u32[]{:S(2)}) collective-permute-start(bf16[128,768]{1,0:T(8,128)(2,1)} %get-tuple-element.98.refs_3_.refs_1_.refs_4_.refs_0_), channel_id=1, source_target_pairs={{0,2},{1,3},{2,0},{3,1},{4,6},{5,7},{6,4},{7,5},{8,10},{9,11},{10,... | collective-permute-start | bytes 589832 | tf_op jit(solution)/shard_map/ppermute | solution.py:688
  17.6 7.1 %collective-permute-start.2 = (bf16[128,768]{1,0:T(8,128)(2,1)S(1)}, bf16[128,768]{1,0:T(8,128)(2,1)S(1)}, u32[]{:S(2)}, u32[]{:S(2)}) collective-permute-start(bf16[128,768]{1,0:T(8,128)(2,1)S(1)} %collective-permute-done.1.refs_4_.refs_5_.refs_6_), channel_id=1, source_target_pairs={{0,2},{1,3},{2,0},{3,1},{4,6},{5,7},{6,4},{7,5},{8,10},{9,11},{10,... | collective-permute-start | bytes 589832 | tf_op jit(solution)/shard_map/ppermute | solution.py:688
  24.8 4.9 %copy-start.4 = (bf16[192,3072]{1,0:T(8,128)(2,1)S(1)}, bf16[192,3072]{1,0:T(8,128)(2,1)}, u32[]{:S(2)}) copy-start(bf16[192,3072]{1,0:T(8,128)(2,1)} %refs_3_.3) | copy-start | bytes 3538948
  24.8 2.5 %collective-permute-start.6 = (bf16[576,768]{1,0:T(8,128)(2,1)S(1)}, bf16[576,768]{1,0:T(8,128)(2,1)S(1)}, u32[]{:S(2)}, u32[]{:S(2)}) collective-permute-start(bf16[576,768]{1,0:T(8,128)(2,1)S(1)} %pack_stack.1.refs_8_), channel_id=1, source_target_pairs={{0,1},{1,0},{2,3},{3,2},{4,5},{5,4},{6,7},{7,6},{8,9},{9,8},{10,11... | collective-permute-start | bytes 2654216 | tf_op jit(solution)/shard_map/ppermute | solution.py:685
  29.4 4.4 %collective-permute-start.7 = (bf16[512,384]{1,0:T(8,128)(2,1)S(1)}, bf16[512,384]{1,0:T(8,128)(2,1)S(1)}, u32[]{:S(2)}, u32[]{:S(2)}) collective-permute-start(bf16[512,384]{1,0:T(8,128)(2,1)S(1)} %get-tuple-element.103.refs_3_), channel_id=1, source_target_pairs={{0,1},{1,0},{2,3},{3,2},{4,5},{5,4},{6,7},{7,6},{8,9},{9,8},{10,11... | collective-permute-start | bytes 1179656 | tf_op jit(solution)/shard_map/ppermute | solution.py:685
  30.2 19.4 %collective-permute-start.11 = (bf16[224,768]{1,0:T(8,128)(2,1)S(1)}, bf16[224,768]{1,0:T(8,128)(2,1)S(1)}, u32[]{:S(2)}, u32[]{:S(2)}) collective-permute-start(bf16[224,768]{1,0:T(8,128)(2,1)S(1)} %get-tuple-element.109), channel_id=1, source_target_pairs={{0,8},{8,0},{16,24},{24,16},{1,9},{9,1},{17,25},{25,17},{2,10},{10... | collective-permute-start | bytes 1032200 | tf_op jit(solution)/shard_map/ppermute | solution.py:693
  31.9 17.7 %collective-permute-start.12 = (bf16[224,768]{1,0:T(8,128)(2,1)S(1)}, bf16[224,768]{1,0:T(8,128)(2,1)S(1)}, u32[]{:S(2)}, u32[]{:S(2)}) collective-permute-start(bf16[224,768]{1,0:T(8,128)(2,1)S(1)} %get-tuple-element.110), channel_id=1, source_target_pairs={{0,16},{8,24},{16,0},{24,8},{1,17},{9,25},{17,1},{25,9},{2,18},{10... | collective-permute-start | bytes 1032200 | tf_op jit(solution)/shard_map/ppermute | solution.py:693
  33.4 16.2 %collective-permute-start.13 = (bf16[224,768]{1,0:T(8,128)(2,1)S(1)}, bf16[224,768]{1,0:T(8,128)(2,1)S(1)}, u32[]{:S(2)}, u32[]{:S(2)}) collective-permute-start(bf16[224,768]{1,0:T(8,128)(2,1)S(1)} %get-tuple-element.111), channel_id=1, source_target_pairs={{0,24},{8,16},{16,8},{24,0},{1,25},{9,17},{17,9},{25,1},{2,26},{10... | collective-permute-start | bytes 1032200 | tf_op jit(solution)/shard_map/ppermute | solution.py:693
  37.6 4.8 %collective-permute-start.8 = (bf16[128,192]{1,0:T(8,128)(2,1)S(1)}, bf16[128,192]{1,0:T(8,128)(2,1)S(1)}, u32[]{:S(2)}, u32[]{:S(2)}) collective-permute-start(bf16[128,192]{1,0:T(8,128)(2,1)S(1)} %get-tuple-element.105), channel_id=1, source_target_pairs={{0,2},{1,3},{2,0},{3,1},{4,6},{5,7},{6,4},{7,5},{8,10},{9,11},{10,... | collective-permute-start | bytes 147464 | tf_op jit(solution)/shard_map/ppermute | solution.py:688
  38.8 6.6 %collective-permute-start.9 = (bf16[128,192]{1,0:T(8,128)(2,1)S(1)}, bf16[128,192]{1,0:T(8,128)(2,1)S(1)}, u32[]{:S(2)}, u32[]{:S(2)}) collective-permute-start(bf16[128,192]{1,0:T(8,128)(2,1)S(1)} %get-tuple-element.106), channel_id=1, source_target_pairs={{0,4},{1,5},{2,6},{3,7},{4,0},{5,1},{6,2},{7,3},{8,12},{9,13},{10,... | collective-permute-start | bytes 147464 | tf_op jit(solution)/shard_map/ppermute | solution.py:688
  42.4 6.1 %collective-permute-start.10 = (bf16[128,192]{1,0:T(8,128)(2,1)S(1)}, bf16[128,192]{1,0:T(8,128)(2,1)S(1)}, u32[]{:S(2)}, u32[]{:S(2)}) collective-permute-start(bf16[128,192]{1,0:T(8,128)(2,1)S(1)} %get-tuple-element.107), channel_id=1, source_target_pairs={{0,6},{1,7},{2,4},{3,5},{4,2},{5,3},{6,0},{7,1},{8,14},{9,15},{10,... | collective-permute-start | bytes 147464 | tf_op jit(solution)/shard_map/ppermute | solution.py:688
  49.6 12.8 %copy-start.7 = (bf16[768,768]{1,0:T(8,128)(2,1)S(1)}, bf16[768,768]{1,0:T(8,128)(2,1)}, u32[]{:S(2)}) copy-start(bf16[768,768]{1,0:T(8,128)(2,1)} %refs_2_.5) | copy-start | bytes 3538948
  49.6 12.8 %copy-start.8 = (bf16[768]{0:T(1024)(128)(2,1)S(1)}, bf16[768]{0:T(1024)(128)(2,1)}, u32[]{:S(2)}) copy-start(bf16[768]{0:T(1024)(128)(2,1)} %refs_1_.8) | copy-start | bytes 4612
  49.7 12.7 %collective-permute-start.14 = (bf16[288,768]{1,0:T(8,128)(2,1)S(1)}, bf16[288,768]{1,0:T(8,128)(2,1)S(1)}, u32[]{:S(2)}, u32[]{:S(2)}) collective-permute-start(bf16[288,768]{1,0:T(8,128)(2,1)S(1)} %expand_stack.1), channel_id=1, source_target_pairs={{0,1},{1,0},{2,3},{3,2},{4,5},{5,4},{6,7},{7,6},{8,9},{9,8},{10,11... | collective-permute-start | bytes 1327112 | tf_op jit(solution)/shard_map/ppermute | solution.py:685
  49.7 8.7 %collective-permute-start.17 = (bf16[128,768]{1,0:T(8,128)(2,1)S(1)}, bf16[128,768]{1,0:T(8,128)(2,1)S(1)}, u32[]{:S(2)}, u32[]{:S(2)}) collective-permute-start(bf16[128,768]{1,0:T(8,128)(2,1)S(1)} %get-tuple-element.112.refs_3_.refs_6_), channel_id=1, source_target_pairs={{0,24},{8,16},{16,8},{24,0},{1,25},{9,17},{17,9},{25,1},{2,26},{10... | collective-permute-start | bytes 589832 | tf_op jit(solution)/shard_map/ppermute | solution.py:693
  52.3 9.9 %collective-permute-start.16 = (bf16[128,768]{1,0:T(8,128)(2,1)S(1)}, bf16[128,768]{1,0:T(8,128)(2,1)S(1)}, u32[]{:S(2)}, u32[]{:S(2)}) collective-permute-start(bf16[128,768]{1,0:T(8,128)(2,1)S(1)} %get-tuple-element.112.refs_3_.refs_6_), channel_id=1, source_target_pairs={{0,16},{8,24},{16,0},{24,8},{1,17},{9,25},{17,1},{25,9},{2,18},{10... | collective-permute-start | bytes 589832 | tf_op jit(solution)/shard_map/ppermute | solution.py:693
  52.8 9.5 %collective-permute-start.15 = (bf16[128,768]{1,0:T(8,128)(2,1)S(1)}, bf16[128,768]{1,0:T(8,128)(2,1)S(1)}, u32[]{:S(2)}, u32[]{:S(2)}) collective-permute-start(bf16[128,768]{1,0:T(8,128)(2,1)S(1)} %get-tuple-element.112.refs_3_.refs_6_), channel_id=1, source_target_pairs={{0,8},{8,0},{16,24},{24,16},{1,9},{9,1},{17,25},{25,17},{2,10},{10... | collective-permute-start | bytes 589832 | tf_op jit(solution)/shard_map/ppermute | solution.py:693
  67.9 2.9 %collective-permute-start.24 = (bf16[4,384,384]{2,1,0:T(8,128)(2,1)S(1)}, bf16[4,384,384]{2,1,0:T(8,128)(2,1)S(1)}, u32[]{:S(2)}, u32[]{:S(2)}) collective-permute-start(bf16[4,384,384]{2,1,0:T(8,128)(2,1)S(1)} %get-tuple-element.125), channel_id=1, source_target_pairs={{0,1},{1,0},{2,3},{3,2},{4,5},{5,4},{6,7},{7,6},{8,9},{9,8},{10,11... | collective-permute-start | bytes 3538952 | tf_op jit(solution)/shard_map/ppermute | solution.py:685
  71.7 20.1 %collective-permute-start.28 = (bf16[2,384,384]{2,1,0:T(8,128)(2,1)S(1)}, bf16[2,384,384]{2,1,0:T(8,128)(2,1)S(1)}, u32[]{:S(2)}, u32[]{:S(2)}) collective-permute-start(bf16[2,384,384]{2,1,0:T(8,128)(2,1)S(1)} %get-tuple-element.126.refs_9_), channel_id=1, source_target_pairs={{0,2},{1,3},{2,0},{3,1},{4,6},{5,7},{6,4},{7,5},{8,10},{9,11},{10,... | collective-permute-start | bytes 1769480 | tf_op jit(solution)/shard_map/ppermute | solution.py:688
  72.4 7.8 %collective-permute-start.21 = (bf16[128,768]{1,0:T(8,128)(2,1)S(1)}, bf16[128,768]{1,0:T(8,128)(2,1)S(1)}, u32[]{:S(2)}, u32[]{:S(2)}) collective-permute-start(bf16[128,768]{1,0:T(8,128)(2,1)S(1)} %get-tuple-element.121), channel_id=1, source_target_pairs={{0,8},{8,0},{16,24},{24,16},{1,9},{9,1},{17,25},{25,17},{2,10},{10... | collective-permute-start | bytes 589832 | tf_op jit(solution)/shard_map/ppermute | solution.py:693
  73.3 10.9 %collective-permute-start.22 = (bf16[128,768]{1,0:T(8,128)(2,1)S(1)}, bf16[128,768]{1,0:T(8,128)(2,1)S(1)}, u32[]{:S(2)}, u32[]{:S(2)}) collective-permute-start(bf16[128,768]{1,0:T(8,128)(2,1)S(1)} %get-tuple-element.122), channel_id=1, source_target_pairs={{0,16},{8,24},{16,0},{24,8},{1,17},{9,25},{17,1},{25,9},{2,18},{10... | collective-permute-start | bytes 589832 | tf_op jit(solution)/shard_map/ppermute | solution.py:693
  74.3 9.9 %collective-permute-start.23 = (bf16[128,768]{1,0:T(8,128)(2,1)S(1)}, bf16[128,768]{1,0:T(8,128)(2,1)S(1)}, u32[]{:S(2)}, u32[]{:S(2)}) collective-permute-start(bf16[128,768]{1,0:T(8,128)(2,1)S(1)} %get-tuple-element.123), channel_id=1, source_target_pairs={{0,24},{8,16},{16,8},{24,0},{1,25},{9,17},{17,9},{25,1},{2,26},{10... | collective-permute-start | bytes 589832 | tf_op jit(solution)/shard_map/ppermute | solution.py:693
  85.6 6.2 %collective-permute-start.27 = (bf16[128,192]{1,0:T(8,128)(2,1)S(1)}, bf16[128,192]{1,0:T(8,128)(2,1)S(1)}, u32[]{:S(2)}, u32[]{:S(2)}) collective-permute-start(bf16[128,192]{1,0:T(8,128)(2,1)S(1)} %get-tuple-element.130), channel_id=1, source_target_pairs={{0,6},{1,7},{2,4},{3,5},{4,2},{5,3},{6,0},{7,1},{8,14},{9,15},{10,... | collective-permute-start | bytes 147464 | tf_op jit(solution)/shard_map/ppermute | solution.py:688
  88.5 4.7 %collective-permute-start.25 = (bf16[128,192]{1,0:T(8,128)(2,1)S(1)}, bf16[128,192]{1,0:T(8,128)(2,1)S(1)}, u32[]{:S(2)}, u32[]{:S(2)}) collective-permute-start(bf16[128,192]{1,0:T(8,128)(2,1)S(1)} %get-tuple-element.128), channel_id=1, source_target_pairs={{0,2},{1,3},{2,0},{3,1},{4,6},{5,7},{6,4},{7,5},{8,10},{9,11},{10,... | collective-permute-start | bytes 147464 | tf_op jit(solution)/shard_map/ppermute | solution.py:688
  89.3 5.2 %collective-permute-start.26 = (bf16[128,192]{1,0:T(8,128)(2,1)S(1)}, bf16[128,192]{1,0:T(8,128)(2,1)S(1)}, u32[]{:S(2)}, u32[]{:S(2)}) collective-permute-start(bf16[128,192]{1,0:T(8,128)(2,1)S(1)} %get-tuple-element.129), channel_id=1, source_target_pairs={{0,4},{1,5},{2,6},{3,7},{4,0},{5,1},{6,2},{7,3},{8,12},{9,13},{10,... | collective-permute-start | bytes 147464 | tf_op jit(solution)/shard_map/ppermute | solution.py:688
  91.1 9.4 %collective-permute-start.32 = (bf16[4,192,384]{2,1,0:T(8,128)(2,1)S(1)}, bf16[4,192,384]{2,1,0:T(8,128)(2,1)S(1)}, u32[]{:S(2)}, u32[]{:S(2)}) collective-permute-start(bf16[4,192,384]{2,1,0:T(8,128)(2,1)S(1)} %get-tuple-element.134.refs_12_), channel_id=1, source_target_pairs={{0,1},{1,0},{2,3},{3,2},{4,5},{5,4},{6,7},{7,6},{8,9},{9,8},{10,11... | collective-permute-start | bytes 1769480 | tf_op jit(solution)/shard_map/ppermute | solution.py:685
  99.5 3.9 %collective-permute-start.29 = (bf16[512,384]{1,0:T(8,128)(2,1)S(1)}, bf16[512,384]{1,0:T(8,128)(2,1)S(1)}, u32[]{:S(2)}, u32[]{:S(2)}) collective-permute-start(bf16[512,384]{1,0:T(8,128)(2,1)S(1)} %get-tuple-element.137), channel_id=1, source_target_pairs={{0,1},{1,0},{2,3},{3,2},{4,5},{5,4},{6,7},{7,6},{8,9},{9,8},{10,11... | collective-permute-start | bytes 1179656 | tf_op jit(solution)/shard_map/ppermute | solution.py:685
  99.6 16.8 %collective-permute-start.31 = (bf16[384,384]{1,0:T(8,128)(2,1)S(1)}, bf16[384,384]{1,0:T(8,128)(2,1)S(1)}, u32[]{:S(2)}, u32[]{:S(2)}) collective-permute-start(bf16[384,384]{1,0:T(8,128)(2,1)S(1)} %get-tuple-element.132.refs_11_), channel_id=1, source_target_pairs={{0,4},{1,5},{2,6},{3,7},{4,0},{5,1},{6,2},{7,3},{8,12},{9,13},{10,... | collective-permute-start | bytes 884744 | tf_op jit(solution)/shard_map/ppermute | solution.py:688
  101.3 15.4 %collective-permute-start.33 = (bf16[4,48,768]{2,1,0:T(8,128)(2,1)S(1)}, bf16[4,48,768]{2,1,0:T(8,128)(2,1)S(1)}, u32[]{:S(2)}, u32[]{:S(2)}) collective-permute-start(bf16[4,48,768]{2,1,0:T(8,128)(2,1)S(1)} %get-tuple-element.152), channel_id=1, source_target_pairs={{0,2},{1,3},{2,0},{3,1},{4,6},{5,7},{6,4},{7,5},{8,10},{9,11},{10,... | collective-permute-start | bytes 884744 | tf_op jit(solution)/shard_map/ppermute | solution.py:688
  105.2 25.2 %collective-permute-start.30 = (bf16[2,128,768]{2,1,0:T(8,128)(2,1)S(1)}, bf16[2,128,768]{2,1,0:T(8,128)(2,1)S(1)}, u32[]{:S(2)}, u32[]{:S(2)}) collective-permute-start(bf16[2,128,768]{2,1,0:T(8,128)(2,1)S(1)} %get-tuple-element.148), channel_id=1, source_target_pairs={{0,2},{1,3},{2,0},{3,1},{4,6},{5,7},{6,4},{7,5},{8,10},{9,11},{10,... | collective-permute-start | bytes 1179656 | tf_op jit(solution)/shard_map/ppermute | solution.py:688
  106.8 10.1 %collective-permute-start.34 = (bf16[96,768]{1,0:T(8,128)(2,1)S(1)}, bf16[96,768]{1,0:T(8,128)(2,1)S(1)}, u32[]{:S(2)}, u32[]{:S(2)}) collective-permute-start(bf16[96,768]{1,0:T(8,128)(2,1)S(1)} %get-tuple-element.153), channel_id=1, source_target_pairs={{0,1},{1,0},{2,3},{3,2},{4,5},{5,4},{6,7},{7,6},{8,9},{9,8},{10,11... | collective-permute-start | bytes 442376 | tf_op jit(solution)/shard_map/ppermute | solution.py:685
  106.9 10.7 %collective-permute-start.35 = (bf16[96,768]{1,0:T(8,128)(2,1)S(1)}, bf16[96,768]{1,0:T(8,128)(2,1)S(1)}, u32[]{:S(2)}, u32[]{:S(2)}) collective-permute-start(bf16[96,768]{1,0:T(8,128)(2,1)S(1)} %get-tuple-element.154), channel_id=1, source_target_pairs={{0,1},{1,0},{2,3},{3,2},{4,5},{5,4},{6,7},{7,6},{8,9},{9,8},{10,11... | collective-permute-start | bytes 442376 | tf_op jit(solution)/shard_map/ppermute | solution.py:685
  116.3 2.5 %collective-permute-start.36 = (bf16[96,768]{1,0:T(8,128)(2,1)S(1)}, bf16[96,768]{1,0:T(8,128)(2,1)S(1)}, u32[]{:S(2)}, u32[]{:S(2)}) collective-permute-start(bf16[96,768]{1,0:T(8,128)(2,1)S(1)} %get-tuple-element.155), channel_id=1, source_target_pairs={{0,1},{1,0},{2,3},{3,2},{4,5},{5,4},{6,7},{7,6},{8,9},{9,8},{10,11... | collective-permute-start | bytes 442376 | tf_op jit(solution)/shard_map/ppermute | solution.py:685
  116.7 3.7 %collective-permute-start.37 = (bf16[96,768]{1,0:T(8,128)(2,1)S(1)}, bf16[96,768]{1,0:T(8,128)(2,1)S(1)}, u32[]{:S(2)}, u32[]{:S(2)}) collective-permute-start(bf16[96,768]{1,0:T(8,128)(2,1)S(1)} %get-tuple-element.156), channel_id=1, source_target_pairs={{0,1},{1,0},{2,3},{3,2},{4,5},{5,4},{6,7},{7,6},{8,9},{9,8},{10,11... | collective-permute-start | bytes 442376 | tf_op jit(solution)/shard_map/ppermute | solution.py:685
  116.8 7.7 %collective-permute-start.18 = (bf16[128,768]{1,0:T(8,128)(2,1)S(1)}, bf16[128,768]{1,0:T(8,128)(2,1)S(1)}, u32[]{:S(2)}, u32[]{:S(2)}) collective-permute-start(bf16[128,768]{1,0:T(8,128)(2,1)S(1)} %get-tuple-element.114), channel_id=1, source_target_pairs={{0,8},{8,0},{16,24},{24,16},{1,9},{9,1},{17,25},{25,17},{2,10},{10... | collective-permute-start | bytes 589832 | tf_op jit(solution)/shard_map/ppermute | solution.py:693
  117.5 11.0 %collective-permute-start.19 = (bf16[128,768]{1,0:T(8,128)(2,1)S(1)}, bf16[128,768]{1,0:T(8,128)(2,1)S(1)}, u32[]{:S(2)}, u32[]{:S(2)}) collective-permute-start(bf16[128,768]{1,0:T(8,128)(2,1)S(1)} %get-tuple-element.115), channel_id=1, source_target_pairs={{0,16},{8,24},{16,0},{24,8},{1,17},{9,25},{17,1},{25,9},{2,18},{10... | collective-permute-start | bytes 589832 | tf_op jit(solution)/shard_map/ppermute | solution.py:693
  118.9 10.8 %collective-permute-start.20 = (bf16[128,768]{1,0:T(8,128)(2,1)S(1)}, bf16[128,768]{1,0:T(8,128)(2,1)S(1)}, u32[]{:S(2)}, u32[]{:S(2)}) collective-permute-start(bf16[128,768]{1,0:T(8,128)(2,1)S(1)} %get-tuple-element.116), channel_id=1, source_target_pairs={{0,24},{8,16},{16,8},{24,0},{1,25},{9,17},{17,9},{25,1},{2,26},{10... | collective-permute-start | bytes 589832 | tf_op jit(solution)/shard_map/ppermute | solution.py:693
  121.3 10.9 %collective-permute-start.43 = (bf16[192,384]{1,0:T(8,128)(2,1)S(1)}, bf16[192,384]{1,0:T(8,128)(2,1)S(1)}, u32[]{:S(2)}, u32[]{:S(2)}) collective-permute-start(bf16[192,384]{1,0:T(8,128)(2,1)S(1)} %get-tuple-element.157.refs_2_.refs_1_), channel_id=1, source_target_pairs={{0,4},{1,5},{2,6},{3,7},{4,0},{5,1},{6,2},{7,3},{8,12},{9,13},{10,... | collective-permute-start | bytes 442376 | tf_op jit(solution)/shard_map/ppermute | solution.py:688
  124.5 8.7 %collective-permute-start.42 = (bf16[192,384]{1,0:T(8,128)(2,1)S(1)}, bf16[192,384]{1,0:T(8,128)(2,1)S(1)}, u32[]{:S(2)}, u32[]{:S(2)}) collective-permute-start(bf16[192,384]{1,0:T(8,128)(2,1)S(1)} %get-tuple-element.157.refs_2_.refs_1_), channel_id=1, source_target_pairs={{0,2},{1,3},{2,0},{3,1},{4,6},{5,7},{6,4},{7,5},{8,10},{9,11},{10,... | collective-permute-start | bytes 442376 | tf_op jit(solution)/shard_map/ppermute | solution.py:688
  128.6 9.0 %collective-permute-start.39 = (bf16[176,768]{1,0:T(8,128)(2,1)S(1)}, bf16[176,768]{1,0:T(8,128)(2,1)S(1)}, u32[]{:S(2)}, u32[]{:S(2)}) collective-permute-start(bf16[176,768]{1,0:T(8,128)(2,1)S(1)} %get-tuple-element.162), channel_id=1, source_target_pairs={{0,8},{8,0},{16,24},{24,16},{1,9},{9,1},{17,25},{25,17},{2,10},{10... | collective-permute-start | bytes 811016 | tf_op jit(solution)/shard_map/ppermute | solution.py:693
  129.7 12.5 %collective-permute-start.40 = (bf16[176,768]{1,0:T(8,128)(2,1)S(1)}, bf16[176,768]{1,0:T(8,128)(2,1)S(1)}, u32[]{:S(2)}, u32[]{:S(2)}) collective-permute-start(bf16[176,768]{1,0:T(8,128)(2,1)S(1)} %get-tuple-element.163), channel_id=1, source_target_pairs={{0,16},{8,24},{16,0},{24,8},{1,17},{9,25},{17,1},{25,9},{2,18},{10... | collective-permute-start | bytes 811016 | tf_op jit(solution)/shard_map/ppermute | solution.py:693
  130.4 11.7 %collective-permute-start.41 = (bf16[176,768]{1,0:T(8,128)(2,1)S(1)}, bf16[176,768]{1,0:T(8,128)(2,1)S(1)}, u32[]{:S(2)}, u32[]{:S(2)}) collective-permute-start(bf16[176,768]{1,0:T(8,128)(2,1)S(1)} %get-tuple-element.164), channel_id=1, source_target_pairs={{0,24},{8,16},{16,8},{24,0},{1,25},{9,17},{17,9},{25,1},{2,26},{10... | collective-permute-start | bytes 811016 | tf_op jit(solution)/shard_map/ppermute | solution.py:693
  132.1 10.4 %collective-permute-start.38 = (bf16[128,768]{1,0:T(8,128)(2,1)S(1)}, bf16[128,768]{1,0:T(8,128)(2,1)S(1)}, u32[]{:S(2)}, u32[]{:S(2)}) collective-permute-start(bf16[128,768]{1,0:T(8,128)(2,1)S(1)} %get-tuple-element.159), channel_id=1, source_target_pairs={{0,4},{1,5},{2,6},{3,7},{4,0},{5,1},{6,2},{7,3},{8,12},{9,13},{10,... | collective-permute-start | bytes 589832 | tf_op jit(solution)/shard_map/ppermute | solution.py:688
  133.2 8.9 %collective-permute-start.44 = (bf16[192,384]{1,0:T(8,128)(2,1)S(1)}, bf16[192,384]{1,0:T(8,128)(2,1)S(1)}, u32[]{:S(2)}, u32[]{:S(2)}) collective-permute-start(bf16[192,384]{1,0:T(8,128)(2,1)S(1)} %collective-permute-done.43.refs_3_), channel_id=1, source_target_pairs={{0,2},{1,3},{2,0},{3,1},{4,6},{5,7},{6,4},{7,5},{8,10},{9,11},{10,... | collective-permute-start | bytes 442376 | tf_op jit(solution)/shard_map/ppermute | solution.py:688
  143.3 18.7 %collective-permute-start.46 = (bf16[240,768]{1,0:T(8,128)(2,1)S(1)}, bf16[240,768]{1,0:T(8,128)(2,1)S(1)}, u32[]{:S(2)}, u32[]{:S(2)}) collective-permute-start(bf16[240,768]{1,0:T(8,128)(2,1)S(1)} %shares.1.refs_1_), channel_id=1, source_target_pairs={{0,4},{1,5},{2,6},{3,7},{4,0},{5,1},{6,2},{7,3},{8,12},{9,13},{10,... | collective-permute-start | bytes 1105928 | tf_op jit(solution)/shard_map/ppermute | solution.py:688
  144.8 17.4 %collective-permute-start.45 = (bf16[240,768]{1,0:T(8,128)(2,1)S(1)}, bf16[240,768]{1,0:T(8,128)(2,1)S(1)}, u32[]{:S(2)}, u32[]{:S(2)}) collective-permute-start(bf16[240,768]{1,0:T(8,128)(2,1)S(1)} %shares.1.refs_1_), channel_id=1, source_target_pairs={{0,2},{1,3},{2,0},{3,1},{4,6},{5,7},{6,4},{7,5},{8,10},{9,11},{10,... | collective-permute-start | bytes 1105928 | tf_op jit(solution)/shard_map/ppermute | solution.py:688
  147.2 1.4 collective-permute-start.47
  147.2 1.6 collective-permute-start.49
  147.8 1.4 collective-permute-start.48
  148.6 1.4 collective-permute-start.50
  162.2 10.4 %collective-permute-start.51 = (bf16[240,768]{1,0:T(8,128)(2,1)S(1)}, bf16[240,768]{1,0:T(8,128)(2,1)S(1)}, u32[]{:S(2)}, u32[]{:S(2)}) collective-permute-start(bf16[240,768]{1,0:T(8,128)(2,1)S(1)} %pass_on.1), channel_id=1, source_target_pairs={{0,2},{1,3},{2,0},{3,1},{4,6},{5,7},{6,4},{7,5},{8,10},{9,11},{10,... | collective-permute-start | bytes 1105928 | tf_op jit(solution)/shard_map/ppermute | solution.py:688
  162.3 10.3 %collective-permute-start.52 = (bf16[240,768]{1,0:T(8,128)(2,1)S(1)}, bf16[240,768]{1,0:T(8,128)(2,1)S(1)}, u32[]{:S(2)}, u32[]{:S(2)}) collective-permute-start(bf16[240,768]{1,0:T(8,128)(2,1)S(1)} %shares.1.refs_1_), channel_id=1, source_target_pairs={{0,1},{1,0},{2,3},{3,2},{4,5},{5,4},{6,7},{7,6},{8,9},{9,8},{10,11... | collective-permute-start | bytes 1105928 | tf_op jit(solution)/shard_map/ppermute | solution.py:685
  162.4 10.2 %collective-permute-start.54 = (bf16[240,768]{1,0:T(8,128)(2,1)S(1)}, bf16[240,768]{1,0:T(8,128)(2,1)S(1)}, u32[]{:S(2)}, u32[]{:S(2)}) collective-permute-start(bf16[240,768]{1,0:T(8,128)(2,1)S(1)} %collective-permute-done.46.refs_0_.refs_3_), channel_id=1, source_target_pairs={{0,1},{1,0},{2,3},{3,2},{4,5},{5,4},{6,7},{7,6},{8,9},{9,8},{10,11... | collective-permute-start | bytes 1105928 | tf_op jit(solution)/shard_map/ppermute | solution.py:685
  162.9 9.7 %collective-permute-start.53 = (bf16[240,768]{1,0:T(8,128)(2,1)S(1)}, bf16[240,768]{1,0:T(8,128)(2,1)S(1)}, u32[]{:S(2)}, u32[]{:S(2)}) collective-permute-start(bf16[240,768]{1,0:T(8,128)(2,1)S(1)} %collective-permute-done.45.refs_3_.refs_2_), channel_id=1, source_target_pairs={{0,1},{1,0},{2,3},{3,2},{4,5},{5,4},{6,7},{7,6},{8,9},{9,8},{10,11... | collective-permute-start | bytes 1105928 | tf_op jit(solution)/shard_map/ppermute | solution.py:685
  172.6 1.7 collective-permute-start.55
  (2 other events, 9.3 us)
